TPU v7x, 32 devices: a whole 2x2x4 slice. The times are simulated.
32 devices in a mesh: groups: 2 (over x), samp: 16 (over z, y, core).
Axes of the slice: x: 2, y: 2, z: 4, core: 2. Of those that a mesh axis runs over, the one named last changes fastest.
Arguments:
- samples: int32 [32, 32768], P('groups', 'samp'), parts along dimension 0, may hold values from 0 to 65520
- generator: int32 [16], replicated, may hold values from 1 to 65520
- weight_index: int32 [16], replicated, may hold values from 0 to 7
- preconditioner: float32 [1024, 1024], P('samp'), may hold values from -2 to 2, as said below
- solution: float32 [32, 1024], P('groups', 'samp'), parts along dimension 0, may hold values from -24 to 24
- residual: float32 [32, 1024], P('groups', 'samp'), parts along dimension 0, may hold values from -24 to 24
- direction: float32 [32, 1024], P('groups', 'samp'), parts along dimension 0, may hold values from -24 to 24
Outputs:
- new_solution: float32 [32, 1024], P('groups', 'samp'), parts along dimension 0
- new_residual: float32 [32, 1024], P('groups', 'samp'), parts along dimension 0
- new_direction: float32 [32, 1024], P('groups', 'samp'), parts along dimension 0
There are 2 independent parts, one for each index of `groups`. A program takes and returns all parts, laid end to end along the dimension named above; an argument that names none is the same for every part. Nothing has to cross between parts.
Inputs may be any that keep to these rules, and one draw needn't show every extreme that they name: generator entries are nonzero residues of the prime 65521. `weight_index`: weight indices select gamma = 0.5 * 0.75 ** index. `preconditioner`: upper triangular, diagonal between 1 and 2.
All inputs are finite; a program needn't handle non-finite values.
Results may differ from a plain program's by a relative error of at most 0.0003.
Values sent between devices are 32-bit elements; how exact they have to be, the bound alone decides.
No kernel may reach another device: no remote copies, remote signals or barrier semaphores. Data moves between devices by JAX's collectives and lax.ppermute only.
A program may use at most 64 MiB of HBM per device.

v0:
```python
import math

import jax
import jax.numpy as jnp
from jax import lax
from jax.sharding import PartitionSpec as P

LATTICE = 65521


ridge_weight = 0.25
bernoulli_factor = 2.0 * math.pi * math.pi


def centre_coords(lattice_index, generator):
    upper_digits = generator // 256
    lower_digits = generator % 256
    column = lattice_index[None, :]
    partial_value = column * upper_digits[:, None] % LATTICE
    return (partial_value * 256 + column * lower_digits[:, None]) % LATTICE


def kernel_block(left_points, right_points, weights_dim):
    product = jnp.ones((left_points.shape[1], right_points.shape[1]), jnp.float32)
    for axis_number in range(left_points.shape[0]):
        offset = (left_points[axis_number][:, None] - right_points[axis_number][None, :]) % LATTICE
        fraction = offset.astype(jnp.float32) / LATTICE
        product = product * (
            1.0
            + weights_dim[axis_number]
            * bernoulli_factor
            * (fraction * fraction - fraction + 1.0 / 6.0)
        )
    return product


def contract_last(left_array, right_array):
    return lax.dot_general(
        left_array,
        right_array,
        (((1,), (1,)), ((), ())),
        precision=lax.Precision.HIGHEST,
        preferred_element_type=jnp.float32,
    )


def body(samples, generator, weight_index, preconditioner, solution, residual, direction):
    highest = lax.Precision.HIGHEST
    devices = lax.axis_size("samp")
    cen_dev = preconditioner.shape[0]
    centres_all = preconditioner.shape[1]
    samples_dev = samples.shape[1]
    weights_dim = 0.5 * jnp.power(0.75, weight_index.astype(jnp.float32))
    centres = centre_coords(jnp.arange(centres_all, dtype=jnp.int32), generator)
    direction_full = lax.all_gather(direction, "samp", axis=1, tiled=True)
    coef_rows = contract_last(direction_full, preconditioner)
    coefficients = lax.all_gather(coef_rows, "samp", axis=1, tiled=True)
    first_row = lax.axis_index("samp") * cen_dev
    own_centres = lax.dynamic_slice_in_dim(centres, first_row, cen_dev, 1)
    kernel_own = kernel_block(own_centres, centres, weights_dim)
    kernel_products = contract_last(coefficients, kernel_own)
    block_rows = min(128, samples_dev)
    turns = samples_dev // block_rows

    def accumulate(step_index, backward):
        points = lax.dynamic_slice_in_dim(samples, step_index * block_rows, block_rows, 1)
        kernel_rows = kernel_block(points, centres, weights_dim)
        fitted = contract_last(coefficients, kernel_rows)
        return backward + jnp.dot(
            fitted, kernel_rows, precision=highest, preferred_element_type=jnp.float32
        )

    backward = lax.fori_loop(
        0, turns, accumulate, jnp.zeros((direction.shape[0], centres_all), jnp.float32)
    )
    summed = lax.psum(backward, "samp")
    backward_rows = lax.dynamic_slice_in_dim(summed, first_row, cen_dev, 1)
    scale_total = float(samples_dev * devices) * float(centres_all)
    applied = backward_rows / scale_total + ridge_weight * kernel_products / centres_all
    partial_image = jnp.dot(
        applied, preconditioner, precision=highest, preferred_element_type=jnp.float32
    )
    image_rows = lax.psum_scatter(partial_image, "samp", scatter_dimension=1, tiled=True)
    norm_old = lax.psum(jnp.sum(residual * residual, axis=1), "samp")
    curvature = lax.psum(jnp.sum(direction * image_rows, axis=1), "samp")
    step_length = norm_old / curvature
    new_residual = residual - step_length[:, None] * image_rows
    norm_new = lax.psum(jnp.sum(new_residual * new_residual, axis=1), "samp")
    new_solution = solution + step_length[:, None] * direction
    new_direction = new_residual + (norm_new / norm_old)[:, None] * direction
    return (new_solution, new_residual, new_direction)


def solution(mesh):
    placed = (
        P("groups", "samp"),
        P(),
        P(),
        P("samp", None),
        P("groups", "samp"),
        P("groups", "samp"),
        P("groups", "samp"),
    )
    return jax.shard_map(
        body,
        mesh=mesh,
        in_specs=placed,
        out_specs=(P("groups", "samp"), P("groups", "samp"), P("groups", "samp")),
        check_vma=False,
    )
```

profile of v0, /device:TPU:0, one launch (start us, length us, event | category | flops | bytes accessed | tf_op | source)
XLA Modules:
  0.0 416.5 jit_solution(17566179077706594592)
XLA Ops:
  7.2 0.6 copy-done.6
  7.9 0.7 fusion.360
  18.7 23.4 %all-gather = f32[16,64,16]{1,2,0:T(8,128)S(1)} all-gather(f32[1,64,16]{1,2,0:T(8,128)S(1)} %bitcast.194), channel_id=1, replica_groups=mesh['groups'=2,'samp'=16] {'samp'}, dimensions={0}, use_global_device_ids=true | all-gather | bytes 69632 | tf_op jit(solution)/shard_map/all_gather | solution.py:55
  42.6 17.8 %all-gather.1 = f32[16,64,16]{1,2,0:T(8,128)S(1)} all-gather(f32[1,64,16]{1,2,0:T(8,128)S(1)} %convolution_bitcast_fusion.1), channel_id=1, replica_groups=mesh['groups'=2,'samp'=16] {'samp'}, dimensions={0}, use_global_device_ids=true | all-gather | bytes 69632 | tf_op jit(solution)/shard_map/all_gather | solution.py:57
  60.7 140.6 %while.16 = (s32[]{:T(128)}, f32[16,1024]{1,0:T(8,128)S(1)}, f32[]{:T(128)}, s32[16,2048]{1,0:T(8,128)}, s32[16,1024]{1,0:T(8,128)S(1)}, /*index=5*/f32[]{:T(128...) while((s32[]{:T(128)}, f32[16,1024]{1,0:T(8,128)S(1)}, ...), condition=%wide.region_3.4_spmd.clone, body=%wide.region_2.3_spmd.clone.sunk | while | flops 81690640 | bytes 2007745 | solution.py:73
  60.7 1.1 dynamic-slice_bitcast_fusion.33
  61.9 6.7 %fusion.383 = f32[128,1024]{1,0:T(8,128)S(1)} fusion(s32[1024]{0:T(1024)S(1)} %bitcast.179, s32[128]{0:T(128)S(1)} %get-tuple-element.594, f32[]{:T(128)} %get-tuple-element.724, s32[1024]{0:T(1024)S(1)} %bitcast.180, s32[128]{0:T(128)S(1)} %get-tuple-element.596, f32[]{:T(128)} %get-tuple-element.723, s32[1024]{0:T(1024)S(1)} %bitcast.181, ...), kind=kLoop, calls=%fused_computation.52.clone.1 | loop fusion | flops 31326208 | bytes 598080 | tf_op jit(solution)/shard_map/while/body/eval_jaxpr/mul | solution.py:28
  68.6 0.5 fusion.384
  69.5 1.1 dynamic-slice_bitcast_fusion.33
  70.7 6.7 %fusion.383 = f32[128,1024]{1,0:T(8,128)S(1)} fusion(s32[1024]{0:T(1024)S(1)} %bitcast.179, s32[128]{0:T(128)S(1)} %get-tuple-element.594, f32[]{:T(128)} %get-tuple-element.724, s32[1024]{0:T(1024)S(1)} %bitcast.180, s32[128]{0:T(128)S(1)} %get-tuple-element.596, f32[]{:T(128)} %get-tuple-element.723, s32[1024]{0:T(1024)S(1)} %bitcast.181, ...), kind=kLoop, calls=%fused_computation.52.clone.1 | loop fusion | flops 31326208 | bytes 598080 | tf_op jit(solution)/shard_map/while/body/eval_jaxpr/mul | solution.py:28
  77.4 0.5 fusion.384
  77.9 0.4 convolution_add_fusion.2
  78.3 1.1 dynamic-slice_bitcast_fusion.33
  79.5 6.7 %fusion.383 = f32[128,1024]{1,0:T(8,128)S(1)} fusion(s32[1024]{0:T(1024)S(1)} %bitcast.179, s32[128]{0:T(128)S(1)} %get-tuple-element.594, f32[]{:T(128)} %get-tuple-element.724, s32[1024]{0:T(1024)S(1)} %bitcast.180, s32[128]{0:T(128)S(1)} %get-tuple-element.596, f32[]{:T(128)} %get-tuple-element.723, s32[1024]{0:T(1024)S(1)} %bitcast.181, ...), kind=kLoop, calls=%fused_computation.52.clone.1 | loop fusion | flops 31326208 | bytes 598080 | tf_op jit(solution)/shard_map/while/body/eval_jaxpr/mul | solution.py:28
  86.2 0.5 fusion.384
  86.7 0.4 convolution_add_fusion.2
  87.1 1.1 dynamic-slice_bitcast_fusion.33
  88.3 6.7 %fusion.383 = f32[128,1024]{1,0:T(8,128)S(1)} fusion(s32[1024]{0:T(1024)S(1)} %bitcast.179, s32[128]{0:T(128)S(1)} %get-tuple-element.594, f32[]{:T(128)} %get-tuple-element.724, s32[1024]{0:T(1024)S(1)} %bitcast.180, s32[128]{0:T(128)S(1)} %get-tuple-element.596, f32[]{:T(128)} %get-tuple-element.723, s32[1024]{0:T(1024)S(1)} %bitcast.181, ...), kind=kLoop, calls=%fused_computation.52.clone.1 | loop fusion | flops 31326208 | bytes 598080 | tf_op jit(solution)/shard_map/while/body/eval_jaxpr/mul | solution.py:28
  95.0 0.5 fusion.384
  95.9 1.1 dynamic-slice_bitcast_fusion.33
  97.1 6.7 %fusion.383 = f32[128,1024]{1,0:T(8,128)S(1)} fusion(s32[1024]{0:T(1024)S(1)} %bitcast.179, s32[128]{0:T(128)S(1)} %get-tuple-element.594, f32[]{:T(128)} %get-tuple-element.724, s32[1024]{0:T(1024)S(1)} %bitcast.180, s32[128]{0:T(128)S(1)} %get-tuple-element.596, f32[]{:T(128)} %get-tuple-element.723, s32[1024]{0:T(1024)S(1)} %bitcast.181, ...), kind=kLoop, calls=%fused_computation.52.clone.1 | loop fusion | flops 31326208 | bytes 598080 | tf_op jit(solution)/shard_map/while/body/eval_jaxpr/mul | solution.py:28
  103.8 0.5 fusion.384
  104.7 1.1 dynamic-slice_bitcast_fusion.33
  105.9 6.7 %fusion.383 = f32[128,1024]{1,0:T(8,128)S(1)} fusion(s32[1024]{0:T(1024)S(1)} %bitcast.179, s32[128]{0:T(128)S(1)} %get-tuple-element.594, f32[]{:T(128)} %get-tuple-element.724, s32[1024]{0:T(1024)S(1)} %bitcast.180, s32[128]{0:T(128)S(1)} %get-tuple-element.596, f32[]{:T(128)} %get-tuple-element.723, s32[1024]{0:T(1024)S(1)} %bitcast.181, ...), kind=kLoop, calls=%fused_computation.52.clone.1 | loop fusion | flops 31326208 | bytes 598080 | tf_op jit(solution)/shard_map/while/body/eval_jaxpr/mul | solution.py:28
  112.6 0.5 fusion.384
  113.5 1.1 dynamic-slice_bitcast_fusion.33
  114.7 6.7 %fusion.383 = f32[128,1024]{1,0:T(8,128)S(1)} fusion(s32[1024]{0:T(1024)S(1)} %bitcast.179, s32[128]{0:T(128)S(1)} %get-tuple-element.594, f32[]{:T(128)} %get-tuple-element.724, s32[1024]{0:T(1024)S(1)} %bitcast.180, s32[128]{0:T(128)S(1)} %get-tuple-element.596, f32[]{:T(128)} %get-tuple-element.723, s32[1024]{0:T(1024)S(1)} %bitcast.181, ...), kind=kLoop, calls=%fused_computation.52.clone.1 | loop fusion | flops 31326208 | bytes 598080 | tf_op jit(solution)/shard_map/while/body/eval_jaxpr/mul | solution.py:28
  121.4 0.5 fusion.384
  122.3 1.1 dynamic-slice_bitcast_fusion.33
  123.5 6.7 %fusion.383 = f32[128,1024]{1,0:T(8,128)S(1)} fusion(s32[1024]{0:T(1024)S(1)} %bitcast.179, s32[128]{0:T(128)S(1)} %get-tuple-element.594, f32[]{:T(128)} %get-tuple-element.724, s32[1024]{0:T(1024)S(1)} %bitcast.180, s32[128]{0:T(128)S(1)} %get-tuple-element.596, f32[]{:T(128)} %get-tuple-element.723, s32[1024]{0:T(1024)S(1)} %bitcast.181, ...), kind=kLoop, calls=%fused_computation.52.clone.1 | loop fusion | flops 31326208 | bytes 598080 | tf_op jit(solution)/shard_map/while/body/eval_jaxpr/mul | solution.py:28
  130.1 0.5 fusion.384
  131.1 1.1 dynamic-slice_bitcast_fusion.33
  132.3 6.7 %fusion.383 = f32[128,1024]{1,0:T(8,128)S(1)} fusion(s32[1024]{0:T(1024)S(1)} %bitcast.179, s32[128]{0:T(128)S(1)} %get-tuple-element.594, f32[]{:T(128)} %get-tuple-element.724, s32[1024]{0:T(1024)S(1)} %bitcast.180, s32[128]{0:T(128)S(1)} %get-tuple-element.596, f32[]{:T(128)} %get-tuple-element.723, s32[1024]{0:T(1024)S(1)} %bitcast.181, ...), kind=kLoop, calls=%fused_computation.52.clone.1 | loop fusion | flops 31326208 | bytes 598080 | tf_op jit(solution)/shard_map/while/body/eval_jaxpr/mul | solution.py:28
  138.9 0.5 fusion.384
  139.8 1.1 dynamic-slice_bitcast_fusion.33
  141.0 6.7 %fusion.383 = f32[128,1024]{1,0:T(8,128)S(1)} fusion(s32[1024]{0:T(1024)S(1)} %bitcast.179, s32[128]{0:T(128)S(1)} %get-tuple-element.594, f32[]{:T(128)} %get-tuple-element.724, s32[1024]{0:T(1024)S(1)} %bitcast.180, s32[128]{0:T(128)S(1)} %get-tuple-element.596, f32[]{:T(128)} %get-tuple-element.723, s32[1024]{0:T(1024)S(1)} %bitcast.181, ...), kind=kLoop, calls=%fused_computation.52.clone.1 | loop fusion | flops 31326208 | bytes 598080 | tf_op jit(solution)/shard_map/while/body/eval_jaxpr/mul | solution.py:28
  147.7 0.5 fusion.384
  148.6 1.1 dynamic-slice_bitcast_fusion.33
  149.8 6.7 %fusion.383 = f32[128,1024]{1,0:T(8,128)S(1)} fusion(s32[1024]{0:T(1024)S(1)} %bitcast.179, s32[128]{0:T(128)S(1)} %get-tuple-element.594, f32[]{:T(128)} %get-tuple-element.724, s32[1024]{0:T(1024)S(1)} %bitcast.180, s32[128]{0:T(128)S(1)} %get-tuple-element.596, f32[]{:T(128)} %get-tuple-element.723, s32[1024]{0:T(1024)S(1)} %bitcast.181, ...), kind=kLoop, calls=%fused_computation.52.clone.1 | loop fusion | flops 31326208 | bytes 598080 | tf_op jit(solution)/shard_map/while/body/eval_jaxpr/mul | solution.py:28
  156.5 0.5 fusion.384
  157.4 1.1 dynamic-slice_bitcast_fusion.33
  158.6 6.7 %fusion.383 = f32[128,1024]{1,0:T(8,128)S(1)} fusion(s32[1024]{0:T(1024)S(1)} %bitcast.179, s32[128]{0:T(128)S(1)} %get-tuple-element.594, f32[]{:T(128)} %get-tuple-element.724, s32[1024]{0:T(1024)S(1)} %bitcast.180, s32[128]{0:T(128)S(1)} %get-tuple-element.596, f32[]{:T(128)} %get-tuple-element.723, s32[1024]{0:T(1024)S(1)} %bitcast.181, ...), kind=kLoop, calls=%fused_computation.52.clone.1 | loop fusion | flops 31326208 | bytes 598080 | tf_op jit(solution)/shard_map/while/body/eval_jaxpr/mul | solution.py:28
  165.3 0.5 fusion.384
  166.2 1.1 dynamic-slice_bitcast_fusion.33
  167.4 6.7 %fusion.383 = f32[128,1024]{1,0:T(8,128)S(1)} fusion(s32[1024]{0:T(1024)S(1)} %bitcast.179, s32[128]{0:T(128)S(1)} %get-tuple-element.594, f32[]{:T(128)} %get-tuple-element.724, s32[1024]{0:T(1024)S(1)} %bitcast.180, s32[128]{0:T(128)S(1)} %get-tuple-element.596, f32[]{:T(128)} %get-tuple-element.723, s32[1024]{0:T(1024)S(1)} %bitcast.181, ...), kind=kLoop, calls=%fused_computation.52.clone.1 | loop fusion | flops 31326208 | bytes 598080 | tf_op jit(solution)/shard_map/while/body/eval_jaxpr/mul | solution.py:28
  174.1 0.5 fusion.384
  175.0 1.1 dynamic-slice_bitcast_fusion.33
  176.2 6.7 %fusion.383 = f32[128,1024]{1,0:T(8,128)S(1)} fusion(s32[1024]{0:T(1024)S(1)} %bitcast.179, s32[128]{0:T(128)S(1)} %get-tuple-element.594, f32[]{:T(128)} %get-tuple-element.724, s32[1024]{0:T(1024)S(1)} %bitcast.180, s32[128]{0:T(128)S(1)} %get-tuple-element.596, f32[]{:T(128)} %get-tuple-element.723, s32[1024]{0:T(1024)S(1)} %bitcast.181, ...), kind=kLoop, calls=%fused_computation.52.clone.1 | loop fusion | flops 31326208 | bytes 598080 | tf_op jit(solution)/shard_map/while/body/eval_jaxpr/mul | solution.py:28
  182.9 0.5 fusion.384
  183.8 1.1 dynamic-slice_bitcast_fusion.33
  185.0 6.7 %fusion.383 = f32[128,1024]{1,0:T(8,128)S(1)} fusion(s32[1024]{0:T(1024)S(1)} %bitcast.179, s32[128]{0:T(128)S(1)} %get-tuple-element.594, f32[]{:T(128)} %get-tuple-element.724, s32[1024]{0:T(1024)S(1)} %bitcast.180, s32[128]{0:T(128)S(1)} %get-tuple-element.596, f32[]{:T(128)} %get-tuple-element.723, s32[1024]{0:T(1024)S(1)} %bitcast.181, ...), kind=kLoop, calls=%fused_computation.52.clone.1 | loop fusion | flops 31326208 | bytes 598080 | tf_op jit(solution)/shard_map/while/body/eval_jaxpr/mul | solution.py:28
  191.7 0.5 fusion.384
  192.6 1.1 dynamic-slice_bitcast_fusion.33
  193.8 6.7 %fusion.383 = f32[128,1024]{1,0:T(8,128)S(1)} fusion(s32[1024]{0:T(1024)S(1)} %bitcast.179, s32[128]{0:T(128)S(1)} %get-tuple-element.594, f32[]{:T(128)} %get-tuple-element.724, s32[1024]{0:T(1024)S(1)} %bitcast.180, s32[128]{0:T(128)S(1)} %get-tuple-element.596, f32[]{:T(128)} %get-tuple-element.723, s32[1024]{0:T(1024)S(1)} %bitcast.181, ...), kind=kLoop, calls=%fused_computation.52.clone.1 | loop fusion | flops 31326208 | bytes 598080 | tf_op jit(solution)/shard_map/while/body/eval_jaxpr/mul | solution.py:28
  200.5 0.5 fusion.384
  201.4 0.6 copy-done.1
  202.5 82.6 %all-reduce.3.cloned.1.call-done = f32[16,1024]{1,0:T(8,128)} async-done(((f32[16,1024]{1,0:T(8,128)}), f32[16,1024]{1,0:T(8,128)}) %all-reduce.3.cloned.1.call-update) | async-done | bytes 65552 | tf_op jit(solution)/shard_map/psum | solution.py:76
  285.1 4.3 %fusion.143 = f32[16,64]{1,0:T(8,128)S(1)} fusion(f32[1024,16]{0,1:T(8,128)S(1)} %bitcast.177, s32[1024]{0:T(1024)S(1)} %bitcast.197, s32[64]{0:T(128)S(1)} %get-tuple-element.395, f32[]{:T(128)} %bitcast.15, s32[1024]{0:T(1024)S(1)} %bitcast.198, s32[64]{0:T(128)S(1)} %get-tuple-element.381, f32[]{:T(128)} %bitcast.14, s32[1024]{0:T(1024)S(1)} %bitcast.199, ...), kind=kOutput, calls=%fused_computation.210 | convolution fusion | flops 28249088 | bytes 143428 | tf_op jit(solution)/shard_map/dot_general | solution.py:38
  289.4 1.8 convolution_bitcast_fusion
  291.2 57.5 %reduce-scatter.4.cloned.1.call-done = f32[64,16]{1,0:T(8,128)} async-done(((f32[1024,16]{1,0:T(8,128)}), f32[64,16]{1,0:T(8,128)}) %reduce-scatter.4.cloned.1.call-update) | async-done | bytes 4112
  348.7 0.8 copy.15
  349.7 29.6 %all-reduce = (f32[16]{0:T(128)S(1)}, f32[16]{0:T(128)S(1)}) all-reduce(f32[16]{0:T(128)S(1)} %get-tuple-element.433, f32[16]{0:T(128)S(1)} %get-tuple-element.432), channel_id=1, replica_groups=mesh['groups'=2,'samp'=16] {'samp'}, use_global_device_ids=true, to_apply=%region_1.2 | all-reduce | flops 32 | bytes 256 | tf_op jit(solution)/shard_map/psum | solution.py:84
  379.5 29.5 %psum.31 = f32[16]{0:T(128)S(1)} all-reduce(f32[16]{0:T(128)S(1)} %get-tuple-element.346), channel_id=1, replica_groups=mesh['groups'=2,'samp'=16] {'samp'}, use_global_device_ids=true, to_apply=%region_9.10 | all-reduce | flops 16 | bytes 128 | tf_op jit(solution)/shard_map/psum | solution.py:88
  409.0 0.7 multiply_add_fusion
  (63 shorter events, 7.7 us)
Async XLA Ops:
  7.2 35.1 %copy-start = (f32[64,1024]{1,0:T(8,128)S(1)}, f32[64,1024]{1,0:T(8,128)}, u32[]{:S(2)}) copy-start(f32[64,1024]{1,0:T(8,128)} %param.12) | copy-start | bytes 786436
  7.2 0.7 copy-start.6
  7.2 277.9 %all-reduce.3.cloned.1.call-start = ((), (), s32[]{:S(2)}) async-start(), calls=%async_computation.1 | async-start | bytes 131072 | tf_op jit(solution)/shard_map/psum | solution.py:76
  16.8 1.9 copy-start.2
  18.0 0.7 copy-start.7
  201.4 0.6 copy-start.1
  202.0 146.7 %reduce-scatter.4.cloned.1.call-start = ((), (), s32[]{:S(2)}) async-start(), calls=%async_computation.2 | async-start | bytes 557056
  348.7 0.8 copy-start.3
  379.3 29.7 %copy-start.5 = (f32[16,64]{1,0:T(8,128)S(1)}, f32[16,64]{1,0:T(8,128)}, u32[]{:S(2)}) copy-start(f32[16,64]{1,0:T(8,128)} %param.13) | copy-start | bytes 12292
  379.5 30.2 %copy-start.4 = (f32[16,64]{1,0:T(8,128)}, f32[16,64]{1,0:T(8,128)S(1)}, u32[]{:S(2)}) copy-start(f32[16,64]{1,0:T(8,128)S(1)} %get-tuple-element.347) | copy-start | bytes 12292
Sparse Core Ops, SparseCore 0:
  202.1 82.8 all-reduce.2
  291.3 57.3 reduce-scatter.3
where the time goes:
time: 418 us; the launch traced here: 417 us
  waiting for transfers between devices  140 us (33%)
  other arithmetic  108 us (26%)
  blocking collectives  100 us (24%)
  between operations  24.2 us (6%)
  local copies, waits for them, and re-layouts  22.3 us (5%)
  matrix products  20.7 us (5%)
    mul x16, other arithmetic, kernel_block(): product * (1.0 + weights_dim[axis_number] * bernoulli_factor * (fraction...  107 us
    psum x1, waiting for transfers between devices, body(): summed = lax.psum(backward, 'samp')  82.6 us
    unnamed x3, waiting for transfers between devices  57.5 us
    psum x1, blocking collectives, body(): norm_old = lax.psum(jnp.sum(residual * residual, axis=1), 'samp')  29.6 us
    psum x1, blocking collectives, body(): norm_new = lax.psum(jnp.sum(new_residual * new_residual, axis=1), 'samp')  29.5 us
    all_gather x1, blocking collectives, body(): direction_full = lax.all_gather(direction, 'samp', axis=1, tiled=True)  23.4 us
    sub x17, local copies, waits for them, and re-layouts, kernel_block(): left_points[axis_number][:, None] - right_points[axis_number][None, :]  18.3 us
    all_gather x1, blocking collectives, body(): coefficients = lax.all_gather(coef_rows, 'samp', axis=1, tiled=True)  17.8 us
  transfers between devices with their start and end apart: 2, of which 2 were waited for; matrix products, arithmetic and copies ran while one was open for 0% of the time, Pallas kernels for 0%

commit v1 on v0

v1 whole, which is shorter than its diff:
```python
import functools
import math

import jax
import jax.numpy as jnp
from jax import lax
from jax.experimental import pallas as pl
from jax.experimental.pallas import tpu as pltpu
from jax.sharding import PartitionSpec as P

LATTICE = 65521

ridge_weight = 0.25
VMEM_BYTES = 48 << 20
STORE_BYTES = 12 << 20
F32 = jnp.float32
BF16 = jnp.bfloat16


def centre_coords(lattice_index, generator):
    upper_digits = generator // 256
    lower_digits = generator % 256
    column = lattice_index[None, :]
    partial_value = column * upper_digits[:, None] % LATTICE
    return (partial_value * 256 + column * lower_digits[:, None]) % LATTICE


def swap(value, bit, devices):
    return lax.ppermute(value, "samp", [(i, i ^ bit) for i in range(devices)])


def reduce_all(value, devices):
    bit = 1
    while bit < devices:
        value = value + swap(value, bit, devices)
        bit *= 2
    return value


def gather_all(value, devices, index):
    bit = 1
    while bit < devices:
        other = swap(value, bit, devices)
        upper = (index & bit) != 0
        value = jnp.where(
            upper,
            jnp.concatenate([other, value], axis=1),
            jnp.concatenate([value, other], axis=1),
        )
        bit *= 2
    return value


def split3(value):
    high = value.astype(BF16)
    rest = value - high.astype(F32)
    middle = rest.astype(BF16)
    low = (rest - middle.astype(F32)).astype(BF16)
    return high, middle, low


def kernel_tile(points, centre_ref, shift_ref, floor_ref, first, width):
    rows, dims = points.shape
    product = None
    for axis_number in range(dims):
        centre = centre_ref[axis_number : axis_number + 1, pl.ds(first, width)]
        point = jnp.broadcast_to(points[:, axis_number : axis_number + 1], (rows, width))
        arm = jnp.abs(point - centre) - shift_ref[axis_number]
        factor = arm * arm + floor_ref[axis_number]
        product = factor if product is None else product * factor
    return product


def fill_kernel(rows, points, centre_ref, shift_ref, floor_ref, high_ref, low_ref):
    centres_all = centre_ref.shape[1]
    width = min(512, centres_all)
    span = min(1024, centres_all)

    def part(base):
        for piece in range(span // width):
            first = base + piece * width
            if not isinstance(first, int):
                first = pl.multiple_of(first, width)
            tile = kernel_tile(points, centre_ref, shift_ref, floor_ref, first, width)
            high = tile.astype(BF16)
            high_ref[rows, pl.ds(first, width)] = high
            low_ref[rows, pl.ds(first, width)] = (tile - high.astype(F32)).astype(BF16)

    if centres_all == span:
        part(0)
    else:
        lax.fori_loop(0, centres_all // span, lambda i, _: part(i * span), None)


def generate(step_rows, shift_ref, floor_ref, scale_ref, sample_ref, centre_ref, high_ref, low_ref):
    for step in range(sample_ref.shape[1] // step_rows):
        rows = pl.ds(step * step_rows, step_rows)
        points = (sample_ref[:, rows].astype(F32) * scale_ref[...]).T
        fill_kernel(rows, points, centre_ref, shift_ref, floor_ref, high_ref, low_ref)


def kernel_rows(samples, first_block, blocks, block_rows, centre_scaled, shift, floor, scale):
    dims, centres_all = centre_scaled.shape
    rows = blocks * block_rows
    smem = pl.BlockSpec(memory_space=pltpu.SMEM)
    return pl.pallas_call(
        functools.partial(generate, 128),
        grid=(blocks,),
        in_specs=[
            smem,
            smem,
            pl.BlockSpec((dims, 1), lambda i: (0, 0)),
            pl.BlockSpec((dims, block_rows), lambda i: (0, first_block + i)),
            pl.BlockSpec((dims, centres_all), lambda i: (0, 0)),
        ],
        out_specs=[pl.BlockSpec((block_rows, centres_all), lambda i: (i, 0))] * 2,
        out_shape=[jax.ShapeDtypeStruct((rows, centres_all), BF16)] * 2,
        compiler_params=pltpu.CompilerParams(vmem_limit_bytes=VMEM_BYTES),
        cost_estimate=pl.CostEstimate(
            flops=6 * dims * rows * centres_all,
            bytes_accessed=4 * rows * centres_all,
            transcendentals=0,
        ),
        name="kernel_rows",
    )(shift, floor, scale, samples, centre_scaled)


def apply_kernel(high, low, coefficients, outs):
    contract = (((1,), (1,)), ((), ()))
    fitted = lax.dot_general(coefficients, high, contract, preferred_element_type=F32)
    fitted = fitted + lax.dot_general(coefficients, low, contract, preferred_element_type=F32)
    return fitted[0:outs] + (fitted[outs : 2 * outs] + fitted[2 * outs : 3 * outs])


def products(
    outs, step_rows, shift_ref, floor_ref, coef_ref, own_ref, centre_ref, first_ref, second_ref,
    backward_ref, own_out_ref, parts_ref, sum_ref, own_high_ref, own_low_ref, *made,
):
    step = pl.program_id(0)
    if made:
        high_ref, low_ref = made
        generate(step_rows, shift_ref, floor_ref, second_ref, first_ref, centre_ref, high_ref, low_ref)
    else:
        high_ref, low_ref = first_ref, second_ref

    @pl.when(step == 0)
    def _():
        high, middle, low = split3(coef_ref[...])
        parts_ref[0:outs] = high
        parts_ref[outs : 2 * outs] = middle
        parts_ref[2 * outs : 3 * outs] = low
        sum_ref[...] = jnp.zeros_like(sum_ref)
        rows = pl.ds(0, own_ref.shape[1])
        fill_kernel(
            rows, own_ref[...].T, centre_ref, shift_ref, floor_ref, own_high_ref, own_low_ref
        )
        own_out_ref[...] = apply_kernel(
            own_high_ref[...], own_low_ref[...], parts_ref[...], outs
        )

    fitted = apply_kernel(high_ref[...], low_ref[...], parts_ref[...], outs)
    parts = jnp.concatenate(split3(fitted), axis=0)
    sum_ref[...] += jnp.dot(parts, high_ref[...], preferred_element_type=F32) + jnp.dot(
        parts, low_ref[...], preferred_element_type=F32
    )

    @pl.when(step == pl.num_programs(0) - 1)
    def _():
        backward_ref[...] = sum_ref[0:outs] + (
            sum_ref[outs : 2 * outs] + sum_ref[2 * outs : 3 * outs]
        )


def apply_products(
    first, second, coefficients, own_scaled, centre_scaled, shift, floor, block_rows, stored
):
    outs, centres_all = coefficients.shape
    dims, own_rows = own_scaled.shape
    rows = first.shape[0] if stored else first.shape[1]
    smem = pl.BlockSpec(memory_space=pltpu.SMEM)

    def whole(shape):
        return pl.BlockSpec(shape, lambda i: (0, 0))

    if stored:
        sources = [pl.BlockSpec((block_rows, centres_all), lambda i: (i, 0))] * 2
        made = []
    else:
        sources = [pl.BlockSpec((dims, block_rows), lambda i: (0, i)), whole((dims, 1))]
        made = [pltpu.VMEM((block_rows, centres_all), BF16)] * 2

    return pl.pallas_call(
        functools.partial(products, outs, 128),
        grid=(rows // block_rows,),
        in_specs=[
            smem,
            smem,
            whole((outs, centres_all)),
            whole((dims, own_rows)),
            whole((dims, centres_all)),
            *sources,
        ],
        out_specs=[whole((outs, centres_all)), whole((outs, own_rows))],
        out_shape=[
            jax.ShapeDtypeStruct((outs, centres_all), F32),
            jax.ShapeDtypeStruct((outs, own_rows), F32),
        ],
        scratch_shapes=[
            pltpu.VMEM((3 * outs, centres_all), BF16),
            pltpu.VMEM((3 * outs, centres_all), F32),
            pltpu.VMEM((own_rows, centres_all), BF16),
            pltpu.VMEM((own_rows, centres_all), BF16),
            *made,
        ],
        compiler_params=pltpu.CompilerParams(vmem_limit_bytes=VMEM_BYTES),
        cost_estimate=pl.CostEstimate(
            flops=24 * outs * rows * centres_all,
            bytes_accessed=4 * rows * centres_all,
            transcendentals=0,
        ),
        name="products",
    )(shift, floor, coefficients, own_scaled, centre_scaled, first, second)


def contract_last(left_array, right_array):
    return lax.dot_general(
        left_array,
        right_array,
        (((1,), (1,)), ((), ())),
        precision=lax.Precision.HIGHEST,
        preferred_element_type=F32,
    )


def body(samples, generator, weight_index, preconditioner, solution, residual, direction):
    highest = lax.Precision.HIGHEST
    devices = lax.axis_size("samp")
    index = lax.axis_index("samp")
    cen_dev, centres_all = preconditioner.shape
    samples_dev = samples.shape[1]
    outs = direction.shape[0]

    weights_dim = 0.5 * jnp.power(0.75, weight_index.astype(F32))
    curve = 2.0 * math.pi * math.pi * weights_dim
    floor = 1.0 - curve / 12.0
    root = jnp.sqrt(curve)
    shift = 0.5 * root
    scale = (root / LATTICE)[:, None]
    centres = centre_coords(jnp.arange(centres_all, dtype=jnp.int32), generator)
    first_row = index * cen_dev
    own = lax.dynamic_slice_in_dim(centres, first_row, cen_dev, 1)
    centre_scaled = centres.astype(F32) * scale
    own_scaled = own.astype(F32) * scale

    state = gather_all(jnp.concatenate([direction, residual], axis=0), devices, index)
    direction_full, residual_full = state[:outs], state[outs:]
    coef_rows = contract_last(direction_full, preconditioner)
    coefficients = gather_all(coef_rows, devices, index)

    block_rows = 256
    stored = 4 * samples_dev * centres_all <= STORE_BYTES
    if stored:
        first, second = kernel_rows(
            samples, 0, samples_dev // block_rows, block_rows, centre_scaled, shift, floor, scale
        )
    else:
        first, second = samples, scale
    backward, kernel_products = apply_products(
        first, second, coefficients, own_scaled, centre_scaled, shift, floor, block_rows, stored
    )
    summed = reduce_all(backward, devices)
    backward_rows = lax.dynamic_slice_in_dim(summed, first_row, cen_dev, 1)
    scale_total = float(samples_dev * devices) * float(centres_all)
    applied = backward_rows / scale_total + ridge_weight * kernel_products / centres_all
    partial_image = jnp.dot(applied, preconditioner, precision=highest, preferred_element_type=F32)
    image = reduce_all(partial_image, devices)

    norm_old = jnp.sum(residual_full * residual_full, axis=1, keepdims=True)
    curvature = jnp.sum(direction_full * image, axis=1, keepdims=True)
    step_length = norm_old / curvature
    next_full = residual_full - step_length * image
    norm_new = jnp.sum(next_full * next_full, axis=1, keepdims=True)
    new_residual = lax.dynamic_slice_in_dim(next_full, first_row, cen_dev, 1)
    new_solution = solution + step_length * direction
    new_direction = new_residual + (norm_new / norm_old) * direction
    return (new_solution, new_residual, new_direction)


def solution(mesh):
    placed = (
        P("groups", "samp"),
        P(),
        P(),
        P("samp", None),
        P("groups", "samp"),
        P("groups", "samp"),
        P("groups", "samp"),
    )
    return jax.shard_map(
        body,
        mesh=mesh,
        in_specs=placed,
        out_specs=(P("groups", "samp"), P("groups", "samp"), P("groups", "samp")),
        check_vma=False,
    )
```

time: 418 us -> 104 us (0.25)
  waiting for transfers between devices: 140 us -> 32.7 us
  other arithmetic: 108 us -> 2.98 us
  blocking collectives: 100 us -> 0 us
  Pallas kernels: 0 us -> 40.8 us
  between operations: 24.2 us -> 0.8 us
  starting transfers between devices: 0.26 us -> 23.4 us
  matrix products: 20.7 us -> 0.56 us
  local copies, waits for them, and re-layouts: 22.3 us -> 2.46 us
    mul x17 -> x2, other arithmetic: 107 us -> 0.22 us  [the longest x1 0.15 us: body(): centre_scaled = centres.astype(F32) * scale]
    psum x1 -> x0, waiting for transfers between devices: 82.6 us -> none  [body(): summed = lax.psum(backward, 'samp')]
    psum x2 -> x0, blocking collectives: 59.1 us -> none  [the longest x1 29.6 us: body(): norm_old = lax.psum(jnp.sum(residual * residual, axis=1), 'samp')]
    unnamed x3 -> x0, waiting for transfers between devices: 57.5 us -> none
    all_gather x2 -> x0, blocking collectives: 41.3 us -> none  [the longest x1 23.4 us: body(): direction_full = lax.all_gather(direction, 'samp', axis=1, tiled=True)]
    pallas_call x0 -> x2, Pallas kernels: none -> 40.8 us  [the longest x1 30.8 us: kernel_rows(): pl.pallas_call(functools.partial(generate, 128), grid=(blocks,), in_specs...]
    ppermute x0 -> x16, waiting for transfers between devices: none -> 32.7 us  [swap(): return lax.ppermute(value, 'samp', [(i, i ^ bit) for i in range(devices)])]
    ppermute x0 -> x16, starting transfers between devices: none -> 23.4 us  [swap(): return lax.ppermute(value, 'samp', [(i, i ^ bit) for i in range(devices)])]
  transfers between devices with their start and end apart: 2 -> 16, of which waited for: 2 -> 15; matrix products, arithmetic and copies ran while one was open for 0% -> 2% of each run, Pallas kernels for 0% -> 30%
where the time goes in v1:
time: 104 us
  Pallas kernels  40.8 us (39%)
  waiting for transfers between devices  32.7 us (31%)
  starting transfers between devices  23.4 us (22%)
  other arithmetic  2.98 us (3%)
  local copies, waits for them, and re-layouts  2.46 us (2%)
    ppermute x16, waiting for transfers between devices, swap(): return lax.ppermute(value, 'samp', [(i, i ^ bit) for i in range(devices)])  32.7 us
    pallas_call x1, Pallas kernels, kernel_rows(): pl.pallas_call(functools.partial(generate, 128), grid=(blocks,), in_specs...  30.8 us
    ppermute x16, starting transfers between devices, swap(): return lax.ppermute(value, 'samp', [(i, i ^ bit) for i in range(devices)])  23.4 us
    pallas_call x1, Pallas kernels, apply_products(): pl.pallas_call(functools.partial(products, outs, 128), grid=(rows // bloc...  10.1 us
  transfers between devices with their start and end apart: 16, of which 15 were waited for; matrix products, arithmetic and copies ran while one was open for 2% of the time, Pallas kernels for 30%

profile of v1, /device:TPU:0, one launch (start us, length us, event | category | flops | bytes accessed | tf_op | source)
XLA Modules:
  0.0 103.7 jit_solution(3636593431588164826)
XLA Ops:
  0.6 0.0 copy-start
  0.6 0.7 constant_dynamic-update-slice_fusion.1
  1.4 0.7 constant_dynamic-update-slice_fusion
  2.1 0.5 collective-permute-start
  2.5 0.8 collective-permute-done
  3.4 0.1 maximum_select_fusion.5
  3.5 2.9 %collective-permute-start.1 = (f32[32,128]{1,0:T(8,128)S(1)}, f32[32,128]{1,0:T(8,128)S(1)}, u32[]{:S(2)}, u32[]{:S(2)}) collective-permute-start(f32[32,128]{1,0:T(8,128)S(1)} %maximum_select_fusion.5), channel_id=1, source_target_pairs={{0,2},{1,3},{2,0},{3,1},{4,6},{5,7},{6,4},{7,5},{8,10},{9,11},{10,... | collective-permute-start | bytes 49160 | tf_op jit(solution)/shard_map/ppermute | solution.py:29
  6.3 1.7 %collective-permute-done.1 = f32[32,128]{1,0:T(8,128)S(1)} collective-permute-done((f32[32,128]{1,0:T(8,128)S(1)}, f32[32,128]{1,0:T(8,128)S(1)}, u32[]{:S(2)}, u32[]{:S(2)}) %collective-permute-start.1) | collective-permute-done | bytes 16416 | tf_op jit(solution)/shard_map/ppermute | solution.py:29
  8.0 2.1 %collective-permute-start.2 = (f32[32,256]{1,0:T(8,128)S(1)}, f32[32,256]{1,0:T(8,128)S(1)}, u32[]{:S(2)}, u32[]{:S(2)}) collective-permute-start(f32[32,256]{1,0:T(8,128)S(1)} %maximum_select_fusion.3), channel_id=1, source_target_pairs={{0,4},{1,5},{2,6},{3,7},{4,0},{5,1},{6,2},{7,3},{8,12},{9,13},{10,... | collective-permute-start | bytes 98312 | tf_op jit(solution)/shard_map/ppermute | solution.py:29
  10.1 1.9 %collective-permute-done.2 = f32[32,256]{1,0:T(8,128)S(1)} collective-permute-done((f32[32,256]{1,0:T(8,128)S(1)}, f32[32,256]{1,0:T(8,128)S(1)}, u32[]{:S(2)}, u32[]{:S(2)}) %collective-permute-start.2) | collective-permute-done | bytes 32800 | tf_op jit(solution)/shard_map/ppermute | solution.py:29
  12.0 3.1 %collective-permute-start.3 = (f32[32,512]{1,0:T(8,128)S(1)}, f32[32,512]{1,0:T(8,128)S(1)}, u32[]{:S(2)}, u32[]{:S(2)}) collective-permute-start(f32[32,512]{1,0:T(8,128)S(1)} %maximum_select_fusion.1), channel_id=1, source_target_pairs={{0,8},{1,9},{2,10},{3,11},{4,12},{5,13},{6,14},{7,15},{8,0},{9,1},... | collective-permute-start | bytes 196616 | tf_op jit(solution)/shard_map/ppermute | solution.py:29
  15.1 0.7 broadcast_multiply_fusion
  15.8 1.6 %collective-permute-done.3 = f32[32,512]{1,0:T(8,128)S(1)} collective-permute-done((f32[32,512]{1,0:T(8,128)S(1)}, f32[32,512]{1,0:T(8,128)S(1)}, u32[]{:S(2)}, u32[]{:S(2)}) %collective-permute-start.3) | collective-permute-done | bytes 65568 | tf_op jit(solution)/shard_map/ppermute | solution.py:29
  17.4 0.0 copy-done
  17.4 0.3 fusion.6
  17.7 0.0 collective-permute-start.4
  17.7 0.7 and_select_fusion.1
  18.4 0.5 collective-permute-done.4
  18.9 0.1 maximum_select_fusion.7
  19.0 1.9 %collective-permute-start.5 = (f32[16,128]{1,0:T(8,128)S(1)}, f32[16,128]{1,0:T(8,128)S(1)}, u32[]{:S(2)}, u32[]{:S(2)}) collective-permute-start(f32[16,128]{1,0:T(8,128)S(1)} %maximum_select_fusion.7), channel_id=1, source_target_pairs={{0,2},{1,3},{2,0},{3,1},{4,6},{5,7},{6,4},{7,5},{8,10},{9,11},{10,... | collective-permute-start | bytes 24584 | tf_op jit(solution)/shard_map/ppermute | solution.py:29
  20.8 0.1 convert_multiply_fusion.centre_ref
  21.0 1.6 %collective-permute-done.5 = f32[16,128]{1,0:T(8,128)S(1)} collective-permute-done((f32[16,128]{1,0:T(8,128)S(1)}, f32[16,128]{1,0:T(8,128)S(1)}, u32[]{:S(2)}, u32[]{:S(2)}) %collective-permute-start.5) | collective-permute-done | bytes 8224 | tf_op jit(solution)/shard_map/ppermute | solution.py:29
  22.6 1.9 %collective-permute-start.6 = (f32[16,256]{1,0:T(8,128)S(1)}, f32[16,256]{1,0:T(8,128)S(1)}, u32[]{:S(2)}, u32[]{:S(2)}) collective-permute-start(f32[16,256]{1,0:T(8,128)S(1)} %maximum_select_fusion.6), channel_id=1, source_target_pairs={{0,4},{1,5},{2,6},{3,7},{4,0},{5,1},{6,2},{7,3},{8,12},{9,13},{10,... | collective-permute-start | bytes 49160 | tf_op jit(solution)/shard_map/ppermute | solution.py:29
  24.5 0.2 add_select_fusion
  24.7 1.7 %collective-permute-done.6 = f32[16,256]{1,0:T(8,128)S(1)} collective-permute-done((f32[16,256]{1,0:T(8,128)S(1)}, f32[16,256]{1,0:T(8,128)S(1)}, u32[]{:S(2)}, u32[]{:S(2)}) %collective-permute-start.6) | collective-permute-done | bytes 16416 | tf_op jit(solution)/shard_map/ppermute | solution.py:29
  26.4 3.1 %collective-permute-start.7 = (f32[16,512]{1,0:T(8,128)S(1)}, f32[16,512]{1,0:T(8,128)S(1)}, u32[]{:S(2)}, u32[]{:S(2)}) collective-permute-start(f32[16,512]{1,0:T(8,128)S(1)} %maximum_select_fusion.4), channel_id=1, source_target_pairs={{0,8},{1,9},{2,10},{3,11},{4,12},{5,13},{6,14},{7,15},{8,0},{9,1},... | collective-permute-start | bytes 98312 | tf_op jit(solution)/shard_map/ppermute | solution.py:29
  29.4 0.1 convert_multiply_fusion.1.own_ref
  29.5 0.1 copy.10.scale_ref
  29.6 0.0 copy-start.1
  29.6 0.9 copy-done.1
  30.5 30.8 %kernel_rows.1 = (bf16[2048,1024]{1,0:T(8,128)(2,1)S(1)}, bf16[2048,1024]{1,0:T(8,128)(2,1)}) custom-call(f32[16]{0:T(128)S(1)} %get-tuple-element.21.shift_ref, f32[16]{0:T(128)S(1)} %get-tuple-element.20.floor_ref, f32[16,1]{1,0:T(8,128)S(1)} %copy.10.scale_ref, s32[16,2048]{1,0:T(8,128)S(1)} %copy-done.1, f32[16,1024]{1,0:T(8,128)S(1)} %convert_multiply_fusion.centre_ref), custom_call_target="tpu_custom_call" | custom-call | flops 201326592 | bytes 8388608 | tf_op jit(solution)/shard_map/kernel_rows/pallas_call | solution.py:106
  61.3 0.0 collective-permute-done.7
  61.3 0.0 copy-start.2
  61.3 0.0 copy-start.3
  61.3 10.1 %products.1 = (f32[16,1024]{1,0:T(8,128)S(1)}, f32[16,64]{1,0:T(8,128)S(1)}) custom-call(f32[16]{0:T(128)S(1)} %get-tuple-element.21.shift_ref, f32[16]{0:T(128)S(1)} %get-tuple-element.20.floor_ref, f32[16,1024]{1,0:T(8,128)S(1)} %maximum_select_fusion.2.coef_ref, f32[16,64]{1,0:T(8,128)S(1)} %convert_multiply_fusion.1.own_ref, ...), custom_call_target="tpu_custom_call" | custom-call | flops 805306368 | bytes 8388608 | tf_op jit(solution)/shard_map/products/pallas_call | solution.py:192
  71.4 0.1 collective-permute-start.8
  71.5 1.2 %collective-permute-done.8 = f32[16,1024]{1,0:T(8,128)S(1)} collective-permute-done((f32[16,1024]{1,0:T(8,128)S(1)}, f32[16,1024]{1,0:T(8,128)S(1)}, u32[]{:S(2)}, u32[]{:S(2)}) %collective-permute-start.8) | collective-permute-done | bytes 65568 | tf_op jit(solution)/shard_map/ppermute | solution.py:29
  72.7 1.6 %collective-permute-start.9 = (f32[16,1024]{1,0:T(8,128)S(1)}, f32[16,1024]{1,0:T(8,128)S(1)}, u32[]{:S(2)}, u32[]{:S(2)}) collective-permute-start(f32[16,1024]{1,0:T(8,128)S(1)} %add.63), channel_id=1, source_target_pairs={{0,2},{1,3},{2,0},{3,1},{4,6},{5,7},{6,4},{7,5},{8,10},{9,11},{10,... | collective-permute-start | bytes 196616 | tf_op jit(solution)/shard_map/ppermute | solution.py:29
  74.3 2.7 %collective-permute-done.9 = f32[16,1024]{1,0:T(8,128)S(1)} collective-permute-done((f32[16,1024]{1,0:T(8,128)S(1)}, f32[16,1024]{1,0:T(8,128)S(1)}, u32[]{:S(2)}, u32[]{:S(2)}) %collective-permute-start.9) | collective-permute-done | bytes 65568 | tf_op jit(solution)/shard_map/ppermute | solution.py:29
  77.1 2.1 %collective-permute-start.10 = (f32[16,1024]{1,0:T(8,128)S(1)}, f32[16,1024]{1,0:T(8,128)S(1)}, u32[]{:S(2)}, u32[]{:S(2)}) collective-permute-start(f32[16,1024]{1,0:T(8,128)S(1)} %add.64), channel_id=1, source_target_pairs={{0,4},{1,5},{2,6},{3,7},{4,0},{5,1},{6,2},{7,3},{8,12},{9,13},{10,... | collective-permute-start | bytes 196616 | tf_op jit(solution)/shard_map/ppermute | solution.py:29
  79.2 2.3 %collective-permute-done.10 = f32[16,1024]{1,0:T(8,128)S(1)} collective-permute-done((f32[16,1024]{1,0:T(8,128)S(1)}, f32[16,1024]{1,0:T(8,128)S(1)}, u32[]{:S(2)}, u32[]{:S(2)}) %collective-permute-start.10) | collective-permute-done | bytes 65568 | tf_op jit(solution)/shard_map/ppermute | solution.py:29
  81.4 0.1 collective-permute-start.11
  81.5 5.2 %collective-permute-done.11 = f32[16,1024]{1,0:T(8,128)S(1)} collective-permute-done((f32[16,1024]{1,0:T(8,128)S(1)}, f32[16,1024]{1,0:T(8,128)S(1)}, u32[]{:S(2)}, u32[]{:S(2)}) %collective-permute-start.11) | collective-permute-done | bytes 65568 | tf_op jit(solution)/shard_map/ppermute | solution.py:29
  86.7 0.3 fusion.10
  87.0 0.1 collective-permute-start.12
  87.0 1.2 %collective-permute-done.12 = f32[16,1024]{1,0:T(8,128)S(1)} collective-permute-done((f32[16,1024]{1,0:T(8,128)S(1)}, f32[16,1024]{1,0:T(8,128)S(1)}, u32[]{:S(2)}, u32[]{:S(2)}) %collective-permute-start.12) | collective-permute-done | bytes 65568 | tf_op jit(solution)/shard_map/ppermute | solution.py:29
  88.3 1.6 %collective-permute-start.13 = (f32[16,1024]{1,0:T(8,128)S(1)}, f32[16,1024]{1,0:T(8,128)S(1)}, u32[]{:S(2)}, u32[]{:S(2)}) collective-permute-start(f32[16,1024]{1,0:T(8,128)S(1)} %add.68), channel_id=1, source_target_pairs={{0,2},{1,3},{2,0},{3,1},{4,6},{5,7},{6,4},{7,5},{8,10},{9,11},{10,... | collective-permute-start | bytes 196616 | tf_op jit(solution)/shard_map/ppermute | solution.py:29
  89.9 2.7 %collective-permute-done.13 = f32[16,1024]{1,0:T(8,128)S(1)} collective-permute-done((f32[16,1024]{1,0:T(8,128)S(1)}, f32[16,1024]{1,0:T(8,128)S(1)}, u32[]{:S(2)}, u32[]{:S(2)}) %collective-permute-start.13) | collective-permute-done | bytes 65568 | tf_op jit(solution)/shard_map/ppermute | solution.py:29
  92.6 2.5 %collective-permute-start.14 = (f32[16,1024]{1,0:T(8,128)S(1)}, f32[16,1024]{1,0:T(8,128)S(1)}, u32[]{:S(2)}, u32[]{:S(2)}) collective-permute-start(f32[16,1024]{1,0:T(8,128)S(1)} %add.69), channel_id=1, source_target_pairs={{0,4},{1,5},{2,6},{3,7},{4,0},{5,1},{6,2},{7,3},{8,12},{9,13},{10,... | collective-permute-start | bytes 196616 | tf_op jit(solution)/shard_map/ppermute | solution.py:29
  95.2 2.3 %collective-permute-done.14 = f32[16,1024]{1,0:T(8,128)S(1)} collective-permute-done((f32[16,1024]{1,0:T(8,128)S(1)}, f32[16,1024]{1,0:T(8,128)S(1)}, u32[]{:S(2)}, u32[]{:S(2)}) %collective-permute-start.14) | collective-permute-done | bytes 65568 | tf_op jit(solution)/shard_map/ppermute | solution.py:29
  97.5 0.1 collective-permute-start.15
  97.5 5.2 %collective-permute-done.15 = f32[16,1024]{1,0:T(8,128)S(1)} collective-permute-done((f32[16,1024]{1,0:T(8,128)S(1)}, f32[16,1024]{1,0:T(8,128)S(1)}, u32[]{:S(2)}, u32[]{:S(2)}) %collective-permute-start.15) | collective-permute-done | bytes 65568 | tf_op jit(solution)/shard_map/ppermute | solution.py:29
  102.7 0.1 multiply_reduce_fusion.1
  102.8 0.2 multiply_reduce_fusion
  103.0 0.0 copy-done.2
  103.0 0.0 copy-done.3
  103.1 0.7 multiply_add_fusion
  (14 shorter events, 0.1 us)
Async XLA Ops:
  0.6 16.8 %copy-start = (f32[64,1024]{1,0:T(8,128)S(1)}, f32[64,1024]{1,0:T(8,128)}, u32[]{:S(2)}) copy-start(f32[64,1024]{1,0:T(8,128)} %param.10) | copy-start | bytes 786436
  2.1 1.3 %collective-permute-start = (f32[32,64]{1,0:T(8,128)S(1)}, f32[32,64]{1,0:T(8,128)S(1)}, u32[]{:S(2)}, u32[]{:S(2)}) collective-permute-start(f32[32,64]{1,0:T(8,128)S(1)} %constant_dynamic-update-slice_fusion), channel_id=1, source_target_pairs={{0,1},{1,0},{2,3},{3,2},{4,5},{5,4},{6,7},{7,6},{8,9},{9,8},{10,11... | collective-permute-start | bytes 24584 | tf_op jit(solution)/shard_map/ppermute | solution.py:29
  3.5 4.6 %collective-permute-start.1 = (f32[32,128]{1,0:T(8,128)S(1)}, f32[32,128]{1,0:T(8,128)S(1)}, u32[]{:S(2)}, u32[]{:S(2)}) collective-permute-start(f32[32,128]{1,0:T(8,128)S(1)} %maximum_select_fusion.5), channel_id=1, source_target_pairs={{0,2},{1,3},{2,0},{3,1},{4,6},{5,7},{6,4},{7,5},{8,10},{9,11},{10,... | collective-permute-start | bytes 49160 | tf_op jit(solution)/shard_map/ppermute | solution.py:29
  8.0 4.0 %collective-permute-start.2 = (f32[32,256]{1,0:T(8,128)S(1)}, f32[32,256]{1,0:T(8,128)S(1)}, u32[]{:S(2)}, u32[]{:S(2)}) collective-permute-start(f32[32,256]{1,0:T(8,128)S(1)} %maximum_select_fusion.3), channel_id=1, source_target_pairs={{0,4},{1,5},{2,6},{3,7},{4,0},{5,1},{6,2},{7,3},{8,12},{9,13},{10,... | collective-permute-start | bytes 98312 | tf_op jit(solution)/shard_map/ppermute | solution.py:29
  12.0 5.3 %collective-permute-start.3 = (f32[32,512]{1,0:T(8,128)S(1)}, f32[32,512]{1,0:T(8,128)S(1)}, u32[]{:S(2)}, u32[]{:S(2)}) collective-permute-start(f32[32,512]{1,0:T(8,128)S(1)} %maximum_select_fusion.1), channel_id=1, source_target_pairs={{0,8},{1,9},{2,10},{3,11},{4,12},{5,13},{6,14},{7,15},{8,0},{9,1},... | collective-permute-start | bytes 196616 | tf_op jit(solution)/shard_map/ppermute | solution.py:29
  17.7 1.2 %collective-permute-start.4 = (f32[16,64]{1,0:T(8,128)S(1)}, f32[16,64]{1,0:T(8,128)S(1)}, u32[]{:S(2)}, u32[]{:S(2)}) collective-permute-start(f32[16,64]{1,0:T(8,128)S(1)} %fusion.6), channel_id=1, source_target_pairs={{0,1},{1,0},{2,3},{3,2},{4,5},{5,4},{6,7},{7,6},{8,9},{9,8},{10,11... | collective-permute-start | bytes 12296 | tf_op jit(solution)/shard_map/ppermute | solution.py:29
  19.0 3.7 %collective-permute-start.5 = (f32[16,128]{1,0:T(8,128)S(1)}, f32[16,128]{1,0:T(8,128)S(1)}, u32[]{:S(2)}, u32[]{:S(2)}) collective-permute-start(f32[16,128]{1,0:T(8,128)S(1)} %maximum_select_fusion.7), channel_id=1, source_target_pairs={{0,2},{1,3},{2,0},{3,1},{4,6},{5,7},{6,4},{7,5},{8,10},{9,11},{10,... | collective-permute-start | bytes 24584 | tf_op jit(solution)/shard_map/ppermute | solution.py:29
  22.6 3.7 %collective-permute-start.6 = (f32[16,256]{1,0:T(8,128)S(1)}, f32[16,256]{1,0:T(8,128)S(1)}, u32[]{:S(2)}, u32[]{:S(2)}) collective-permute-start(f32[16,256]{1,0:T(8,128)S(1)} %maximum_select_fusion.6), channel_id=1, source_target_pairs={{0,4},{1,5},{2,6},{3,7},{4,0},{5,1},{6,2},{7,3},{8,12},{9,13},{10,... | collective-permute-start | bytes 49160 | tf_op jit(solution)/shard_map/ppermute | solution.py:29
  26.4 34.9 %collective-permute-start.7 = (f32[16,512]{1,0:T(8,128)S(1)}, f32[16,512]{1,0:T(8,128)S(1)}, u32[]{:S(2)}, u32[]{:S(2)}) collective-permute-start(f32[16,512]{1,0:T(8,128)S(1)} %maximum_select_fusion.4), channel_id=1, source_target_pairs={{0,8},{1,9},{2,10},{3,11},{4,12},{5,13},{6,14},{7,15},{8,0},{9,1},... | collective-permute-start | bytes 98312 | tf_op jit(solution)/shard_map/ppermute | solution.py:29
  29.6 0.9 copy-start.1
  61.3 41.8 %copy-start.2 = (f32[16,64]{1,0:T(8,128)S(1)}, f32[16,64]{1,0:T(8,128)}, u32[]{:S(2)}) copy-start(f32[16,64]{1,0:T(8,128)} %param.13) | copy-start | bytes 12292
  61.3 41.8 %copy-start.3 = (f32[16,64]{1,0:T(8,128)S(1)}, f32[16,64]{1,0:T(8,128)}, u32[]{:S(2)}) copy-start(f32[16,64]{1,0:T(8,128)} %param.11) | copy-start | bytes 12292
  71.4 1.3 %collective-permute-start.8 = (f32[16,1024]{1,0:T(8,128)S(1)}, f32[16,1024]{1,0:T(8,128)S(1)}, u32[]{:S(2)}, u32[]{:S(2)}) collective-permute-start(f32[16,1024]{1,0:T(8,128)S(1)} %get-tuple-element.9), channel_id=1, source_target_pairs={{0,1},{1,0},{2,3},{3,2},{4,5},{5,4},{6,7},{7,6},{8,9},{9,8},{10,11... | collective-permute-start | bytes 196616 | tf_op jit(solution)/shard_map/ppermute | solution.py:29
  72.7 4.3 %collective-permute-start.9 = (f32[16,1024]{1,0:T(8,128)S(1)}, f32[16,1024]{1,0:T(8,128)S(1)}, u32[]{:S(2)}, u32[]{:S(2)}) collective-permute-start(f32[16,1024]{1,0:T(8,128)S(1)} %add.63), channel_id=1, source_target_pairs={{0,2},{1,3},{2,0},{3,1},{4,6},{5,7},{6,4},{7,5},{8,10},{9,11},{10,... | collective-permute-start | bytes 196616 | tf_op jit(solution)/shard_map/ppermute | solution.py:29
  77.1 4.4 %collective-permute-start.10 = (f32[16,1024]{1,0:T(8,128)S(1)}, f32[16,1024]{1,0:T(8,128)S(1)}, u32[]{:S(2)}, u32[]{:S(2)}) collective-permute-start(f32[16,1024]{1,0:T(8,128)S(1)} %add.64), channel_id=1, source_target_pairs={{0,4},{1,5},{2,6},{3,7},{4,0},{5,1},{6,2},{7,3},{8,12},{9,13},{10,... | collective-permute-start | bytes 196616 | tf_op jit(solution)/shard_map/ppermute | solution.py:29
  81.4 5.2 %collective-permute-start.11 = (f32[16,1024]{1,0:T(8,128)S(1)}, f32[16,1024]{1,0:T(8,128)S(1)}, u32[]{:S(2)}, u32[]{:S(2)}) collective-permute-start(f32[16,1024]{1,0:T(8,128)S(1)} %add.65), channel_id=1, source_target_pairs={{0,8},{1,9},{2,10},{3,11},{4,12},{5,13},{6,14},{7,15},{8,0},{9,1},... | collective-permute-start | bytes 196616 | tf_op jit(solution)/shard_map/ppermute | solution.py:29
  87.0 1.3 %collective-permute-start.12 = (f32[16,1024]{1,0:T(8,128)S(1)}, f32[16,1024]{1,0:T(8,128)S(1)}, u32[]{:S(2)}, u32[]{:S(2)}) collective-permute-start(f32[16,1024]{1,0:T(8,128)S(1)} %fusion.10), channel_id=1, source_target_pairs={{0,1},{1,0},{2,3},{3,2},{4,5},{5,4},{6,7},{7,6},{8,9},{9,8},{10,11... | collective-permute-start | bytes 196616 | tf_op jit(solution)/shard_map/ppermute | solution.py:29
  88.3 4.3 %collective-permute-start.13 = (f32[16,1024]{1,0:T(8,128)S(1)}, f32[16,1024]{1,0:T(8,128)S(1)}, u32[]{:S(2)}, u32[]{:S(2)}) collective-permute-start(f32[16,1024]{1,0:T(8,128)S(1)} %add.68), channel_id=1, source_target_pairs={{0,2},{1,3},{2,0},{3,1},{4,6},{5,7},{6,4},{7,5},{8,10},{9,11},{10,... | collective-permute-start | bytes 196616 | tf_op jit(solution)/shard_map/ppermute | solution.py:29
  92.6 4.8 %collective-permute-start.14 = (f32[16,1024]{1,0:T(8,128)S(1)}, f32[16,1024]{1,0:T(8,128)S(1)}, u32[]{:S(2)}, u32[]{:S(2)}) collective-permute-start(f32[16,1024]{1,0:T(8,128)S(1)} %add.69), channel_id=1, source_target_pairs={{0,4},{1,5},{2,6},{3,7},{4,0},{5,1},{6,2},{7,3},{8,12},{9,13},{10,... | collective-permute-start | bytes 196616 | tf_op jit(solution)/shard_map/ppermute | solution.py:29
  97.5 5.2 %collective-permute-start.15 = (f32[16,1024]{1,0:T(8,128)S(1)}, f32[16,1024]{1,0:T(8,128)S(1)}, u32[]{:S(2)}, u32[]{:S(2)}) collective-permute-start(f32[16,1024]{1,0:T(8,128)S(1)} %add.70), channel_id=1, source_target_pairs={{0,8},{1,9},{2,10},{3,11},{4,12},{5,13},{6,14},{7,15},{8,0},{9,1},... | collective-permute-start | bytes 196616 | tf_op jit(solution)/shard_map/ppermute | solution.py:29

commit v2 on v1

v2 whole, which is shorter than its diff:
```python
import functools
import math

import jax
import jax.numpy as jnp
from jax import lax
from jax.experimental import pallas as pl
from jax.experimental.pallas import tpu as pltpu
from jax.sharding import PartitionSpec as P

LATTICE = 65521

ridge_weight = 0.25
VMEM_BYTES = 48 << 20
STORE_BYTES = 12 << 20
HELD_BYTES = 16 << 20
F32 = jnp.float32
BF16 = jnp.bfloat16


def centre_coords(lattice_index, generator):
    upper_digits = generator // 256
    lower_digits = generator % 256
    column = lattice_index[None, :]
    partial_value = column * upper_digits[:, None] % LATTICE
    return (partial_value * 256 + column * lower_digits[:, None]) % LATTICE


def swap(value, bit, devices):
    return lax.ppermute(value, "samp", [(i, i ^ bit) for i in range(devices)])


def after(value, *others):
    return lax.optimization_barrier((value, *others))[0]


def reduce_all(value, devices):
    bit = 1
    while bit < devices:
        value = value + swap(value, bit, devices)
        bit *= 2
    return value


def plan(devices, piece_bytes):
    bits = [1 << k for k in range(devices.bit_length() - 1)]
    held = []
    for bit in [b for b in (devices // 4, *bits) if 0 < b < devices // 2]:
        if bit not in held and (2 << len(held)) * piece_bytes <= HELD_BYTES:
            held.append(bit)
    held = held[:1] + held[:0:-1] if len(held) > 1 else held
    return held, [b for b in bits if b not in held]


def split3(value):
    high = value.astype(BF16)
    rest = value - high.astype(F32)
    middle = rest.astype(BF16)
    low = (rest - middle.astype(F32)).astype(BF16)
    return high, middle, low


def kernel_tile(points, centre_ref, shift_ref, floor_ref, first, width):
    rows, dims = points.shape
    product = None
    for axis_number in range(dims):
        centre = centre_ref[axis_number : axis_number + 1, pl.ds(first, width)]
        point = jnp.broadcast_to(points[:, axis_number : axis_number + 1], (rows, width))
        arm = jnp.abs(point - centre) - shift_ref[axis_number]
        factor = arm * arm + floor_ref[axis_number]
        product = factor if product is None else product * factor
    return product


def fill_kernel(rows, points, centre_ref, shift_ref, floor_ref, high_ref, low_ref):
    centres_all = centre_ref.shape[1]
    width = min(512, centres_all)
    span = min(1024, centres_all)

    def part(base):
        for piece in range(span // width):
            first = base + piece * width
            if not isinstance(first, int):
                first = pl.multiple_of(first, width)
            tile = kernel_tile(points, centre_ref, shift_ref, floor_ref, first, width)
            high = tile.astype(BF16)
            high_ref[rows, pl.ds(first, width)] = high
            low_ref[rows, pl.ds(first, width)] = (tile - high.astype(F32)).astype(BF16)

    if centres_all == span:
        part(0)
    else:
        lax.fori_loop(0, centres_all // span, lambda i, _: part(i * span), None)


def generate(step_rows, rows_all, shift_ref, floor_ref, scale_ref, sample_ref, centre_ref, high_ref, low_ref):
    for step in range(rows_all // step_rows):
        rows = pl.ds(step * step_rows, step_rows)
        points = (sample_ref[:, rows].astype(F32) * scale_ref[...]).T
        fill_kernel(rows, points, centre_ref, shift_ref, floor_ref, high_ref, low_ref)


def store_rows(step_rows, shift_ref, floor_ref, scale_ref, sample_ref, centre_ref, *refs):
    high_ref, low_ref, token_ref = refs[-3:]
    generate(
        step_rows, sample_ref.shape[1], shift_ref, floor_ref, scale_ref, sample_ref, centre_ref,
        high_ref, low_ref,
    )
    token_ref[...] = jnp.zeros_like(token_ref)


def kernel_rows(store, samples, first_block, blocks, block_rows, rows_stored, constants):
    centre_scaled, shift, floor, scale = constants
    dims, centres_all = centre_scaled.shape
    rows = blocks * block_rows
    smem = pl.BlockSpec(memory_space=pltpu.SMEM)
    given = [] if store is None else list(store)
    kept = jax.ShapeDtypeStruct((rows_stored, centres_all), BF16)
    high, low, token = pl.pallas_call(
        functools.partial(store_rows, 128),
        grid=(blocks,),
        in_specs=[
            smem,
            smem,
            pl.BlockSpec((dims, 1), lambda i: (0, 0)),
            pl.BlockSpec((dims, block_rows), lambda i: (0, first_block + i)),
            pl.BlockSpec((dims, centres_all), lambda i: (0, 0)),
            *[pl.BlockSpec(memory_space=pl.ANY)] * len(given),
        ],
        out_specs=[
            *[pl.BlockSpec((block_rows, centres_all), lambda i: (first_block + i, 0))] * 2,
            pl.BlockSpec((8, 128), lambda i: (0, 0)),
        ],
        out_shape=[kept, kept, jax.ShapeDtypeStruct((8, 128), F32)],
        input_output_aliases={5: 0, 6: 1} if given else {},
        compiler_params=pltpu.CompilerParams(vmem_limit_bytes=VMEM_BYTES),
        cost_estimate=pl.CostEstimate(
            flops=6 * dims * rows * centres_all,
            bytes_accessed=4 * rows * centres_all,
            transcendentals=0,
        ),
        name="kernel_rows",
    )(shift, floor, scale, samples, centre_scaled, *given)
    return (high, low), token


def apply_kernel(high, low, coefficients, outs):
    contract = (((1,), (1,)), ((), ()))
    fitted = lax.dot_general(coefficients, high, contract, preferred_element_type=F32)
    fitted = fitted + lax.dot_general(coefficients, low, contract, preferred_element_type=F32)
    return fitted[0:outs] + (fitted[outs : 2 * outs] + fitted[2 * outs : 3 * outs])


def back_products(high, low, coefficients, outs):
    parts = jnp.concatenate(split3(apply_kernel(high, low, coefficients, outs)), axis=0)
    return jnp.dot(parts, high, preferred_element_type=F32) + jnp.dot(
        parts, low, preferred_element_type=F32
    )


def products(
    outs, step_rows, stored, shift_ref, floor_ref, scale_ref, coef_ref, own_ref, centre_ref,
    sample_ref, *refs,
):
    step = pl.program_id(0)
    steps = pl.num_programs(0)
    if stored:
        high_ref, low_ref, *refs = refs
    backward_ref, own_out_ref, parts_ref, sum_ref, made_high, made_low = refs
    own_rows = own_ref.shape[1]

    @pl.when(step == 0)
    def _():
        high, middle, low = split3(coef_ref[...])
        parts_ref[0:outs] = high
        parts_ref[outs : 2 * outs] = middle
        parts_ref[2 * outs : 3 * outs] = low
        sum_ref[...] = jnp.zeros_like(sum_ref)
        own_high, own_low = made_high.at[1], made_low.at[1]
        rows = pl.ds(0, own_rows)
        fill_kernel(rows, own_ref[...].T, centre_ref, shift_ref, floor_ref, own_high, own_low)
        own_out_ref[...] = apply_kernel(own_high[rows], own_low[rows], parts_ref[...], outs)
        made_high[1] = jnp.zeros(made_high.shape[1:], BF16)
        made_low[1] = jnp.zeros(made_low.shape[1:], BF16)

    now = lax.rem(step, 2)
    coefficients = parts_ref[...]
    before = 1 - now
    total = back_products(made_high[before], made_low[before], coefficients, outs)
    if stored:
        total = total + back_products(high_ref[...], low_ref[...], coefficients, outs)
    generate(
        step_rows, sample_ref.shape[1], shift_ref, floor_ref, scale_ref, sample_ref, centre_ref,
        made_high.at[now], made_low.at[now],
    )
    sum_ref[...] += total

    @pl.when(step == steps - 1)
    def _():
        last = sum_ref[...] + back_products(made_high[now], made_low[now], coefficients, outs)
        backward_ref[...] = last[0:outs] + (last[outs : 2 * outs] + last[2 * outs : 3 * outs])


def apply_products(store, samples, coefficients, own_scaled, block_rows, constants):
    centre_scaled, shift, floor, scale = constants
    outs, centres_all = coefficients.shape
    dims, own_rows = own_scaled.shape
    rows_stored = 0 if store is None else store[0].shape[0]
    first = rows_stored // block_rows
    steps = samples.shape[1] // block_rows - first
    smem = pl.BlockSpec(memory_space=pltpu.SMEM)

    def whole(shape):
        return pl.BlockSpec(shape, lambda i: (0, 0))

    made = pltpu.VMEM((2, block_rows, centres_all), BF16)
    given = [] if store is None else list(store)
    return pl.pallas_call(
        functools.partial(products, outs, 128, store is not None),
        grid=(steps,),
        in_specs=[
            smem,
            smem,
            whole((dims, 1)),
            whole((outs, centres_all)),
            whole((dims, own_rows)),
            whole((dims, centres_all)),
            pl.BlockSpec((dims, block_rows), lambda i: (0, first + i)),
            *[pl.BlockSpec((block_rows, centres_all), lambda i: (i, 0))] * len(given),
        ],
        out_specs=[whole((outs, centres_all)), whole((outs, own_rows))],
        out_shape=[
            jax.ShapeDtypeStruct((outs, centres_all), F32),
            jax.ShapeDtypeStruct((outs, own_rows), F32),
        ],
        scratch_shapes=[
            pltpu.VMEM((3 * outs, centres_all), BF16),
            pltpu.VMEM((3 * outs, centres_all), F32),
            made,
            made,
        ],
        compiler_params=pltpu.CompilerParams(vmem_limit_bytes=VMEM_BYTES),
        cost_estimate=pl.CostEstimate(
            flops=6 * dims * steps * block_rows * centres_all,
            bytes_accessed=4 * rows_stored * centres_all,
            transcendentals=0,
        ),
        name="products",
    )(shift, floor, scale, coefficients, own_scaled, centre_scaled, samples, *given)


def contract_last(left_array, right_array):
    return lax.dot_general(
        left_array,
        right_array,
        (((1,), (1,)), ((), ())),
        precision=lax.Precision.HIGHEST,
        preferred_element_type=F32,
    )


def body(samples, generator, weight_index, preconditioner, solution, residual, direction):
    highest = lax.Precision.HIGHEST
    devices = lax.axis_size("samp")
    index = lax.axis_index("samp")
    cen_dev, centres_all = preconditioner.shape
    samples_dev = samples.shape[1]
    outs = direction.shape[0]
    held, others = plan(devices, 4 * cen_dev * centres_all)

    weights_dim = 0.5 * jnp.power(0.75, weight_index.astype(F32))
    curve = 2.0 * math.pi * math.pi * weights_dim
    floor = 1.0 - curve / 12.0
    root = jnp.sqrt(curve)
    shift = 0.5 * root
    scale = (root / LATTICE)[:, None]

    order = [0]
    for bit in (*held, *others):
        order = order + [k ^ bit for k in order]
    owners = index ^ jnp.array(order, jnp.int32)
    lattice_index = owners[:, None] * cen_dev + jnp.arange(cen_dev, dtype=jnp.int32)[None, :]
    centres = centre_coords(lattice_index.reshape(centres_all), generator)
    centre_scaled = centres.astype(F32) * scale
    own_scaled = centre_scaled[:, :cen_dev]
    constants = (centre_scaled, shift, floor, scale)

    block_rows = 128
    half = samples_dev // 2
    use_store = 4 * half * centres_all <= STORE_BYTES
    store, token, filled = None, None, 0

    def fill(blocks, *ready):
        nonlocal store, token, filled
        if use_store:
            blocks = min(blocks, half // block_rows - filled)
            if blocks > 0:
                tied = (centre_scaled, shift, floor, after(scale, *ready))
                store, token = kernel_rows(
                    store, samples, filled, blocks, block_rows, half, tied
                )
                filled += blocks

    def then(value):
        return value if token is None else after(value, token)

    state = jnp.concatenate([direction, residual], axis=0)
    pieces = [preconditioner]
    waiting = list(held)
    bit = 1
    while bit < devices:
        if waiting and bit in (1, devices // 4):
            pieces.append(swap(jnp.concatenate(pieces, axis=0), waiting.pop(0), devices))
        tied = then(state)
        other = swap(tied, bit, devices)
        if bit > 1:
            fill(2 if 2 * bit == devices else 1, tied)
        upper = (index & bit) != 0
        state = jnp.where(
            upper,
            jnp.concatenate([other, tied], axis=1),
            jnp.concatenate([tied, other], axis=1),
        )
        bit *= 2
    direction_full, residual_full = state[:outs], state[outs:]
    fill(2, state)
    for bit in waiting:
        joined = jnp.concatenate(pieces, axis=0)
        pieces.append(swap(then(joined), bit, devices))

    coefficients = jnp.concatenate([contract_last(direction_full, p) for p in pieces], axis=1)
    for bit in others:
        tied = then(coefficients)
        other = swap(tied, bit, devices)
        fill(2, tied)
        coefficients = jnp.concatenate([tied, other], axis=1)
    fill(half // block_rows, coefficients)

    backward, kernel_products = apply_products(
        store, samples, coefficients, own_scaled, 256, constants
    )
    for bit in reversed(others):
        width = backward.shape[1] // 2
        backward = backward[:, :width] + swap(backward[:, width:], bit, devices)
    scale_total = float(samples_dev * devices) * float(centres_all)
    own_term = ridge_weight * kernel_products / centres_all
    applied = backward / scale_total + jnp.pad(
        own_term, ((0, 0), (0, backward.shape[1] - cen_dev))
    )
    partial_image, first = 0.0, 0
    for p in pieces:
        part = applied[:, first : first + p.shape[0]]
        partial_image += jnp.dot(part, p, precision=highest, preferred_element_type=F32)
        first += p.shape[0]
    image = reduce_all(partial_image, devices)

    first_row = index * cen_dev
    norm_old = jnp.sum(residual_full * residual_full, axis=1, keepdims=True)
    curvature = jnp.sum(direction_full * image, axis=1, keepdims=True)
    step_length = norm_old / curvature
    next_full = residual_full - step_length * image
    norm_new = jnp.sum(next_full * next_full, axis=1, keepdims=True)
    new_residual = lax.dynamic_slice_in_dim(next_full, first_row, cen_dev, 1)
    new_solution = solution + step_length * direction
    new_direction = new_residual + (norm_new / norm_old) * direction
    return (new_solution, new_residual, new_direction)


def solution(mesh):
    placed = (
        P("groups", "samp"),
        P(),
        P(),
        P("samp", None),
        P("groups", "samp"),
        P("groups", "samp"),
        P("groups", "samp"),
    )
    return jax.shard_map(
        body,
        mesh=mesh,
        in_specs=placed,
        out_specs=(P("groups", "samp"), P("groups", "samp"), P("groups", "samp")),
        check_vma=False,
    )
```

time: 104 us -> 102 us (0.981)
  waiting for transfers between devices: 32.7 us -> 18.8 us
  local copies, waits for them, and re-layouts: 2.46 us -> 14.2 us
  starting transfers between devices: 23.4 us -> 16.8 us
  other arithmetic: 2.98 us -> 6.08 us
  matrix products: 0.56 us -> 3.59 us
    ppermute x16 -> x13, waiting for transfers between devices: 32.7 us -> 18.8 us  [swap(): return lax.ppermute(value, 'samp', [(i, i ^ bit) for i in range(devices)])]
    unnamed x9 -> x33, local copies, waits for them, and re-layouts: 1.68 us -> 13 us
    ppermute x16 -> x13, starting transfers between devices: 23.4 us -> 16.8 us  [swap(): return lax.ppermute(value, 'samp', [(i, i ^ bit) for i in range(devices)])]
    concatenate x0 -> x4, other arithmetic: none -> 2.71 us  [the longest x1 1.8 us: body(): jnp.concatenate(pieces, axis=0)]
    dot_general x1 -> x4, matrix products: 0.27 us -> 2.08 us  [contract_last(): lax.dot_general(left_array, right_array, (((1,), (1,)), ((), ())), precis...]
    dot_general x1 -> x4, matrix products: 0.29 us -> 1.52 us  [body(): jnp.dot(part, p, precision=highest, preferred_element_type=F32)]
    pallas_call x2 -> x6, Pallas kernels: 40.8 us -> 41.3 us  [the longest x5 21 us: kernel_rows(): pl.pallas_call(functools.partial(store_rows, 128), grid=(blocks,), in_spe...]
  transfers between devices with their start and end apart: 16 -> 13, of which waited for: 15 -> 8; matrix products, arithmetic and copies ran while one was open for 2% -> 6% of each run, Pallas kernels for 30% -> 21%
where the time goes in v2:
time: 102 us
  Pallas kernels  41.3 us (40%)
  waiting for transfers between devices  18.8 us (18%)
  starting transfers between devices  16.8 us (16%)
  local copies, waits for them, and re-layouts  14.2 us (14%)
  other arithmetic  6.08 us (6%)
  matrix products  3.59 us (4%)
    pallas_call x5, Pallas kernels, kernel_rows(): pl.pallas_call(functools.partial(store_rows, 128), grid=(blocks,), in_spe...  21 us
    pallas_call x1, Pallas kernels, apply_products(): pl.pallas_call(functools.partial(products, outs, 128, store is not None),...  20.3 us
    ppermute x13, waiting for transfers between devices, swap(): return lax.ppermute(value, 'samp', [(i, i ^ bit) for i in range(devices)])  18.8 us
    ppermute x13, starting transfers between devices, swap(): return lax.ppermute(value, 'samp', [(i, i ^ bit) for i in range(devices)])  16.8 us
    unnamed x33, local copies, waits for them, and re-layouts  13 us
    dot_general x4, matrix products, contract_last(): lax.dot_general(left_array, right_array, (((1,), (1,)), ((), ())), precis...  2.08 us
  transfers between devices with their start and end apart: 13, of which 8 were waited for; matrix products, arithmetic and copies ran while one was open for 6% of the time, Pallas kernels for 21%

profile of v2, /device:TPU:0, one launch (start us, length us, event | category | flops | bytes accessed | tf_op | source)
XLA Modules:
  0.0 101.7 jit_solution(6628004609776131851)
XLA Ops:
  0.6 0.7 constant_dynamic-update-slice_fusion.1
  1.3 0.7 constant_dynamic-update-slice_fusion
  2.0 0.5 collective-permute-start
  2.5 2.6 %collective-permute-start.4 = (f32[64,1024]{1,0:T(8,128)}, f32[64,1024]{1,0:T(8,128)S(1)}, u32[]{:S(2)}, u32[]{:S(2)}) collective-permute-start(f32[64,1024]{1,0:T(8,128)} %param.11), channel_id=1, source_target_pairs={{0,4},{1,5},{2,6},{3,7},{4,0},{5,1},{6,2},{7,3},{8,12},{9,13},{10,... | collective-permute-start | bytes 786440 | tf_op jit(solution)/shard_map/ppermute | solution.py:30
  5.1 0.7 xor_multiply_fusion
  5.7 0.1 iota_add_fusion
  5.8 0.1 maximum_select_fusion.3
  5.9 1.5 %collective-permute-start.1 = (f32[32,128]{1,0:T(8,128)S(1)}, f32[32,128]{1,0:T(8,128)S(1)}, u32[]{:S(2)}, u32[]{:S(2)}) collective-permute-start(f32[32,128]{1,0:T(8,128)S(1)} %maximum_select_fusion.3), channel_id=1, source_target_pairs={{0,2},{1,3},{2,0},{3,1},{4,6},{5,7},{6,4},{7,5},{8,10},{9,11},{10,... | collective-permute-start | bytes 49160 | tf_op jit(solution)/shard_map/ppermute | solution.py:30
  7.4 0.7 broadcast_multiply_fusion.1
  8.1 1.6 %collective-permute-done.1 = f32[32,128]{1,0:T(8,128)S(1)} collective-permute-done((f32[32,128]{1,0:T(8,128)S(1)}, f32[32,128]{1,0:T(8,128)S(1)}, u32[]{:S(2)}, u32[]{:S(2)}) %collective-permute-start.1) | collective-permute-done | bytes 16416 | tf_op jit(solution)/shard_map/ppermute | solution.py:30
  9.6 0.4 collective-permute-start.2
  10.1 2.4 %collective-permute-done.4 = f32[64,1024]{1,0:T(8,128)S(1)} collective-permute-done((f32[64,1024]{1,0:T(8,128)}, f32[64,1024]{1,0:T(8,128)S(1)}, u32[]{:S(2)}, u32[]{:S(2)}) %collective-permute-start.4) | collective-permute-done | bytes 262176 | tf_op jit(solution)/shard_map/ppermute | solution.py:30
  12.4 1.8 %pad_maximum_fusion.1 = f32[128,1024]{1,0:T(8,128)} fusion(f32[64,1024]{1,0:T(8,128)S(1)} %collective-permute-done.4, f32[64,1024]{1,0:T(8,128)} %param.11), kind=kLoop, calls=%fused_computation.4 | loop fusion | flops 131072 | bytes 1048576 | tf_op jit(solution)/shard_map/concatenate | solution.py:313
  14.2 1.9 %collective-permute-start.5 = (f32[128,1024]{1,0:T(8,128)}, f32[128,1024]{1,0:T(8,128)S(1)}, u32[]{:S(2)}, u32[]{:S(2)}) collective-permute-start(f32[128,1024]{1,0:T(8,128)} %pad_maximum_fusion.1), channel_id=1, source_target_pairs={{0,2},{1,3},{2,0},{3,1},{4,6},{5,7},{6,4},{7,5},{8,10},{9,11},{10,... | collective-permute-start | bytes 1572872 | tf_op jit(solution)/shard_map/ppermute | solution.py:30
  16.1 0.7 and_select_fusion.1
  16.8 2.7 %collective-permute-start.3 = (f32[32,512]{1,0:T(8,128)S(1)}, f32[32,512]{1,0:T(8,128)S(1)}, u32[]{:S(2)}, u32[]{:S(2)}) collective-permute-start(f32[32,512]{1,0:T(8,128)S(1)} %maximum_select_fusion.1), channel_id=1, source_target_pairs={{0,8},{1,9},{2,10},{3,11},{4,12},{5,13},{6,14},{7,15},{8,0},{9,1},... | collective-permute-start | bytes 196616 | tf_op jit(solution)/shard_map/ppermute | solution.py:30
  19.5 0.1 fusion.6.centre_ref
  19.6 0.1 copy.19.scale_ref
  19.7 0.9 copy-done.8
  20.6 3.0 %kernel_rows.5 = (bf16[1024,1024]{1,0:T(8,128)(2,1)S(1)}, bf16[1024,1024]{1,0:T(8,128)(2,1)S(1)}, f32[8,128]{1,0:T(8,128)}) custom-call(f32[16]{0:T(128)S(1)} %get-tuple-element.55.shift_ref, f32[16]{0:T(128)S(1)} %get-tuple-element.54.floor_ref, f32[16,1]{1,0:T(8,128)S(1)} %copy.19.scale_ref, s32[16,2048]{1,0:T(8,128)S(1)} %copy-done.8, ...), custom_call_target="tpu_custom_call" | custom-call | flops 12582912 | bytes 524288 | tf_op jit(solution)/shard_map/kernel_rows/pallas_call | solution.py:119
  23.7 1.3 %copy-done = bf16[1024,1024]{1,0:T(8,128)(2,1)} copy-done((bf16[1024,1024]{1,0:T(8,128)(2,1)}, bf16[1024,1024]{1,0:T(8,128)(2,1)S(1)}, u32[]{:S(2)}) %copy-start) | copy-done | bytes 2097176
  25.0 0.1 copy.20.scale_ref
  25.1 1.6 %copy-done.1 = bf16[1024,1024]{1,0:T(8,128)(2,1)S(1)} copy-done((bf16[1024,1024]{1,0:T(8,128)(2,1)S(1)}, bf16[1024,1024]{1,0:T(8,128)(2,1)}, u32[]{:S(2)}) %copy-start.1) | copy-done | bytes 2097176
  26.7 0.9 copy-done.9
  27.6 3.0 %kernel_rows.6 = (bf16[1024,1024]{1,0:T(8,128)(2,1)S(1)}, bf16[1024,1024]{1,0:T(8,128)(2,1)S(1)}, f32[8,128]{1,0:T(8,128)}) custom-call(f32[16]{0:T(128)S(1)} %get-tuple-element.55.shift_ref, f32[16]{0:T(128)S(1)} %get-tuple-element.54.floor_ref, f32[16,1]{1,0:T(8,128)S(1)} %copy.20.scale_ref, ...), custom_call_target="tpu_custom_call", output_to_operand_aliasing={{0}: (5, {}), {1}: (6, {})} | custom-call | flops 12582912 | bytes 524288 | tf_op jit(solution)/shard_map/kernel_rows/pallas_call | solution.py:119
  30.6 1.3 %copy-done.2 = bf16[1024,1024]{1,0:T(8,128)(2,1)} copy-done((bf16[1024,1024]{1,0:T(8,128)(2,1)}, bf16[1024,1024]{1,0:T(8,128)(2,1)S(1)}, u32[]{:S(2)}) %copy-start.2) | copy-done | bytes 2097176
  32.0 0.1 copy.21.scale_ref
  32.1 1.6 %copy-done.3 = bf16[1024,1024]{1,0:T(8,128)(2,1)S(1)} copy-done((bf16[1024,1024]{1,0:T(8,128)(2,1)S(1)}, bf16[1024,1024]{1,0:T(8,128)(2,1)}, u32[]{:S(2)}) %copy-start.3) | copy-done | bytes 2097176
  33.7 5.0 %kernel_rows.7 = (bf16[1024,1024]{1,0:T(8,128)(2,1)S(1)}, bf16[1024,1024]{1,0:T(8,128)(2,1)S(1)}, f32[8,128]{1,0:T(8,128)}) custom-call(f32[16]{0:T(128)S(1)} %get-tuple-element.55.shift_ref, f32[16]{0:T(128)S(1)} %get-tuple-element.54.floor_ref, f32[16,1]{1,0:T(8,128)S(1)} %copy.21.scale_ref, ...), custom_call_target="tpu_custom_call", output_to_operand_aliasing={{0}: (5, {}), {1}: (6, {})} | custom-call | flops 25165824 | bytes 1048576 | tf_op jit(solution)/shard_map/kernel_rows/pallas_call | solution.py:119
  38.7 1.3 %copy-done.4 = bf16[1024,1024]{1,0:T(8,128)(2,1)} copy-done((bf16[1024,1024]{1,0:T(8,128)(2,1)}, bf16[1024,1024]{1,0:T(8,128)(2,1)S(1)}, u32[]{:S(2)}) %copy-start.4) | copy-done | bytes 2097176
  40.0 0.1 copy.22.scale_ref
  40.1 1.6 %copy-done.5 = bf16[1024,1024]{1,0:T(8,128)(2,1)S(1)} copy-done((bf16[1024,1024]{1,0:T(8,128)(2,1)S(1)}, bf16[1024,1024]{1,0:T(8,128)(2,1)}, u32[]{:S(2)}) %copy-start.5) | copy-done | bytes 2097176
  41.7 5.0 %kernel_rows.8 = (bf16[1024,1024]{1,0:T(8,128)(2,1)S(1)}, bf16[1024,1024]{1,0:T(8,128)(2,1)S(1)}, f32[8,128]{1,0:T(8,128)}) custom-call(f32[16]{0:T(128)S(1)} %get-tuple-element.55.shift_ref, f32[16]{0:T(128)S(1)} %get-tuple-element.54.floor_ref, f32[16,1]{1,0:T(8,128)S(1)} %copy.22.scale_ref, ...), custom_call_target="tpu_custom_call", output_to_operand_aliasing={{0}: (5, {}), {1}: (6, {})} | custom-call | flops 25165824 | bytes 1048576 | tf_op jit(solution)/shard_map/kernel_rows/pallas_call | solution.py:119
  46.8 0.1 collective-permute-start.6
  46.9 0.3 fusion.16
  47.1 0.3 fusion.14
  47.4 0.6 fusion.12
  48.0 1.5 %collective-permute-done.6 = f32[256,1024]{1,0:T(8,128)S(1)} collective-permute-done((f32[256,1024]{1,0:T(8,128)S(1)}, f32[256,1024]{1,0:T(8,128)S(1)}, u32[]{:S(2)}, u32[]{:S(2)}) %collective-permute-start.6) | collective-permute-done | bytes 1048608 | tf_op jit(solution)/shard_map/ppermute | solution.py:30
  49.5 0.9 fusion.10
  50.4 0.1 pad_maximum_fusion.3
  50.5 0.3 collective-permute-start.7
  50.9 0.1 copy.24.scale_ref
  51.0 0.1 copy.23.scale_ref
  51.0 1.6 %copy-done.7 = bf16[1024,1024]{1,0:T(8,128)(2,1)S(1)} copy-done((bf16[1024,1024]{1,0:T(8,128)(2,1)S(1)}, bf16[1024,1024]{1,0:T(8,128)(2,1)}, u32[]{:S(2)}) %copy-start.7) | copy-done | bytes 2097176
  52.6 5.0 %kernel_rows.9 = (bf16[1024,1024]{1,0:T(8,128)(2,1)S(1)}, bf16[1024,1024]{1,0:T(8,128)(2,1)S(1)}, f32[8,128]{1,0:T(8,128)}) custom-call(f32[16]{0:T(128)S(1)} %get-tuple-element.55.shift_ref, f32[16]{0:T(128)S(1)} %get-tuple-element.54.floor_ref, f32[16,1]{1,0:T(8,128)S(1)} %copy.23.scale_ref, ...), custom_call_target="tpu_custom_call", output_to_operand_aliasing={{0}: (5, {}), {1}: (6, {})} | custom-call | flops 25165824 | bytes 1048576 | tf_op jit(solution)/shard_map/kernel_rows/pallas_call | solution.py:119
  57.6 0.8 pad_maximum_fusion.2.coef_ref
  58.4 20.3 %products.1 = (f32[16,1024]{1,0:T(8,128)S(1)}, f32[16,64]{1,0:T(8,128)S(1)}) custom-call(f32[16]{0:T(128)S(1)} %get-tuple-element.55.shift_ref, f32[16]{0:T(128)S(1)} %get-tuple-element.54.floor_ref, f32[16,1]{1,0:T(8,128)S(1)} %copy.24.scale_ref, f32[16,1024]{1,0:T(8,128)S(1)} %pad_maximum_fusion.2.coef_ref, f32[16,64]{1,0:T(8,128)S(1)} %slice.38.own_ref, ...), custom_call_target="tpu_custom_call" | custom-call | flops 100663296 | bytes 4194304 | tf_op jit(solution)/shard_map/products/pallas_call | solution.py:218
  78.7 2.7 %collective-permute-start.8 = (f32[16,512]{1,0:T(8,128)S(1)}, f32[16,512]{1,0:T(8,128)S(1)}, u32[]{:S(2)}, u32[]{:S(2)}) collective-permute-start(f32[16,512]{1,0:T(8,128)S(1)} %slice.31), channel_id=1, source_target_pairs={{0,8},{1,9},{2,10},{3,11},{4,12},{5,13},{6,14},{7,15},{8,0},{9,1},... | collective-permute-start | bytes 98312 | tf_op jit(solution)/shard_map/ppermute | solution.py:30
  81.4 2.5 %collective-permute-done.8 = f32[16,512]{1,0:T(8,128)S(1)} collective-permute-done((f32[16,512]{1,0:T(8,128)S(1)}, f32[16,512]{1,0:T(8,128)S(1)}, u32[]{:S(2)}, u32[]{:S(2)}) %collective-permute-start.8) | collective-permute-done | bytes 32800 | tf_op jit(solution)/shard_map/ppermute | solution.py:30
  83.8 0.3 fusion.22
  84.1 0.4 fusion.20
  84.5 0.6 fusion.18
  85.1 0.3 fusion.1
  85.4 0.1 collective-permute-start.9
  85.5 1.2 %collective-permute-done.9 = f32[16,1024]{1,0:T(8,128)S(1)} collective-permute-done((f32[16,1024]{1,0:T(8,128)S(1)}, f32[16,1024]{1,0:T(8,128)S(1)}, u32[]{:S(2)}, u32[]{:S(2)}) %collective-permute-start.9) | collective-permute-done | bytes 65568 | tf_op jit(solution)/shard_map/ppermute | solution.py:30
  86.7 0.4 collective-permute-start.10
  87.1 4.0 %collective-permute-done.10 = f32[16,1024]{1,0:T(8,128)S(1)} collective-permute-done((f32[16,1024]{1,0:T(8,128)S(1)}, f32[16,1024]{1,0:T(8,128)S(1)}, u32[]{:S(2)}, u32[]{:S(2)}) %collective-permute-start.10) | collective-permute-done | bytes 65568 | tf_op jit(solution)/shard_map/ppermute | solution.py:30
  91.0 1.4 %collective-permute-start.11 = (f32[16,1024]{1,0:T(8,128)S(1)}, f32[16,1024]{1,0:T(8,128)S(1)}, u32[]{:S(2)}, u32[]{:S(2)}) collective-permute-start(f32[16,1024]{1,0:T(8,128)S(1)} %add.92), channel_id=1, source_target_pairs={{0,4},{1,5},{2,6},{3,7},{4,0},{5,1},{6,2},{7,3},{8,12},{9,13},{10,... | collective-permute-start | bytes 196616 | tf_op jit(solution)/shard_map/ppermute | solution.py:30
  92.4 2.9 %collective-permute-done.11 = f32[16,1024]{1,0:T(8,128)S(1)} collective-permute-done((f32[16,1024]{1,0:T(8,128)S(1)}, f32[16,1024]{1,0:T(8,128)S(1)}, u32[]{:S(2)}, u32[]{:S(2)}) %collective-permute-start.11) | collective-permute-done | bytes 65568 | tf_op jit(solution)/shard_map/ppermute | solution.py:30
  95.4 2.4 %collective-permute-start.12 = (f32[16,1024]{1,0:T(8,128)S(1)}, f32[16,1024]{1,0:T(8,128)S(1)}, u32[]{:S(2)}, u32[]{:S(2)}) collective-permute-start(f32[16,1024]{1,0:T(8,128)S(1)} %add.93), channel_id=1, source_target_pairs={{0,8},{1,9},{2,10},{3,11},{4,12},{5,13},{6,14},{7,15},{8,0},{9,1},... | collective-permute-start | bytes 196616 | tf_op jit(solution)/shard_map/ppermute | solution.py:30
  97.8 2.8 %collective-permute-done.12 = f32[16,1024]{1,0:T(8,128)S(1)} collective-permute-done((f32[16,1024]{1,0:T(8,128)S(1)}, f32[16,1024]{1,0:T(8,128)S(1)}, u32[]{:S(2)}, u32[]{:S(2)}) %collective-permute-start.12) | collective-permute-done | bytes 65568 | tf_op jit(solution)/shard_map/ppermute | solution.py:30
  100.6 0.1 multiply_reduce_fusion.1
  100.8 0.2 multiply_reduce_fusion
  101.0 0.7 multiply_add_fusion
  (42 shorter events, 0.3 us)
Async XLA Ops:
  2.0 3.8 %collective-permute-start = (f32[32,64]{1,0:T(8,128)S(1)}, f32[32,64]{1,0:T(8,128)S(1)}, u32[]{:S(2)}, u32[]{:S(2)}) collective-permute-start(f32[32,64]{1,0:T(8,128)S(1)} %constant_dynamic-update-slice_fusion), channel_id=1, source_target_pairs={{0,1},{1,0},{2,3},{3,2},{4,5},{5,4},{6,7},{7,6},{8,9},{9,8},{10,11... | collective-permute-start | bytes 24584 | tf_op jit(solution)/shard_map/ppermute | solution.py:30
  2.5 9.9 %collective-permute-start.4 = (f32[64,1024]{1,0:T(8,128)}, f32[64,1024]{1,0:T(8,128)S(1)}, u32[]{:S(2)}, u32[]{:S(2)}) collective-permute-start(f32[64,1024]{1,0:T(8,128)} %param.11), channel_id=1, source_target_pairs={{0,4},{1,5},{2,6},{3,7},{4,0},{5,1},{6,2},{7,3},{8,12},{9,13},{10,... | collective-permute-start | bytes 786440 | tf_op jit(solution)/shard_map/ppermute | solution.py:30
  5.9 3.7 %collective-permute-start.1 = (f32[32,128]{1,0:T(8,128)S(1)}, f32[32,128]{1,0:T(8,128)S(1)}, u32[]{:S(2)}, u32[]{:S(2)}) collective-permute-start(f32[32,128]{1,0:T(8,128)S(1)} %maximum_select_fusion.3), channel_id=1, source_target_pairs={{0,2},{1,3},{2,0},{3,1},{4,6},{5,7},{6,4},{7,5},{8,10},{9,11},{10,... | collective-permute-start | bytes 49160 | tf_op jit(solution)/shard_map/ppermute | solution.py:30
  9.6 7.2 %collective-permute-start.2 = (f32[32,256]{1,0:T(8,128)S(1)}, f32[32,256]{1,0:T(8,128)S(1)}, u32[]{:S(2)}, u32[]{:S(2)}) collective-permute-start(f32[32,256]{1,0:T(8,128)S(1)} %maximum_select_fusion.2), channel_id=1, source_target_pairs={{0,4},{1,5},{2,6},{3,7},{4,0},{5,1},{6,2},{7,3},{8,12},{9,13},{10,... | collective-permute-start | bytes 98312 | tf_op jit(solution)/shard_map/ppermute | solution.py:30
  14.2 32.5 %collective-permute-start.5 = (f32[128,1024]{1,0:T(8,128)}, f32[128,1024]{1,0:T(8,128)S(1)}, u32[]{:S(2)}, u32[]{:S(2)}) collective-permute-start(f32[128,1024]{1,0:T(8,128)} %pad_maximum_fusion.1), channel_id=1, source_target_pairs={{0,2},{1,3},{2,0},{3,1},{4,6},{5,7},{6,4},{7,5},{8,10},{9,11},{10,... | collective-permute-start | bytes 1572872 | tf_op jit(solution)/shard_map/ppermute | solution.py:30
  16.8 23.2 %collective-permute-start.3 = (f32[32,512]{1,0:T(8,128)S(1)}, f32[32,512]{1,0:T(8,128)S(1)}, u32[]{:S(2)}, u32[]{:S(2)}) collective-permute-start(f32[32,512]{1,0:T(8,128)S(1)} %maximum_select_fusion.1), channel_id=1, source_target_pairs={{0,8},{1,9},{2,10},{3,11},{4,12},{5,13},{6,14},{7,15},{8,0},{9,1},... | collective-permute-start | bytes 196616 | tf_op jit(solution)/shard_map/ppermute | solution.py:30
  19.7 0.9 copy-start.8
  23.7 1.3 %copy-start = (bf16[1024,1024]{1,0:T(8,128)(2,1)}, bf16[1024,1024]{1,0:T(8,128)(2,1)S(1)}, u32[]{:S(2)}) copy-start(bf16[1024,1024]{1,0:T(8,128)(2,1)S(1)} %get-tuple-element.28.refs_1_) | copy-start | bytes 6291460
  25.1 1.6 %copy-start.1 = (bf16[1024,1024]{1,0:T(8,128)(2,1)S(1)}, bf16[1024,1024]{1,0:T(8,128)(2,1)}, u32[]{:S(2)}) copy-start(bf16[1024,1024]{1,0:T(8,128)(2,1)} %copy-done) | copy-start | bytes 6291460
  26.7 0.9 copy-start.9
  27.6 4.5 %copy-start.10 = (s32[16,2048]{1,0:T(8,128)S(1)}, s32[16,2048]{1,0:T(8,128)}, u32[]{:S(2)}) copy-start(s32[16,2048]{1,0:T(8,128)} %sample_ref.11) | copy-start | bytes 393220
  30.6 1.3 %copy-start.2 = (bf16[1024,1024]{1,0:T(8,128)(2,1)}, bf16[1024,1024]{1,0:T(8,128)(2,1)S(1)}, u32[]{:S(2)}) copy-start(bf16[1024,1024]{1,0:T(8,128)(2,1)S(1)} %get-tuple-element.30.refs_1_) | copy-start | bytes 6291460
  32.1 1.6 %copy-start.3 = (bf16[1024,1024]{1,0:T(8,128)(2,1)S(1)}, bf16[1024,1024]{1,0:T(8,128)(2,1)}, u32[]{:S(2)}) copy-start(bf16[1024,1024]{1,0:T(8,128)(2,1)} %copy-done.2) | copy-start | bytes 6291460
  38.7 1.3 %copy-start.4 = (bf16[1024,1024]{1,0:T(8,128)(2,1)}, bf16[1024,1024]{1,0:T(8,128)(2,1)S(1)}, u32[]{:S(2)}) copy-start(bf16[1024,1024]{1,0:T(8,128)(2,1)S(1)} %get-tuple-element.32.refs_1_) | copy-start | bytes 6291460
  40.1 1.6 %copy-start.5 = (bf16[1024,1024]{1,0:T(8,128)(2,1)S(1)}, bf16[1024,1024]{1,0:T(8,128)(2,1)}, u32[]{:S(2)}) copy-start(bf16[1024,1024]{1,0:T(8,128)(2,1)} %copy-done.4) | copy-start | bytes 6291460
  41.7 5.0 %copy-start.13 = (f32[64,1024]{1,0:T(8,128)S(1)}, f32[64,1024]{1,0:T(8,128)}, u32[]{:S(2)}) copy-start(f32[64,1024]{1,0:T(8,128)} %param.11) | copy-start | bytes 786436
  46.7 3.7 %copy-start.6 = (bf16[1024,1024]{1,0:T(8,128)(2,1)}, bf16[1024,1024]{1,0:T(8,128)(2,1)S(1)}, u32[]{:S(2)}) copy-start(bf16[1024,1024]{1,0:T(8,128)(2,1)S(1)} %get-tuple-element.38.refs_1_) | copy-start | bytes 6291460
  46.8 2.7 %collective-permute-start.6 = (f32[256,1024]{1,0:T(8,128)S(1)}, f32[256,1024]{1,0:T(8,128)S(1)}, u32[]{:S(2)}, u32[]{:S(2)}) collective-permute-start(f32[256,1024]{1,0:T(8,128)S(1)} %pad_maximum_fusion), channel_id=1, source_target_pairs={{0,1},{1,0},{2,3},{3,2},{4,5},{5,4},{6,7},{7,6},{8,9},{9,8},{10,11... | collective-permute-start | bytes 3145736 | tf_op jit(solution)/shard_map/ppermute | solution.py:30
  49.5 1.4 %copy-start.11 = (f32[256,1024]{1,0:T(8,128)}, f32[256,1024]{1,0:T(8,128)S(1)}, u32[]{:S(2)}) copy-start(f32[256,1024]{1,0:T(8,128)S(1)} %collective-permute-done.6) | copy-start | bytes 3145732
  50.5 7.1 %collective-permute-start.7 = (f32[16,512]{1,0:T(8,128)S(1)}, f32[16,512]{1,0:T(8,128)}, u32[]{:S(2)}, u32[]{:S(2)}) collective-permute-start(f32[16,512]{1,0:T(8,128)S(1)} %pad_maximum_fusion.3), channel_id=1, source_target_pairs={{0,8},{1,9},{2,10},{3,11},{4,12},{5,13},{6,14},{7,15},{8,0},{9,1},... | collective-permute-start | bytes 98312 | tf_op jit(solution)/shard_map/ppermute | solution.py:30
  51.0 1.6 %copy-start.7 = (bf16[1024,1024]{1,0:T(8,128)(2,1)S(1)}, bf16[1024,1024]{1,0:T(8,128)(2,1)}, u32[]{:S(2)}) copy-start(bf16[1024,1024]{1,0:T(8,128)(2,1)} %copy-done.6) | copy-start | bytes 6291460
  58.4 26.1 %copy-start.12 = (f32[256,1024]{1,0:T(8,128)S(1)}, f32[256,1024]{1,0:T(8,128)}, u32[]{:S(2)}) copy-start(f32[256,1024]{1,0:T(8,128)} %copy-done.11) | copy-start | bytes 3145732
  78.7 22.3 %copy-start.14 = (f32[16,64]{1,0:T(8,128)S(1)}, f32[16,64]{1,0:T(8,128)}, u32[]{:S(2)}) copy-start(f32[16,64]{1,0:T(8,128)} %param.14) | copy-start | bytes 12292
  78.7 22.3 %copy-start.15 = (f32[16,64]{1,0:T(8,128)S(1)}, f32[16,64]{1,0:T(8,128)}, u32[]{:S(2)}) copy-start(f32[16,64]{1,0:T(8,128)} %param.12) | copy-start | bytes 12292
  78.7 5.1 %collective-permute-start.8 = (f32[16,512]{1,0:T(8,128)S(1)}, f32[16,512]{1,0:T(8,128)S(1)}, u32[]{:S(2)}, u32[]{:S(2)}) collective-permute-start(f32[16,512]{1,0:T(8,128)S(1)} %slice.31), channel_id=1, source_target_pairs={{0,8},{1,9},{2,10},{3,11},{4,12},{5,13},{6,14},{7,15},{8,0},{9,1},... | collective-permute-start | bytes 98312 | tf_op jit(solution)/shard_map/ppermute | solution.py:30
  85.4 1.3 %collective-permute-start.9 = (f32[16,1024]{1,0:T(8,128)S(1)}, f32[16,1024]{1,0:T(8,128)S(1)}, u32[]{:S(2)}, u32[]{:S(2)}) collective-permute-start(f32[16,1024]{1,0:T(8,128)S(1)} %fusion.1), channel_id=1, source_target_pairs={{0,1},{1,0},{2,3},{3,2},{4,5},{5,4},{6,7},{7,6},{8,9},{9,8},{10,11... | collective-permute-start | bytes 196616 | tf_op jit(solution)/shard_map/ppermute | solution.py:30
  86.7 4.3 %collective-permute-start.10 = (f32[16,1024]{1,0:T(8,128)S(1)}, f32[16,1024]{1,0:T(8,128)S(1)}, u32[]{:S(2)}, u32[]{:S(2)}) collective-permute-start(f32[16,1024]{1,0:T(8,128)S(1)} %add.91), channel_id=1, source_target_pairs={{0,2},{1,3},{2,0},{3,1},{4,6},{5,7},{6,4},{7,5},{8,10},{9,11},{10,... | collective-permute-start | bytes 196616 | tf_op jit(solution)/shard_map/ppermute | solution.py:30
  91.0 4.3 %collective-permute-start.11 = (f32[16,1024]{1,0:T(8,128)S(1)}, f32[16,1024]{1,0:T(8,128)S(1)}, u32[]{:S(2)}, u32[]{:S(2)}) collective-permute-start(f32[16,1024]{1,0:T(8,128)S(1)} %add.92), channel_id=1, source_target_pairs={{0,4},{1,5},{2,6},{3,7},{4,0},{5,1},{6,2},{7,3},{8,12},{9,13},{10,... | collective-permute-start | bytes 196616 | tf_op jit(solution)/shard_map/ppermute | solution.py:30
  95.4 5.2 %collective-permute-start.12 = (f32[16,1024]{1,0:T(8,128)S(1)}, f32[16,1024]{1,0:T(8,128)S(1)}, u32[]{:S(2)}, u32[]{:S(2)}) collective-permute-start(f32[16,1024]{1,0:T(8,128)S(1)} %add.93), channel_id=1, source_target_pairs={{0,8},{1,9},{2,10},{3,11},{4,12},{5,13},{6,14},{7,15},{8,0},{9,1},... | collective-permute-start | bytes 196616 | tf_op jit(solution)/shard_map/ppermute | solution.py:30

commit v3 on v2

v3 whole, which is shorter than its diff:
```python
import functools
import math

import jax
import jax.numpy as jnp
from jax import lax
from jax.experimental import pallas as pl
from jax.experimental.pallas import tpu as pltpu
from jax.sharding import PartitionSpec as P

LATTICE = 65521

ridge_weight = 0.25
VMEM_BYTES = 48 << 20
STORE_BYTES = 12 << 20
HELD_BYTES = 16 << 20
F32 = jnp.float32
BF16 = jnp.bfloat16


def swap(value, bit, devices):
    return lax.ppermute(value, "samp", [(i, i ^ bit) for i in range(devices)])


def after(value, *others):
    return lax.optimization_barrier((value, *others))[0]


def reduce_all(value, devices):
    bit = 1
    while bit < devices:
        value = value + swap(value, bit, devices)
        bit *= 2
    return value


def plan(devices, piece_bytes):
    bits = [1 << k for k in range(devices.bit_length() - 1)]
    held = []
    for bit in [b for b in (devices // 4, *bits) if 0 < b < devices // 2]:
        if bit not in held and (2 << len(held)) * piece_bytes <= HELD_BYTES:
            held.append(bit)
    held = held[:1] + held[:0:-1] if len(held) > 1 else held
    return held, [b for b in bits if b not in held]


def split3(value):
    high = value.astype(BF16)
    rest = value - high.astype(F32)
    middle = rest.astype(BF16)
    low = (rest - middle.astype(F32)).astype(BF16)
    return high, middle, low


def kernel_tile(points, centre_ref, shift_ref, floor_ref, first, width):
    rows, dims = points.shape
    product = None
    for axis_number in range(dims):
        centre = centre_ref[axis_number : axis_number + 1, pl.ds(first, width)]
        point = jnp.broadcast_to(points[:, axis_number : axis_number + 1], (rows, width))
        arm = jnp.abs(point - centre) - shift_ref[axis_number]
        factor = arm * arm + floor_ref[axis_number]
        product = factor if product is None else product * factor
    return product


def fill_kernel(rows, points, centre_ref, shift_ref, floor_ref, high_ref, low_ref):
    centres_all = centre_ref.shape[1]
    width = min(512, centres_all)
    span = min(1024, centres_all)

    def part(base):
        for piece in range(span // width):
            first = base + piece * width
            if not isinstance(first, int):
                first = pl.multiple_of(first, width)
            tile = kernel_tile(points, centre_ref, shift_ref, floor_ref, first, width)
            high = tile.astype(BF16)
            high_ref[rows, pl.ds(first, width)] = high
            low_ref[rows, pl.ds(first, width)] = (tile - high.astype(F32)).astype(BF16)

    if centres_all == span:
        part(0)
    else:
        lax.fori_loop(0, centres_all // span, lambda i, _: part(i * span), None)


def generate(step_rows, rows_all, shift_ref, floor_ref, scale_ref, sample_ref, centre_ref, high_ref, low_ref):
    for step in range(rows_all // step_rows):
        rows = pl.ds(step * step_rows, step_rows)
        points = (sample_ref[:, rows].astype(F32) * scale_ref[...]).T
        fill_kernel(rows, points, centre_ref, shift_ref, floor_ref, high_ref, low_ref)


def store_rows(
    row_sets, step_rows, shift_ref, floor_ref, scale_ref, sample_ref, centre_ref, ready_ref, *refs
):
    high_ref, low_ref, token_ref = refs[-3:]
    del ready_ref

    def step(i, _):
        first = pl.multiple_of(row_sets[0] + i * step_rows, step_rows)
        rows = pl.ds(first, step_rows)
        points = (sample_ref[:, rows].astype(F32) * scale_ref[...]).T
        fill_kernel(rows, points, centre_ref, shift_ref, floor_ref, high_ref, low_ref)

    lax.fori_loop(0, row_sets[1], step, None)
    token_ref[...] = jnp.zeros_like(token_ref)


def kernel_rows(store, ready, samples, first_row, rows, rows_stored, constants):
    centre_scaled, shift, floor, scale = constants
    dims, centres_all = centre_scaled.shape
    smem = pl.BlockSpec(memory_space=pltpu.SMEM)
    vmem = pl.BlockSpec(memory_space=pltpu.VMEM)
    free = pl.BlockSpec(memory_space=pl.ANY)
    given = [] if store is None else list(store)
    kept = pltpu.VMEM((rows_stored, centres_all), BF16)
    step_rows = min(128, rows)
    high, low, token = pl.pallas_call(
        functools.partial(store_rows, (first_row, rows // step_rows), step_rows),
        in_specs=[smem, smem, vmem, vmem, vmem, free, *[vmem] * len(given)],
        out_specs=[vmem, vmem, vmem],
        out_shape=[kept, kept, jax.ShapeDtypeStruct((8, 128), jnp.int32)],
        input_output_aliases={6: 0, 7: 1} if given else {},
        compiler_params=pltpu.CompilerParams(vmem_limit_bytes=VMEM_BYTES),
        cost_estimate=pl.CostEstimate(
            flops=6 * dims * rows * centres_all,
            bytes_accessed=4 * rows * centres_all,
            transcendentals=0,
        ),
        name="kernel_rows",
    )(shift, floor, scale, samples, centre_scaled, ready, *given)
    return (high, low), token[0, 0]


def apply_kernel(high, low, coefficients, outs):
    contract = (((1,), (1,)), ((), ()))
    fitted = lax.dot_general(coefficients, high, contract, preferred_element_type=F32)
    fitted = fitted + lax.dot_general(coefficients, low, contract, preferred_element_type=F32)
    return fitted[0:outs] + (fitted[outs : 2 * outs] + fitted[2 * outs : 3 * outs])


def back_products(high, low, coefficients, outs):
    parts = jnp.concatenate(split3(apply_kernel(high, low, coefficients, outs)), axis=0)
    return jnp.dot(parts, high, preferred_element_type=F32) + jnp.dot(
        parts, low, preferred_element_type=F32
    )


def products(
    outs, block_rows, stored_rows, shift_ref, floor_ref, scale_ref, coef_ref, own_ref, centre_ref,
    sample_ref, *refs,
):
    if stored_rows:
        high_ref, low_ref, *refs = refs
    backward_ref, own_out_ref, parts_ref, sum_ref, made_high, made_low = refs
    own_rows = own_ref.shape[1]
    steps = (sample_ref.shape[1] - stored_rows) // block_rows
    share = stored_rows // steps

    high, middle, low = split3(coef_ref[...])
    parts_ref[0:outs] = high
    parts_ref[outs : 2 * outs] = middle
    parts_ref[2 * outs : 3 * outs] = low
    sum_ref[...] = jnp.zeros_like(sum_ref)
    own_high, own_low = made_high.at[1], made_low.at[1]
    rows = pl.ds(0, own_rows)
    fill_kernel(rows, own_ref[...].T, centre_ref, shift_ref, floor_ref, own_high, own_low)
    own_out_ref[...] = apply_kernel(own_high[rows], own_low[rows], parts_ref[...], outs)
    made_high[1] = jnp.zeros(made_high.shape[1:], BF16)
    made_low[1] = jnp.zeros(made_low.shape[1:], BF16)

    def step(i, _):
        now = lax.rem(i, 2)
        before = 1 - now
        coefficients = parts_ref[...]
        total = back_products(made_high[before], made_low[before], coefficients, outs)
        if share:
            rows = pl.ds(pl.multiple_of(i * share, share), share)
            total = total + back_products(high_ref[rows], low_ref[rows], coefficients, outs)
        columns = pl.ds(pl.multiple_of(stored_rows + i * block_rows, block_rows), block_rows)
        points = (sample_ref[:, columns].astype(F32) * scale_ref[...]).T
        for first in range(0, block_rows, 128):
            rows = pl.ds(first, 128)
            fill_kernel(
                rows, points[first : first + 128], centre_ref, shift_ref, floor_ref,
                made_high.at[now], made_low.at[now],
            )
        sum_ref[...] += total

    lax.fori_loop(0, steps, step, None)
    now = (steps - 1) % 2
    last = sum_ref[...] + back_products(made_high[now], made_low[now], parts_ref[...], outs)
    backward_ref[...] = last[0:outs] + (last[outs : 2 * outs] + last[2 * outs : 3 * outs])


def apply_products(store, samples, coefficients, own_scaled, block_rows, constants):
    centre_scaled, shift, floor, scale = constants
    outs, centres_all = coefficients.shape
    dims, own_rows = own_scaled.shape
    given = [] if store is None else list(store)
    stored_rows = given[0].shape[0] if given else 0
    smem = pl.BlockSpec(memory_space=pltpu.SMEM)
    vmem = pl.BlockSpec(memory_space=pltpu.VMEM)
    made = pltpu.VMEM((2, block_rows, centres_all), BF16)
    return pl.pallas_call(
        functools.partial(products, outs, block_rows, stored_rows),
        in_specs=[smem, smem, *[vmem] * (5 + len(given))],
        out_specs=[vmem, vmem],
        out_shape=[
            jax.ShapeDtypeStruct((outs, centres_all), F32),
            jax.ShapeDtypeStruct((outs, own_rows), F32),
        ],
        scratch_shapes=[
            pltpu.VMEM((3 * outs, centres_all), BF16),
            pltpu.VMEM((3 * outs, centres_all), F32),
            made,
            made,
        ],
        compiler_params=pltpu.CompilerParams(vmem_limit_bytes=VMEM_BYTES),
        cost_estimate=pl.CostEstimate(
            flops=6 * dims * (samples.shape[1] - stored_rows) * centres_all,
            bytes_accessed=4 * stored_rows * centres_all,
            transcendentals=0,
        ),
        name="products",
    )(shift, floor, scale, coefficients, own_scaled, centre_scaled, samples, *given)


def modulo(value):
    turns = (value.astype(F32) * (1.0 / LATTICE)).astype(jnp.int32)
    rest = value - turns * LATTICE
    rest = jnp.where(rest < 0, rest + LATTICE, rest)
    return jnp.where(rest >= LATTICE, rest - LATTICE, rest)


def prepare(lattice_ref, generator_ref, scale_ref, direction_ref, residual_ref, state_ref, centre_ref):
    outs = direction_ref.shape[0]
    state_ref[:outs] = direction_ref[...]
    state_ref[outs:] = residual_ref[...]
    generator = generator_ref[...]
    column = lattice_ref[...]
    upper = modulo(column * (generator >> 8))
    centre = modulo(upper * 256 + column * (generator & 255))
    centre_ref[...] = centre.astype(F32) * scale_ref[...]


def contract_last(left_array, right_array):
    return lax.dot_general(
        left_array,
        right_array,
        (((1,), (1,)), ((), ())),
        precision=lax.Precision.HIGHEST,
        preferred_element_type=F32,
    )


def body(samples, generator, weight_index, preconditioner, solution, residual, direction):
    highest = lax.Precision.HIGHEST
    devices = lax.axis_size("samp")
    index = lax.axis_index("samp")
    cen_dev, centres_all = preconditioner.shape
    samples_dev = samples.shape[1]
    outs = direction.shape[0]
    held, others = plan(devices, 4 * cen_dev * centres_all)

    weights_dim = 0.5 * jnp.power(0.75, weight_index.astype(F32))
    curve = 2.0 * math.pi * math.pi * weights_dim
    floor = 1.0 - curve / 12.0
    root = jnp.sqrt(curve)
    shift = 0.5 * root
    scale = (root / LATTICE)[:, None]

    order = [0]
    for bit in (*held, *others):
        order = order + [k ^ bit for k in order]
    lattice_index = (index ^ jnp.array(order, jnp.int32))[:, None] * cen_dev
    lattice_index = lattice_index + jnp.arange(cen_dev, dtype=jnp.int32)[None, :]
    state, centre_scaled = pl.pallas_call(
        prepare,
        out_shape=[
            jax.ShapeDtypeStruct((2 * outs, cen_dev), F32),
            jax.ShapeDtypeStruct((generator.shape[0], centres_all), F32),
        ],
        name="prepare",
    )(lattice_index.reshape(1, centres_all), generator[:, None], scale, direction, residual)
    own_scaled = centre_scaled[:, :cen_dev]
    constants = (centre_scaled, shift, floor, scale)

    half = samples_dev // 2
    use_store = 4 * half * centres_all <= STORE_BYTES
    store, filled = None, 0

    def fill(rows, ready):
        nonlocal store, filled
        rows = min(rows, half - filled) if use_store else 0
        if rows == 0:
            return 0
        store, token = kernel_rows(store, ready, samples, filled, rows, half, constants)
        filled += rows
        return token

    pieces = [preconditioner]
    early = [swap(preconditioner, bit, devices) for bit in held[:2]]
    pieces += early[:1]
    if len(early) > 1:
        pieces += [early[1], swap(early[0], held[1], devices)]
    bit = 1
    while bit < devices:
        other = swap(state, bit, devices)
        token = 0
        if bit > 1:
            token = fill(256 if 2 * bit == devices else 128, state)
        upper = (index & bit) + token != 0
        state = jnp.where(
            upper,
            jnp.concatenate([other, state], axis=1),
            jnp.concatenate([state, other], axis=1),
        )
        bit *= 2
    direction_full, residual_full = state[:outs], state[outs:]
    for bit in held[2:]:
        pieces += [swap(p, bit, devices) for p in pieces]

    coefficients = jnp.concatenate([contract_last(direction_full, p) for p in pieces], axis=1)
    token = fill(256, state)
    for bit in others:
        other = swap(coefficients, bit, devices)
        token = token + fill(256, coefficients)
        coefficients = jnp.concatenate([coefficients, other + jnp.asarray(token, F32)], axis=1)
    if use_store and filled < half:
        fill(half, coefficients)

    backward, kernel_products = apply_products(
        store, samples, coefficients, own_scaled, 256, constants
    )
    for bit in reversed(others):
        width = backward.shape[1] // 2
        backward = backward[:, :width] + swap(backward[:, width:], bit, devices)
    scale_total = float(samples_dev * devices) * float(centres_all)
    own_term = ridge_weight * kernel_products / centres_all
    applied = backward / scale_total + jnp.pad(
        own_term, ((0, 0), (0, backward.shape[1] - cen_dev))
    )
    partial_image, first = 0.0, 0
    for p in pieces:
        part = applied[:, first : first + p.shape[0]]
        partial_image += jnp.dot(part, p, precision=highest, preferred_element_type=F32)
        first += p.shape[0]
    image = reduce_all(partial_image, devices)

    first_row = index * cen_dev
    norm_old = jnp.sum(residual_full * residual_full, axis=1, keepdims=True)
    curvature = jnp.sum(direction_full * image, axis=1, keepdims=True)
    step_length = norm_old / curvature
    next_full = residual_full - step_length * image
    norm_new = jnp.sum(next_full * next_full, axis=1, keepdims=True)
    new_residual = lax.dynamic_slice_in_dim(next_full, first_row, cen_dev, 1)
    new_solution = solution + step_length * direction
    new_direction = new_residual + (norm_new / norm_old) * direction
    return (new_solution, new_residual, new_direction)


def solution(mesh):
    placed = (
        P("groups", "samp"),
        P(),
        P(),
        P("samp", None),
        P("groups", "samp"),
        P("groups", "samp"),
        P("groups", "samp"),
    )
    return jax.shard_map(
        body,
        mesh=mesh,
        in_specs=placed,
        out_specs=(P("groups", "samp"), P("groups", "samp"), P("groups", "samp")),
        check_vma=False,
    )
```

time: 102 us -> 118 us (1.16)
  local copies, waits for them, and re-layouts: 14.2 us -> 22.9 us
  matrix products: 3.59 us -> 10.1 us
  between operations: 0.8 us -> 4.41 us
  other arithmetic: 6.08 us -> 3.37 us
  starting transfers between devices: 16.8 us -> 19.5 us
  waiting for transfers between devices: 18.8 us -> 16.6 us
  Pallas kernels: 41.3 us -> 40 us
    unnamed x33 -> x48, local copies, waits for them, and re-layouts: 13 us -> 17.4 us
    dot_general x4 -> x8, matrix products: 1.52 us -> 5 us  [body(): jnp.dot(part, p, precision=highest, preferred_element_type=F32)]
    dot_general x4 -> x8, matrix products: 2.08 us -> 5.06 us  [contract_last(): lax.dot_general(left_array, right_array, (((1,), (1,)), ((), ())), precis...]
    ppermute x13 -> x17, starting transfers between devices: 16.8 us -> 19.5 us  [swap(): return lax.ppermute(value, 'samp', [(i, i ^ bit) for i in range(devices)])]
    concatenate x4 -> x0, other arithmetic: 2.71 us -> none  [the longest x1 1.8 us: body(): jnp.concatenate(pieces, axis=0)]
    slice x0 -> x5, local copies, waits for them, and re-layouts: none -> 2.56 us  [kernel_rows(): return ((high, low), token[0, 0])]
    ppermute x13 -> x17, waiting for transfers between devices: 18.8 us -> 16.6 us  [swap(): return lax.ppermute(value, 'samp', [(i, i ^ bit) for i in range(devices)])]
    pallas_call x6 -> x7, Pallas kernels: 41.3 us -> 40 us  [the longest x1 20.2 us: apply_products(): pl.pallas_call(functools.partial(products, outs, block_rows, stored_rows)...]
  transfers between devices with their start and end apart: 13 -> 17, of which waited for: 8 -> 9; matrix products, arithmetic and copies ran while one was open for 6% -> 6% of each run, Pallas kernels for 21% -> 16%
where the time goes in v3:
time: 118 us; the launch traced here: 117 us
  Pallas kernels  40 us (34%)
  local copies, waits for them, and re-layouts  22.9 us (19%)
  starting transfers between devices  19.5 us (17%)
  waiting for transfers between devices  16.6 us (14%)
  matrix products  10.1 us (9%)
  between operations  4.41 us (4%)
  other arithmetic  3.37 us (3%)
    pallas_call x1, Pallas kernels, apply_products(): pl.pallas_call(functools.partial(products, outs, block_rows, stored_rows)...  20.2 us
    ppermute x17, starting transfers between devices, swap(): return lax.ppermute(value, 'samp', [(i, i ^ bit) for i in range(devices)])  19.5 us
    pallas_call x5, Pallas kernels, kernel_rows(): pl.pallas_call(functools.partial(store_rows, (first_row, rows // step_row...  18.2 us
    unnamed x48, local copies, waits for them, and re-layouts  17.4 us
    ppermute x17, waiting for transfers between devices, swap(): return lax.ppermute(value, 'samp', [(i, i ^ bit) for i in range(devices)])  16.6 us
    dot_general x8, matrix products, contract_last(): lax.dot_general(left_array, right_array, (((1,), (1,)), ((), ())), precis...  5.06 us
    dot_general x8, matrix products, body(): jnp.dot(part, p, precision=highest, preferred_element_type=F32)  5 us
    slice x5, local copies, waits for them, and re-layouts, kernel_rows(): return ((high, low), token[0, 0])  2.56 us
  transfers between devices with their start and end apart: 17, of which 9 were waited for; matrix products, arithmetic and copies ran while one was open for 6% of the time, Pallas kernels for 16%

profile of v3, /device:TPU:0, one launch (start us, length us, event | category | flops | bytes accessed | tf_op | source)
XLA Modules:
  0.0 116.8 jit_solution(11259213991923153332)
XLA Ops:
  0.6 0.7 multiply_subtract_fusion.1
  1.3 0.7 copy.23.scale_ref
  2.0 0.7 xor_multiply_fusion
  2.7 0.7 add.95.lattice_ref
  3.4 1.3 %copy.19.generator_ref = s32[16,1]{1,0:T(8,128)} copy(s32[16,1]{0,1:T(1,128)} %bitcast.23) | data formatting | bytes 128 | tf_op jit(solution)/shard_map/broadcast_in_dim | solution.py:287
  4.7 1.5 %prepare.1 = (f32[32,64]{1,0:T(8,128)}, f32[16,1024]{1,0:T(8,128)}) custom-call(s32[1,1024]{1,0:T(1,128)} %add.95.lattice_ref, s32[16,1]{1,0:T(8,128)} %copy.19.generator_ref, f32[16,1]{1,0:T(8,128)} %copy.23.scale_ref, f32[16,64]{1,0:T(8,128)} %direction_ref.1, f32[16,64]{1,0:T(8,128)} %residual_ref.1), custom_call_target="tpu_custom_call" | custom-call | tf_op jit(solution)/shard_map/prepare/pallas_call | solution.py:280
  6.2 0.5 collective-permute-start
  6.7 1.0 collective-permute-done
  7.7 0.9 maximum_select_fusion.3.ready_ref
  8.6 2.9 %collective-permute-start.1 = (f32[32,128]{1,0:T(8,128)S(1)}, f32[32,128]{1,0:T(8,128)S(1)}, u32[]{:S(2)}, u32[]{:S(2)}) collective-permute-start(f32[32,128]{1,0:T(8,128)S(1)} %maximum_select_fusion.3.ready_ref), channel_id=1, source_target_pairs={{0,2},{1,3},{2,0},{3,1},{4,6},{5,7},{6,4},{7,5},{8,10},{9,11},{10,... | collective-permute-start | bytes 49160 | tf_op jit(solution)/shard_map/ppermute | solution.py:22
  11.5 0.9 copy-done.8
  12.4 0.8 copy-done.11
  13.2 0.7 copy-done.14
  13.9 2.5 %kernel_rows.5 = (bf16[1024,1024]{1,0:T(8,128)(2,1)S(1)}, bf16[1024,1024]{1,0:T(8,128)(2,1)S(1)}, s32[8,128]{1,0:T(8,128)S(1)}) custom-call(f32[16]{0:T(128)S(1)} %get-tuple-element.51.shift_ref, f32[16]{0:T(128)S(1)} %get-tuple-element.49.floor_ref, f32[16,1]{1,0:T(8,128)S(1)} %copy-done.14, s32[16,2048]{1,0:T(8,128)S(1)} %copy-done.8, ...), custom_call_target="tpu_custom_call" | custom-call | flops 12582912 | bytes 524288 | tf_op jit(solution)/shard_map/kernel_rows/pallas_call | solution.py:120
  16.4 1.4 %copy-done = bf16[1024,1024]{1,0:T(8,128)(2,1)} copy-done((bf16[1024,1024]{1,0:T(8,128)(2,1)}, bf16[1024,1024]{1,0:T(8,128)(2,1)S(1)}, u32[]{:S(2)}) %copy-start) | copy-done | bytes 2097176
  17.8 0.5 slice.54
  19.0 1.6 %collective-permute-start.2 = (f32[32,256]{1,0:T(8,128)S(1)}, f32[32,256]{1,0:T(8,128)S(1)}, u32[]{:S(2)}, u32[]{:S(2)}) collective-permute-start(f32[32,256]{1,0:T(8,128)S(1)} %maximum_select_fusion.2.ready_ref), channel_id=1, source_target_pairs={{0,4},{1,5},{2,6},{3,7},{4,0},{5,1},{6,2},{7,3},{8,12},{9,13},{10,... | collective-permute-start | bytes 98312 | tf_op jit(solution)/shard_map/ppermute | solution.py:22
  20.6 1.6 %copy-done.1 = bf16[1024,1024]{1,0:T(8,128)(2,1)S(1)} copy-done((bf16[1024,1024]{1,0:T(8,128)(2,1)S(1)}, bf16[1024,1024]{1,0:T(8,128)(2,1)}, u32[]{:S(2)}) %copy-start.1) | copy-done | bytes 2097176
  22.2 0.9 copy-done.9
  23.1 0.8 copy-done.12
  23.9 0.7 copy-done.15
  24.6 2.5 %kernel_rows.6 = (bf16[1024,1024]{1,0:T(8,128)(2,1)S(1)}, bf16[1024,1024]{1,0:T(8,128)(2,1)S(1)}, s32[8,128]{1,0:T(8,128)S(1)}) custom-call(f32[16]{0:T(128)S(1)} %get-tuple-element.51.shift_ref, f32[16]{0:T(128)S(1)} %get-tuple-element.49.floor_ref, f32[16,1]{1,0:T(8,128)S(1)} %copy-done.15, ...), custom_call_target="tpu_custom_call", output_to_operand_aliasing={{0}: (6, {}), {1}: (7, {})} | custom-call | flops 12582912 | bytes 524288 | tf_op jit(solution)/shard_map/kernel_rows/pallas_call | solution.py:120
  27.1 1.4 %copy-done.2 = bf16[1024,1024]{1,0:T(8,128)(2,1)} copy-done((bf16[1024,1024]{1,0:T(8,128)(2,1)}, bf16[1024,1024]{1,0:T(8,128)(2,1)S(1)}, u32[]{:S(2)}) %copy-start.2) | copy-done | bytes 2097176
  28.5 0.5 slice.55
  29.7 2.7 %collective-permute-start.3 = (f32[32,512]{1,0:T(8,128)S(1)}, f32[32,512]{1,0:T(8,128)S(1)}, u32[]{:S(2)}, u32[]{:S(2)}) collective-permute-start(f32[32,512]{1,0:T(8,128)S(1)} %maximum_select_fusion.1.ready_ref), channel_id=1, source_target_pairs={{0,8},{1,9},{2,10},{3,11},{4,12},{5,13},{6,14},{7,15},{8,0},{9,1},... | collective-permute-start | bytes 196616 | tf_op jit(solution)/shard_map/ppermute | solution.py:22
  32.3 0.4 collective-permute-start.4
  32.8 0.5 collective-permute-start.5
  33.3 1.6 %copy-done.3 = bf16[1024,1024]{1,0:T(8,128)(2,1)S(1)} copy-done((bf16[1024,1024]{1,0:T(8,128)(2,1)S(1)}, bf16[1024,1024]{1,0:T(8,128)(2,1)}, u32[]{:S(2)}) %copy-start.3) | copy-done | bytes 2097176
  34.9 4.5 %kernel_rows.7 = (bf16[1024,1024]{1,0:T(8,128)(2,1)S(1)}, bf16[1024,1024]{1,0:T(8,128)(2,1)S(1)}, s32[8,128]{1,0:T(8,128)S(1)}) custom-call(f32[16]{0:T(128)S(1)} %get-tuple-element.51.shift_ref, f32[16]{0:T(128)S(1)} %get-tuple-element.49.floor_ref, f32[16,1]{1,0:T(8,128)S(1)} %copy-done.16, ...), custom_call_target="tpu_custom_call", output_to_operand_aliasing={{0}: (6, {}), {1}: (7, {})} | custom-call | flops 25165824 | bytes 1048576 | tf_op jit(solution)/shard_map/kernel_rows/pallas_call | solution.py:120
  39.5 1.4 %copy-done.4 = bf16[1024,1024]{1,0:T(8,128)(2,1)} copy-done((bf16[1024,1024]{1,0:T(8,128)(2,1)}, bf16[1024,1024]{1,0:T(8,128)(2,1)S(1)}, u32[]{:S(2)}) %copy-start.4) | copy-done | bytes 2097176
  40.8 0.5 slice.56
  42.4 1.6 %collective-permute-start.6 = (f32[64,1024]{1,0:T(8,128)}, f32[64,1024]{1,0:T(8,128)S(1)}, u32[]{:S(2)}, u32[]{:S(2)}) collective-permute-start(f32[64,1024]{1,0:T(8,128)} %collective-permute-done.4), channel_id=1, source_target_pairs={{0,2},{1,3},{2,0},{3,1},{4,6},{5,7},{6,4},{7,5},{8,10},{9,11},{10,... | collective-permute-start | bytes 786440 | tf_op jit(solution)/shard_map/ppermute | solution.py:22
  44.2 0.3 collective-permute-start.9
  44.5 1.2 %fusion.12 = f32[16,64]{1,0:T(8,128)S(1)} fusion(f32[64,1024]{1,0:T(8,128)} %collective-permute-done.5, f32[32,1024]{1,0:T(8,128)S(1)} %maximum_select_fusion.ready_ref), kind=kOutput, calls=%fused_computation.23 | convolution fusion | flops 12582912 | bytes 331776 | tf_op jit(solution)/shard_map/dot_general | solution.py:250
  45.7 1.3 %fusion.14 = f32[16,64]{1,0:T(8,128)S(1)} fusion(f32[64,1024]{1,0:T(8,128)} %collective-permute-done.4, f32[32,1024]{1,0:T(8,128)S(1)} %maximum_select_fusion.ready_ref), kind=kOutput, calls=%fused_computation.25 | convolution fusion | flops 12582912 | bytes 331776 | tf_op jit(solution)/shard_map/dot_general | solution.py:250
  47.0 1.2 %fusion.8 = f32[16,64]{1,0:T(8,128)S(1)} fusion(f32[64,1024]{1,0:T(8,128)} %collective-permute-done.7, f32[32,1024]{1,0:T(8,128)S(1)} %maximum_select_fusion.ready_ref), kind=kOutput, calls=%fused_computation.19 | convolution fusion | flops 12582912 | bytes 331776 | tf_op jit(solution)/shard_map/dot_general | solution.py:250
  48.2 3.1 %collective-permute-done.6 = f32[64,1024]{1,0:T(8,128)S(1)} collective-permute-done((f32[64,1024]{1,0:T(8,128)}, f32[64,1024]{1,0:T(8,128)S(1)}, u32[]{:S(2)}, u32[]{:S(2)}) %collective-permute-start.6) | collective-permute-done | bytes 262176 | tf_op jit(solution)/shard_map/ppermute | solution.py:22
  52.0 0.3 fusion.6
  52.3 0.6 collective-permute-done.10
  52.9 0.7 copy-done.20
  54.2 1.6 %copy-done.5 = bf16[1024,1024]{1,0:T(8,128)(2,1)S(1)} copy-done((bf16[1024,1024]{1,0:T(8,128)(2,1)S(1)}, bf16[1024,1024]{1,0:T(8,128)(2,1)}, u32[]{:S(2)}) %copy-start.5) | copy-done | bytes 2097176
  55.8 4.4 %kernel_rows.8 = (bf16[1024,1024]{1,0:T(8,128)(2,1)S(1)}, bf16[1024,1024]{1,0:T(8,128)(2,1)S(1)}, s32[8,128]{1,0:T(8,128)S(1)}) custom-call(f32[16]{0:T(128)S(1)} %get-tuple-element.51.shift_ref, f32[16]{0:T(128)S(1)} %get-tuple-element.49.floor_ref, f32[16,1]{1,0:T(8,128)S(1)} %copy-done.16, ...), custom_call_target="tpu_custom_call", output_to_operand_aliasing={{0}: (6, {}), {1}: (7, {})} | custom-call | flops 25165824 | bytes 1048576 | tf_op jit(solution)/shard_map/kernel_rows/pallas_call | solution.py:120
  60.2 0.5 slice.59
  60.7 4.4 %kernel_rows.9 = (bf16[1024,1024]{1,0:T(8,128)(2,1)S(1)}, bf16[1024,1024]{1,0:T(8,128)(2,1)S(1)}, s32[8,128]{1,0:T(8,128)S(1)}) custom-call(f32[16]{0:T(128)S(1)} %get-tuple-element.51.shift_ref, f32[16]{0:T(128)S(1)} %get-tuple-element.49.floor_ref, f32[16,1]{1,0:T(8,128)S(1)} %copy-done.16, ...), custom_call_target="tpu_custom_call", output_to_operand_aliasing={{0}: (6, {}), {1}: (7, {})} | custom-call | flops 25165824 | bytes 1048576 | tf_op jit(solution)/shard_map/kernel_rows/pallas_call | solution.py:120
  65.1 1.4 %copy-done.6 = bf16[1024,1024]{1,0:T(8,128)(2,1)} copy-done((bf16[1024,1024]{1,0:T(8,128)(2,1)}, bf16[1024,1024]{1,0:T(8,128)(2,1)S(1)}, u32[]{:S(2)}) %copy-start.6) | copy-done | bytes 2097176
  66.4 0.5 slice.60
  68.3 1.6 %copy-done.7 = bf16[1024,1024]{1,0:T(8,128)(2,1)S(1)} copy-done((bf16[1024,1024]{1,0:T(8,128)(2,1)S(1)}, bf16[1024,1024]{1,0:T(8,128)(2,1)}, u32[]{:S(2)}) %copy-start.7) | copy-done | bytes 2097176
  69.9 20.2 %products.1 = (f32[16,1024]{1,0:T(8,128)S(1)}, f32[16,64]{1,0:T(8,128)S(1)}) custom-call(f32[16]{0:T(128)S(1)} %get-tuple-element.51.shift_ref, f32[16]{0:T(128)S(1)} %get-tuple-element.49.floor_ref, f32[16,1]{1,0:T(8,128)S(1)} %copy-done.16, f32[16,1024]{1,0:T(8,128)S(1)} %concatenate.40.coef_ref, f32[16,64]{1,0:T(8,128)S(1)} %slice.61.own_ref, ...), custom_call_target="tpu_custom_call" | custom-call | flops 100663296 | bytes 4194304 | tf_op jit(solution)/shard_map/products/pallas_call | solution.py:207
  90.2 2.9 %collective-permute-start.12 = (f32[16,512]{1,0:T(8,128)S(1)}, f32[16,512]{1,0:T(8,128)S(1)}, u32[]{:S(2)}, u32[]{:S(2)}) collective-permute-start(f32[16,512]{1,0:T(8,128)S(1)} %slice.63), channel_id=1, source_target_pairs={{0,8},{1,9},{2,10},{3,11},{4,12},{5,13},{6,14},{7,15},{8,0},{9,1},... | collective-permute-start | bytes 98312 | tf_op jit(solution)/shard_map/ppermute | solution.py:22
  93.1 2.4 %collective-permute-done.12 = f32[16,512]{1,0:T(8,128)S(1)} collective-permute-done((f32[16,512]{1,0:T(8,128)S(1)}, f32[16,512]{1,0:T(8,128)S(1)}, u32[]{:S(2)}, u32[]{:S(2)}) %collective-permute-start.12) | collective-permute-done | bytes 32800 | tf_op jit(solution)/shard_map/ppermute | solution.py:22
  95.4 1.2 %fusion.26 = f32[16,1024]{1,0:T(8,128)S(1)} fusion(f32[64,1024]{1,0:T(8,128)} %collective-permute-done.4, f32[16,512]{1,0:T(8,128)S(1)} %pad_add_fusion), kind=kOutput, calls=%fused_computation.41 | convolution fusion | flops 12582912 | bytes 335872 | tf_op jit(solution)/shard_map/dot_general | solution.py:349
  96.9 1.2 %fusion.22 = f32[16,1024]{1,0:T(8,128)S(1)} fusion(f32[64,1024]{1,0:T(8,128)} %collective-permute-done.7, f32[16,512]{1,0:T(8,128)S(1)} %pad_add_fusion), kind=kOutput, calls=%fused_computation.37 | convolution fusion | flops 12582912 | bytes 335872 | tf_op jit(solution)/shard_map/dot_general | solution.py:349
  98.4 1.2 %convolution_add_fusion.3 = f32[16,1024]{1,0:T(8,128)S(1)} fusion(f32[16,1024]{1,0:T(8,128)S(1)} %convolution_add_fusion.4, f32[64,1024]{1,0:T(8,128)} %collective-permute-done.5, f32[16,512]{1,0:T(8,128)S(1)} %pad_add_fusion), kind=kOutput, calls=%fused_computation.3 | convolution fusion | flops 12599296 | bytes 401408 | tf_op jit(solution)/shard_map/dot_general | solution.py:349
  99.6 0.3 fusion
  99.9 0.3 fusion.1
  100.2 0.3 convolution_add_fusion
  100.6 1.2 %collective-permute-done.13 = f32[16,1024]{1,0:T(8,128)S(1)} collective-permute-done((f32[16,1024]{1,0:T(8,128)S(1)}, f32[16,1024]{1,0:T(8,128)S(1)}, u32[]{:S(2)}, u32[]{:S(2)}) %collective-permute-start.13) | collective-permute-done | bytes 65568 | tf_op jit(solution)/shard_map/ppermute | solution.py:22
  101.9 1.7 %collective-permute-start.14 = (f32[16,1024]{1,0:T(8,128)S(1)}, f32[16,1024]{1,0:T(8,128)S(1)}, u32[]{:S(2)}, u32[]{:S(2)}) collective-permute-start(f32[16,1024]{1,0:T(8,128)S(1)} %add.111), channel_id=1, source_target_pairs={{0,2},{1,3},{2,0},{3,1},{4,6},{5,7},{6,4},{7,5},{8,10},{9,11},{10,... | collective-permute-start | bytes 196616 | tf_op jit(solution)/shard_map/ppermute | solution.py:22
  103.6 2.6 %collective-permute-done.14 = f32[16,1024]{1,0:T(8,128)S(1)} collective-permute-done((f32[16,1024]{1,0:T(8,128)S(1)}, f32[16,1024]{1,0:T(8,128)S(1)}, u32[]{:S(2)}, u32[]{:S(2)}) %collective-permute-start.14) | collective-permute-done | bytes 65568 | tf_op jit(solution)/shard_map/ppermute | solution.py:22
  106.2 1.5 %collective-permute-start.15 = (f32[16,1024]{1,0:T(8,128)S(1)}, f32[16,1024]{1,0:T(8,128)S(1)}, u32[]{:S(2)}, u32[]{:S(2)}) collective-permute-start(f32[16,1024]{1,0:T(8,128)S(1)} %add.112), channel_id=1, source_target_pairs={{0,4},{1,5},{2,6},{3,7},{4,0},{5,1},{6,2},{7,3},{8,12},{9,13},{10,... | collective-permute-start | bytes 196616 | tf_op jit(solution)/shard_map/ppermute | solution.py:22
  107.7 2.8 %collective-permute-done.15 = f32[16,1024]{1,0:T(8,128)S(1)} collective-permute-done((f32[16,1024]{1,0:T(8,128)S(1)}, f32[16,1024]{1,0:T(8,128)S(1)}, u32[]{:S(2)}, u32[]{:S(2)}) %collective-permute-start.15) | collective-permute-done | bytes 65568 | tf_op jit(solution)/shard_map/ppermute | solution.py:22
  110.5 2.5 %collective-permute-start.16 = (f32[16,1024]{1,0:T(8,128)S(1)}, f32[16,1024]{1,0:T(8,128)S(1)}, u32[]{:S(2)}, u32[]{:S(2)}) collective-permute-start(f32[16,1024]{1,0:T(8,128)S(1)} %add.113), channel_id=1, source_target_pairs={{0,8},{1,9},{2,10},{3,11},{4,12},{5,13},{6,14},{7,15},{8,0},{9,1},... | collective-permute-start | bytes 196616 | tf_op jit(solution)/shard_map/ppermute | solution.py:22
  113.1 2.7 %collective-permute-done.16 = f32[16,1024]{1,0:T(8,128)S(1)} collective-permute-done((f32[16,1024]{1,0:T(8,128)S(1)}, f32[16,1024]{1,0:T(8,128)S(1)}, u32[]{:S(2)}, u32[]{:S(2)}) %collective-permute-start.16) | collective-permute-done | bytes 65568 | tf_op jit(solution)/shard_map/ppermute | solution.py:22
  116.1 0.7 multiply_add_fusion
  (71 shorter events, 2.9 us)
Async XLA Ops:
  6.2 1.5 %collective-permute-start = (f32[32,64]{1,0:T(8,128)}, f32[32,64]{1,0:T(8,128)S(1)}, u32[]{:S(2)}, u32[]{:S(2)}) collective-permute-start(f32[32,64]{1,0:T(8,128)} %get-tuple-element.23), channel_id=1, source_target_pairs={{0,1},{1,0},{2,3},{3,2},{4,5},{5,4},{6,7},{7,6},{8,9},{9,8},{10,11... | collective-permute-start | bytes 24584 | tf_op jit(solution)/shard_map/ppermute | solution.py:22
  8.6 10.3 %collective-permute-start.1 = (f32[32,128]{1,0:T(8,128)S(1)}, f32[32,128]{1,0:T(8,128)S(1)}, u32[]{:S(2)}, u32[]{:S(2)}) collective-permute-start(f32[32,128]{1,0:T(8,128)S(1)} %maximum_select_fusion.3.ready_ref), channel_id=1, source_target_pairs={{0,2},{1,3},{2,0},{3,1},{4,6},{5,7},{6,4},{7,5},{8,10},{9,11},{10,... | collective-permute-start | bytes 49160 | tf_op jit(solution)/shard_map/ppermute | solution.py:22
  11.5 0.9 copy-start.8
  12.4 0.8 copy-start.11
  13.2 0.7 copy-start.14
  16.4 1.4 %copy-start = (bf16[1024,1024]{1,0:T(8,128)(2,1)}, bf16[1024,1024]{1,0:T(8,128)(2,1)S(1)}, u32[]{:S(2)}) copy-start(bf16[1024,1024]{1,0:T(8,128)(2,1)S(1)} %get-tuple-element.26.refs_1_) | copy-start | bytes 6291460
  19.0 10.7 %collective-permute-start.2 = (f32[32,256]{1,0:T(8,128)S(1)}, f32[32,256]{1,0:T(8,128)S(1)}, u32[]{:S(2)}, u32[]{:S(2)}) collective-permute-start(f32[32,256]{1,0:T(8,128)S(1)} %maximum_select_fusion.2.ready_ref), channel_id=1, source_target_pairs={{0,4},{1,5},{2,6},{3,7},{4,0},{5,1},{6,2},{7,3},{8,12},{9,13},{10,... | collective-permute-start | bytes 98312 | tf_op jit(solution)/shard_map/ppermute | solution.py:22
  20.6 1.6 %copy-start.1 = (bf16[1024,1024]{1,0:T(8,128)(2,1)S(1)}, bf16[1024,1024]{1,0:T(8,128)(2,1)}, u32[]{:S(2)}) copy-start(bf16[1024,1024]{1,0:T(8,128)(2,1)} %copy-done) | copy-start | bytes 6291460
  22.2 0.9 copy-start.9
  23.1 0.8 copy-start.12
  23.9 0.7 copy-start.15
  24.6 7.7 %copy-start.17 = (f32[64,1024]{1,0:T(8,128)S(1)}, f32[64,1024]{1,0:T(8,128)}, u32[]{:S(2)}) copy-start(f32[64,1024]{1,0:T(8,128)} %param.11) | copy-start | bytes 786436
  24.6 8.7 %copy-start.10 = (s32[16,2048]{1,0:T(8,128)S(1)}, s32[16,2048]{1,0:T(8,128)}, u32[]{:S(2)}) copy-start(s32[16,2048]{1,0:T(8,128)} %sample_ref.11) | copy-start | bytes 393220
  24.6 8.7 %copy-start.13 = (f32[16,1024]{1,0:T(8,128)S(1)}, f32[16,1024]{1,0:T(8,128)}, u32[]{:S(2)}) copy-start(f32[16,1024]{1,0:T(8,128)} %get-tuple-element.22.centre_ref) | copy-start | bytes 196612
  24.6 8.7 %copy-start.16 = (f32[16,1]{1,0:T(8,128)S(1)}, f32[16,1]{1,0:T(8,128)}, u32[]{:S(2)}) copy-start(f32[16,1]{1,0:T(8,128)} %copy.23.scale_ref) | copy-start | bytes 196
  27.1 1.4 %copy-start.2 = (bf16[1024,1024]{1,0:T(8,128)(2,1)}, bf16[1024,1024]{1,0:T(8,128)(2,1)S(1)}, u32[]{:S(2)}) copy-start(bf16[1024,1024]{1,0:T(8,128)(2,1)S(1)} %get-tuple-element.29.refs_1_) | copy-start | bytes 6291460
  29.7 12.3 %collective-permute-start.3 = (f32[32,512]{1,0:T(8,128)S(1)}, f32[32,512]{1,0:T(8,128)S(1)}, u32[]{:S(2)}, u32[]{:S(2)}) collective-permute-start(f32[32,512]{1,0:T(8,128)S(1)} %maximum_select_fusion.1.ready_ref), channel_id=1, source_target_pairs={{0,8},{1,9},{2,10},{3,11},{4,12},{5,13},{6,14},{7,15},{8,0},{9,1},... | collective-permute-start | bytes 196616 | tf_op jit(solution)/shard_map/ppermute | solution.py:22
  32.3 10.0 %collective-permute-start.4 = (f32[64,1024]{1,0:T(8,128)S(1)}, f32[64,1024]{1,0:T(8,128)}, u32[]{:S(2)}, u32[]{:S(2)}) collective-permute-start(f32[64,1024]{1,0:T(8,128)S(1)} %copy-done.17), channel_id=1, source_target_pairs={{0,4},{1,5},{2,6},{3,7},{4,0},{5,1},{6,2},{7,3},{8,12},{9,13},{10,... | collective-permute-start | bytes 786440 | tf_op jit(solution)/shard_map/ppermute | solution.py:22
  32.8 11.4 %collective-permute-start.5 = (f32[64,1024]{1,0:T(8,128)S(1)}, f32[64,1024]{1,0:T(8,128)}, u32[]{:S(2)}, u32[]{:S(2)}) collective-permute-start(f32[64,1024]{1,0:T(8,128)S(1)} %copy-done.17), channel_id=1, source_target_pairs={{0,2},{1,3},{2,0},{3,1},{4,6},{5,7},{6,4},{7,5},{8,10},{9,11},{10,... | collective-permute-start | bytes 786440 | tf_op jit(solution)/shard_map/ppermute | solution.py:22
  33.3 13.7 %collective-permute-start.7 = (f32[64,1024]{1,0:T(8,128)S(1)}, f32[64,1024]{1,0:T(8,128)}, u32[]{:S(2)}, u32[]{:S(2)}) collective-permute-start(f32[64,1024]{1,0:T(8,128)S(1)} %copy-done.17), channel_id=1, source_target_pairs={{0,1},{1,0},{2,3},{3,2},{4,5},{5,4},{6,7},{7,6},{8,9},{9,8},{10,11... | collective-permute-start | bytes 786440 | tf_op jit(solution)/shard_map/ppermute | solution.py:22
  33.3 1.6 %copy-start.3 = (bf16[1024,1024]{1,0:T(8,128)(2,1)S(1)}, bf16[1024,1024]{1,0:T(8,128)(2,1)}, u32[]{:S(2)}) copy-start(bf16[1024,1024]{1,0:T(8,128)(2,1)} %copy-done.2) | copy-start | bytes 6291460
  39.5 1.4 %copy-start.4 = (bf16[1024,1024]{1,0:T(8,128)(2,1)}, bf16[1024,1024]{1,0:T(8,128)(2,1)S(1)}, u32[]{:S(2)}) copy-start(bf16[1024,1024]{1,0:T(8,128)(2,1)S(1)} %get-tuple-element.32.refs_1_) | copy-start | bytes 6291460
  42.4 9.0 %collective-permute-start.6 = (f32[64,1024]{1,0:T(8,128)}, f32[64,1024]{1,0:T(8,128)S(1)}, u32[]{:S(2)}, u32[]{:S(2)}) collective-permute-start(f32[64,1024]{1,0:T(8,128)} %collective-permute-done.4), channel_id=1, source_target_pairs={{0,2},{1,3},{2,0},{3,1},{4,6},{5,7},{6,4},{7,5},{8,10},{9,11},{10,... | collective-permute-start | bytes 786440 | tf_op jit(solution)/shard_map/ppermute | solution.py:22
  43.9 8.0 %collective-permute-start.8 = (f32[64,1024]{1,0:T(8,128)}, f32[64,1024]{1,0:T(8,128)S(1)}, u32[]{:S(2)}, u32[]{:S(2)}) collective-permute-start(f32[64,1024]{1,0:T(8,128)} %collective-permute-done.4), channel_id=1, source_target_pairs={{0,1},{1,0},{2,3},{3,2},{4,5},{5,4},{6,7},{7,6},{8,9},{9,8},{10,11... | collective-permute-start | bytes 786440 | tf_op jit(solution)/shard_map/ppermute | solution.py:22
  44.2 7.5 %collective-permute-start.9 = (f32[64,1024]{1,0:T(8,128)}, f32[64,1024]{1,0:T(8,128)S(1)}, u32[]{:S(2)}, u32[]{:S(2)}) collective-permute-start(f32[64,1024]{1,0:T(8,128)} %collective-permute-done.5), channel_id=1, source_target_pairs={{0,1},{1,0},{2,3},{3,2},{4,5},{5,4},{6,7},{7,6},{8,9},{9,8},{10,11... | collective-permute-start | bytes 786440 | tf_op jit(solution)/shard_map/ppermute | solution.py:22
  51.3 1.5 %collective-permute-start.10 = (f32[64,1024]{1,0:T(8,128)S(1)}, f32[64,1024]{1,0:T(8,128)S(1)}, u32[]{:S(2)}, u32[]{:S(2)}) collective-permute-start(f32[64,1024]{1,0:T(8,128)S(1)} %collective-permute-done.6), channel_id=1, source_target_pairs={{0,1},{1,0},{2,3},{3,2},{4,5},{5,4},{6,7},{7,6},{8,9},{9,8},{10,11... | collective-permute-start | bytes 786440 | tf_op jit(solution)/shard_map/ppermute | solution.py:22
  51.7 1.2 %copy-start.18 = (f32[64,1024]{1,0:T(8,128)}, f32[64,1024]{1,0:T(8,128)S(1)}, u32[]{:S(2)}) copy-start(f32[64,1024]{1,0:T(8,128)S(1)} %collective-permute-done.9) | copy-start | bytes 786436
  52.9 0.7 copy-start.20
  54.0 14.2 %collective-permute-start.11 = (f32[16,512]{1,0:T(8,128)S(1)}, f32[16,512]{1,0:T(8,128)S(1)}, u32[]{:S(2)}, u32[]{:S(2)}) collective-permute-start(f32[16,512]{1,0:T(8,128)S(1)} %concatenate.39.ready_ref), channel_id=1, source_target_pairs={{0,8},{1,9},{2,10},{3,11},{4,12},{5,13},{6,14},{7,15},{8,0},{9,1},... | collective-permute-start | bytes 98312 | tf_op jit(solution)/shard_map/ppermute | solution.py:22
  54.2 1.6 %copy-start.5 = (bf16[1024,1024]{1,0:T(8,128)(2,1)S(1)}, bf16[1024,1024]{1,0:T(8,128)(2,1)}, u32[]{:S(2)}) copy-start(bf16[1024,1024]{1,0:T(8,128)(2,1)} %copy-done.4) | copy-start | bytes 6291460
  65.0 1.4 %copy-start.6 = (bf16[1024,1024]{1,0:T(8,128)(2,1)}, bf16[1024,1024]{1,0:T(8,128)(2,1)S(1)}, u32[]{:S(2)}) copy-start(bf16[1024,1024]{1,0:T(8,128)(2,1)S(1)} %get-tuple-element.38.refs_1_) | copy-start | bytes 6291460
  68.3 1.6 %copy-start.7 = (bf16[1024,1024]{1,0:T(8,128)(2,1)S(1)}, bf16[1024,1024]{1,0:T(8,128)(2,1)}, u32[]{:S(2)}) copy-start(bf16[1024,1024]{1,0:T(8,128)(2,1)} %copy-done.6) | copy-start | bytes 6291460
  69.9 28.2 %copy-start.19 = (f32[64,1024]{1,0:T(8,128)S(1)}, f32[64,1024]{1,0:T(8,128)}, u32[]{:S(2)}) copy-start(f32[64,1024]{1,0:T(8,128)} %copy-done.18) | copy-start | bytes 786436
  90.2 10.1 %copy-start.21 = (f32[64,1024]{1,0:T(8,128)S(1)}, f32[64,1024]{1,0:T(8,128)}, u32[]{:S(2)}) copy-start(f32[64,1024]{1,0:T(8,128)} %copy-done.20) | copy-start | bytes 786436
  90.2 5.2 %collective-permute-start.12 = (f32[16,512]{1,0:T(8,128)S(1)}, f32[16,512]{1,0:T(8,128)S(1)}, u32[]{:S(2)}, u32[]{:S(2)}) collective-permute-start(f32[16,512]{1,0:T(8,128)S(1)} %slice.63), channel_id=1, source_target_pairs={{0,8},{1,9},{2,10},{3,11},{4,12},{5,13},{6,14},{7,15},{8,0},{9,1},... | collective-permute-start | bytes 98312 | tf_op jit(solution)/shard_map/ppermute | solution.py:22
  95.4 20.7 %copy-start.22 = (f32[16,64]{1,0:T(8,128)S(1)}, f32[16,64]{1,0:T(8,128)}, u32[]{:S(2)}) copy-start(f32[16,64]{1,0:T(8,128)} %direction_ref.1) | copy-start | bytes 12292
  95.4 20.7 %copy-start.23 = (f32[16,64]{1,0:T(8,128)S(1)}, f32[16,64]{1,0:T(8,128)}, u32[]{:S(2)}) copy-start(f32[16,64]{1,0:T(8,128)} %param.12) | copy-start | bytes 12292
  100.5 1.3 %collective-permute-start.13 = (f32[16,1024]{1,0:T(8,128)S(1)}, f32[16,1024]{1,0:T(8,128)S(1)}, u32[]{:S(2)}, u32[]{:S(2)}) collective-permute-start(f32[16,1024]{1,0:T(8,128)S(1)} %convolution_add_fusion), channel_id=1, source_target_pairs={{0,1},{1,0},{2,3},{3,2},{4,5},{5,4},{6,7},{7,6},{8,9},{9,8},{10,11... | collective-permute-start | bytes 196616 | tf_op jit(solution)/shard_map/ppermute | solution.py:22
  101.9 4.3 %collective-permute-start.14 = (f32[16,1024]{1,0:T(8,128)S(1)}, f32[16,1024]{1,0:T(8,128)S(1)}, u32[]{:S(2)}, u32[]{:S(2)}) collective-permute-start(f32[16,1024]{1,0:T(8,128)S(1)} %add.111), channel_id=1, source_target_pairs={{0,2},{1,3},{2,0},{3,1},{4,6},{5,7},{6,4},{7,5},{8,10},{9,11},{10,... | collective-permute-start | bytes 196616 | tf_op jit(solution)/shard_map/ppermute | solution.py:22
  106.2 4.3 %collective-permute-start.15 = (f32[16,1024]{1,0:T(8,128)S(1)}, f32[16,1024]{1,0:T(8,128)S(1)}, u32[]{:S(2)}, u32[]{:S(2)}) collective-permute-start(f32[16,1024]{1,0:T(8,128)S(1)} %add.112), channel_id=1, source_target_pairs={{0,4},{1,5},{2,6},{3,7},{4,0},{5,1},{6,2},{7,3},{8,12},{9,13},{10,... | collective-permute-start | bytes 196616 | tf_op jit(solution)/shard_map/ppermute | solution.py:22
  110.5 5.2 %collective-permute-start.16 = (f32[16,1024]{1,0:T(8,128)S(1)}, f32[16,1024]{1,0:T(8,128)S(1)}, u32[]{:S(2)}, u32[]{:S(2)}) collective-permute-start(f32[16,1024]{1,0:T(8,128)S(1)} %add.113), channel_id=1, source_target_pairs={{0,8},{1,9},{2,10},{3,11},{4,12},{5,13},{6,14},{7,15},{8,0},{9,1},... | collective-permute-start | bytes 196616 | tf_op jit(solution)/shard_map/ppermute | solution.py:22

commit v4 on v3

v4 whole, which is shorter than its diff:
```python
import functools
import math

import jax
import jax.numpy as jnp
from jax import lax
from jax.experimental import pallas as pl
from jax.experimental.pallas import tpu as pltpu
from jax.sharding import PartitionSpec as P

LATTICE = 65521

ridge_weight = 0.25
STORE_BYTES = 12 << 20
HELD_BYTES = 16 << 20
VMEM = pl.BlockSpec(memory_space=pltpu.VMEM)
SMEM = pl.BlockSpec(memory_space=pltpu.SMEM)
F32 = jnp.float32
BF16 = jnp.bfloat16


def swap(value, bit, devices):
    return lax.ppermute(value, "samp", [(i, i ^ bit) for i in range(devices)])


def plan(devices, piece_bytes):
    bits = [1 << k for k in range(devices.bit_length() - 1)]
    held = []
    for bit in [b for b in (devices // 4, *bits) if 0 < b < devices // 2]:
        if bit not in held and (2 << len(held)) * piece_bytes <= HELD_BYTES:
            held.append(bit)
    held = held[:1] + held[:0:-1] if len(held) > 1 else held
    return held, [b for b in bits if b not in held]


def split3(value):
    high = value.astype(BF16)
    rest = value - high.astype(F32)
    middle = rest.astype(BF16)
    low = (rest - middle.astype(F32)).astype(BF16)
    return high, middle, low


def stack3(value):
    return jnp.concatenate(split3(value), axis=0)


def add_parts(value, outs):
    return value[:outs] + (value[outs : 2 * outs] + value[2 * outs :])


def kernel_tile(points, centre_ref, shift_ref, floor_ref, first, width):
    rows, dims = points.shape
    product = None
    for axis_number in range(dims):
        centre = centre_ref[axis_number : axis_number + 1, pl.ds(first, width)]
        point = jnp.broadcast_to(points[:, axis_number : axis_number + 1], (rows, width))
        arm = jnp.abs(point - centre) - shift_ref[axis_number]
        factor = arm * arm + floor_ref[axis_number]
        product = factor if product is None else product * factor
    return product


def fill_kernel(rows, points, centre_ref, shift_ref, floor_ref, high_ref, low_ref):
    centres_all = centre_ref.shape[1]
    width = min(512, centres_all)
    span = min(1024, centres_all)

    def part(base):
        for piece in range(span // width):
            first = base + piece * width
            if not isinstance(first, int):
                first = pl.multiple_of(first, width)
            tile = kernel_tile(points, centre_ref, shift_ref, floor_ref, first, width)
            high = tile.astype(BF16)
            high_ref[rows, pl.ds(first, width)] = high
            low_ref[rows, pl.ds(first, width)] = (tile - high.astype(F32)).astype(BF16)

    if centres_all == span:
        part(0)
    else:
        lax.fori_loop(0, centres_all // span, lambda i, _: part(i * span), None)


def store_rows(row_set, step_rows, shift_ref, floor_ref, scale_ref, sample_ref, centre_ref, passed_ref, *refs):
    high_ref, low_ref, handed_ref = refs[-3:]

    def step(i, _):
        first = pl.multiple_of(row_set[0] + i * step_rows, step_rows)
        rows = pl.ds(first, step_rows)
        points = (sample_ref[:, rows].astype(F32) * scale_ref[...]).T
        fill_kernel(rows, points, centre_ref, shift_ref, floor_ref, high_ref, low_ref)

    lax.fori_loop(0, row_set[1], step, None)
    handed_ref[...] = passed_ref[...]


def kernel_rows(store, passed, samples, first_row, rows, rows_stored, constants):
    centre_scaled, shift, floor, scale = constants
    dims, centres_all = centre_scaled.shape
    given = [] if store is None else list(store)
    kept = pltpu.VMEM((rows_stored, centres_all), BF16)
    step_rows = min(128, rows)
    high, low, handed = pl.pallas_call(
        functools.partial(store_rows, (first_row, rows // step_rows), step_rows),
        in_specs=[SMEM, SMEM, *[VMEM] * (4 + len(given))],
        out_specs=[VMEM, VMEM, VMEM],
        out_shape=[kept, kept, jax.ShapeDtypeStruct(passed.shape, passed.dtype)],
        input_output_aliases={6: 0, 7: 1} if given else {},
        compiler_params=pltpu.CompilerParams(vmem_limit_bytes=8 << 20),
        cost_estimate=pl.CostEstimate(
            flops=6 * dims * rows * centres_all,
            bytes_accessed=4 * rows * centres_all,
            transcendentals=0,
        ),
        name="kernel_rows",
    )(shift, floor, scale, samples, centre_scaled, passed, *given)
    return (high, low), handed


def apply_kernel(high, low, coefficients, outs):
    contract = (((1,), (1,)), ((), ()))
    fitted = lax.dot_general(coefficients, high, contract, preferred_element_type=F32)
    fitted = fitted + lax.dot_general(coefficients, low, contract, preferred_element_type=F32)
    return add_parts(fitted, outs)


def back_products(high, low, coefficients, outs):
    parts = stack3(apply_kernel(high, low, coefficients, outs))
    return jnp.dot(parts, high, preferred_element_type=F32) + jnp.dot(
        parts, low, preferred_element_type=F32
    )


def products(
    outs, block_rows, stored_rows, shift_ref, floor_ref, scale_ref, coef_ref, centre_ref,
    sample_ref, *refs,
):
    if stored_rows:
        high_ref, low_ref, *refs = refs
    *backward_refs, own_out_ref, parts_ref, sum_ref, made_high, made_low = refs
    own_rows = own_out_ref.shape[1]
    steps = (sample_ref.shape[1] - stored_rows) // block_rows
    share = stored_rows // steps

    parts_ref[...] = stack3(coef_ref[...])
    sum_ref[...] = jnp.zeros_like(sum_ref)
    own_high, own_low = made_high.at[1], made_low.at[1]
    rows = pl.ds(0, own_rows)
    own_points = centre_ref[:, :own_rows]
    fill_kernel(rows, own_points.T, centre_ref, shift_ref, floor_ref, own_high, own_low)
    own_out_ref[...] = apply_kernel(own_high[rows], own_low[rows], parts_ref[...], outs)
    made_high[1] = jnp.zeros(made_high.shape[1:], BF16)
    made_low[1] = jnp.zeros(made_low.shape[1:], BF16)

    def step(i, _):
        now = lax.rem(i, 2)
        before = 1 - now
        coefficients = parts_ref[...]
        total = back_products(made_high[before], made_low[before], coefficients, outs)
        if share:
            rows = pl.ds(pl.multiple_of(i * share, share), share)
            total = total + back_products(high_ref[rows], low_ref[rows], coefficients, outs)
        columns = pl.ds(pl.multiple_of(stored_rows + i * block_rows, block_rows), block_rows)
        points = (sample_ref[:, columns].astype(F32) * scale_ref[...]).T
        for first in range(0, block_rows, 128):
            rows = pl.ds(first, 128)
            fill_kernel(
                rows, points[first : first + 128], centre_ref, shift_ref, floor_ref,
                made_high.at[now], made_low.at[now],
            )
        sum_ref[...] += total

    lax.fori_loop(0, steps, step, None)
    now = (steps - 1) % 2
    last = sum_ref[...] + back_products(made_high[now], made_low[now], parts_ref[...], outs)
    last = add_parts(last, outs)
    width = last.shape[1] // len(backward_refs)
    for i, backward_ref in enumerate(backward_refs):
        backward_ref[...] = last[:, i * width : (i + 1) * width]


def apply_products(store, samples, coefficients, own_rows, block_rows, constants):
    centre_scaled, shift, floor, scale = constants
    outs, centres_all = coefficients.shape
    dims = centre_scaled.shape[0]
    given = [] if store is None else list(store)
    stored_rows = given[0].shape[0] if given else 0
    made = pltpu.VMEM((2, block_rows, centres_all), BF16)
    return pl.pallas_call(
        functools.partial(products, outs, block_rows, stored_rows),
        in_specs=[SMEM, SMEM, *[VMEM] * (4 + len(given))],
        out_specs=[VMEM, VMEM, VMEM],
        out_shape=[
            jax.ShapeDtypeStruct((outs, centres_all // 2), F32),
            jax.ShapeDtypeStruct((outs, centres_all // 2), F32),
            jax.ShapeDtypeStruct((outs, own_rows), F32),
        ],
        scratch_shapes=[
            pltpu.VMEM((3 * outs, centres_all), BF16),
            pltpu.VMEM((3 * outs, centres_all), F32),
            made,
            made,
        ],
        compiler_params=pltpu.CompilerParams(vmem_limit_bytes=(10 << 20) + 16 * block_rows * centres_all),
        cost_estimate=pl.CostEstimate(
            flops=6 * dims * (samples.shape[1] - stored_rows) * centres_all,
            bytes_accessed=4 * stored_rows * centres_all,
            transcendentals=0,
        ),
        name="products",
    )(shift, floor, scale, coefficients, centre_scaled, samples, *given)


def modulo(value):
    turns = (value.astype(F32) * (1.0 / LATTICE)).astype(jnp.int32)
    rest = value - turns * LATTICE
    rest = jnp.where(rest < 0, rest + LATTICE, rest)
    return jnp.where(rest >= LATTICE, rest - LATTICE, rest)


def prepare(order_bits, cen_dev, generator_ref, root_ref, scale_ref, centre_ref):
    dims, centres_all = centre_ref.shape
    row = lax.broadcasted_iota(jnp.int32, (dims, 1), 0)
    generator = jnp.zeros((dims, 1), jnp.int32)
    root = jnp.zeros((dims, 1), F32)
    for axis_number in range(dims):
        here = row == axis_number
        generator = jnp.where(here, generator_ref[axis_number], generator)
        root = jnp.where(here, root_ref[axis_number], root)
    scale = root * (1.0 / LATTICE)
    scale_ref[...] = scale
    place = lax.broadcasted_iota(jnp.int32, (1, centres_all), 1)
    owner = jnp.zeros_like(place) + lax.axis_index("samp")
    for k, bit in enumerate(order_bits):
        block_bit = cen_dev << k
        owner = jnp.where((place & block_bit) != 0, owner ^ bit, owner)
    column = owner * cen_dev + (place & (cen_dev - 1))
    upper = modulo(column * (generator >> 8))
    centre = modulo(upper * 256 + column * (generator & 255))
    centre_ref[...] = centre.astype(F32) * scale


def row_products(outs, count, state_ref, *refs):
    coef_ref, parts_ref = refs[count:]
    state = stack3(state_ref[:outs])
    cen_dev = refs[0].shape[0]
    for i, piece_ref in enumerate(refs[:count]):
        rows = slice(i * cen_dev, (i + 1) * cen_dev)
        for k, part in enumerate(split3(piece_ref[...])):
            parts_ref[k, rows] = part
    total = None
    for k in range(3):
        term = lax.dot_general(
            state, parts_ref[k], (((1,), (1,)), ((), ())), preferred_element_type=F32
        )
        total = term if total is None else total + term
    coef_ref[...] = add_parts(total, outs)


def image_rows(scale_total, ridge, kept_ref, came_ref, own_ref, *refs):
    *part_refs, image_ref = refs
    outs, cen_dev = own_ref.shape
    applied = (kept_ref[...] + came_ref[...]) * (1.0 / scale_total)
    own = ridge * own_ref[...]
    rest = applied.shape[1] - cen_dev
    if rest:
        own = jnp.concatenate([own, jnp.zeros((outs, rest), F32)], axis=1)
    rows = stack3(applied + own)
    total, first = None, 0
    for part_ref in part_refs:
        some = rows[:, first : first + part_ref.shape[1]]
        first += part_ref.shape[1]
        for k in range(3):
            term = jnp.dot(some, part_ref[k], preferred_element_type=F32)
            total = term if total is None else total + term
    image_ref[...] = add_parts(total, outs)


def finish(
    image_ref, more_ref, state_ref, solution_ref, residual_ref, direction_ref,
    new_solution_ref, new_residual_ref, new_direction_ref,
):
    outs, cen_dev = solution_ref.shape
    image = image_ref[...] + more_ref[...]
    residual_full = state_ref[outs:]
    norm_old = jnp.sum(residual_full * residual_full, axis=1, keepdims=True)
    curvature = jnp.sum(state_ref[:outs] * image, axis=1, keepdims=True)
    step_length = norm_old / curvature
    next_full = residual_full - step_length * image
    norm_new = jnp.sum(next_full * next_full, axis=1, keepdims=True)
    direction = direction_ref[...]
    new_solution_ref[...] = solution_ref[...] + step_length * direction
    first = lax.axis_index("samp") * cen_dev
    turn = lax.rem(image.shape[1] - first, image.shape[1])
    own_image = pltpu.roll(image, turn, 1)[:, :cen_dev]
    new_residual = residual_ref[...] - step_length * own_image
    new_residual_ref[...] = new_residual
    new_direction_ref[...] = new_residual + (norm_new / norm_old) * direction


def body(samples, generator, weight_index, preconditioner, solution, residual, direction):
    devices = lax.axis_size("samp")
    index = lax.axis_index("samp")
    cen_dev, centres_all = preconditioner.shape
    samples_dev = samples.shape[1]
    outs = direction.shape[0]
    held, others = plan(devices, 4 * cen_dev * centres_all)

    weights_dim = 0.5 * jnp.power(0.75, weight_index.astype(F32))
    curve = 2.0 * math.pi * math.pi * weights_dim
    floor = 1.0 - curve / 12.0
    root = jnp.sqrt(curve)
    shift = 0.5 * root

    scale, centre_scaled = pl.pallas_call(
        functools.partial(prepare, (*held, *others), cen_dev),
        in_specs=[SMEM, SMEM],
        out_shape=[
            jax.ShapeDtypeStruct((generator.shape[0], 1), F32),
            jax.ShapeDtypeStruct((generator.shape[0], centres_all), F32),
        ],
        name="prepare",
    )(generator, root)
    constants = (centre_scaled, shift, floor, scale)

    half = samples_dev // 2
    use_store = 4 * half * centres_all <= STORE_BYTES
    store, filled = None, 0

    def fill(rows, passed):
        nonlocal store, filled
        rows = min(rows, half - filled) if use_store else 0
        if rows == 0:
            return passed
        store, handed = kernel_rows(store, passed, samples, filled, rows, half, constants)
        filled += rows
        return handed

    pieces = [preconditioner]
    early = [swap(preconditioner, bit, devices) for bit in held[:2]]
    pieces += early[:1]
    if len(early) > 1:
        pieces += [early[1], swap(early[0], held[1], devices)]
    bit = 1
    state = None
    while bit < devices:
        upper = (index & bit) != 0
        if state is None:
            mine = [direction, residual]
            other = [swap(direction, bit, devices), swap(residual, bit, devices)]
            joined = [jnp.concatenate(pair, axis=1) for pair in zip(other, mine)]
            turned = [jnp.concatenate(pair, axis=1) for pair in zip(mine, other)]
            state = jnp.where(upper, jnp.concatenate(joined), jnp.concatenate(turned))
        else:
            other = swap(state, bit, devices)
            mine = fill(256 if 2 * bit == devices else 128, state)
            state = jnp.where(
                upper,
                jnp.concatenate([other, mine], axis=1),
                jnp.concatenate([mine, other], axis=1),
            )
        bit *= 2

    def coefficients_of(group):
        rows = len(group) * cen_dev
        return pl.pallas_call(
            functools.partial(row_products, outs, len(group)),
            out_shape=[
                jax.ShapeDtypeStruct((outs, rows), F32),
                jax.ShapeDtypeStruct((3, rows, centres_all), BF16),
            ],
            compiler_params=pltpu.CompilerParams(
                vmem_limit_bytes=(4 << 20) + 24 * rows * centres_all
            ),
            name="row_products",
        )(state, *group)

    groups = [pieces]
    for bit in held[2:]:
        groups.append([swap(p, bit, devices) for p in sum(groups, [])])
    made = [coefficients_of(group) for group in groups]
    coefficients = jnp.concatenate([m[0] for m in made], axis=1)
    parts = [m[1] for m in made]
    for bit in others:
        other = swap(coefficients, bit, devices)
        mine = fill(512, coefficients)
        coefficients = jnp.concatenate([mine, other], axis=1)
    coefficients = fill(half, coefficients)

    kept, sent, kernel_products = apply_products(
        store, samples, coefficients, cen_dev, 256, constants
    )
    for bit in reversed(others):
        came = swap(sent, bit, devices)
        if bit != others[0]:
            summed = kept + came
            width = summed.shape[1] // 2
            kept, sent = summed[:, :width], summed[:, width:]
    scale_total = float(samples_dev * devices) * float(centres_all)
    image = pl.pallas_call(
        functools.partial(image_rows, scale_total, ridge_weight / centres_all),
        out_shape=jax.ShapeDtypeStruct((outs, centres_all), F32),
        compiler_params=pltpu.CompilerParams(
            vmem_limit_bytes=(4 << 20) + 8 * kept.shape[1] * centres_all
        ),
        name="image_rows",
    )(kept, came, kernel_products, *parts)
    bit = 1
    while 2 * bit < devices:
        image = image + swap(image, bit, devices)
        bit *= 2
    more = swap(image, bit, devices)
    own = jax.ShapeDtypeStruct(solution.shape, F32)
    return pl.pallas_call(
        finish,
        out_shape=[own, own, own],
        name="finish",
    )(image, more, state, solution, residual, direction)


def solution(mesh):
    placed = (
        P("groups", "samp"),
        P(),
        P(),
        P("samp", None),
        P("groups", "samp"),
        P("groups", "samp"),
        P("groups", "samp"),
    )
    return jax.shard_map(
        body,
        mesh=mesh,
        in_specs=placed,
        out_specs=(P("groups", "samp"), P("groups", "samp"), P("groups", "samp")),
        check_vma=False,
    )
```

time: 118 us -> 92.2 us (0.78)
  matrix products: 10.1 us -> 0 us
  local copies, waits for them, and re-layouts: 22.9 us -> 12.8 us
  Pallas kernels: 40 us -> 44 us
  between operations: 4.41 us -> 0.83 us
  waiting for transfers between devices: 16.6 us -> 13.1 us
  other arithmetic: 3.37 us -> 2.1 us
    dot_general x16 -> x0, matrix products: 10.1 us -> none  [the longest x8 5.06 us: contract_last(): lax.dot_general(left_array, right_array, (((1,), (1,)), ((), ())), precis...]
    unnamed x48 -> x39, local copies, waits for them, and re-layouts: 17.4 us -> 12.7 us
    pallas_call x1 -> x5, Pallas kernels: 1.52 us -> 6.11 us  [the longest x2 2.34 us: coefficients_of(): pl.pallas_call(functools.partial(row_products, outs, len(group)), out_sha...]
    ppermute x17 -> x18, waiting for transfers between devices: 16.6 us -> 13.1 us  [swap(): return lax.ppermute(value, 'samp', [(i, i ^ bit) for i in range(devices)])]
    slice x7 -> x0, local copies, waits for them, and re-layouts: 2.57 us -> none  [the longest x5 2.56 us: kernel_rows(): return ((high, low), token[0, 0])]
    broadcast_in_dim x2 -> x0, local copies, waits for them, and re-layouts: 2.02 us -> none  [the longest x1 1.33 us: body(): generator[:, None]]
    sqrt x0 -> x1, other arithmetic: none -> 1.18 us  [body(): root = jnp.sqrt(curve)]
    ppermute x17 -> x18, starting transfers between devices: 19.5 us -> 18.9 us  [swap(): return lax.ppermute(value, 'samp', [(i, i ^ bit) for i in range(devices)])]
  transfers between devices with their start and end apart: 17 -> 18, of which waited for: 9 -> 5; matrix products, arithmetic and copies ran while one was open for 6% -> 2% of each run, Pallas kernels for 16% -> 21%
where the time goes in v4:
time: 92.2 us; the launch traced here: 91.7 us
  Pallas kernels  44 us (48%)
  starting transfers between devices  18.9 us (20%)
  waiting for transfers between devices  13.1 us (14%)
  local copies, waits for them, and re-layouts  12.8 us (14%)
  other arithmetic  2.1 us (2%)
    pallas_call x1, Pallas kernels, apply_products(): pl.pallas_call(functools.partial(products, outs, block_rows, stored_rows)...  20.1 us
    ppermute x18, starting transfers between devices, swap(): return lax.ppermute(value, 'samp', [(i, i ^ bit) for i in range(devices)])  18.9 us
    pallas_call x4, Pallas kernels, kernel_rows(): pl.pallas_call(functools.partial(store_rows, (first_row, rows // step_row...  17.7 us
    ppermute x18, waiting for transfers between devices, swap(): return lax.ppermute(value, 'samp', [(i, i ^ bit) for i in range(devices)])  13.1 us
    unnamed x39, local copies, waits for them, and re-layouts  12.7 us
    pallas_call x2, Pallas kernels, coefficients_of(): pl.pallas_call(functools.partial(row_products, outs, len(group)), out_sha...  2.34 us
  transfers between devices with their start and end apart: 18, of which 5 were waited for; matrix products, arithmetic and copies ran while one was open for 2% of the time, Pallas kernels for 21%

profile of v4, /device:TPU:0, one launch (start us, length us, event | category | flops | bytes accessed | tf_op | source)
XLA Modules:
  0.0 91.7 jit_solution(90776335212002629)
XLA Ops:
  0.6 0.5 collective-permute-start.1
  1.1 0.1 collective-permute-start
  1.2 2.9 %collective-permute-start.6 = (f32[64,1024]{1,0:T(8,128)}, f32[64,1024]{1,0:T(8,128)S(1)}, u32[]{:S(2)}, u32[]{:S(2)}) collective-permute-start(f32[64,1024]{1,0:T(8,128)} %refs_0_.1), channel_id=1, source_target_pairs={{0,2},{1,3},{2,0},{3,1},{4,6},{5,7},{6,4},{7,5},{8,10},{9,11},{10,... | collective-permute-start | bytes 786440 | tf_op jit(solution)/shard_map/ppermute | solution.py:23
  4.2 1.6 %collective-permute-start.5 = (f32[64,1024]{1,0:T(8,128)}, f32[64,1024]{1,0:T(8,128)S(1)}, u32[]{:S(2)}, u32[]{:S(2)}) collective-permute-start(f32[64,1024]{1,0:T(8,128)} %refs_0_.1), channel_id=1, source_target_pairs={{0,4},{1,5},{2,6},{3,7},{4,0},{5,1},{6,2},{7,3},{8,12},{9,13},{10,... | collective-permute-start | bytes 786440 | tf_op jit(solution)/shard_map/ppermute | solution.py:23
  5.7 0.0 collective-permute-done.1
  5.8 0.0 collective-permute-done
  5.8 0.9 maximum_select_fusion.3.passed_ref
  6.6 0.5 collective-permute-start.2
  7.1 1.2 %multiply_sqrt_fusion = (f32[16]{0:T(128)}, f32[16]{0:T(128)S(1)}, f32[16]{0:T(128)S(1)}) fusion(s32[16]{0:T(128)} %param.9), kind=kLoop, calls=%fused_computation.8 | loop fusion | flops 80 | bytes 256 | tf_op jit(solution)/shard_map/sqrt | solution.py:313
  8.3 1.4 %prepare.1 = (f32[16,1]{1,0:T(8,128)}, f32[16,1024]{1,0:T(8,128)}) custom-call(s32[16]{0:T(128)} %generator_ref.1, f32[16]{0:T(128)} %get-tuple-element.45.root_ref), custom_call_target="tpu_custom_call" | custom-call | tf_op jit(solution)/shard_map/prepare/pallas_call | solution.py:316
  9.7 0.9 copy-done.6
  10.6 0.8 copy-done.10
  11.5 0.7 copy-done.14
  12.2 2.5 %kernel_rows.4 = (bf16[1024,1024]{1,0:T(8,128)(2,1)S(1)}, bf16[1024,1024]{1,0:T(8,128)(2,1)S(1)}, f32[32,128]{1,0:T(8,128)S(1)}) custom-call(f32[16]{0:T(128)S(1)} %get-tuple-element.46.shift_ref, f32[16]{0:T(128)S(1)} %get-tuple-element.47.floor_ref, f32[16,1]{1,0:T(8,128)S(1)} %copy-done.14, s32[16,2048]{1,0:T(8,128)S(1)} %copy-done.6, ...), custom_call_target="tpu_custom_call" | custom-call | flops 12582912 | bytes 524288 | tf_op jit(solution)/shard_map/kernel_rows/pallas_call | solution.py:104
  14.6 0.0 copy-start
  14.7 1.3 %copy-done = bf16[1024,1024]{1,0:T(8,128)(2,1)} copy-done((bf16[1024,1024]{1,0:T(8,128)(2,1)}, bf16[1024,1024]{1,0:T(8,128)(2,1)S(1)}, u32[]{:S(2)}) %copy-start) | copy-done | bytes 2097176
  16.0 0.0 collective-permute-done.5.refs_1_
  16.0 1.5 %collective-permute-start.7 = (f32[64,1024]{1,0:T(8,128)S(1)}, f32[64,1024]{1,0:T(8,128)S(1)}, u32[]{:S(2)}, u32[]{:S(2)}) collective-permute-start(f32[64,1024]{1,0:T(8,128)S(1)} %collective-permute-done.5.refs_1_), channel_id=1, source_target_pairs={{0,2},{1,3},{2,0},{3,1},{4,6},{5,7},{6,4},{7,5},{8,10},{9,11},{10,... | collective-permute-start | bytes 786440 | tf_op jit(solution)/shard_map/ppermute | solution.py:23
  17.5 0.0 collective-permute-done.2
  17.5 0.5 collective-permute-start.3
  18.0 1.6 %copy-done.1 = bf16[1024,1024]{1,0:T(8,128)(2,1)S(1)} copy-done((bf16[1024,1024]{1,0:T(8,128)(2,1)S(1)}, bf16[1024,1024]{1,0:T(8,128)(2,1)}, u32[]{:S(2)}) %copy-start.1) | copy-done | bytes 2097176
  19.6 0.9 copy-done.7
  20.5 0.8 copy-done.11
  21.4 0.7 copy-done.15
  22.1 2.5 %kernel_rows.5 = (bf16[1024,1024]{1,0:T(8,128)(2,1)S(1)}, bf16[1024,1024]{1,0:T(8,128)(2,1)S(1)}, f32[32,256]{1,0:T(8,128)S(1)}) custom-call(f32[16]{0:T(128)S(1)} %get-tuple-element.46.shift_ref, f32[16]{0:T(128)S(1)} %get-tuple-element.47.floor_ref, f32[16,1]{1,0:T(8,128)S(1)} %copy-done.15, ...), custom_call_target="tpu_custom_call", output_to_operand_aliasing={{0}: (6, {}), {1}: (7, {})} | custom-call | flops 12582912 | bytes 524288 | tf_op jit(solution)/shard_map/kernel_rows/pallas_call | solution.py:104
  24.6 0.0 copy-start.2
  24.6 1.3 %copy-done.2 = bf16[1024,1024]{1,0:T(8,128)(2,1)} copy-done((bf16[1024,1024]{1,0:T(8,128)(2,1)}, bf16[1024,1024]{1,0:T(8,128)(2,1)S(1)}, u32[]{:S(2)}) %copy-start.2) | copy-done | bytes 2097176
  25.9 0.0 collective-permute-done.3
  25.9 2.7 %collective-permute-start.4 = (f32[32,512]{1,0:T(8,128)S(1)}, f32[32,512]{1,0:T(8,128)S(1)}, u32[]{:S(2)}, u32[]{:S(2)}) collective-permute-start(f32[32,512]{1,0:T(8,128)S(1)} %maximum_select_fusion.1.passed_ref), channel_id=1, source_target_pairs={{0,8},{1,9},{2,10},{3,11},{4,12},{5,13},{6,14},{7,15},{8,0},{9,1},... | collective-permute-start | bytes 196616 | tf_op jit(solution)/shard_map/ppermute | solution.py:23
  28.6 0.0 collective-permute-start.8
  28.6 0.5 collective-permute-start.9
  29.1 0.0 collective-permute-done.6.refs_2_
  29.1 0.0 collective-permute-start.10
  29.1 0.0 collective-permute-done.7.refs_3_
  29.1 0.5 collective-permute-start.11
  29.6 0.0 copy-done.12
  29.6 1.6 %copy-done.3 = bf16[1024,1024]{1,0:T(8,128)(2,1)S(1)} copy-done((bf16[1024,1024]{1,0:T(8,128)(2,1)S(1)}, bf16[1024,1024]{1,0:T(8,128)(2,1)}, u32[]{:S(2)}) %copy-start.3) | copy-done | bytes 2097176
  31.2 4.5 %kernel_rows.6 = (bf16[1024,1024]{1,0:T(8,128)(2,1)S(1)}, bf16[1024,1024]{1,0:T(8,128)(2,1)S(1)}, f32[32,512]{1,0:T(8,128)S(1)}) custom-call(f32[16]{0:T(128)S(1)} %get-tuple-element.46.shift_ref, f32[16]{0:T(128)S(1)} %get-tuple-element.47.floor_ref, f32[16,1]{1,0:T(8,128)S(1)} %copy-done.16, ...), custom_call_target="tpu_custom_call", output_to_operand_aliasing={{0}: (6, {}), {1}: (7, {})} | custom-call | flops 25165824 | bytes 1048576 | tf_op jit(solution)/shard_map/kernel_rows/pallas_call | solution.py:104
  35.8 1.3 %copy-done.4 = bf16[1024,1024]{1,0:T(8,128)(2,1)} copy-done((bf16[1024,1024]{1,0:T(8,128)(2,1)}, bf16[1024,1024]{1,0:T(8,128)(2,1)S(1)}, u32[]{:S(2)}) %copy-start.4) | copy-done | bytes 2097176
  37.1 0.0 collective-permute-done.4
  37.2 0.0 copy-start.9
  37.2 0.6 row_products.2
  37.7 0.0 collective-permute-done.8.refs_0_
  37.8 0.0 collective-permute-done.10.refs_2_
  37.8 0.0 collective-permute-done.9.refs_1_
  37.8 0.0 collective-permute-done.11.refs_3_
  37.8 1.8 %row_products.3 = (f32[16,256]{1,0:T(8,128)S(1)}, bf16[3,256,1024]{2,1,0:T(8,128)(2,1)S(1)}) custom-call(f32[32,1024]{1,0:T(8,128)S(1)} %maximum_select_fusion.state_ref, f32[64,1024]{1,0:T(8,128)} %collective-permute-done.8.refs_0_, f32[64,1024]{1,0:T(8,128)} %collective-permute-done.9.refs_1_, f32[64,1024]{1,0:T(8,128)} %collective-permute-done.10.refs_2_, ...), custom_call_target="tpu_custom_call" | custom-call | tf_op jit(solution)/shard_map/row_products/pallas_call | solution.py:367
  39.6 0.4 collective-permute-start.12
  40.0 8.2 %kernel_rows.7 = (bf16[1024,1024]{1,0:T(8,128)(2,1)S(1)}, bf16[1024,1024]{1,0:T(8,128)(2,1)S(1)}, f32[16,512]{1,0:T(8,128)S(1)}) custom-call(f32[16]{0:T(128)S(1)} %get-tuple-element.46.shift_ref, f32[16]{0:T(128)S(1)} %get-tuple-element.47.floor_ref, f32[16,1]{1,0:T(8,128)S(1)} %copy-done.16, ...), custom_call_target="tpu_custom_call", output_to_operand_aliasing={{0}: (6, {}), {1}: (7, {})} | custom-call | flops 50331648 | bytes 2097152 | tf_op jit(solution)/shard_map/kernel_rows/pallas_call | solution.py:104
  48.2 0.0 collective-permute-done.12
  48.3 20.1 %products.1 = (f32[16,512]{1,0:T(8,128)S(1)}, f32[16,512]{1,0:T(8,128)S(1)}, f32[16,64]{1,0:T(8,128)S(1)}) custom-call(f32[16]{0:T(128)S(1)} %get-tuple-element.46.shift_ref, f32[16]{0:T(128)S(1)} %get-tuple-element.47.floor_ref, f32[16,1]{1,0:T(8,128)S(1)} %copy-done.16, f32[16,1024]{1,0:T(8,128)S(1)} %pad_maximum_fusion.coef_ref, ...), custom_call_target="tpu_custom_call" | custom-call | flops 100663296 | bytes 4194304 | tf_op jit(solution)/shard_map/products/pallas_call | solution.py:190
  68.4 2.6 %collective-permute-start.13 = (f32[16,512]{1,0:T(8,128)S(1)}, f32[16,512]{1,0:T(8,128)S(1)}, u32[]{:S(2)}, u32[]{:S(2)}) collective-permute-start(f32[16,512]{1,0:T(8,128)S(1)} %get-tuple-element.41), channel_id=1, source_target_pairs={{0,8},{1,9},{2,10},{3,11},{4,12},{5,13},{6,14},{7,15},{8,0},{9,1},... | collective-permute-start | bytes 98312 | tf_op jit(solution)/shard_map/ppermute | solution.py:23
  71.0 2.4 %collective-permute-done.13.came_ref = f32[16,512]{1,0:T(8,128)S(1)} collective-permute-done((f32[16,512]{1,0:T(8,128)S(1)}, f32[16,512]{1,0:T(8,128)S(1)}, u32[]{:S(2)}, u32[]{:S(2)}) %collective-permute-start.13) | collective-permute-done | bytes 32800 | tf_op jit(solution)/shard_map/ppermute | solution.py:23
  73.4 0.6 image_rows.1
  74.0 0.0 collective-permute-start.14
  74.0 1.3 %collective-permute-done.14 = f32[16,1024]{1,0:T(8,128)S(1)} collective-permute-done((f32[16,1024]{1,0:T(8,128)S(1)}, f32[16,1024]{1,0:T(8,128)S(1)}, u32[]{:S(2)}, u32[]{:S(2)}) %collective-permute-start.14) | collective-permute-done | bytes 65568 | tf_op jit(solution)/shard_map/ppermute | solution.py:23
  75.3 0.6 collective-permute-start.15
  75.9 3.8 %collective-permute-done.15 = f32[16,1024]{1,0:T(8,128)S(1)} collective-permute-done((f32[16,1024]{1,0:T(8,128)S(1)}, f32[16,1024]{1,0:T(8,128)S(1)}, u32[]{:S(2)}, u32[]{:S(2)}) %collective-permute-start.15) | collective-permute-done | bytes 65568 | tf_op jit(solution)/shard_map/ppermute | solution.py:23
  79.7 1.4 %collective-permute-start.16 = (f32[16,1024]{1,0:T(8,128)S(1)}, f32[16,1024]{1,0:T(8,128)S(1)}, u32[]{:S(2)}, u32[]{:S(2)}) collective-permute-start(f32[16,1024]{1,0:T(8,128)S(1)} %add.10), channel_id=1, source_target_pairs={{0,4},{1,5},{2,6},{3,7},{4,0},{5,1},{6,2},{7,3},{8,12},{9,13},{10,... | collective-permute-start | bytes 196616 | tf_op jit(solution)/shard_map/ppermute | solution.py:23
  81.1 2.9 %collective-permute-done.16 = f32[16,1024]{1,0:T(8,128)S(1)} collective-permute-done((f32[16,1024]{1,0:T(8,128)S(1)}, f32[16,1024]{1,0:T(8,128)S(1)}, u32[]{:S(2)}, u32[]{:S(2)}) %collective-permute-start.16) | collective-permute-done | bytes 65568 | tf_op jit(solution)/shard_map/ppermute | solution.py:23
  84.0 2.5 %collective-permute-start.17 = (f32[16,1024]{1,0:T(8,128)S(1)}, f32[16,1024]{1,0:T(8,128)S(1)}, u32[]{:S(2)}, u32[]{:S(2)}) collective-permute-start(f32[16,1024]{1,0:T(8,128)S(1)} %add.11.image_ref), channel_id=1, source_target_pairs={{0,8},{1,9},{2,10},{3,11},{4,12},{5,13},{6,14},{7,15},{8,0},{9,1},... | collective-permute-start | bytes 196616 | tf_op jit(solution)/shard_map/ppermute | solution.py:23
  86.5 2.7 %collective-permute-done.17.more_ref = f32[16,1024]{1,0:T(8,128)S(1)} collective-permute-done((f32[16,1024]{1,0:T(8,128)S(1)}, f32[16,1024]{1,0:T(8,128)S(1)}, u32[]{:S(2)}, u32[]{:S(2)}) %collective-permute-start.17) | collective-permute-done | bytes 65568 | tf_op jit(solution)/shard_map/ppermute | solution.py:23
  89.3 0.6 copy-done.18
  89.9 1.8 %finish.1 = (f32[16,64]{1,0:T(8,128)}, f32[16,64]{1,0:T(8,128)}, f32[16,64]{1,0:T(8,128)}) custom-call(f32[16,1024]{1,0:T(8,128)} %copy-done.17, f32[16,1024]{1,0:T(8,128)} %copy-done.18, f32[32,1024]{1,0:T(8,128)} %copy-done.9, f32[16,64]{1,0:T(8,128)} %solution_ref.1, f32[16,64]{1,0:T(8,128)} %residual_ref.1, f32[16,64]{1,0:T(8,128)} %direction_ref.1), custom_call_target="tpu_custom_call" | custom-call | tf_op jit(solution)/shard_map/finish/pallas_call | solution.py:415
  (31 shorter events, 0.1 us)
Async XLA Ops:
  0.6 5.1 %collective-permute-start.1 = (f32[16,64]{1,0:T(8,128)}, f32[16,64]{1,0:T(8,128)S(1)}, u32[]{:S(2)}, u32[]{:S(2)}) collective-permute-start(f32[16,64]{1,0:T(8,128)} %residual_ref.1), channel_id=1, source_target_pairs={{0,1},{1,0},{2,3},{3,2},{4,5},{5,4},{6,7},{7,6},{8,9},{9,8},{10,11... | collective-permute-start | bytes 12296 | tf_op jit(solution)/shard_map/ppermute | solution.py:23
  1.1 4.6 %collective-permute-start = (f32[16,64]{1,0:T(8,128)}, f32[16,64]{1,0:T(8,128)S(1)}, u32[]{:S(2)}, u32[]{:S(2)}) collective-permute-start(f32[16,64]{1,0:T(8,128)} %direction_ref.1), channel_id=1, source_target_pairs={{0,1},{1,0},{2,3},{3,2},{4,5},{5,4},{6,7},{7,6},{8,9},{9,8},{10,11... | collective-permute-start | bytes 12296 | tf_op jit(solution)/shard_map/ppermute | solution.py:23
  1.2 27.9 %collective-permute-start.6 = (f32[64,1024]{1,0:T(8,128)}, f32[64,1024]{1,0:T(8,128)S(1)}, u32[]{:S(2)}, u32[]{:S(2)}) collective-permute-start(f32[64,1024]{1,0:T(8,128)} %refs_0_.1), channel_id=1, source_target_pairs={{0,2},{1,3},{2,0},{3,1},{4,6},{5,7},{6,4},{7,5},{8,10},{9,11},{10,... | collective-permute-start | bytes 786440 | tf_op jit(solution)/shard_map/ppermute | solution.py:23
  4.2 11.8 %collective-permute-start.5 = (f32[64,1024]{1,0:T(8,128)}, f32[64,1024]{1,0:T(8,128)S(1)}, u32[]{:S(2)}, u32[]{:S(2)}) collective-permute-start(f32[64,1024]{1,0:T(8,128)} %refs_0_.1), channel_id=1, source_target_pairs={{0,4},{1,5},{2,6},{3,7},{4,0},{5,1},{6,2},{7,3},{8,12},{9,13},{10,... | collective-permute-start | bytes 786440 | tf_op jit(solution)/shard_map/ppermute | solution.py:23
  6.6 10.9 %collective-permute-start.2 = (f32[32,128]{1,0:T(8,128)S(1)}, f32[32,128]{1,0:T(8,128)S(1)}, u32[]{:S(2)}, u32[]{:S(2)}) collective-permute-start(f32[32,128]{1,0:T(8,128)S(1)} %maximum_select_fusion.3.passed_ref), channel_id=1, source_target_pairs={{0,2},{1,3},{2,0},{3,1},{4,6},{5,7},{6,4},{7,5},{8,10},{9,11},{10,... | collective-permute-start | bytes 49160 | tf_op jit(solution)/shard_map/ppermute | solution.py:23
  9.7 0.9 copy-start.6
  10.6 0.8 copy-start.10
  11.5 0.7 copy-start.14
  14.6 1.4 %copy-start = (bf16[1024,1024]{1,0:T(8,128)(2,1)}, bf16[1024,1024]{1,0:T(8,128)(2,1)S(1)}, u32[]{:S(2)}) copy-start(bf16[1024,1024]{1,0:T(8,128)(2,1)S(1)} %get-tuple-element.28.refs_1_) | copy-start | bytes 6291460
  16.0 13.1 %collective-permute-start.7 = (f32[64,1024]{1,0:T(8,128)S(1)}, f32[64,1024]{1,0:T(8,128)S(1)}, u32[]{:S(2)}, u32[]{:S(2)}) collective-permute-start(f32[64,1024]{1,0:T(8,128)S(1)} %collective-permute-done.5.refs_1_), channel_id=1, source_target_pairs={{0,2},{1,3},{2,0},{3,1},{4,6},{5,7},{6,4},{7,5},{8,10},{9,11},{10,... | collective-permute-start | bytes 786440 | tf_op jit(solution)/shard_map/ppermute | solution.py:23
  17.5 8.4 %collective-permute-start.3 = (f32[32,256]{1,0:T(8,128)S(1)}, f32[32,256]{1,0:T(8,128)S(1)}, u32[]{:S(2)}, u32[]{:S(2)}) collective-permute-start(f32[32,256]{1,0:T(8,128)S(1)} %maximum_select_fusion.2.passed_ref), channel_id=1, source_target_pairs={{0,4},{1,5},{2,6},{3,7},{4,0},{5,1},{6,2},{7,3},{8,12},{9,13},{10,... | collective-permute-start | bytes 98312 | tf_op jit(solution)/shard_map/ppermute | solution.py:23
  18.0 1.6 %copy-start.1 = (bf16[1024,1024]{1,0:T(8,128)(2,1)S(1)}, bf16[1024,1024]{1,0:T(8,128)(2,1)}, u32[]{:S(2)}) copy-start(bf16[1024,1024]{1,0:T(8,128)(2,1)} %copy-done) | copy-start | bytes 6291460
  19.6 0.9 copy-start.7
  20.5 0.8 copy-start.11
  21.4 0.7 copy-start.15
  22.1 6.5 %copy-start.13 = (f32[64,1024]{1,0:T(8,128)S(1)}, f32[64,1024]{1,0:T(8,128)}, u32[]{:S(2)}) copy-start(f32[64,1024]{1,0:T(8,128)} %refs_0_.1) | copy-start | bytes 786436
  22.1 7.6 %copy-start.8 = (s32[16,2048]{1,0:T(8,128)S(1)}, s32[16,2048]{1,0:T(8,128)}, u32[]{:S(2)}) copy-start(s32[16,2048]{1,0:T(8,128)} %sample_ref.9) | copy-start | bytes 393220
  22.1 7.6 %copy-start.12 = (f32[16,1024]{1,0:T(8,128)S(1)}, f32[16,1024]{1,0:T(8,128)}, u32[]{:S(2)}) copy-start(f32[16,1024]{1,0:T(8,128)} %get-tuple-element.25.centre_ref) | copy-start | bytes 196612
  22.1 7.6 %copy-start.16 = (f32[16,1]{1,0:T(8,128)S(1)}, f32[16,1]{1,0:T(8,128)}, u32[]{:S(2)}) copy-start(f32[16,1]{1,0:T(8,128)} %get-tuple-element.24.scale_ref) | copy-start | bytes 196
  24.6 1.4 %copy-start.2 = (bf16[1024,1024]{1,0:T(8,128)(2,1)}, bf16[1024,1024]{1,0:T(8,128)(2,1)S(1)}, u32[]{:S(2)}) copy-start(bf16[1024,1024]{1,0:T(8,128)(2,1)S(1)} %get-tuple-element.31.refs_1_) | copy-start | bytes 6291460
  25.9 11.2 %collective-permute-start.4 = (f32[32,512]{1,0:T(8,128)S(1)}, f32[32,512]{1,0:T(8,128)S(1)}, u32[]{:S(2)}, u32[]{:S(2)}) collective-permute-start(f32[32,512]{1,0:T(8,128)S(1)} %maximum_select_fusion.1.passed_ref), channel_id=1, source_target_pairs={{0,8},{1,9},{2,10},{3,11},{4,12},{5,13},{6,14},{7,15},{8,0},{9,1},... | collective-permute-start | bytes 196616 | tf_op jit(solution)/shard_map/ppermute | solution.py:23
  28.6 9.2 %collective-permute-start.8 = (f32[64,1024]{1,0:T(8,128)S(1)}, f32[64,1024]{1,0:T(8,128)}, u32[]{:S(2)}, u32[]{:S(2)}) collective-permute-start(f32[64,1024]{1,0:T(8,128)S(1)} %copy-done.13), channel_id=1, source_target_pairs={{0,1},{1,0},{2,3},{3,2},{4,5},{5,4},{6,7},{7,6},{8,9},{9,8},{10,11... | collective-permute-start | bytes 786440 | tf_op jit(solution)/shard_map/ppermute | solution.py:23
  28.6 9.2 %collective-permute-start.9 = (f32[64,1024]{1,0:T(8,128)S(1)}, f32[64,1024]{1,0:T(8,128)}, u32[]{:S(2)}, u32[]{:S(2)}) collective-permute-start(f32[64,1024]{1,0:T(8,128)S(1)} %collective-permute-done.5.refs_1_), channel_id=1, source_target_pairs={{0,1},{1,0},{2,3},{3,2},{4,5},{5,4},{6,7},{7,6},{8,9},{9,8},{10,11... | collective-permute-start | bytes 786440 | tf_op jit(solution)/shard_map/ppermute | solution.py:23
  29.1 8.7 %collective-permute-start.10 = (f32[64,1024]{1,0:T(8,128)S(1)}, f32[64,1024]{1,0:T(8,128)}, u32[]{:S(2)}, u32[]{:S(2)}) collective-permute-start(f32[64,1024]{1,0:T(8,128)S(1)} %collective-permute-done.6.refs_2_), channel_id=1, source_target_pairs={{0,1},{1,0},{2,3},{3,2},{4,5},{5,4},{6,7},{7,6},{8,9},{9,8},{10,11... | collective-permute-start | bytes 786440 | tf_op jit(solution)/shard_map/ppermute | solution.py:23
  29.1 8.7 %collective-permute-start.11 = (f32[64,1024]{1,0:T(8,128)S(1)}, f32[64,1024]{1,0:T(8,128)}, u32[]{:S(2)}, u32[]{:S(2)}) collective-permute-start(f32[64,1024]{1,0:T(8,128)S(1)} %collective-permute-done.7.refs_3_), channel_id=1, source_target_pairs={{0,1},{1,0},{2,3},{3,2},{4,5},{5,4},{6,7},{7,6},{8,9},{9,8},{10,11... | collective-permute-start | bytes 786440 | tf_op jit(solution)/shard_map/ppermute | solution.py:23
  29.6 1.6 %copy-start.3 = (bf16[1024,1024]{1,0:T(8,128)(2,1)S(1)}, bf16[1024,1024]{1,0:T(8,128)(2,1)}, u32[]{:S(2)}) copy-start(bf16[1024,1024]{1,0:T(8,128)(2,1)} %copy-done.2) | copy-start | bytes 6291460
  35.8 1.4 %copy-start.4 = (bf16[1024,1024]{1,0:T(8,128)(2,1)}, bf16[1024,1024]{1,0:T(8,128)(2,1)S(1)}, u32[]{:S(2)}) copy-start(bf16[1024,1024]{1,0:T(8,128)(2,1)S(1)} %get-tuple-element.36.refs_1_) | copy-start | bytes 6291460
  37.1 2.9 %copy-start.5 = (bf16[1024,1024]{1,0:T(8,128)(2,1)S(1)}, bf16[1024,1024]{1,0:T(8,128)(2,1)}, u32[]{:S(2)}) copy-start(bf16[1024,1024]{1,0:T(8,128)(2,1)} %copy-done.4) | copy-start | bytes 6291460
  37.2 11.1 %copy-start.9 = (f32[32,1024]{1,0:T(8,128)}, f32[32,1024]{1,0:T(8,128)S(1)}, u32[]{:S(2)}) copy-start(f32[32,1024]{1,0:T(8,128)S(1)} %maximum_select_fusion.state_ref) | copy-start | bytes 393220
  39.6 8.6 %collective-permute-start.12 = (f32[16,512]{1,0:T(8,128)S(1)}, f32[16,512]{1,0:T(8,128)S(1)}, u32[]{:S(2)}, u32[]{:S(2)}) collective-permute-start(f32[16,512]{1,0:T(8,128)S(1)} %constant_dynamic-update-slice_fusion.passed_ref), channel_id=1, source_target_pairs={{0,8},{1,9},{2,10},{3,11},{4,12},{5,13},{6,14},{7,15},{8,0},{9,1},... | collective-permute-start | bytes 98312 | tf_op jit(solution)/shard_map/ppermute | solution.py:23
  68.4 5.0 %collective-permute-start.13 = (f32[16,512]{1,0:T(8,128)S(1)}, f32[16,512]{1,0:T(8,128)S(1)}, u32[]{:S(2)}, u32[]{:S(2)}) collective-permute-start(f32[16,512]{1,0:T(8,128)S(1)} %get-tuple-element.41), channel_id=1, source_target_pairs={{0,8},{1,9},{2,10},{3,11},{4,12},{5,13},{6,14},{7,15},{8,0},{9,1},... | collective-permute-start | bytes 98312 | tf_op jit(solution)/shard_map/ppermute | solution.py:23
  74.0 1.3 %collective-permute-start.14 = (f32[16,1024]{1,0:T(8,128)S(1)}, f32[16,1024]{1,0:T(8,128)S(1)}, u32[]{:S(2)}, u32[]{:S(2)}) collective-permute-start(f32[16,1024]{1,0:T(8,128)S(1)} %image_rows.1), channel_id=1, source_target_pairs={{0,1},{1,0},{2,3},{3,2},{4,5},{5,4},{6,7},{7,6},{8,9},{9,8},{10,11... | collective-permute-start | bytes 196616 | tf_op jit(solution)/shard_map/ppermute | solution.py:23
  75.3 4.3 %collective-permute-start.15 = (f32[16,1024]{1,0:T(8,128)S(1)}, f32[16,1024]{1,0:T(8,128)S(1)}, u32[]{:S(2)}, u32[]{:S(2)}) collective-permute-start(f32[16,1024]{1,0:T(8,128)S(1)} %add.9), channel_id=1, source_target_pairs={{0,2},{1,3},{2,0},{3,1},{4,6},{5,7},{6,4},{7,5},{8,10},{9,11},{10,... | collective-permute-start | bytes 196616 | tf_op jit(solution)/shard_map/ppermute | solution.py:23
  79.7 4.3 %collective-permute-start.16 = (f32[16,1024]{1,0:T(8,128)S(1)}, f32[16,1024]{1,0:T(8,128)S(1)}, u32[]{:S(2)}, u32[]{:S(2)}) collective-permute-start(f32[16,1024]{1,0:T(8,128)S(1)} %add.10), channel_id=1, source_target_pairs={{0,4},{1,5},{2,6},{3,7},{4,0},{5,1},{6,2},{7,3},{8,12},{9,13},{10,... | collective-permute-start | bytes 196616 | tf_op jit(solution)/shard_map/ppermute | solution.py:23
  84.0 5.2 %copy-start.17 = (f32[16,1024]{1,0:T(8,128)}, f32[16,1024]{1,0:T(8,128)S(1)}, u32[]{:S(2)}) copy-start(f32[16,1024]{1,0:T(8,128)S(1)} %add.11.image_ref) | copy-start | bytes 196612
  84.0 5.2 %collective-permute-start.17 = (f32[16,1024]{1,0:T(8,128)S(1)}, f32[16,1024]{1,0:T(8,128)S(1)}, u32[]{:S(2)}, u32[]{:S(2)}) collective-permute-start(f32[16,1024]{1,0:T(8,128)S(1)} %add.11.image_ref), channel_id=1, source_target_pairs={{0,8},{1,9},{2,10},{3,11},{4,12},{5,13},{6,14},{7,15},{8,0},{9,1},... | collective-permute-start | bytes 196616 | tf_op jit(solution)/shard_map/ppermute | solution.py:23
  89.3 0.6 copy-start.18

commit v5 on v4

--- a/solution.py
+++ b/solution.py
@@ -14,6 +14,7 @@
 STORE_BYTES = 12 << 20
 HELD_BYTES = 16 << 20
 VMEM = pl.BlockSpec(memory_space=pltpu.VMEM)
+FREE = pl.BlockSpec(memory_space=pl.ANY)
 SMEM = pl.BlockSpec(memory_space=pltpu.SMEM)
 F32 = jnp.float32
 BF16 = jnp.bfloat16
@@ -82,39 +83,94 @@
         lax.fori_loop(0, centres_all // span, lambda i, _: part(i * span), None)
 
 
-def store_rows(row_set, step_rows, shift_ref, floor_ref, scale_ref, sample_ref, centre_ref, passed_ref, *refs):
-    high_ref, low_ref, handed_ref = refs[-3:]
+def fetch(pairs, sems):
+    copies = [pltpu.make_async_copy(src, dst, sems.at[i]) for i, (src, dst) in enumerate(pairs)]
+    for copy in copies:
+        copy.start()
+    return copies
+
+
+def scale_column(shift_ref, dims):
+    row = lax.broadcasted_iota(jnp.int32, (dims, 1), 0)
+    scale = jnp.zeros((dims, 1), F32)
+    for axis_number in range(dims):
+        scale = jnp.where(row == axis_number, shift_ref[axis_number], scale)
+    return scale * (2.0 / LATTICE)
+
+
+def store_rows(
+    first_row, step_rows, shift_ref, floor_ref, samples_hbm, centres_hbm, passed_ref,
+    high_hbm, low_hbm, handed_ref, sample_ref, centre_ref, high_ref, low_ref, in_sems, out_sems,
+):
+    rows_all = high_hbm.shape[0]
+    copies = fetch(
+        [(samples_hbm.at[:, pl.ds(first_row, rows_all)], sample_ref), (centres_hbm, centre_ref)],
+        in_sems,
+    )
+    handed_ref[...] = passed_ref[...]
+    scale = scale_column(shift_ref, sample_ref.shape[0])
+    for copy in copies:
+        copy.wait()
+
+    def sends(step):
+        slot = lax.rem(step, 2)
+        rows = pl.ds(pl.multiple_of(step * step_rows, step_rows), step_rows)
+        return [
+            pltpu.make_async_copy(high_ref.at[slot], high_hbm.at[rows], out_sems.at[slot, 0]),
+            pltpu.make_async_copy(low_ref.at[slot], low_hbm.at[rows], out_sems.at[slot, 1]),
+        ]
+
+    steps = rows_all // step_rows
 
     def step(i, _):
-        first = pl.multiple_of(row_set[0] + i * step_rows, step_rows)
-        rows = pl.ds(first, step_rows)
-        points = (sample_ref[:, rows].astype(F32) * scale_ref[...]).T
-        fill_kernel(rows, points, centre_ref, shift_ref, floor_ref, high_ref, low_ref)
-
-    lax.fori_loop(0, row_set[1], step, None)
-    handed_ref[...] = passed_ref[...]
-
-
-def kernel_rows(store, passed, samples, first_row, rows, rows_stored, constants):
-    centre_scaled, shift, floor, scale = constants
+        slot = lax.rem(i, 2)
+
+        @pl.when(i >= 2)
+        def _():
+            for copy in sends(i - 2):
+                copy.wait()
+
+        columns = pl.ds(pl.multiple_of(i * step_rows, step_rows), step_rows)
+        points = (sample_ref[:, columns].astype(F32) * scale).T
+        rows = pl.ds(0, step_rows)
+        fill_kernel(
+            rows, points, centre_ref, shift_ref, floor_ref, high_ref.at[slot], low_ref.at[slot]
+        )
+        for copy in sends(i):
+            copy.start()
+
+    lax.fori_loop(0, steps, step, None)
+    for last in range(max(0, steps - 2), steps):
+        for copy in sends(last):
+            copy.wait()
+
+
+def kernel_rows(passed, samples, first_row, rows, constants):
+    centre_scaled, shift, floor = constants
     dims, centres_all = centre_scaled.shape
-    given = [] if store is None else list(store)
-    kept = pltpu.VMEM((rows_stored, centres_all), BF16)
+    kept = jax.ShapeDtypeStruct((rows, centres_all), BF16)
     step_rows = min(128, rows)
     high, low, handed = pl.pallas_call(
-        functools.partial(store_rows, (first_row, rows // step_rows), step_rows),
-        in_specs=[SMEM, SMEM, *[VMEM] * (4 + len(given))],
-        out_specs=[VMEM, VMEM, VMEM],
+        functools.partial(store_rows, first_row, step_rows),
+        in_specs=[SMEM, SMEM, FREE, FREE, VMEM],
+        out_specs=[FREE, FREE, VMEM],
         out_shape=[kept, kept, jax.ShapeDtypeStruct(passed.shape, passed.dtype)],
-        input_output_aliases={6: 0, 7: 1} if given else {},
-        compiler_params=pltpu.CompilerParams(vmem_limit_bytes=8 << 20),
+        scratch_shapes=[
+            pltpu.VMEM((dims, rows), jnp.int32),
+            pltpu.VMEM((dims, centres_all), F32),
+            pltpu.VMEM((2, step_rows, centres_all), BF16),
+            pltpu.VMEM((2, step_rows, centres_all), BF16),
+            pltpu.SemaphoreType.DMA((2,)),
+            pltpu.SemaphoreType.DMA((2, 2)),
+        ],
+        compiler_params=pltpu.CompilerParams(vmem_limit_bytes=12 << 20),
         cost_estimate=pl.CostEstimate(
             flops=6 * dims * rows * centres_all,
             bytes_accessed=4 * rows * centres_all,
             transcendentals=0,
         ),
         name="kernel_rows",
-    )(shift, floor, scale, samples, centre_scaled, passed, *given)
+    )(shift, floor, samples, centre_scaled, passed)
     return (high, low), handed
 
 
@@ -133,25 +189,38 @@
 
 
 def products(
-    outs, block_rows, stored_rows, shift_ref, floor_ref, scale_ref, coef_ref, centre_ref,
-    sample_ref, *refs,
+    outs, block_rows, stored, shift_ref, floor_ref, coef_ref, samples_hbm, centres_hbm, *refs
 ):
-    if stored_rows:
-        high_ref, low_ref, *refs = refs
-    *backward_refs, own_out_ref, parts_ref, sum_ref, made_high, made_low = refs
+    stored_hbm, refs = refs[: 2 * len(stored)], refs[2 * len(stored) :]
+    *backward_refs, own_out_ref = refs[:3]
+    parts_ref, sum_ref, made_high, made_low, sample_ref, centre_ref, high_ref, low_ref, sems = refs[3:]
     own_rows = own_out_ref.shape[1]
-    steps = (sample_ref.shape[1] - stored_rows) // block_rows
+    steps = sample_ref.shape[1] // block_rows
+    stored_rows = sum(stored)
     share = stored_rows // steps
-
+    columns = pl.ds(stored_rows, sample_ref.shape[1])
+    copies = fetch([(samples_hbm.at[:, columns], sample_ref), (centres_hbm, centre_ref)], sems)
+    first = 0
+    for i, rows in enumerate(stored):
+        pairs = zip(stored_hbm[2 * i : 2 * i + 2], (high_ref, low_ref))
+        place = pl.ds(first, rows)
+        copies += fetch([(src, dst.at[place]) for src, dst in pairs], sems.at[pl.ds(2 + 2 * i, 2)])
+        first += rows
+
+    scale = scale_column(shift_ref, sample_ref.shape[0])
     parts_ref[...] = stack3(coef_ref[...])
     sum_ref[...] = jnp.zeros_like(sum_ref)
-    own_high, own_low = made_high.at[1], made_low.at[1]
+    made_high[1] = jnp.zeros(made_high.shape[1:], BF16)
+    made_low[1] = jnp.zeros(made_low.shape[1:], BF16)
+    copies[0].wait()
+    copies[1].wait()
+    own_high, own_low = made_high.at[0], made_low.at[0]
     rows = pl.ds(0, own_rows)
     own_points = centre_ref[:, :own_rows]
     fill_kernel(rows, own_points.T, centre_ref, shift_ref, floor_ref, own_high, own_low)
     own_out_ref[...] = apply_kernel(own_high[rows], own_low[rows], parts_ref[...], outs)
-    made_high[1] = jnp.zeros(made_high.shape[1:], BF16)
-    made_low[1] = jnp.zeros(made_low.shape[1:], BF16)
+    for copy in copies[2:]:
+        copy.wait()
 
     def step(i, _):
         now = lax.rem(i, 2)
@@ -161,8 +230,8 @@
         if share:
             rows = pl.ds(pl.multiple_of(i * share, share), share)
             total = total + back_products(high_ref[rows], low_ref[rows], coefficients, outs)
-        columns = pl.ds(pl.multiple_of(stored_rows + i * block_rows, block_rows), block_rows)
-        points = (sample_ref[:, columns].astype(F32) * scale_ref[...]).T
+        columns = pl.ds(pl.multiple_of(i * block_rows, block_rows), block_rows)
+        points = (sample_ref[:, columns].astype(F32) * scale).T
         for first in range(0, block_rows, 128):
             rows = pl.ds(first, 128)
             fill_kernel(
@@ -181,15 +250,16 @@
 
 
 def apply_products(store, samples, coefficients, own_rows, block_rows, constants):
-    centre_scaled, shift, floor, scale = constants
+    centre_scaled, shift, floor = constants
     outs, centres_all = coefficients.shape
     dims = centre_scaled.shape[0]
-    given = [] if store is None else list(store)
-    stored_rows = given[0].shape[0] if given else 0
+    stored = tuple(high.shape[0] for high, _ in store)
     made = pltpu.VMEM((2, block_rows, centres_all), BF16)
+    kept = pltpu.VMEM((max(16, sum(stored)), centres_all), BF16)
+    rows = samples.shape[1] - sum(stored)
     return pl.pallas_call(
-        functools.partial(products, outs, block_rows, stored_rows),
-        in_specs=[SMEM, SMEM, *[VMEM] * (4 + len(given))],
+        functools.partial(products, outs, block_rows, stored),
+        in_specs=[SMEM, SMEM, VMEM, *[FREE] * (2 + 2 * len(stored))],
         out_specs=[VMEM, VMEM, VMEM],
         out_shape=[
             jax.ShapeDtypeStruct((outs, centres_all // 2), F32),
@@ -201,15 +271,22 @@
             pltpu.VMEM((3 * outs, centres_all), F32),
             made,
             made,
+            pltpu.VMEM((dims, rows), jnp.int32),
+            pltpu.VMEM((dims, centres_all), F32),
+            kept,
+            kept,
+            pltpu.SemaphoreType.DMA((2 + 2 * len(stored),)),
         ],
-        compiler_params=pltpu.CompilerParams(vmem_limit_bytes=(10 << 20) + 16 * block_rows * centres_all),
+        compiler_params=pltpu.CompilerParams(
+            vmem_limit_bytes=(14 << 20) + (16 * block_rows + 4 * sum(stored)) * centres_all
+        ),
         cost_estimate=pl.CostEstimate(
-            flops=6 * dims * (samples.shape[1] - stored_rows) * centres_all,
-            bytes_accessed=4 * stored_rows * centres_all,
+            flops=6 * dims * rows * centres_all,
+            bytes_accessed=4 * sum(stored) * centres_all,
             transcendentals=0,
         ),
         name="products",
-    )(shift, floor, scale, coefficients, centre_scaled, samples, *given)
+    )(shift, floor, coefficients, samples, centre_scaled, *[part for pair in store for part in pair])
 
 
 def modulo(value):
@@ -219,17 +296,12 @@
     return jnp.where(rest >= LATTICE, rest - LATTICE, rest)
 
 
-def prepare(order_bits, cen_dev, generator_ref, root_ref, scale_ref, centre_ref):
+def prepare(order_bits, cen_dev, generator_ref, shift_ref, centre_ref):
     dims, centres_all = centre_ref.shape
     row = lax.broadcasted_iota(jnp.int32, (dims, 1), 0)
     generator = jnp.zeros((dims, 1), jnp.int32)
-    root = jnp.zeros((dims, 1), F32)
     for axis_number in range(dims):
-        here = row == axis_number
-        generator = jnp.where(here, generator_ref[axis_number], generator)
-        root = jnp.where(here, root_ref[axis_number], root)
-    scale = root * (1.0 / LATTICE)
-    scale_ref[...] = scale
+        generator = jnp.where(row == axis_number, generator_ref[axis_number], generator)
     place = lax.broadcasted_iota(jnp.int32, (1, centres_all), 1)
     owner = jnp.zeros_like(place) + lax.axis_index("samp")
     for k, bit in enumerate(order_bits):
@@ -238,7 +310,7 @@
     column = owner * cen_dev + (place & (cen_dev - 1))
     upper = modulo(column * (generator >> 8))
     centre = modulo(upper * 256 + column * (generator & 255))
-    centre_ref[...] = centre.astype(F32) * scale
+    centre_ref[...] = centre.astype(F32) * scale_column(shift_ref, dims)
 
 
 def row_products(outs, count, state_ref, *refs):
@@ -310,30 +382,27 @@
     weights_dim = 0.5 * jnp.power(0.75, weight_index.astype(F32))
     curve = 2.0 * math.pi * math.pi * weights_dim
     floor = 1.0 - curve / 12.0
-    root = jnp.sqrt(curve)
-    shift = 0.5 * root
-
-    scale, centre_scaled = pl.pallas_call(
+    shift = 0.5 * jnp.sqrt(curve)
+
+    centre_scaled = pl.pallas_call(
         functools.partial(prepare, (*held, *others), cen_dev),
         in_specs=[SMEM, SMEM],
-        out_shape=[
-            jax.ShapeDtypeStruct((generator.shape[0], 1), F32),
-            jax.ShapeDtypeStruct((generator.shape[0], centres_all), F32),
-        ],
+        out_shape=jax.ShapeDtypeStruct((generator.shape[0], centres_all), F32),
         name="prepare",
-    )(generator, root)
-    constants = (centre_scaled, shift, floor, scale)
+    )(generator, shift)
+    constants = (centre_scaled, shift, floor)
 
     half = samples_dev // 2
     use_store = 4 * half * centres_all <= STORE_BYTES
-    store, filled = None, 0
+    store, filled = [], 0
 
     def fill(rows, passed):
-        nonlocal store, filled
+        nonlocal filled
         rows = min(rows, half - filled) if use_store else 0
         if rows == 0:
             return passed
-        store, handed = kernel_rows(store, passed, samples, filled, rows, half, constants)
+        made, handed = kernel_rows(passed, samples, filled, rows, constants)
+        store.append(made)
         filled += rows
         return handed
 

time: 92.2 us -> 88.7 us (0.962)
  local copies, waits for them, and re-layouts: 12.8 us -> 8.79 us
    unnamed x39 -> x33, local copies, waits for them, and re-layouts: 12.7 us -> 8.79 us
    pallas_call x5, Pallas kernels: 37.8 us -> 39.5 us  [the longest x1 21.5 us: apply_products(): pl.pallas_call(functools.partial(products, outs, block_rows, stored), in_...]
    pallas_call x2, Pallas kernels: 2.34 us -> 1.12 us  [coefficients_of(): pl.pallas_call(functools.partial(row_products, outs, len(group)), out_sha...]
    sub x0 -> x1, other arithmetic: none -> 1.18 us  [body(): floor = 1.0 - curve / 12.0]
    sqrt x1 -> x0, other arithmetic: 1.18 us -> none  [body(): root = jnp.sqrt(curve)]
  transfers between devices with their start and end apart: 18 -> 18, of which waited for: 5 -> 5; matrix products, arithmetic and copies ran while one was open for 2% -> 2% of each run, Pallas kernels for 21% -> 23%
where the time goes in v5:
time: 88.7 us; the launch traced here: 88.2 us
  Pallas kernels  44.4 us (50%)
  starting transfers between devices  19 us (21%)
  waiting for transfers between devices  13.1 us (15%)
  local copies, waits for them, and re-layouts  8.79 us (10%)
  other arithmetic  2.11 us (2%)
    pallas_call x1, Pallas kernels, apply_products(): pl.pallas_call(functools.partial(products, outs, block_rows, stored), in_...  21.5 us
    ppermute x18, starting transfers between devices, swap(): return lax.ppermute(value, 'samp', [(i, i ^ bit) for i in range(devices)])  19 us
    pallas_call x4, Pallas kernels, kernel_rows(): pl.pallas_call(functools.partial(store_rows, first_row, step_rows), in_sp...  18 us
    ppermute x18, waiting for transfers between devices, swap(): return lax.ppermute(value, 'samp', [(i, i ^ bit) for i in range(devices)])  13.1 us
    unnamed x33, local copies, waits for them, and re-layouts  8.79 us
    pallas_call x1, Pallas kernels, body(): pl.pallas_call(finish, out_shape=[own, own, own], name='finish')  1.79 us
  transfers between devices with their start and end apart: 18, of which 5 were waited for; matrix products, arithmetic and copies ran while one was open for 2% of the time, Pallas kernels for 23%

profile of v5, /device:TPU:0, one launch (start us, length us, event | category | flops | bytes accessed | tf_op | source)
XLA Modules:
  0.0 88.2 jit_solution(6677588359556118738)
XLA Ops:
  0.6 0.5 collective-permute-start.1
  1.1 0.1 collective-permute-start
  1.2 2.9 %collective-permute-start.6 = (f32[64,1024]{1,0:T(8,128)}, f32[64,1024]{1,0:T(8,128)S(1)}, u32[]{:S(2)}, u32[]{:S(2)}) collective-permute-start(f32[64,1024]{1,0:T(8,128)} %refs_0_.1), channel_id=1, source_target_pairs={{0,2},{1,3},{2,0},{3,1},{4,6},{5,7},{6,4},{7,5},{8,10},{9,11},{10,... | collective-permute-start | bytes 786440 | tf_op jit(solution)/shard_map/ppermute | solution.py:24
  4.2 1.6 %collective-permute-start.5 = (f32[64,1024]{1,0:T(8,128)}, f32[64,1024]{1,0:T(8,128)S(1)}, u32[]{:S(2)}, u32[]{:S(2)}) collective-permute-start(f32[64,1024]{1,0:T(8,128)} %refs_0_.1), channel_id=1, source_target_pairs={{0,4},{1,5},{2,6},{3,7},{4,0},{5,1},{6,2},{7,3},{8,12},{9,13},{10,... | collective-permute-start | bytes 786440 | tf_op jit(solution)/shard_map/ppermute | solution.py:24
  5.7 0.0 collective-permute-done.1
  5.8 0.0 collective-permute-done
  5.8 0.9 maximum_select_fusion.3.passed_ref
  6.6 0.5 collective-permute-start.2
  7.1 1.2 %multiply_subtract_fusion = (f32[16]{0:T(128)S(1)}, f32[16]{0:T(128)}) fusion(s32[16]{0:T(128)} %param.9), kind=kLoop, calls=%fused_computation.7 | loop fusion | flops 80 | bytes 192 | tf_op jit(solution)/shard_map/sub | solution.py:384
  8.3 1.4 %prepare.1.centres_hbm = f32[16,1024]{1,0:T(8,128)} custom-call(s32[16]{0:T(128)} %generator_ref.1, f32[16]{0:T(128)} %get-tuple-element.42.shift_ref), custom_call_target="tpu_custom_call" | custom-call | tf_op jit(solution)/shard_map/prepare/pallas_call | solution.py:387
  9.7 0.9 %copy-done = s32[16,2048]{1,0:T(8,128)S(1)} copy-done((s32[16,2048]{1,0:T(8,128)S(1)}, s32[16,2048]{1,0:T(8,128)}, u32[]{:S(2)}) %copy-start) | copy-done | bytes 131096
  10.6 0.8 copy-done.4
  11.5 0.7 copy-done.10
  12.1 2.6 %kernel_rows.4 = (bf16[128,1024]{1,0:T(8,128)(2,1)S(1)}, bf16[128,1024]{1,0:T(8,128)(2,1)S(1)}, f32[32,128]{1,0:T(8,128)S(1)}) custom-call(f32[16]{0:T(128)S(1)} %copy-done.10, f32[16]{0:T(128)S(1)} %get-tuple-element.41.floor_ref, s32[16,2048]{1,0:T(8,128)S(1)} %copy-done, f32[16,1024]{1,0:T(8,128)S(1)} %copy-done.4, ...), custom_call_target="tpu_custom_call" | custom-call | flops 12582912 | bytes 524288 | tf_op jit(solution)/shard_map/kernel_rows/pallas_call | solution.py:153
  14.7 0.0 collective-permute-done.5.refs_1_
  14.7 1.6 %collective-permute-start.7 = (f32[64,1024]{1,0:T(8,128)S(1)}, f32[64,1024]{1,0:T(8,128)S(1)}, u32[]{:S(2)}, u32[]{:S(2)}) collective-permute-start(f32[64,1024]{1,0:T(8,128)S(1)} %collective-permute-done.5.refs_1_), channel_id=1, source_target_pairs={{0,2},{1,3},{2,0},{3,1},{4,6},{5,7},{6,4},{7,5},{8,10},{9,11},{10,... | collective-permute-start | bytes 786440 | tf_op jit(solution)/shard_map/ppermute | solution.py:24
  16.3 0.0 collective-permute-done.2
  16.3 0.5 collective-permute-start.3
  16.8 0.9 %copy-done.1 = s32[16,2048]{1,0:T(8,128)S(1)} copy-done((s32[16,2048]{1,0:T(8,128)S(1)}, s32[16,2048]{1,0:T(8,128)}, u32[]{:S(2)}) %copy-start.1) | copy-done | bytes 131096
  17.7 0.8 copy-done.5
  18.6 0.7 copy-done.11
  19.2 2.6 %kernel_rows.5 = (bf16[128,1024]{1,0:T(8,128)(2,1)S(1)}, bf16[128,1024]{1,0:T(8,128)(2,1)S(1)}, f32[32,256]{1,0:T(8,128)S(1)}) custom-call(f32[16]{0:T(128)S(1)} %copy-done.11, f32[16]{0:T(128)S(1)} %get-tuple-element.41.floor_ref, s32[16,2048]{1,0:T(8,128)S(1)} %copy-done.1, f32[16,1024]{1,0:T(8,128)S(1)} %copy-done.5, ...), custom_call_target="tpu_custom_call" | custom-call | flops 12582912 | bytes 524288 | tf_op jit(solution)/shard_map/kernel_rows/pallas_call | solution.py:153
  21.8 0.0 copy-start.3
  21.8 0.0 collective-permute-done.3
  21.9 2.7 %collective-permute-start.4 = (f32[32,512]{1,0:T(8,128)S(1)}, f32[32,512]{1,0:T(8,128)S(1)}, u32[]{:S(2)}, u32[]{:S(2)}) collective-permute-start(f32[32,512]{1,0:T(8,128)S(1)} %maximum_select_fusion.1.passed_ref), channel_id=1, source_target_pairs={{0,8},{1,9},{2,10},{3,11},{4,12},{5,13},{6,14},{7,15},{8,0},{9,1},... | collective-permute-start | bytes 196616 | tf_op jit(solution)/shard_map/ppermute | solution.py:24
  24.5 0.0 collective-permute-start.8
  24.5 0.5 collective-permute-start.9
  25.0 0.0 collective-permute-done.6.refs_2_
  25.0 0.0 collective-permute-start.10
  25.0 0.0 collective-permute-done.7.refs_3_
  25.0 0.5 collective-permute-start.11
  25.6 0.9 %copy-done.2 = s32[16,2048]{1,0:T(8,128)S(1)} copy-done((s32[16,2048]{1,0:T(8,128)S(1)}, s32[16,2048]{1,0:T(8,128)}, u32[]{:S(2)}) %copy-start.2) | copy-done | bytes 131096
  26.5 0.8 copy-done.6
  27.3 0.7 copy-done.12
  27.9 4.5 %kernel_rows.6 = (bf16[256,1024]{1,0:T(8,128)(2,1)S(1)}, bf16[256,1024]{1,0:T(8,128)(2,1)S(1)}, f32[32,512]{1,0:T(8,128)S(1)}) custom-call(f32[16]{0:T(128)S(1)} %copy-done.12, f32[16]{0:T(128)S(1)} %get-tuple-element.41.floor_ref, s32[16,2048]{1,0:T(8,128)S(1)} %copy-done.2, f32[16,1024]{1,0:T(8,128)S(1)} %copy-done.6, ...), custom_call_target="tpu_custom_call" | custom-call | flops 25165824 | bytes 1048576 | tf_op jit(solution)/shard_map/kernel_rows/pallas_call | solution.py:153
  32.5 0.0 copy-start.13
  32.5 0.0 collective-permute-done.4
  32.5 0.0 copy-start.9
  32.5 0.9 %copy-done.9 = f32[64,1024]{1,0:T(8,128)S(1)} copy-done((f32[64,1024]{1,0:T(8,128)S(1)}, f32[64,1024]{1,0:T(8,128)}, u32[]{:S(2)}) %copy-start.9) | copy-done | bytes 262168
  33.5 0.6 row_products.2
  34.0 0.0 collective-permute-done.8.refs_0_
  34.1 0.0 collective-permute-done.10.refs_2_
  34.1 0.0 collective-permute-done.9.refs_1_
  34.1 0.0 collective-permute-done.11.refs_3_
  34.1 0.6 row_products.3
  34.7 0.4 collective-permute-start.12
  35.0 0.0 copy-done.7
  35.0 0.0 copy-done.3
  35.0 8.3 %kernel_rows.7 = (bf16[512,1024]{1,0:T(8,128)(2,1)S(1)}, bf16[512,1024]{1,0:T(8,128)(2,1)S(1)}, f32[16,512]{1,0:T(8,128)S(1)}) custom-call(f32[16]{0:T(128)S(1)} %copy-done.12, f32[16]{0:T(128)S(1)} %get-tuple-element.41.floor_ref, s32[16,2048]{1,0:T(8,128)S(1)} %copy-done.3, f32[16,1024]{1,0:T(8,128)S(1)} %copy-done.7, ...), custom_call_target="tpu_custom_call" | custom-call | flops 50331648 | bytes 2097152 | tf_op jit(solution)/shard_map/kernel_rows/pallas_call | solution.py:153
  43.3 0.0 collective-permute-done.12
  43.4 21.5 %products.1 = (f32[16,512]{1,0:T(8,128)S(1)}, f32[16,512]{1,0:T(8,128)S(1)}, f32[16,64]{1,0:T(8,128)S(1)}) custom-call(f32[16]{0:T(128)S(1)} %copy-done.13, f32[16]{0:T(128)S(1)} %get-tuple-element.41.floor_ref, f32[16,1024]{1,0:T(8,128)S(1)} %pad_maximum_fusion.coef_ref, s32[16,2048]{1,0:T(8,128)S(1)} %copy-done.3, f32[16,1024]{1,0:T(8,128)S(1)} %copy-done.7, ...), custom_call_target="tpu_custom_call" | custom-call | flops 100663296 | bytes 4194304 | tf_op jit(solution)/shard_map/products/pallas_call | solution.py:260
  64.9 2.7 %collective-permute-start.13 = (f32[16,512]{1,0:T(8,128)S(1)}, f32[16,512]{1,0:T(8,128)S(1)}, u32[]{:S(2)}, u32[]{:S(2)}) collective-permute-start(f32[16,512]{1,0:T(8,128)S(1)} %get-tuple-element.37), channel_id=1, source_target_pairs={{0,8},{1,9},{2,10},{3,11},{4,12},{5,13},{6,14},{7,15},{8,0},{9,1},... | collective-permute-start | bytes 98312 | tf_op jit(solution)/shard_map/ppermute | solution.py:24
  67.6 2.4 %collective-permute-done.13.came_ref = f32[16,512]{1,0:T(8,128)S(1)} collective-permute-done((f32[16,512]{1,0:T(8,128)S(1)}, f32[16,512]{1,0:T(8,128)S(1)}, u32[]{:S(2)}, u32[]{:S(2)}) %collective-permute-start.13) | collective-permute-done | bytes 32800 | tf_op jit(solution)/shard_map/ppermute | solution.py:24
  70.0 0.6 image_rows.1
  70.6 0.0 collective-permute-start.14
  70.6 1.3 %collective-permute-done.14 = f32[16,1024]{1,0:T(8,128)S(1)} collective-permute-done((f32[16,1024]{1,0:T(8,128)S(1)}, f32[16,1024]{1,0:T(8,128)S(1)}, u32[]{:S(2)}, u32[]{:S(2)}) %collective-permute-start.14) | collective-permute-done | bytes 65568 | tf_op jit(solution)/shard_map/ppermute | solution.py:24
  71.9 0.6 collective-permute-start.15
  72.5 3.8 %collective-permute-done.15 = f32[16,1024]{1,0:T(8,128)S(1)} collective-permute-done((f32[16,1024]{1,0:T(8,128)S(1)}, f32[16,1024]{1,0:T(8,128)S(1)}, u32[]{:S(2)}, u32[]{:S(2)}) %collective-permute-start.15) | collective-permute-done | bytes 65568 | tf_op jit(solution)/shard_map/ppermute | solution.py:24
  76.2 1.5 %collective-permute-start.16 = (f32[16,1024]{1,0:T(8,128)S(1)}, f32[16,1024]{1,0:T(8,128)S(1)}, u32[]{:S(2)}, u32[]{:S(2)}) collective-permute-start(f32[16,1024]{1,0:T(8,128)S(1)} %add.10), channel_id=1, source_target_pairs={{0,4},{1,5},{2,6},{3,7},{4,0},{5,1},{6,2},{7,3},{8,12},{9,13},{10,... | collective-permute-start | bytes 196616 | tf_op jit(solution)/shard_map/ppermute | solution.py:24
  77.7 2.9 %collective-permute-done.16 = f32[16,1024]{1,0:T(8,128)S(1)} collective-permute-done((f32[16,1024]{1,0:T(8,128)S(1)}, f32[16,1024]{1,0:T(8,128)S(1)}, u32[]{:S(2)}, u32[]{:S(2)}) %collective-permute-start.16) | collective-permute-done | bytes 65568 | tf_op jit(solution)/shard_map/ppermute | solution.py:24
  80.6 2.5 %collective-permute-start.17 = (f32[16,1024]{1,0:T(8,128)S(1)}, f32[16,1024]{1,0:T(8,128)S(1)}, u32[]{:S(2)}, u32[]{:S(2)}) collective-permute-start(f32[16,1024]{1,0:T(8,128)S(1)} %add.11.image_ref), channel_id=1, source_target_pairs={{0,8},{1,9},{2,10},{3,11},{4,12},{5,13},{6,14},{7,15},{8,0},{9,1},... | collective-permute-start | bytes 196616 | tf_op jit(solution)/shard_map/ppermute | solution.py:24
  83.1 2.7 %collective-permute-done.17.more_ref = f32[16,1024]{1,0:T(8,128)S(1)} collective-permute-done((f32[16,1024]{1,0:T(8,128)S(1)}, f32[16,1024]{1,0:T(8,128)S(1)}, u32[]{:S(2)}, u32[]{:S(2)}) %collective-permute-start.17) | collective-permute-done | bytes 65568 | tf_op jit(solution)/shard_map/ppermute | solution.py:24
  85.8 0.6 copy-done.15
  86.4 1.8 %finish.1 = (f32[16,64]{1,0:T(8,128)}, f32[16,64]{1,0:T(8,128)}, f32[16,64]{1,0:T(8,128)}) custom-call(f32[16,1024]{1,0:T(8,128)} %copy-done.14, f32[16,1024]{1,0:T(8,128)} %copy-done.15, f32[32,1024]{1,0:T(8,128)} %copy-done.8, f32[16,64]{1,0:T(8,128)} %solution_ref.1, f32[16,64]{1,0:T(8,128)} %residual_ref.1, f32[16,64]{1,0:T(8,128)} %direction_ref.1), custom_call_target="tpu_custom_call" | custom-call | tf_op jit(solution)/shard_map/finish/pallas_call | solution.py:484
  (25 shorter events, 0.1 us)
Async XLA Ops:
  0.6 5.1 %collective-permute-start.1 = (f32[16,64]{1,0:T(8,128)}, f32[16,64]{1,0:T(8,128)S(1)}, u32[]{:S(2)}, u32[]{:S(2)}) collective-permute-start(f32[16,64]{1,0:T(8,128)} %residual_ref.1), channel_id=1, source_target_pairs={{0,1},{1,0},{2,3},{3,2},{4,5},{5,4},{6,7},{7,6},{8,9},{9,8},{10,11... | collective-permute-start | bytes 12296 | tf_op jit(solution)/shard_map/ppermute | solution.py:24
  1.1 4.6 %collective-permute-start = (f32[16,64]{1,0:T(8,128)}, f32[16,64]{1,0:T(8,128)S(1)}, u32[]{:S(2)}, u32[]{:S(2)}) collective-permute-start(f32[16,64]{1,0:T(8,128)} %direction_ref.1), channel_id=1, source_target_pairs={{0,1},{1,0},{2,3},{3,2},{4,5},{5,4},{6,7},{7,6},{8,9},{9,8},{10,11... | collective-permute-start | bytes 12296 | tf_op jit(solution)/shard_map/ppermute | solution.py:24
  1.2 23.8 %collective-permute-start.6 = (f32[64,1024]{1,0:T(8,128)}, f32[64,1024]{1,0:T(8,128)S(1)}, u32[]{:S(2)}, u32[]{:S(2)}) collective-permute-start(f32[64,1024]{1,0:T(8,128)} %refs_0_.1), channel_id=1, source_target_pairs={{0,2},{1,3},{2,0},{3,1},{4,6},{5,7},{6,4},{7,5},{8,10},{9,11},{10,... | collective-permute-start | bytes 786440 | tf_op jit(solution)/shard_map/ppermute | solution.py:24
  4.2 10.5 %collective-permute-start.5 = (f32[64,1024]{1,0:T(8,128)}, f32[64,1024]{1,0:T(8,128)S(1)}, u32[]{:S(2)}, u32[]{:S(2)}) collective-permute-start(f32[64,1024]{1,0:T(8,128)} %refs_0_.1), channel_id=1, source_target_pairs={{0,4},{1,5},{2,6},{3,7},{4,0},{5,1},{6,2},{7,3},{8,12},{9,13},{10,... | collective-permute-start | bytes 786440 | tf_op jit(solution)/shard_map/ppermute | solution.py:24
  6.6 9.7 %collective-permute-start.2 = (f32[32,128]{1,0:T(8,128)S(1)}, f32[32,128]{1,0:T(8,128)S(1)}, u32[]{:S(2)}, u32[]{:S(2)}) collective-permute-start(f32[32,128]{1,0:T(8,128)S(1)} %maximum_select_fusion.3.passed_ref), channel_id=1, source_target_pairs={{0,2},{1,3},{2,0},{3,1},{4,6},{5,7},{6,4},{7,5},{8,10},{9,11},{10,... | collective-permute-start | bytes 49160 | tf_op jit(solution)/shard_map/ppermute | solution.py:24
  9.7 0.9 %copy-start = (s32[16,2048]{1,0:T(8,128)S(1)}, s32[16,2048]{1,0:T(8,128)}, u32[]{:S(2)}) copy-start(s32[16,2048]{1,0:T(8,128)} %samples_hbm.9) | copy-start | bytes 393220
  10.6 0.8 copy-start.4
  11.5 0.7 copy-start.10
  14.7 10.3 %collective-permute-start.7 = (f32[64,1024]{1,0:T(8,128)S(1)}, f32[64,1024]{1,0:T(8,128)S(1)}, u32[]{:S(2)}, u32[]{:S(2)}) collective-permute-start(f32[64,1024]{1,0:T(8,128)S(1)} %collective-permute-done.5.refs_1_), channel_id=1, source_target_pairs={{0,2},{1,3},{2,0},{3,1},{4,6},{5,7},{6,4},{7,5},{8,10},{9,11},{10,... | collective-permute-start | bytes 786440 | tf_op jit(solution)/shard_map/ppermute | solution.py:24
  16.3 5.5 %collective-permute-start.3 = (f32[32,256]{1,0:T(8,128)S(1)}, f32[32,256]{1,0:T(8,128)S(1)}, u32[]{:S(2)}, u32[]{:S(2)}) collective-permute-start(f32[32,256]{1,0:T(8,128)S(1)} %maximum_select_fusion.2.passed_ref), channel_id=1, source_target_pairs={{0,4},{1,5},{2,6},{3,7},{4,0},{5,1},{6,2},{7,3},{8,12},{9,13},{10,... | collective-permute-start | bytes 98312 | tf_op jit(solution)/shard_map/ppermute | solution.py:24
  16.8 0.9 %copy-start.1 = (s32[16,2048]{1,0:T(8,128)S(1)}, s32[16,2048]{1,0:T(8,128)}, u32[]{:S(2)}) copy-start(s32[16,2048]{1,0:T(8,128)} %samples_hbm.9) | copy-start | bytes 393220
  17.7 0.8 copy-start.5
  18.6 0.7 copy-start.11
  19.2 15.8 %copy-start.7 = (f32[16,1024]{1,0:T(8,128)S(1)}, f32[16,1024]{1,0:T(8,128)}, u32[]{:S(2)}) copy-start(f32[16,1024]{1,0:T(8,128)} %prepare.1.centres_hbm) | copy-start | bytes 196612
  21.8 13.2 %copy-start.3 = (s32[16,2048]{1,0:T(8,128)S(1)}, s32[16,2048]{1,0:T(8,128)}, u32[]{:S(2)}) copy-start(s32[16,2048]{1,0:T(8,128)} %samples_hbm.9) | copy-start | bytes 393220
  21.9 10.6 %collective-permute-start.4 = (f32[32,512]{1,0:T(8,128)S(1)}, f32[32,512]{1,0:T(8,128)S(1)}, u32[]{:S(2)}, u32[]{:S(2)}) collective-permute-start(f32[32,512]{1,0:T(8,128)S(1)} %maximum_select_fusion.1.passed_ref), channel_id=1, source_target_pairs={{0,8},{1,9},{2,10},{3,11},{4,12},{5,13},{6,14},{7,15},{8,0},{9,1},... | collective-permute-start | bytes 196616 | tf_op jit(solution)/shard_map/ppermute | solution.py:24
  24.5 9.5 %collective-permute-start.8 = (f32[64,1024]{1,0:T(8,128)}, f32[64,1024]{1,0:T(8,128)S(1)}, u32[]{:S(2)}, u32[]{:S(2)}) collective-permute-start(f32[64,1024]{1,0:T(8,128)} %refs_0_.1), channel_id=1, source_target_pairs={{0,1},{1,0},{2,3},{3,2},{4,5},{5,4},{6,7},{7,6},{8,9},{9,8},{10,11... | collective-permute-start | bytes 786440 | tf_op jit(solution)/shard_map/ppermute | solution.py:24
  24.5 9.5 %collective-permute-start.9 = (f32[64,1024]{1,0:T(8,128)S(1)}, f32[64,1024]{1,0:T(8,128)S(1)}, u32[]{:S(2)}, u32[]{:S(2)}) collective-permute-start(f32[64,1024]{1,0:T(8,128)S(1)} %collective-permute-done.5.refs_1_), channel_id=1, source_target_pairs={{0,1},{1,0},{2,3},{3,2},{4,5},{5,4},{6,7},{7,6},{8,9},{9,8},{10,11... | collective-permute-start | bytes 786440 | tf_op jit(solution)/shard_map/ppermute | solution.py:24
  25.0 9.0 %collective-permute-start.10 = (f32[64,1024]{1,0:T(8,128)S(1)}, f32[64,1024]{1,0:T(8,128)S(1)}, u32[]{:S(2)}, u32[]{:S(2)}) collective-permute-start(f32[64,1024]{1,0:T(8,128)S(1)} %collective-permute-done.6.refs_2_), channel_id=1, source_target_pairs={{0,1},{1,0},{2,3},{3,2},{4,5},{5,4},{6,7},{7,6},{8,9},{9,8},{10,11... | collective-permute-start | bytes 786440 | tf_op jit(solution)/shard_map/ppermute | solution.py:24
  25.0 9.0 %collective-permute-start.11 = (f32[64,1024]{1,0:T(8,128)S(1)}, f32[64,1024]{1,0:T(8,128)S(1)}, u32[]{:S(2)}, u32[]{:S(2)}) collective-permute-start(f32[64,1024]{1,0:T(8,128)S(1)} %collective-permute-done.7.refs_3_), channel_id=1, source_target_pairs={{0,1},{1,0},{2,3},{3,2},{4,5},{5,4},{6,7},{7,6},{8,9},{9,8},{10,11... | collective-permute-start | bytes 786440 | tf_op jit(solution)/shard_map/ppermute | solution.py:24
  25.5 0.9 %copy-start.2 = (s32[16,2048]{1,0:T(8,128)S(1)}, s32[16,2048]{1,0:T(8,128)}, u32[]{:S(2)}) copy-start(s32[16,2048]{1,0:T(8,128)} %samples_hbm.9) | copy-start | bytes 393220
  26.5 0.8 copy-start.6
  27.3 0.7 copy-start.12
  32.5 10.9 %copy-start.13 = (f32[16]{0:T(128)S(1)}, f32[16]{0:T(128)}, u32[]{:S(2)}) copy-start(f32[16]{0:T(128)} %get-tuple-element.42.shift_ref) | copy-start | bytes 196
  32.5 1.0 %copy-start.9 = (f32[64,1024]{1,0:T(8,128)S(1)}, f32[64,1024]{1,0:T(8,128)}, u32[]{:S(2)}) copy-start(f32[64,1024]{1,0:T(8,128)} %refs_0_.1) | copy-start | bytes 786436
  33.5 31.5 %copy-start.8 = (f32[32,1024]{1,0:T(8,128)}, f32[32,1024]{1,0:T(8,128)S(1)}, u32[]{:S(2)}) copy-start(f32[32,1024]{1,0:T(8,128)S(1)} %maximum_select_fusion.state_ref) | copy-start | bytes 393220
  34.7 8.7 %collective-permute-start.12 = (f32[16,512]{1,0:T(8,128)S(1)}, f32[16,512]{1,0:T(8,128)S(1)}, u32[]{:S(2)}, u32[]{:S(2)}) collective-permute-start(f32[16,512]{1,0:T(8,128)S(1)} %constant_dynamic-update-slice_fusion.passed_ref), channel_id=1, source_target_pairs={{0,8},{1,9},{2,10},{3,11},{4,12},{5,13},{6,14},{7,15},{8,0},{9,1},... | collective-permute-start | bytes 98312 | tf_op jit(solution)/shard_map/ppermute | solution.py:24
  64.9 5.1 %collective-permute-start.13 = (f32[16,512]{1,0:T(8,128)S(1)}, f32[16,512]{1,0:T(8,128)S(1)}, u32[]{:S(2)}, u32[]{:S(2)}) collective-permute-start(f32[16,512]{1,0:T(8,128)S(1)} %get-tuple-element.37), channel_id=1, source_target_pairs={{0,8},{1,9},{2,10},{3,11},{4,12},{5,13},{6,14},{7,15},{8,0},{9,1},... | collective-permute-start | bytes 98312 | tf_op jit(solution)/shard_map/ppermute | solution.py:24
  70.6 1.3 %collective-permute-start.14 = (f32[16,1024]{1,0:T(8,128)S(1)}, f32[16,1024]{1,0:T(8,128)S(1)}, u32[]{:S(2)}, u32[]{:S(2)}) collective-permute-start(f32[16,1024]{1,0:T(8,128)S(1)} %image_rows.1), channel_id=1, source_target_pairs={{0,1},{1,0},{2,3},{3,2},{4,5},{5,4},{6,7},{7,6},{8,9},{9,8},{10,11... | collective-permute-start | bytes 196616 | tf_op jit(solution)/shard_map/ppermute | solution.py:24
  71.9 4.3 %collective-permute-start.15 = (f32[16,1024]{1,0:T(8,128)S(1)}, f32[16,1024]{1,0:T(8,128)S(1)}, u32[]{:S(2)}, u32[]{:S(2)}) collective-permute-start(f32[16,1024]{1,0:T(8,128)S(1)} %add.9), channel_id=1, source_target_pairs={{0,2},{1,3},{2,0},{3,1},{4,6},{5,7},{6,4},{7,5},{8,10},{9,11},{10,... | collective-permute-start | bytes 196616 | tf_op jit(solution)/shard_map/ppermute | solution.py:24
  76.2 4.3 %collective-permute-start.16 = (f32[16,1024]{1,0:T(8,128)S(1)}, f32[16,1024]{1,0:T(8,128)S(1)}, u32[]{:S(2)}, u32[]{:S(2)}) collective-permute-start(f32[16,1024]{1,0:T(8,128)S(1)} %add.10), channel_id=1, source_target_pairs={{0,4},{1,5},{2,6},{3,7},{4,0},{5,1},{6,2},{7,3},{8,12},{9,13},{10,... | collective-permute-start | bytes 196616 | tf_op jit(solution)/shard_map/ppermute | solution.py:24
  80.6 5.2 %copy-start.14 = (f32[16,1024]{1,0:T(8,128)}, f32[16,1024]{1,0:T(8,128)S(1)}, u32[]{:S(2)}) copy-start(f32[16,1024]{1,0:T(8,128)S(1)} %add.11.image_ref) | copy-start | bytes 196612
  80.6 5.2 %collective-permute-start.17 = (f32[16,1024]{1,0:T(8,128)S(1)}, f32[16,1024]{1,0:T(8,128)S(1)}, u32[]{:S(2)}, u32[]{:S(2)}) collective-permute-start(f32[16,1024]{1,0:T(8,128)S(1)} %add.11.image_ref), channel_id=1, source_target_pairs={{0,8},{1,9},{2,10},{3,11},{4,12},{5,13},{6,14},{7,15},{8,0},{9,1},... | collective-permute-start | bytes 196616 | tf_op jit(solution)/shard_map/ppermute | solution.py:24
  85.8 0.6 copy-start.15

commit v6 on v5

--- a/solution.py
+++ b/solution.py
@@ -15,6 +15,7 @@
 HELD_BYTES = 16 << 20
 VMEM = pl.BlockSpec(memory_space=pltpu.VMEM)
 FREE = pl.BlockSpec(memory_space=pl.ANY)
+HBM = pl.BlockSpec(memory_space=pltpu.HBM)
 SMEM = pl.BlockSpec(memory_space=pltpu.SMEM)
 F32 = jnp.float32
 BF16 = jnp.bfloat16
@@ -90,27 +91,64 @@
     return copies
 
 
-def scale_column(shift_ref, dims):
+def modulo(value):
+    turns = (value.astype(F32) * (1.0 / LATTICE)).astype(jnp.int32)
+    rest = value - turns * LATTICE
+    rest = jnp.where(rest < 0, rest + LATTICE, rest)
+    return jnp.where(rest >= LATTICE, rest - LATTICE, rest)
+
+
+def column_of(values_ref, dims, dtype):
     row = lax.broadcasted_iota(jnp.int32, (dims, 1), 0)
-    scale = jnp.zeros((dims, 1), F32)
+    column = jnp.zeros((dims, 1), dtype)
     for axis_number in range(dims):
-        scale = jnp.where(row == axis_number, shift_ref[axis_number], scale)
-    return scale * (2.0 / LATTICE)
+        column = jnp.where(row == axis_number, values_ref[axis_number], column)
+    return column
+
+
+def set_up(order_bits, cen_dev, generator_ref, weight_ref, shift_ref, floor_ref, centre_ref):
+    dims, centres_all = centre_ref.shape
+    curves = [math.pi * math.pi * 0.75**weight for weight in range(8)]
+    for axis_number in range(dims):
+        weight = weight_ref[axis_number]
+        shift, floor = 0.5 * math.sqrt(curves[7]), 1.0 - curves[7] / 12.0
+        for k in range(7):
+            shift = jnp.where(weight == k, F32(0.5 * math.sqrt(curves[k])), shift)
+            floor = jnp.where(weight == k, F32(1.0 - curves[k] / 12.0), floor)
+        shift_ref[axis_number] = shift
+        floor_ref[axis_number] = floor
+    scale = column_of(shift_ref, dims, F32) * (2.0 / LATTICE)
+    generator = column_of(generator_ref, dims, jnp.int32)
+    place = lax.broadcasted_iota(jnp.int32, (1, centres_all), 1)
+    owner = jnp.zeros_like(place) + lax.axis_index("samp")
+    for k, bit in enumerate(order_bits):
+        owner = jnp.where((place & (cen_dev << k)) != 0, owner ^ bit, owner)
+    column = owner * cen_dev + (place & (cen_dev - 1))
+    upper = modulo(column * (generator >> 8))
+    centre = modulo(upper * 256 + column * (generator & 255))
+    centre_ref[...] = centre.astype(F32) * scale
+    return scale
 
 
 def store_rows(
-    first_row, step_rows, shift_ref, floor_ref, samples_hbm, centres_hbm, passed_ref,
-    high_hbm, low_hbm, handed_ref, sample_ref, centre_ref, high_ref, low_ref, in_sems, out_sems,
+    first_row, step_rows, order, generator_hbm, weight_hbm, samples_hbm, passed_ref,
+    high_hbm, low_hbm, handed_ref, generator_ref, weight_ref, shift_ref, floor_ref, sample_ref,
+    centre_ref, high_ref, low_ref, in_sems, out_sems,
 ):
     rows_all = high_hbm.shape[0]
     copies = fetch(
-        [(samples_hbm.at[:, pl.ds(first_row, rows_all)], sample_ref), (centres_hbm, centre_ref)],
+        [
+            (generator_hbm, generator_ref),
+            (weight_hbm, weight_ref),
+            (samples_hbm.at[:, pl.ds(first_row, rows_all)], sample_ref),
+        ],
         in_sems,
     )
     handed_ref[...] = passed_ref[...]
-    scale = scale_column(shift_ref, sample_ref.shape[0])
-    for copy in copies:
-        copy.wait()
+    copies[0].wait()
+    copies[1].wait()
+    scale = set_up(*order, generator_ref, weight_ref, shift_ref, floor_ref, centre_ref)
+    copies[2].wait()
 
     def sends(step):
         slot = lax.rem(step, 2)
@@ -145,22 +183,31 @@
             copy.wait()
 
 
-def kernel_rows(passed, samples, first_row, rows, constants):
-    centre_scaled, shift, floor = constants
-    dims, centres_all = centre_scaled.shape
+def set_up_scratch(dims, rows, centres_all):
+    return [
+        pltpu.SMEM((dims,), jnp.int32),
+        pltpu.SMEM((dims,), jnp.int32),
+        pltpu.SMEM((dims,), F32),
+        pltpu.SMEM((dims,), F32),
+        pltpu.VMEM((dims, rows), jnp.int32),
+        pltpu.VMEM((dims, centres_all), F32),
+    ]
+
+
+def kernel_rows(passed, first_row, rows, order, centres_all, lattice):
+    dims = lattice[2].shape[0]
     kept = jax.ShapeDtypeStruct((rows, centres_all), BF16)
     step_rows = min(128, rows)
     high, low, handed = pl.pallas_call(
-        functools.partial(store_rows, first_row, step_rows),
-        in_specs=[SMEM, SMEM, FREE, FREE, VMEM],
+        functools.partial(store_rows, first_row, step_rows, order),
+        in_specs=[HBM, HBM, HBM, VMEM],
         out_specs=[FREE, FREE, VMEM],
         out_shape=[kept, kept, jax.ShapeDtypeStruct(passed.shape, passed.dtype)],
         scratch_shapes=[
-            pltpu.VMEM((dims, rows), jnp.int32),
-            pltpu.VMEM((dims, centres_all), F32),
+            *set_up_scratch(dims, rows, centres_all),
             pltpu.VMEM((2, step_rows, centres_all), BF16),
             pltpu.VMEM((2, step_rows, centres_all), BF16),
-            pltpu.SemaphoreType.DMA((2,)),
+            pltpu.SemaphoreType.DMA((3,)),
             pltpu.SemaphoreType.DMA((2, 2)),
         ],
         compiler_params=pltpu.CompilerParams(vmem_limit_bytes=12 << 20),
@@ -170,7 +217,7 @@
             transcendentals=0,
         ),
         name="kernel_rows",
-    )(shift, floor, samples, centre_scaled, passed)
+    )(*lattice, passed)
     return (high, low), handed
 
 
@@ -189,31 +236,39 @@
 
 
 def products(
-    outs, block_rows, stored, shift_ref, floor_ref, coef_ref, samples_hbm, centres_hbm, *refs
+    outs, block_rows, stored, order, coef_ref, generator_hbm, weight_hbm, samples_hbm, *refs
 ):
     stored_hbm, refs = refs[: 2 * len(stored)], refs[2 * len(stored) :]
     *backward_refs, own_out_ref = refs[:3]
-    parts_ref, sum_ref, made_high, made_low, sample_ref, centre_ref, high_ref, low_ref, sems = refs[3:]
+    generator_ref, weight_ref, shift_ref, floor_ref, sample_ref, centre_ref = refs[3:9]
+    parts_ref, sum_ref, made_high, made_low, high_ref, low_ref, sems = refs[9:]
     own_rows = own_out_ref.shape[1]
     steps = sample_ref.shape[1] // block_rows
     stored_rows = sum(stored)
     share = stored_rows // steps
     columns = pl.ds(stored_rows, sample_ref.shape[1])
-    copies = fetch([(samples_hbm.at[:, columns], sample_ref), (centres_hbm, centre_ref)], sems)
+    copies = fetch(
+        [
+            (generator_hbm, generator_ref),
+            (weight_hbm, weight_ref),
+            (samples_hbm.at[:, columns], sample_ref),
+        ],
+        sems,
+    )
     first = 0
     for i, rows in enumerate(stored):
         pairs = zip(stored_hbm[2 * i : 2 * i + 2], (high_ref, low_ref))
         place = pl.ds(first, rows)
-        copies += fetch([(src, dst.at[place]) for src, dst in pairs], sems.at[pl.ds(2 + 2 * i, 2)])
+        copies += fetch([(src, dst.at[place]) for src, dst in pairs], sems.at[pl.ds(3 + 2 * i, 2)])
         first += rows
 
-    scale = scale_column(shift_ref, sample_ref.shape[0])
     parts_ref[...] = stack3(coef_ref[...])
     sum_ref[...] = jnp.zeros_like(sum_ref)
     made_high[1] = jnp.zeros(made_high.shape[1:], BF16)
     made_low[1] = jnp.zeros(made_low.shape[1:], BF16)
     copies[0].wait()
     copies[1].wait()
+    scale = set_up(*order, generator_ref, weight_ref, shift_ref, floor_ref, centre_ref)
     own_high, own_low = made_high.at[0], made_low.at[0]
     rows = pl.ds(0, own_rows)
     own_points = centre_ref[:, :own_rows]
@@ -249,17 +304,16 @@
         backward_ref[...] = last[:, i * width : (i + 1) * width]
 
 
-def apply_products(store, samples, coefficients, own_rows, block_rows, constants):
-    centre_scaled, shift, floor = constants
+def apply_products(store, coefficients, own_rows, block_rows, order, lattice):
     outs, centres_all = coefficients.shape
-    dims = centre_scaled.shape[0]
+    dims, samples_dev = lattice[2].shape
     stored = tuple(high.shape[0] for high, _ in store)
     made = pltpu.VMEM((2, block_rows, centres_all), BF16)
     kept = pltpu.VMEM((max(16, sum(stored)), centres_all), BF16)
-    rows = samples.shape[1] - sum(stored)
+    rows = samples_dev - sum(stored)
     return pl.pallas_call(
-        functools.partial(products, outs, block_rows, stored),
-        in_specs=[SMEM, SMEM, VMEM, *[FREE] * (2 + 2 * len(stored))],
+        functools.partial(products, outs, block_rows, stored, order),
+        in_specs=[VMEM, HBM, HBM, HBM, *[FREE] * (2 * len(stored))],
         out_specs=[VMEM, VMEM, VMEM],
         out_shape=[
             jax.ShapeDtypeStruct((outs, centres_all // 2), F32),
@@ -267,15 +321,14 @@
             jax.ShapeDtypeStruct((outs, own_rows), F32),
         ],
         scratch_shapes=[
+            *set_up_scratch(dims, rows, centres_all),
             pltpu.VMEM((3 * outs, centres_all), BF16),
             pltpu.VMEM((3 * outs, centres_all), F32),
             made,
             made,
-            pltpu.VMEM((dims, rows), jnp.int32),
-            pltpu.VMEM((dims, centres_all), F32),
             kept,
             kept,
-            pltpu.SemaphoreType.DMA((2 + 2 * len(stored),)),
+            pltpu.SemaphoreType.DMA((3 + 2 * len(stored),)),
         ],
         compiler_params=pltpu.CompilerParams(
             vmem_limit_bytes=(14 << 20) + (16 * block_rows + 4 * sum(stored)) * centres_all
@@ -286,38 +339,19 @@
             transcendentals=0,
         ),
         name="products",
-    )(shift, floor, coefficients, samples, centre_scaled, *[part for pair in store for part in pair])
-
-
-def modulo(value):
-    turns = (value.astype(F32) * (1.0 / LATTICE)).astype(jnp.int32)
-    rest = value - turns * LATTICE
-    rest = jnp.where(rest < 0, rest + LATTICE, rest)
-    return jnp.where(rest >= LATTICE, rest - LATTICE, rest)
-
-
-def prepare(order_bits, cen_dev, generator_ref, shift_ref, centre_ref):
-    dims, centres_all = centre_ref.shape
-    row = lax.broadcasted_iota(jnp.int32, (dims, 1), 0)
-    generator = jnp.zeros((dims, 1), jnp.int32)
-    for axis_number in range(dims):
-        generator = jnp.where(row == axis_number, generator_ref[axis_number], generator)
-    place = lax.broadcasted_iota(jnp.int32, (1, centres_all), 1)
-    owner = jnp.zeros_like(place) + lax.axis_index("samp")
-    for k, bit in enumerate(order_bits):
-        block_bit = cen_dev << k
-        owner = jnp.where((place & block_bit) != 0, owner ^ bit, owner)
-    column = owner * cen_dev + (place & (cen_dev - 1))
-    upper = modulo(column * (generator >> 8))
-    centre = modulo(upper * 256 + column * (generator & 255))
-    centre_ref[...] = centre.astype(F32) * scale_column(shift_ref, dims)
+    )(coefficients, *lattice, *[part for pair in store for part in pair])
 
 
 def row_products(outs, count, state_ref, *refs):
-    coef_ref, parts_ref = refs[count:]
+    coef_ref, parts_ref, fetched_ref, sems = refs[count:]
+    copy = pltpu.make_async_copy(refs[0], fetched_ref, sems.at[0])
+    copy.start()
     state = stack3(state_ref[:outs])
     cen_dev = refs[0].shape[0]
-    for i, piece_ref in enumerate(refs[:count]):
+    piece_refs = [*enumerate(refs[1:count], 1), (0, fetched_ref)]
+    for i, piece_ref in piece_refs:
+        if i == 0:
+            copy.wait()
         rows = slice(i * cen_dev, (i + 1) * cen_dev)
         for k, part in enumerate(split3(piece_ref[...])):
             parts_ref[k, rows] = part
@@ -350,22 +384,39 @@
 
 
 def finish(
-    image_ref, more_ref, state_ref, solution_ref, residual_ref, direction_ref,
+    image_ref, more_ref, state_ref, solution_hbm, residual_hbm, direction_hbm,
     new_solution_ref, new_residual_ref, new_direction_ref,
+    total_ref, solution_ref, residual_ref, direction_ref, sems,
 ):
     outs, cen_dev = solution_ref.shape
+    copies = fetch(
+        [
+            (solution_hbm, solution_ref),
+            (residual_hbm, residual_ref),
+            (direction_hbm, direction_ref),
+        ],
+        sems,
+    )
     image = image_ref[...] + more_ref[...]
+    total_ref[...] = image
     residual_full = state_ref[outs:]
     norm_old = jnp.sum(residual_full * residual_full, axis=1, keepdims=True)
     curvature = jnp.sum(state_ref[:outs] * image, axis=1, keepdims=True)
     step_length = norm_old / curvature
     next_full = residual_full - step_length * image
     norm_new = jnp.sum(next_full * next_full, axis=1, keepdims=True)
+    index = lax.axis_index("samp")
+    share = 128 // cen_dev
+    first = pl.multiple_of((index // share) * 128, 128)
+    wide = total_ref[:, pl.ds(first, 128)]
+    own_image = wide[:, :cen_dev]
+    for k in range(1, share):
+        here = lax.rem(index, share) == k
+        own_image = jnp.where(here, wide[:, k * cen_dev : (k + 1) * cen_dev], own_image)
+    for copy in copies:
+        copy.wait()
     direction = direction_ref[...]
     new_solution_ref[...] = solution_ref[...] + step_length * direction
-    first = lax.axis_index("samp") * cen_dev
-    turn = lax.rem(image.shape[1] - first, image.shape[1])
-    own_image = pltpu.roll(image, turn, 1)[:, :cen_dev]
     new_residual = residual_ref[...] - step_length * own_image
     new_residual_ref[...] = new_residual
     new_direction_ref[...] = new_residual + (norm_new / norm_old) * direction
@@ -379,18 +430,8 @@
     outs = direction.shape[0]
     held, others = plan(devices, 4 * cen_dev * centres_all)
 
-    weights_dim = 0.5 * jnp.power(0.75, weight_index.astype(F32))
-    curve = 2.0 * math.pi * math.pi * weights_dim
-    floor = 1.0 - curve / 12.0
-    shift = 0.5 * jnp.sqrt(curve)
-
-    centre_scaled = pl.pallas_call(
-        functools.partial(prepare, (*held, *others), cen_dev),
-        in_specs=[SMEM, SMEM],
-        out_shape=jax.ShapeDtypeStruct((generator.shape[0], centres_all), F32),
-        name="prepare",
-    )(generator, shift)
-    constants = (centre_scaled, shift, floor)
+    order = ((*held, *others), cen_dev)
+    lattice = (generator, weight_index, samples)
 
     half = samples_dev // 2
     use_store = 4 * half * centres_all <= STORE_BYTES
@@ -401,7 +442,7 @@
         rows = min(rows, half - filled) if use_store else 0
         if rows == 0:
             return passed
-        made, handed = kernel_rows(passed, samples, filled, rows, constants)
+        made, handed = kernel_rows(passed, filled, rows, order, centres_all, lattice)
         store.append(made)
         filled += rows
         return handed
@@ -439,6 +480,11 @@
                 jax.ShapeDtypeStruct((outs, rows), F32),
                 jax.ShapeDtypeStruct((3, rows, centres_all), BF16),
             ],
+            in_specs=[VMEM, HBM, *[VMEM] * (len(group) - 1)],
+            scratch_shapes=[
+                pltpu.VMEM((cen_dev, centres_all), F32),
+                pltpu.SemaphoreType.DMA((1,)),
+            ],
             compiler_params=pltpu.CompilerParams(
                 vmem_limit_bytes=(4 << 20) + 24 * rows * centres_all
             ),
@@ -458,7 +504,7 @@
     coefficients = fill(half, coefficients)
 
     kept, sent, kernel_products = apply_products(
-        store, samples, coefficients, cen_dev, 256, constants
+        store, coefficients, cen_dev, 256, order, lattice
     )
     for bit in reversed(others):
         came = swap(sent, bit, devices)
@@ -483,7 +529,13 @@
     own = jax.ShapeDtypeStruct(solution.shape, F32)
     return pl.pallas_call(
         finish,
+        in_specs=[VMEM, VMEM, VMEM, HBM, HBM, HBM],
         out_shape=[own, own, own],
+        scratch_shapes=[
+            pltpu.VMEM((outs, centres_all), F32),
+            *[pltpu.VMEM(solution.shape, F32)] * 3,
+            pltpu.SemaphoreType.DMA((3,)),
+        ],
         name="finish",
     )(image, more, state, solution, residual, direction)
 

time: 88.7 us -> 87.8 us (0.990)
  other arithmetic: 2.11 us -> 0.92 us
    sub x1 -> x0, other arithmetic: 1.18 us -> none  [body(): floor = 1.0 - curve / 12.0]
    pallas_call x7 -> x6, Pallas kernels: 42.7 us -> 41.9 us  [the longest x1 21.2 us: apply_products(): pl.pallas_call(functools.partial(products, outs, block_rows, stored, orde...]
  transfers between devices with their start and end apart: 18 -> 18, of which waited for: 5 -> 7; matrix products, arithmetic and copies ran while one was open for 2% -> 1% of each run, Pallas kernels for 23% -> 22%
where the time goes in v6:
time: 87.8 us; the launch traced here: 87.4 us
  Pallas kernels  44.1 us (50%)
  starting transfers between devices  19.4 us (22%)
  waiting for transfers between devices  13.7 us (16%)
  local copies, waits for them, and re-layouts  8.24 us (9%)
  between operations  1.03 us (1%)
  other arithmetic  0.92 us (1%)
    pallas_call x1, Pallas kernels, apply_products(): pl.pallas_call(functools.partial(products, outs, block_rows, stored, orde...  21.2 us
    ppermute x18, starting transfers between devices, swap(): return lax.ppermute(value, 'samp', [(i, i ^ bit) for i in range(devices)])  19.4 us
    pallas_call x4, Pallas kernels, kernel_rows(): pl.pallas_call(functools.partial(store_rows, first_row, step_rows, order)...  18.3 us
    ppermute x18, waiting for transfers between devices, swap(): return lax.ppermute(value, 'samp', [(i, i ^ bit) for i in range(devices)])  13.7 us
    unnamed x33, local copies, waits for them, and re-layouts  8.23 us
    pallas_call x1, Pallas kernels, body(): pl.pallas_call(finish, in_specs=[VMEM, VMEM, VMEM, HBM, HBM, HBM], out_sh...  2.4 us
  transfers between devices with their start and end apart: 18, of which 7 were waited for; matrix products, arithmetic and copies ran while one was open for 1% of the time, Pallas kernels for 22%

profile of v6, /device:TPU:0, one launch (start us, length us, event | category | flops | bytes accessed | tf_op | source)
XLA Modules:
  0.0 87.4 jit_solution(10893640355568041240)
XLA Ops:
  0.6 3.1 %collective-permute-start.5 = (f32[64,1024]{1,0:T(8,128)}, f32[64,1024]{1,0:T(8,128)S(1)}, u32[]{:S(2)}, u32[]{:S(2)}) collective-permute-start(f32[64,1024]{1,0:T(8,128)} %refs_0_.1), channel_id=1, source_target_pairs={{0,4},{1,5},{2,6},{3,7},{4,0},{5,1},{6,2},{7,3},{8,12},{9,13},{10,... | collective-permute-start | bytes 786440 | tf_op jit(solution)/shard_map/ppermute | solution.py:25
  3.7 0.0 collective-permute-start.1
  3.7 0.5 collective-permute-start
  4.2 0.9 collective-permute-done.1
  5.1 0.2 collective-permute-done
  5.3 0.9 maximum_select_fusion.3.passed_ref
  6.1 1.5 %collective-permute-start.2 = (f32[32,128]{1,0:T(8,128)S(1)}, f32[32,128]{1,0:T(8,128)S(1)}, u32[]{:S(2)}, u32[]{:S(2)}) collective-permute-start(f32[32,128]{1,0:T(8,128)S(1)} %maximum_select_fusion.3.passed_ref), channel_id=1, source_target_pairs={{0,2},{1,3},{2,0},{3,1},{4,6},{5,7},{6,4},{7,5},{8,10},{9,11},{10,... | collective-permute-start | bytes 49160 | tf_op jit(solution)/shard_map/ppermute | solution.py:25
  7.7 0.5 collective-permute-start.6
  8.2 0.9 %copy-done.1 = s32[16,2048]{1,0:T(8,128)S(1)} copy-done((s32[16,2048]{1,0:T(8,128)S(1)}, s32[16,2048]{1,0:T(8,128)}, u32[]{:S(2)}) %copy-start.1) | copy-done | bytes 131096
  9.1 0.7 copy-done.6
  9.7 0.7 copy-done.10
  10.4 2.7 %kernel_rows.4 = (bf16[128,1024]{1,0:T(8,128)(2,1)S(1)}, bf16[128,1024]{1,0:T(8,128)(2,1)S(1)}, f32[32,128]{1,0:T(8,128)S(1)}) custom-call(s32[16]{0:T(128)S(1)} %copy-done.6, s32[16]{0:T(128)S(1)} %copy-done.10, s32[16,2048]{1,0:T(8,128)S(1)} %copy-done.1, f32[32,128]{1,0:T(8,128)S(1)} %maximum_select_fusion.3.passed_ref), custom_call_target="tpu_custom_call" | custom-call | flops 12582912 | bytes 524288 | tf_op jit(solution)/shard_map/kernel_rows/pallas_call | solution.py:201
  13.1 0.0 collective-permute-done.5.refs_1_
  13.1 1.6 %collective-permute-start.7 = (f32[64,1024]{1,0:T(8,128)S(1)}, f32[64,1024]{1,0:T(8,128)S(1)}, u32[]{:S(2)}, u32[]{:S(2)}) collective-permute-start(f32[64,1024]{1,0:T(8,128)S(1)} %collective-permute-done.5.refs_1_), channel_id=1, source_target_pairs={{0,2},{1,3},{2,0},{3,1},{4,6},{5,7},{6,4},{7,5},{8,10},{9,11},{10,... | collective-permute-start | bytes 786440 | tf_op jit(solution)/shard_map/ppermute | solution.py:25
  14.7 0.0 collective-permute-done.2
  14.7 0.5 collective-permute-start.3
  15.2 0.9 %copy-done.2 = s32[16,2048]{1,0:T(8,128)S(1)} copy-done((s32[16,2048]{1,0:T(8,128)S(1)}, s32[16,2048]{1,0:T(8,128)}, u32[]{:S(2)}) %copy-start.2) | copy-done | bytes 131096
  16.1 0.7 copy-done.7
  16.8 0.7 copy-done.11
  17.4 2.7 %kernel_rows.5 = (bf16[128,1024]{1,0:T(8,128)(2,1)S(1)}, bf16[128,1024]{1,0:T(8,128)(2,1)S(1)}, f32[32,256]{1,0:T(8,128)S(1)}) custom-call(s32[16]{0:T(128)S(1)} %copy-done.7, s32[16]{0:T(128)S(1)} %copy-done.11, s32[16,2048]{1,0:T(8,128)S(1)} %copy-done.2, f32[32,256]{1,0:T(8,128)S(1)} %maximum_select_fusion.2.passed_ref), custom_call_target="tpu_custom_call" | custom-call | flops 12582912 | bytes 524288 | tf_op jit(solution)/shard_map/kernel_rows/pallas_call | solution.py:201
  20.1 0.0 collective-permute-done.3
  20.2 2.7 %collective-permute-start.4 = (f32[32,512]{1,0:T(8,128)S(1)}, f32[32,512]{1,0:T(8,128)S(1)}, u32[]{:S(2)}, u32[]{:S(2)}) collective-permute-start(f32[32,512]{1,0:T(8,128)S(1)} %maximum_select_fusion.1.passed_ref), channel_id=1, source_target_pairs={{0,8},{1,9},{2,10},{3,11},{4,12},{5,13},{6,14},{7,15},{8,0},{9,1},... | collective-permute-start | bytes 196616 | tf_op jit(solution)/shard_map/ppermute | solution.py:25
  22.8 0.0 collective-permute-start.8
  22.8 0.5 collective-permute-start.9
  23.3 0.0 collective-permute-done.6.refs_2_
  23.3 0.0 collective-permute-start.10
  23.3 0.0 collective-permute-done.7.refs_3_
  23.3 0.5 collective-permute-start.11
  23.8 0.9 %copy-done.3 = s32[16,2048]{1,0:T(8,128)S(1)} copy-done((s32[16,2048]{1,0:T(8,128)S(1)}, s32[16,2048]{1,0:T(8,128)}, u32[]{:S(2)}) %copy-start.3) | copy-done | bytes 131096
  24.8 0.7 copy-done.8
  25.4 0.7 copy-done.12
  26.1 4.6 %kernel_rows.6 = (bf16[256,1024]{1,0:T(8,128)(2,1)S(1)}, bf16[256,1024]{1,0:T(8,128)(2,1)S(1)}, f32[32,512]{1,0:T(8,128)S(1)}) custom-call(s32[16]{0:T(128)S(1)} %copy-done.8, s32[16]{0:T(128)S(1)} %copy-done.12, s32[16,2048]{1,0:T(8,128)S(1)} %copy-done.3, f32[32,512]{1,0:T(8,128)S(1)} %maximum_select_fusion.1.passed_ref), custom_call_target="tpu_custom_call" | custom-call | flops 25165824 | bytes 1048576 | tf_op jit(solution)/shard_map/kernel_rows/pallas_call | solution.py:201
  30.6 0.0 collective-permute-done.4
  30.7 0.0 copy-start.5
  30.7 0.9 %copy-done.5 = f32[64,1024]{1,0:T(8,128)S(1)} copy-done((f32[64,1024]{1,0:T(8,128)S(1)}, f32[64,1024]{1,0:T(8,128)}, u32[]{:S(2)}) %copy-start.5) | copy-done | bytes 262168
  31.6 0.8 row_products.2
  32.5 0.0 collective-permute-done.8.refs_0_
  32.5 0.0 collective-permute-done.10.refs_2_
  32.5 0.0 collective-permute-done.9.refs_1_
  32.5 0.0 collective-permute-done.11.refs_3_
  32.5 0.8 row_products.3
  33.3 0.6 collective-permute-start.12
  33.9 0.0 copy-done.4
  33.9 8.4 %kernel_rows.7 = (bf16[512,1024]{1,0:T(8,128)(2,1)S(1)}, bf16[512,1024]{1,0:T(8,128)(2,1)S(1)}, f32[16,512]{1,0:T(8,128)S(1)}) custom-call(s32[16]{0:T(128)S(1)} %copy-done.8, s32[16]{0:T(128)S(1)} %copy-done.12, s32[16,2048]{1,0:T(8,128)S(1)} %copy-done.4, f32[16,512]{1,0:T(8,128)S(1)} %constant_dynamic-update-slice_fusion.passed_ref), custom_call_target="tpu_custom_call" | custom-call | flops 50331648 | bytes 2097152 | tf_op jit(solution)/shard_map/kernel_rows/pallas_call | solution.py:201
  42.3 0.0 collective-permute-done.12
  42.3 0.0 copy-done.9
  42.3 0.0 copy-done.13
  42.3 21.2 %products.1 = (f32[16,512]{1,0:T(8,128)S(1)}, f32[16,512]{1,0:T(8,128)S(1)}, f32[16,64]{1,0:T(8,128)S(1)}) custom-call(f32[16,1024]{1,0:T(8,128)S(1)} %pad_maximum_fusion.coef_ref, s32[16]{0:T(128)S(1)} %copy-done.9, s32[16]{0:T(128)S(1)} %copy-done.13, s32[16,2048]{1,0:T(8,128)S(1)} %copy-done.4, bf16[128,1024]{1,0:T(8,128)(2,1)S(1)} %get-tuple-element.28.refs_0_, ...), custom_call_target="tpu_custom_call" | custom-call | flops 100663296 | bytes 4194304 | tf_op jit(solution)/shard_map/products/pallas_call | solution.py:314
  63.5 0.0 copy-done
  63.5 2.5 %collective-permute-start.13 = (f32[16,512]{1,0:T(8,128)S(1)}, f32[16,512]{1,0:T(8,128)S(1)}, u32[]{:S(2)}, u32[]{:S(2)}) collective-permute-start(f32[16,512]{1,0:T(8,128)S(1)} %get-tuple-element.37), channel_id=1, source_target_pairs={{0,8},{1,9},{2,10},{3,11},{4,12},{5,13},{6,14},{7,15},{8,0},{9,1},... | collective-permute-start | bytes 98312 | tf_op jit(solution)/shard_map/ppermute | solution.py:25
  66.0 2.4 %collective-permute-done.13.came_ref = f32[16,512]{1,0:T(8,128)S(1)} collective-permute-done((f32[16,512]{1,0:T(8,128)S(1)}, f32[16,512]{1,0:T(8,128)S(1)}, u32[]{:S(2)}, u32[]{:S(2)}) %collective-permute-start.13) | collective-permute-done | bytes 32800 | tf_op jit(solution)/shard_map/ppermute | solution.py:25
  68.4 0.6 image_rows.1
  69.0 0.0 collective-permute-start.14
  69.0 1.3 %collective-permute-done.14 = f32[16,1024]{1,0:T(8,128)S(1)} collective-permute-done((f32[16,1024]{1,0:T(8,128)S(1)}, f32[16,1024]{1,0:T(8,128)S(1)}, u32[]{:S(2)}, u32[]{:S(2)}) %collective-permute-start.14) | collective-permute-done | bytes 65568 | tf_op jit(solution)/shard_map/ppermute | solution.py:25
  70.3 1.0 %collective-permute-start.15 = (f32[16,1024]{1,0:T(8,128)S(1)}, f32[16,1024]{1,0:T(8,128)S(1)}, u32[]{:S(2)}, u32[]{:S(2)}) collective-permute-start(f32[16,1024]{1,0:T(8,128)S(1)} %add.9), channel_id=1, source_target_pairs={{0,2},{1,3},{2,0},{3,1},{4,6},{5,7},{6,4},{7,5},{8,10},{9,11},{10,... | collective-permute-start | bytes 196616 | tf_op jit(solution)/shard_map/ppermute | solution.py:25
  71.3 3.4 %collective-permute-done.15 = f32[16,1024]{1,0:T(8,128)S(1)} collective-permute-done((f32[16,1024]{1,0:T(8,128)S(1)}, f32[16,1024]{1,0:T(8,128)S(1)}, u32[]{:S(2)}, u32[]{:S(2)}) %collective-permute-start.15) | collective-permute-done | bytes 65568 | tf_op jit(solution)/shard_map/ppermute | solution.py:25
  74.6 1.5 %collective-permute-start.16 = (f32[16,1024]{1,0:T(8,128)S(1)}, f32[16,1024]{1,0:T(8,128)S(1)}, u32[]{:S(2)}, u32[]{:S(2)}) collective-permute-start(f32[16,1024]{1,0:T(8,128)S(1)} %add.10), channel_id=1, source_target_pairs={{0,4},{1,5},{2,6},{3,7},{4,0},{5,1},{6,2},{7,3},{8,12},{9,13},{10,... | collective-permute-start | bytes 196616 | tf_op jit(solution)/shard_map/ppermute | solution.py:25
  76.1 2.9 %collective-permute-done.16 = f32[16,1024]{1,0:T(8,128)S(1)} collective-permute-done((f32[16,1024]{1,0:T(8,128)S(1)}, f32[16,1024]{1,0:T(8,128)S(1)}, u32[]{:S(2)}, u32[]{:S(2)}) %collective-permute-start.16) | collective-permute-done | bytes 65568 | tf_op jit(solution)/shard_map/ppermute | solution.py:25
  79.0 0.0 copy-start.14
  79.0 2.5 %collective-permute-start.17 = (f32[16,1024]{1,0:T(8,128)S(1)}, f32[16,1024]{1,0:T(8,128)S(1)}, u32[]{:S(2)}, u32[]{:S(2)}) collective-permute-start(f32[16,1024]{1,0:T(8,128)S(1)} %add.11.image_ref), channel_id=1, source_target_pairs={{0,8},{1,9},{2,10},{3,11},{4,12},{5,13},{6,14},{7,15},{8,0},{9,1},... | collective-permute-start | bytes 196616 | tf_op jit(solution)/shard_map/ppermute | solution.py:25
  81.5 2.7 %collective-permute-done.17.more_ref = f32[16,1024]{1,0:T(8,128)S(1)} collective-permute-done((f32[16,1024]{1,0:T(8,128)S(1)}, f32[16,1024]{1,0:T(8,128)S(1)}, u32[]{:S(2)}, u32[]{:S(2)}) %collective-permute-start.17) | collective-permute-done | bytes 65568 | tf_op jit(solution)/shard_map/ppermute | solution.py:25
  84.2 0.0 copy-done.14
  84.2 0.6 copy-done.15
  84.9 2.4 %finish.1 = (f32[16,64]{1,0:T(8,128)}, f32[16,64]{1,0:T(8,128)}, f32[16,64]{1,0:T(8,128)}) custom-call(f32[16,1024]{1,0:T(8,128)} %copy-done.14, f32[16,1024]{1,0:T(8,128)} %copy-done.15, f32[32,1024]{1,0:T(8,128)} %copy-done, f32[16,64]{1,0:T(8,128)} %solution_hbm.1, f32[16,64]{1,0:T(8,128)} %residual_hbm.1, f32[16,64]{1,0:T(8,128)} %direction_hbm.1), custom_call_target="tpu_custom_call" | custom-call | tf_op jit(solution)/shard_map/finish/pallas_call | solution.py:530
  (23 shorter events, 0.1 us)
Async XLA Ops:
  0.6 12.5 %collective-permute-start.5 = (f32[64,1024]{1,0:T(8,128)}, f32[64,1024]{1,0:T(8,128)S(1)}, u32[]{:S(2)}, u32[]{:S(2)}) collective-permute-start(f32[64,1024]{1,0:T(8,128)} %refs_0_.1), channel_id=1, source_target_pairs={{0,4},{1,5},{2,6},{3,7},{4,0},{5,1},{6,2},{7,3},{8,12},{9,13},{10,... | collective-permute-start | bytes 786440 | tf_op jit(solution)/shard_map/ppermute | solution.py:25
  3.7 1.4 %collective-permute-start.1 = (f32[16,64]{1,0:T(8,128)}, f32[16,64]{1,0:T(8,128)S(1)}, u32[]{:S(2)}, u32[]{:S(2)}) collective-permute-start(f32[16,64]{1,0:T(8,128)} %residual_hbm.1), channel_id=1, source_target_pairs={{0,1},{1,0},{2,3},{3,2},{4,5},{5,4},{6,7},{7,6},{8,9},{9,8},{10,11... | collective-permute-start | bytes 12296 | tf_op jit(solution)/shard_map/ppermute | solution.py:25
  3.7 1.5 %collective-permute-start = (f32[16,64]{1,0:T(8,128)}, f32[16,64]{1,0:T(8,128)S(1)}, u32[]{:S(2)}, u32[]{:S(2)}) collective-permute-start(f32[16,64]{1,0:T(8,128)} %direction_hbm.1), channel_id=1, source_target_pairs={{0,1},{1,0},{2,3},{3,2},{4,5},{5,4},{6,7},{7,6},{8,9},{9,8},{10,11... | collective-permute-start | bytes 12296 | tf_op jit(solution)/shard_map/ppermute | solution.py:25
  6.1 8.6 %collective-permute-start.2 = (f32[32,128]{1,0:T(8,128)S(1)}, f32[32,128]{1,0:T(8,128)S(1)}, u32[]{:S(2)}, u32[]{:S(2)}) collective-permute-start(f32[32,128]{1,0:T(8,128)S(1)} %maximum_select_fusion.3.passed_ref), channel_id=1, source_target_pairs={{0,2},{1,3},{2,0},{3,1},{4,6},{5,7},{6,4},{7,5},{8,10},{9,11},{10,... | collective-permute-start | bytes 49160 | tf_op jit(solution)/shard_map/ppermute | solution.py:25
  7.7 15.7 %collective-permute-start.6 = (f32[64,1024]{1,0:T(8,128)}, f32[64,1024]{1,0:T(8,128)S(1)}, u32[]{:S(2)}, u32[]{:S(2)}) collective-permute-start(f32[64,1024]{1,0:T(8,128)} %refs_0_.1), channel_id=1, source_target_pairs={{0,2},{1,3},{2,0},{3,1},{4,6},{5,7},{6,4},{7,5},{8,10},{9,11},{10,... | collective-permute-start | bytes 786440 | tf_op jit(solution)/shard_map/ppermute | solution.py:25
  8.2 0.9 %copy-start.1 = (s32[16,2048]{1,0:T(8,128)S(1)}, s32[16,2048]{1,0:T(8,128)}, u32[]{:S(2)}) copy-start(s32[16,2048]{1,0:T(8,128)} %samples_hbm.9) | copy-start | bytes 393220
  9.1 0.7 copy-start.6
  9.7 0.7 copy-start.10
  13.1 10.2 %collective-permute-start.7 = (f32[64,1024]{1,0:T(8,128)S(1)}, f32[64,1024]{1,0:T(8,128)S(1)}, u32[]{:S(2)}, u32[]{:S(2)}) collective-permute-start(f32[64,1024]{1,0:T(8,128)S(1)} %collective-permute-done.5.refs_1_), channel_id=1, source_target_pairs={{0,2},{1,3},{2,0},{3,1},{4,6},{5,7},{6,4},{7,5},{8,10},{9,11},{10,... | collective-permute-start | bytes 786440 | tf_op jit(solution)/shard_map/ppermute | solution.py:25
  14.7 5.4 %collective-permute-start.3 = (f32[32,256]{1,0:T(8,128)S(1)}, f32[32,256]{1,0:T(8,128)S(1)}, u32[]{:S(2)}, u32[]{:S(2)}) collective-permute-start(f32[32,256]{1,0:T(8,128)S(1)} %maximum_select_fusion.2.passed_ref), channel_id=1, source_target_pairs={{0,4},{1,5},{2,6},{3,7},{4,0},{5,1},{6,2},{7,3},{8,12},{9,13},{10,... | collective-permute-start | bytes 98312 | tf_op jit(solution)/shard_map/ppermute | solution.py:25
  15.2 0.9 %copy-start.2 = (s32[16,2048]{1,0:T(8,128)S(1)}, s32[16,2048]{1,0:T(8,128)}, u32[]{:S(2)}) copy-start(s32[16,2048]{1,0:T(8,128)} %samples_hbm.9) | copy-start | bytes 393220
  16.1 0.7 copy-start.7
  16.8 0.7 copy-start.11
  17.4 16.5 %copy-start.4 = (s32[16,2048]{1,0:T(8,128)S(1)}, s32[16,2048]{1,0:T(8,128)}, u32[]{:S(2)}) copy-start(s32[16,2048]{1,0:T(8,128)} %samples_hbm.9) | copy-start | bytes 393220
  20.2 10.5 %collective-permute-start.4 = (f32[32,512]{1,0:T(8,128)S(1)}, f32[32,512]{1,0:T(8,128)S(1)}, u32[]{:S(2)}, u32[]{:S(2)}) collective-permute-start(f32[32,512]{1,0:T(8,128)S(1)} %maximum_select_fusion.1.passed_ref), channel_id=1, source_target_pairs={{0,8},{1,9},{2,10},{3,11},{4,12},{5,13},{6,14},{7,15},{8,0},{9,1},... | collective-permute-start | bytes 196616 | tf_op jit(solution)/shard_map/ppermute | solution.py:25
  22.8 9.6 %collective-permute-start.8 = (f32[64,1024]{1,0:T(8,128)}, f32[64,1024]{1,0:T(8,128)S(1)}, u32[]{:S(2)}, u32[]{:S(2)}) collective-permute-start(f32[64,1024]{1,0:T(8,128)} %refs_0_.1), channel_id=1, source_target_pairs={{0,1},{1,0},{2,3},{3,2},{4,5},{5,4},{6,7},{7,6},{8,9},{9,8},{10,11... | collective-permute-start | bytes 786440 | tf_op jit(solution)/shard_map/ppermute | solution.py:25
  22.8 9.7 %collective-permute-start.9 = (f32[64,1024]{1,0:T(8,128)S(1)}, f32[64,1024]{1,0:T(8,128)S(1)}, u32[]{:S(2)}, u32[]{:S(2)}) collective-permute-start(f32[64,1024]{1,0:T(8,128)S(1)} %collective-permute-done.5.refs_1_), channel_id=1, source_target_pairs={{0,1},{1,0},{2,3},{3,2},{4,5},{5,4},{6,7},{7,6},{8,9},{9,8},{10,11... | collective-permute-start | bytes 786440 | tf_op jit(solution)/shard_map/ppermute | solution.py:25
  23.3 9.1 %collective-permute-start.10 = (f32[64,1024]{1,0:T(8,128)S(1)}, f32[64,1024]{1,0:T(8,128)S(1)}, u32[]{:S(2)}, u32[]{:S(2)}) collective-permute-start(f32[64,1024]{1,0:T(8,128)S(1)} %collective-permute-done.6.refs_2_), channel_id=1, source_target_pairs={{0,1},{1,0},{2,3},{3,2},{4,5},{5,4},{6,7},{7,6},{8,9},{9,8},{10,11... | collective-permute-start | bytes 786440 | tf_op jit(solution)/shard_map/ppermute | solution.py:25
  23.3 9.1 %collective-permute-start.11 = (f32[64,1024]{1,0:T(8,128)S(1)}, f32[64,1024]{1,0:T(8,128)S(1)}, u32[]{:S(2)}, u32[]{:S(2)}) collective-permute-start(f32[64,1024]{1,0:T(8,128)S(1)} %collective-permute-done.7.refs_3_), channel_id=1, source_target_pairs={{0,1},{1,0},{2,3},{3,2},{4,5},{5,4},{6,7},{7,6},{8,9},{9,8},{10,11... | collective-permute-start | bytes 786440 | tf_op jit(solution)/shard_map/ppermute | solution.py:25
  23.8 0.9 %copy-start.3 = (s32[16,2048]{1,0:T(8,128)S(1)}, s32[16,2048]{1,0:T(8,128)}, u32[]{:S(2)}) copy-start(s32[16,2048]{1,0:T(8,128)} %samples_hbm.9) | copy-start | bytes 393220
  24.8 0.7 copy-start.8
  25.4 0.7 copy-start.12
  26.1 16.2 %copy-start.9 = (s32[16]{0:T(128)S(1)}, s32[16]{0:T(128)}, u32[]{:S(2)}) copy-start(s32[16]{0:T(128)} %generator_hbm.9) | copy-start | bytes 196
  26.1 16.2 %copy-start.13 = (s32[16]{0:T(128)S(1)}, s32[16]{0:T(128)}, u32[]{:S(2)}) copy-start(s32[16]{0:T(128)} %weight_hbm.9) | copy-start | bytes 196
  30.7 1.0 %copy-start.5 = (f32[64,1024]{1,0:T(8,128)S(1)}, f32[64,1024]{1,0:T(8,128)}, u32[]{:S(2)}) copy-start(f32[64,1024]{1,0:T(8,128)} %refs_0_.1) | copy-start | bytes 786436
  31.6 31.9 %copy-start = (f32[32,1024]{1,0:T(8,128)}, f32[32,1024]{1,0:T(8,128)S(1)}, u32[]{:S(2)}) copy-start(f32[32,1024]{1,0:T(8,128)S(1)} %maximum_select_fusion.state_ref) | copy-start | bytes 393220
  33.3 8.9 %collective-permute-start.12 = (f32[16,512]{1,0:T(8,128)S(1)}, f32[16,512]{1,0:T(8,128)S(1)}, u32[]{:S(2)}, u32[]{:S(2)}) collective-permute-start(f32[16,512]{1,0:T(8,128)S(1)} %constant_dynamic-update-slice_fusion.passed_ref), channel_id=1, source_target_pairs={{0,8},{1,9},{2,10},{3,11},{4,12},{5,13},{6,14},{7,15},{8,0},{9,1},... | collective-permute-start | bytes 98312 | tf_op jit(solution)/shard_map/ppermute | solution.py:25
  63.5 4.9 %collective-permute-start.13 = (f32[16,512]{1,0:T(8,128)S(1)}, f32[16,512]{1,0:T(8,128)S(1)}, u32[]{:S(2)}, u32[]{:S(2)}) collective-permute-start(f32[16,512]{1,0:T(8,128)S(1)} %get-tuple-element.37), channel_id=1, source_target_pairs={{0,8},{1,9},{2,10},{3,11},{4,12},{5,13},{6,14},{7,15},{8,0},{9,1},... | collective-permute-start | bytes 98312 | tf_op jit(solution)/shard_map/ppermute | solution.py:25
  69.0 1.3 %collective-permute-start.14 = (f32[16,1024]{1,0:T(8,128)S(1)}, f32[16,1024]{1,0:T(8,128)S(1)}, u32[]{:S(2)}, u32[]{:S(2)}) collective-permute-start(f32[16,1024]{1,0:T(8,128)S(1)} %image_rows.1), channel_id=1, source_target_pairs={{0,1},{1,0},{2,3},{3,2},{4,5},{5,4},{6,7},{7,6},{8,9},{9,8},{10,11... | collective-permute-start | bytes 196616 | tf_op jit(solution)/shard_map/ppermute | solution.py:25
  70.3 4.3 %collective-permute-start.15 = (f32[16,1024]{1,0:T(8,128)S(1)}, f32[16,1024]{1,0:T(8,128)S(1)}, u32[]{:S(2)}, u32[]{:S(2)}) collective-permute-start(f32[16,1024]{1,0:T(8,128)S(1)} %add.9), channel_id=1, source_target_pairs={{0,2},{1,3},{2,0},{3,1},{4,6},{5,7},{6,4},{7,5},{8,10},{9,11},{10,... | collective-permute-start | bytes 196616 | tf_op jit(solution)/shard_map/ppermute | solution.py:25
  74.6 4.3 %collective-permute-start.16 = (f32[16,1024]{1,0:T(8,128)S(1)}, f32[16,1024]{1,0:T(8,128)S(1)}, u32[]{:S(2)}, u32[]{:S(2)}) collective-permute-start(f32[16,1024]{1,0:T(8,128)S(1)} %add.10), channel_id=1, source_target_pairs={{0,4},{1,5},{2,6},{3,7},{4,0},{5,1},{6,2},{7,3},{8,12},{9,13},{10,... | collective-permute-start | bytes 196616 | tf_op jit(solution)/shard_map/ppermute | solution.py:25
  79.0 5.2 %copy-start.14 = (f32[16,1024]{1,0:T(8,128)}, f32[16,1024]{1,0:T(8,128)S(1)}, u32[]{:S(2)}) copy-start(f32[16,1024]{1,0:T(8,128)S(1)} %add.11.image_ref) | copy-start | bytes 196612
  79.0 5.2 %collective-permute-start.17 = (f32[16,1024]{1,0:T(8,128)S(1)}, f32[16,1024]{1,0:T(8,128)S(1)}, u32[]{:S(2)}, u32[]{:S(2)}) collective-permute-start(f32[16,1024]{1,0:T(8,128)S(1)} %add.11.image_ref), channel_id=1, source_target_pairs={{0,8},{1,9},{2,10},{3,11},{4,12},{5,13},{6,14},{7,15},{8,0},{9,1},... | collective-permute-start | bytes 196616 | tf_op jit(solution)/shard_map/ppermute | solution.py:25
  84.2 0.6 copy-start.15

commit v7 on v6

--- a/solution.py
+++ b/solution.py
@@ -192,6 +192,10 @@
         pltpu.VMEM((dims, rows), jnp.int32),
         pltpu.VMEM((dims, centres_all), F32),
     ]
+
+
+def in_hbm(*values):
+    return [pltpu.with_memory_space_constraint(value, pltpu.HBM) for value in values]
 
 
 def kernel_rows(passed, first_row, rows, order, centres_all, lattice):
@@ -217,7 +221,7 @@
             transcendentals=0,
         ),
         name="kernel_rows",
-    )(*lattice, passed)
+    )(*in_hbm(*lattice), passed)
     return (high, low), handed
 
 
@@ -236,12 +240,13 @@
 
 
 def products(
-    outs, block_rows, stored, order, coef_ref, generator_hbm, weight_hbm, samples_hbm, *refs
+    outs, block_rows, stored, order, coef_ref, generator_hbm, weight_hbm, samples_hbm,
+    solution_hbm, residual_hbm, direction_hbm, *refs,
 ):
     stored_hbm, refs = refs[: 2 * len(stored)], refs[2 * len(stored) :]
-    *backward_refs, own_out_ref = refs[:3]
-    generator_ref, weight_ref, shift_ref, floor_ref, sample_ref, centre_ref = refs[3:9]
-    parts_ref, sum_ref, made_high, made_low, high_ref, low_ref, sems = refs[9:]
+    *backward_refs, own_out_ref, own_state_ref = refs[:4]
+    generator_ref, weight_ref, shift_ref, floor_ref, sample_ref, centre_ref = refs[4:10]
+    parts_ref, sum_ref, made_high, made_low, high_ref, low_ref, sems = refs[10:]
     own_rows = own_out_ref.shape[1]
     steps = sample_ref.shape[1] // block_rows
     stored_rows = sum(stored)
@@ -252,6 +257,9 @@
             (generator_hbm, generator_ref),
             (weight_hbm, weight_ref),
             (samples_hbm.at[:, columns], sample_ref),
+            (solution_hbm, own_state_ref.at[pl.ds(0, outs)]),
+            (residual_hbm, own_state_ref.at[pl.ds(outs, outs)]),
+            (direction_hbm, own_state_ref.at[pl.ds(2 * outs, outs)]),
         ],
         sems,
     )
@@ -259,7 +267,7 @@
     for i, rows in enumerate(stored):
         pairs = zip(stored_hbm[2 * i : 2 * i + 2], (high_ref, low_ref))
         place = pl.ds(first, rows)
-        copies += fetch([(src, dst.at[place]) for src, dst in pairs], sems.at[pl.ds(3 + 2 * i, 2)])
+        copies += fetch([(src, dst.at[place]) for src, dst in pairs], sems.at[pl.ds(6 + 2 * i, 2)])
         first += rows
 
     parts_ref[...] = stack3(coef_ref[...])
@@ -304,8 +312,9 @@
         backward_ref[...] = last[:, i * width : (i + 1) * width]
 
 
-def apply_products(store, coefficients, own_rows, block_rows, order, lattice):
+def apply_products(store, coefficients, own_state, block_rows, order, lattice):
     outs, centres_all = coefficients.shape
+    own_rows = own_state[0].shape[1]
     dims, samples_dev = lattice[2].shape
     stored = tuple(high.shape[0] for high, _ in store)
     made = pltpu.VMEM((2, block_rows, centres_all), BF16)
@@ -313,12 +322,13 @@
     rows = samples_dev - sum(stored)
     return pl.pallas_call(
         functools.partial(products, outs, block_rows, stored, order),
-        in_specs=[VMEM, HBM, HBM, HBM, *[FREE] * (2 * len(stored))],
-        out_specs=[VMEM, VMEM, VMEM],
+        in_specs=[VMEM, *[HBM] * 6, *[FREE] * (2 * len(stored))],
+        out_specs=[VMEM, VMEM, VMEM, VMEM],
         out_shape=[
             jax.ShapeDtypeStruct((outs, centres_all // 2), F32),
             jax.ShapeDtypeStruct((outs, centres_all // 2), F32),
             jax.ShapeDtypeStruct((outs, own_rows), F32),
+            jax.ShapeDtypeStruct((3 * outs, own_rows), F32),
         ],
         scratch_shapes=[
             *set_up_scratch(dims, rows, centres_all),
@@ -328,7 +338,7 @@
             made,
             kept,
             kept,
-            pltpu.SemaphoreType.DMA((3 + 2 * len(stored),)),
+            pltpu.SemaphoreType.DMA((6 + 2 * len(stored),)),
         ],
         compiler_params=pltpu.CompilerParams(
             vmem_limit_bytes=(14 << 20) + (16 * block_rows + 4 * sum(stored)) * centres_all
@@ -339,7 +349,7 @@
             transcendentals=0,
         ),
         name="products",
-    )(coefficients, *lattice, *[part for pair in store for part in pair])
+    )(coefficients, *in_hbm(*lattice, *own_state), *[part for pair in store for part in pair])
 
 
 def row_products(outs, count, state_ref, *refs):
@@ -384,19 +394,9 @@
 
 
 def finish(
-    image_ref, more_ref, state_ref, solution_hbm, residual_hbm, direction_hbm,
-    new_solution_ref, new_residual_ref, new_direction_ref,
-    total_ref, solution_ref, residual_ref, direction_ref, sems,
+    image_ref, more_ref, state_ref, own_ref, new_solution_ref, new_residual_ref, new_direction_ref, total_ref
 ):
-    outs, cen_dev = solution_ref.shape
-    copies = fetch(
-        [
-            (solution_hbm, solution_ref),
-            (residual_hbm, residual_ref),
-            (direction_hbm, direction_ref),
-        ],
-        sems,
-    )
+    outs, cen_dev = new_solution_ref.shape
     image = image_ref[...] + more_ref[...]
     total_ref[...] = image
     residual_full = state_ref[outs:]
@@ -406,18 +406,16 @@
     next_full = residual_full - step_length * image
     norm_new = jnp.sum(next_full * next_full, axis=1, keepdims=True)
     index = lax.axis_index("samp")
-    share = 128 // cen_dev
+    share = max(1, 128 // cen_dev)
     first = pl.multiple_of((index // share) * 128, 128)
     wide = total_ref[:, pl.ds(first, 128)]
     own_image = wide[:, :cen_dev]
     for k in range(1, share):
         here = lax.rem(index, share) == k
         own_image = jnp.where(here, wide[:, k * cen_dev : (k + 1) * cen_dev], own_image)
-    for copy in copies:
-        copy.wait()
-    direction = direction_ref[...]
-    new_solution_ref[...] = solution_ref[...] + step_length * direction
-    new_residual = residual_ref[...] - step_length * own_image
+    direction = own_ref[2 * outs :]
+    new_solution_ref[...] = own_ref[:outs] + step_length * direction
+    new_residual = own_ref[outs : 2 * outs] - step_length * own_image
     new_residual_ref[...] = new_residual
     new_direction_ref[...] = new_residual + (norm_new / norm_old) * direction
 
@@ -489,7 +487,7 @@
                 vmem_limit_bytes=(4 << 20) + 24 * rows * centres_all
             ),
             name="row_products",
-        )(state, *group)
+        )(state, *in_hbm(group[0]), *group[1:])
 
     groups = [pieces]
     for bit in held[2:]:
@@ -503,8 +501,8 @@
         coefficients = jnp.concatenate([mine, other], axis=1)
     coefficients = fill(half, coefficients)
 
-    kept, sent, kernel_products = apply_products(
-        store, coefficients, cen_dev, 256, order, lattice
+    kept, sent, kernel_products, own_state = apply_products(
+        store, coefficients, (solution, residual, direction), 256, order, lattice
     )
     for bit in reversed(others):
         came = swap(sent, bit, devices)
@@ -529,15 +527,10 @@
     own = jax.ShapeDtypeStruct(solution.shape, F32)
     return pl.pallas_call(
         finish,
-        in_specs=[VMEM, VMEM, VMEM, HBM, HBM, HBM],
         out_shape=[own, own, own],
-        scratch_shapes=[
-            pltpu.VMEM((outs, centres_all), F32),
-            *[pltpu.VMEM(solution.shape, F32)] * 3,
-            pltpu.SemaphoreType.DMA((3,)),
-        ],
+        scratch_shapes=[pltpu.VMEM((outs, centres_all), F32)],
         name="finish",
-    )(image, more, state, solution, residual, direction)
+    )(image, more, state, own_state)
 
 
 def solution(mesh):

time: 87.8 us -> 87.1 us (level)
  waiting for transfers between devices: 13.7 us -> 22.3 us
  local copies, waits for them, and re-layouts: 8.24 us -> 1.3 us
  starting transfers between devices: 19.4 us -> 15.4 us
  Pallas kernels: 44.1 us -> 45.8 us
    ppermute x18, waiting for transfers between devices: 13.7 us -> 22.3 us  [swap(): return lax.ppermute(value, 'samp', [(i, i ^ bit) for i in range(devices)])]
    unnamed x33 -> x11, local copies, waits for them, and re-layouts: 8.23 us -> 1.29 us
    ppermute x18, starting transfers between devices: 19.4 us -> 15.4 us  [swap(): return lax.ppermute(value, 'samp', [(i, i ^ bit) for i in range(devices)])]
    pallas_call x2, Pallas kernels: 1.61 us -> 3.09 us  [coefficients_of(): pl.pallas_call(functools.partial(row_products, outs, len(group)), out_sha...]
  transfers between devices with their start and end apart: 18 -> 18, of which waited for: 7 -> 9; matrix products, arithmetic and copies ran while one was open for 1% -> 1% of each run, Pallas kernels for 22% -> 24%
where the time goes in v7:
time: 87.1 us; the launch traced here: 86.6 us
  Pallas kernels  45.8 us (53%)
  waiting for transfers between devices  22.3 us (26%)
  starting transfers between devices  15.4 us (18%)
  local copies, waits for them, and re-layouts  1.3 us (1%)
  other arithmetic  0.92 us (1%)
    ppermute x18, waiting for transfers between devices, swap(): return lax.ppermute(value, 'samp', [(i, i ^ bit) for i in range(devices)])  22.3 us
    pallas_call x1, Pallas kernels, apply_products(): pl.pallas_call(functools.partial(products, outs, block_rows, stored, orde...  21.4 us
    pallas_call x4, Pallas kernels, kernel_rows(): pl.pallas_call(functools.partial(store_rows, first_row, step_rows, order)...  19 us
    ppermute x18, starting transfers between devices, swap(): return lax.ppermute(value, 'samp', [(i, i ^ bit) for i in range(devices)])  15.4 us
    pallas_call x2, Pallas kernels, coefficients_of(): pl.pallas_call(functools.partial(row_products, outs, len(group)), out_sha...  3.09 us
    pallas_call x1, Pallas kernels, body(): pl.pallas_call(finish, out_shape=[own, own, own], scratch_shapes=[pltpu.V...  1.77 us
  transfers between devices with their start and end apart: 18, of which 9 were waited for; matrix products, arithmetic and copies ran while one was open for 1% of the time, Pallas kernels for 24%

profile of v7, /device:TPU:0, one launch (start us, length us, event | category | flops | bytes accessed | tf_op | source)
XLA Modules:
  0.0 86.6 jit_solution(14127489418101971037)
XLA Ops:
  0.6 3.1 %collective-permute-start.5 = (f32[64,1024]{1,0:T(8,128)}, f32[64,1024]{1,0:T(8,128)S(1)}, u32[]{:S(2)}, u32[]{:S(2)}) collective-permute-start(f32[64,1024]{1,0:T(8,128)} %refs_0_.1), channel_id=1, source_target_pairs={{0,4},{1,5},{2,6},{3,7},{4,0},{5,1},{6,2},{7,3},{8,12},{9,13},{10,... | collective-permute-start | bytes 786440 | tf_op jit(solution)/shard_map/ppermute | solution.py:25
  3.7 0.0 collective-permute-start.1
  3.7 0.5 collective-permute-start
  4.2 0.9 %collective-permute-done.1 = f32[16,64]{1,0:T(8,128)S(1)} collective-permute-done((f32[16,64]{1,0:T(8,128)}, f32[16,64]{1,0:T(8,128)S(1)}, u32[]{:S(2)}, u32[]{:S(2)}) %collective-permute-start.1) | collective-permute-done | bytes 4128 | tf_op jit(solution)/shard_map/ppermute | solution.py:25
  5.1 0.2 collective-permute-done
  5.3 0.9 maximum_select_fusion.3.passed_ref
  6.1 1.5 %collective-permute-start.2 = (f32[32,128]{1,0:T(8,128)S(1)}, f32[32,128]{1,0:T(8,128)S(1)}, u32[]{:S(2)}, u32[]{:S(2)}) collective-permute-start(f32[32,128]{1,0:T(8,128)S(1)} %maximum_select_fusion.3.passed_ref), channel_id=1, source_target_pairs={{0,2},{1,3},{2,0},{3,1},{4,6},{5,7},{6,4},{7,5},{8,10},{9,11},{10,... | collective-permute-start | bytes 49160 | tf_op jit(solution)/shard_map/ppermute | solution.py:25
  7.7 0.5 collective-permute-start.6
  8.2 3.0 %kernel_rows.4 = (bf16[128,1024]{1,0:T(8,128)(2,1)S(1)}, bf16[128,1024]{1,0:T(8,128)(2,1)S(1)}, f32[32,128]{1,0:T(8,128)S(1)}) custom-call(s32[16]{0:T(128)} %generator_hbm.9, s32[16]{0:T(128)} %weight_hbm.9, s32[16,2048]{1,0:T(8,128)} %samples_hbm.9, f32[32,128]{1,0:T(8,128)S(1)} %maximum_select_fusion.3.passed_ref), custom_call_target="tpu_custom_call" | custom-call | flops 12582912 | bytes 524288 | tf_op jit(solution)/shard_map/kernel_rows/pallas_call | solution.py:205
  11.2 0.0 collective-permute-done.5.refs_1_
  11.2 1.6 %collective-permute-start.7 = (f32[64,1024]{1,0:T(8,128)S(1)}, f32[64,1024]{1,0:T(8,128)S(1)}, u32[]{:S(2)}, u32[]{:S(2)}) collective-permute-start(f32[64,1024]{1,0:T(8,128)S(1)} %collective-permute-done.5.refs_1_), channel_id=1, source_target_pairs={{0,2},{1,3},{2,0},{3,1},{4,6},{5,7},{6,4},{7,5},{8,10},{9,11},{10,... | collective-permute-start | bytes 786440 | tf_op jit(solution)/shard_map/ppermute | solution.py:25
  12.8 0.0 collective-permute-done.2
  12.8 0.8 collective-permute-start.3
  13.6 2.8 %kernel_rows.5 = (bf16[128,1024]{1,0:T(8,128)(2,1)S(1)}, bf16[128,1024]{1,0:T(8,128)(2,1)S(1)}, f32[32,256]{1,0:T(8,128)S(1)}) custom-call(s32[16]{0:T(128)} %generator_hbm.9, s32[16]{0:T(128)} %weight_hbm.9, s32[16,2048]{1,0:T(8,128)} %samples_hbm.9, f32[32,256]{1,0:T(8,128)S(1)} %maximum_select_fusion.2.passed_ref), custom_call_target="tpu_custom_call" | custom-call | flops 12582912 | bytes 524288 | tf_op jit(solution)/shard_map/kernel_rows/pallas_call | solution.py:205
  16.4 0.4 collective-permute-done.3
  16.8 2.7 %collective-permute-start.4 = (f32[32,512]{1,0:T(8,128)S(1)}, f32[32,512]{1,0:T(8,128)S(1)}, u32[]{:S(2)}, u32[]{:S(2)}) collective-permute-start(f32[32,512]{1,0:T(8,128)S(1)} %maximum_select_fusion.1.passed_ref), channel_id=1, source_target_pairs={{0,8},{1,9},{2,10},{3,11},{4,12},{5,13},{6,14},{7,15},{8,0},{9,1},... | collective-permute-start | bytes 196616 | tf_op jit(solution)/shard_map/ppermute | solution.py:25
  19.4 0.0 collective-permute-start.8
  19.4 0.5 collective-permute-start.9
  19.9 0.0 collective-permute-done.6.refs_2_
  19.9 0.0 collective-permute-start.10
  19.9 1.8 %collective-permute-done.7.refs_3_ = f32[64,1024]{1,0:T(8,128)S(1)} collective-permute-done((f32[64,1024]{1,0:T(8,128)S(1)}, f32[64,1024]{1,0:T(8,128)S(1)}, u32[]{:S(2)}, u32[]{:S(2)}) %collective-permute-start.7) | collective-permute-done | bytes 262176 | tf_op jit(solution)/shard_map/ppermute | solution.py:25
  21.8 0.0 collective-permute-start.11
  21.8 4.7 %kernel_rows.6 = (bf16[256,1024]{1,0:T(8,128)(2,1)S(1)}, bf16[256,1024]{1,0:T(8,128)(2,1)S(1)}, f32[32,512]{1,0:T(8,128)S(1)}) custom-call(s32[16]{0:T(128)} %generator_hbm.9, s32[16]{0:T(128)} %weight_hbm.9, s32[16,2048]{1,0:T(8,128)} %samples_hbm.9, f32[32,512]{1,0:T(8,128)S(1)} %maximum_select_fusion.1.passed_ref), custom_call_target="tpu_custom_call" | custom-call | flops 25165824 | bytes 1048576 | tf_op jit(solution)/shard_map/kernel_rows/pallas_call | solution.py:205
  26.5 0.0 collective-permute-done.4
  26.5 0.0 copy-start
  26.5 1.6 %row_products.2 = (f32[16,256]{1,0:T(8,128)S(1)}, bf16[3,256,1024]{2,1,0:T(8,128)(2,1)S(1)}) custom-call(f32[32,1024]{1,0:T(8,128)S(1)} %maximum_select_fusion.state_ref, f32[64,1024]{1,0:T(8,128)} %refs_0_.1, f32[64,1024]{1,0:T(8,128)S(1)} %collective-permute-done.5.refs_1_, f32[64,1024]{1,0:T(8,128)S(1)} %collective-permute-done.6.refs_2_, ...), custom_call_target="tpu_custom_call" | custom-call | tf_op jit(solution)/shard_map/row_products/pallas_call | solution.py:475
  28.1 0.0 collective-permute-done.8.refs_0_
  28.1 0.0 copy-start.3
  28.1 0.0 collective-permute-done.10.refs_2_
  28.1 0.0 collective-permute-done.9.refs_1_
  28.1 0.0 collective-permute-done.11.refs_3_
  28.2 0.7 copy-done.3
  28.8 1.5 %row_products.3 = (f32[16,256]{1,0:T(8,128)S(1)}, bf16[3,256,1024]{2,1,0:T(8,128)(2,1)S(1)}) custom-call(f32[32,1024]{1,0:T(8,128)S(1)} %maximum_select_fusion.state_ref, f32[64,1024]{1,0:T(8,128)} %copy-done.3, f32[64,1024]{1,0:T(8,128)S(1)} %collective-permute-done.9.refs_1_, f32[64,1024]{1,0:T(8,128)S(1)} %collective-permute-done.10.refs_2_, ...), custom_call_target="tpu_custom_call" | custom-call | tf_op jit(solution)/shard_map/row_products/pallas_call | solution.py:475
  30.4 2.7 %collective-permute-start.12 = (f32[16,512]{1,0:T(8,128)S(1)}, f32[16,512]{1,0:T(8,128)S(1)}, u32[]{:S(2)}, u32[]{:S(2)}) collective-permute-start(f32[16,512]{1,0:T(8,128)S(1)} %constant_dynamic-update-slice_fusion.passed_ref), channel_id=1, source_target_pairs={{0,8},{1,9},{2,10},{3,11},{4,12},{5,13},{6,14},{7,15},{8,0},{9,1},... | collective-permute-start | bytes 98312 | tf_op jit(solution)/shard_map/ppermute | solution.py:25
  33.0 8.5 %kernel_rows.7 = (bf16[512,1024]{1,0:T(8,128)(2,1)S(1)}, bf16[512,1024]{1,0:T(8,128)(2,1)S(1)}, f32[16,512]{1,0:T(8,128)S(1)}) custom-call(s32[16]{0:T(128)} %generator_hbm.9, s32[16]{0:T(128)} %weight_hbm.9, s32[16,2048]{1,0:T(8,128)} %samples_hbm.9, f32[16,512]{1,0:T(8,128)S(1)} %constant_dynamic-update-slice_fusion.passed_ref), custom_call_target="tpu_custom_call" | custom-call | flops 50331648 | bytes 2097152 | tf_op jit(solution)/shard_map/kernel_rows/pallas_call | solution.py:205
  41.5 0.0 collective-permute-done.12
  41.5 21.4 %products.1 = (f32[16,512]{1,0:T(8,128)S(1)}, f32[16,512]{1,0:T(8,128)S(1)}, f32[16,64]{1,0:T(8,128)S(1)}, f32[48,64]{1,0:T(8,128)S(1)}) custom-call(f32[16,1024]{1,0:T(8,128)S(1)} %pad_maximum_fusion.coef_ref, s32[16]{0:T(128)} %generator_hbm.9, s32[16]{0:T(128)} %weight_hbm.9, s32[16,2048]{1,0:T(8,128)} %samples_hbm.9, f32[16,64]{1,0:T(8,128)} %solution_hbm.1, ...), custom_call_target="tpu_custom_call" | custom-call | flops 100663296 | bytes 4194304 | tf_op jit(solution)/shard_map/products/pallas_call | solution.py:323
  62.9 0.0 copy-done
  62.9 0.0 copy-start.1
  62.9 0.4 collective-permute-start.13
  63.3 4.7 %collective-permute-done.13.came_ref = f32[16,512]{1,0:T(8,128)S(1)} collective-permute-done((f32[16,512]{1,0:T(8,128)S(1)}, f32[16,512]{1,0:T(8,128)S(1)}, u32[]{:S(2)}, u32[]{:S(2)}) %collective-permute-start.13) | collective-permute-done | bytes 32800 | tf_op jit(solution)/shard_map/ppermute | solution.py:25
  68.1 0.6 image_rows.1
  68.7 0.0 copy-done.1
  68.7 0.0 collective-permute-start.14
  68.7 1.3 %collective-permute-done.14 = f32[16,1024]{1,0:T(8,128)S(1)} collective-permute-done((f32[16,1024]{1,0:T(8,128)S(1)}, f32[16,1024]{1,0:T(8,128)S(1)}, u32[]{:S(2)}, u32[]{:S(2)}) %collective-permute-start.14) | collective-permute-done | bytes 65568 | tf_op jit(solution)/shard_map/ppermute | solution.py:25
  70.0 0.7 collective-permute-start.15
  70.7 3.6 %collective-permute-done.15 = f32[16,1024]{1,0:T(8,128)S(1)} collective-permute-done((f32[16,1024]{1,0:T(8,128)S(1)}, f32[16,1024]{1,0:T(8,128)S(1)}, u32[]{:S(2)}, u32[]{:S(2)}) %collective-permute-start.15) | collective-permute-done | bytes 65568 | tf_op jit(solution)/shard_map/ppermute | solution.py:25
  74.3 0.3 collective-permute-start.16
  74.6 4.1 %collective-permute-done.16 = f32[16,1024]{1,0:T(8,128)S(1)} collective-permute-done((f32[16,1024]{1,0:T(8,128)S(1)}, f32[16,1024]{1,0:T(8,128)S(1)}, u32[]{:S(2)}, u32[]{:S(2)}) %collective-permute-start.16) | collective-permute-done | bytes 65568 | tf_op jit(solution)/shard_map/ppermute | solution.py:25
  78.6 0.0 copy-start.2
  78.7 0.2 collective-permute-start.17
  78.8 5.4 %collective-permute-done.17.more_ref = f32[16,1024]{1,0:T(8,128)S(1)} collective-permute-done((f32[16,1024]{1,0:T(8,128)S(1)}, f32[16,1024]{1,0:T(8,128)S(1)}, u32[]{:S(2)}, u32[]{:S(2)}) %collective-permute-start.17) | collective-permute-done | bytes 65568 | tf_op jit(solution)/shard_map/ppermute | solution.py:25
  84.2 0.0 copy-start.4
  84.2 0.0 copy-done.2
  84.2 0.6 copy-done.4
  84.8 1.8 %finish.1 = (f32[16,64]{1,0:T(8,128)}, f32[16,64]{1,0:T(8,128)}, f32[16,64]{1,0:T(8,128)}) custom-call(f32[16,1024]{1,0:T(8,128)} %copy-done.2, f32[16,1024]{1,0:T(8,128)} %copy-done.4, f32[32,1024]{1,0:T(8,128)} %copy-done, f32[48,64]{1,0:T(8,128)} %copy-done.1), custom_call_target="tpu_custom_call" | custom-call | tf_op jit(solution)/shard_map/finish/pallas_call | solution.py:528
  (9 shorter events, 0.1 us)
Async XLA Ops:
  0.6 10.5 %collective-permute-start.5 = (f32[64,1024]{1,0:T(8,128)}, f32[64,1024]{1,0:T(8,128)S(1)}, u32[]{:S(2)}, u32[]{:S(2)}) collective-permute-start(f32[64,1024]{1,0:T(8,128)} %refs_0_.1), channel_id=1, source_target_pairs={{0,4},{1,5},{2,6},{3,7},{4,0},{5,1},{6,2},{7,3},{8,12},{9,13},{10,... | collective-permute-start | bytes 786440 | tf_op jit(solution)/shard_map/ppermute | solution.py:25
  3.7 1.4 %collective-permute-start.1 = (f32[16,64]{1,0:T(8,128)}, f32[16,64]{1,0:T(8,128)S(1)}, u32[]{:S(2)}, u32[]{:S(2)}) collective-permute-start(f32[16,64]{1,0:T(8,128)} %residual_hbm.1), channel_id=1, source_target_pairs={{0,1},{1,0},{2,3},{3,2},{4,5},{5,4},{6,7},{7,6},{8,9},{9,8},{10,11... | collective-permute-start | bytes 12296 | tf_op jit(solution)/shard_map/ppermute | solution.py:25
  3.7 1.5 %collective-permute-start = (f32[16,64]{1,0:T(8,128)}, f32[16,64]{1,0:T(8,128)S(1)}, u32[]{:S(2)}, u32[]{:S(2)}) collective-permute-start(f32[16,64]{1,0:T(8,128)} %direction_hbm.1), channel_id=1, source_target_pairs={{0,1},{1,0},{2,3},{3,2},{4,5},{5,4},{6,7},{7,6},{8,9},{9,8},{10,11... | collective-permute-start | bytes 12296 | tf_op jit(solution)/shard_map/ppermute | solution.py:25
  6.1 6.6 %collective-permute-start.2 = (f32[32,128]{1,0:T(8,128)S(1)}, f32[32,128]{1,0:T(8,128)S(1)}, u32[]{:S(2)}, u32[]{:S(2)}) collective-permute-start(f32[32,128]{1,0:T(8,128)S(1)} %maximum_select_fusion.3.passed_ref), channel_id=1, source_target_pairs={{0,2},{1,3},{2,0},{3,1},{4,6},{5,7},{6,4},{7,5},{8,10},{9,11},{10,... | collective-permute-start | bytes 49160 | tf_op jit(solution)/shard_map/ppermute | solution.py:25
  7.7 12.3 %collective-permute-start.6 = (f32[64,1024]{1,0:T(8,128)}, f32[64,1024]{1,0:T(8,128)S(1)}, u32[]{:S(2)}, u32[]{:S(2)}) collective-permute-start(f32[64,1024]{1,0:T(8,128)} %refs_0_.1), channel_id=1, source_target_pairs={{0,2},{1,3},{2,0},{3,1},{4,6},{5,7},{6,4},{7,5},{8,10},{9,11},{10,... | collective-permute-start | bytes 786440 | tf_op jit(solution)/shard_map/ppermute | solution.py:25
  11.2 10.6 %collective-permute-start.7 = (f32[64,1024]{1,0:T(8,128)S(1)}, f32[64,1024]{1,0:T(8,128)S(1)}, u32[]{:S(2)}, u32[]{:S(2)}) collective-permute-start(f32[64,1024]{1,0:T(8,128)S(1)} %collective-permute-done.5.refs_1_), channel_id=1, source_target_pairs={{0,2},{1,3},{2,0},{3,1},{4,6},{5,7},{6,4},{7,5},{8,10},{9,11},{10,... | collective-permute-start | bytes 786440 | tf_op jit(solution)/shard_map/ppermute | solution.py:25
  12.8 4.0 %collective-permute-start.3 = (f32[32,256]{1,0:T(8,128)S(1)}, f32[32,256]{1,0:T(8,128)S(1)}, u32[]{:S(2)}, u32[]{:S(2)}) collective-permute-start(f32[32,256]{1,0:T(8,128)S(1)} %maximum_select_fusion.2.passed_ref), channel_id=1, source_target_pairs={{0,4},{1,5},{2,6},{3,7},{4,0},{5,1},{6,2},{7,3},{8,12},{9,13},{10,... | collective-permute-start | bytes 98312 | tf_op jit(solution)/shard_map/ppermute | solution.py:25
  16.8 9.7 %collective-permute-start.4 = (f32[32,512]{1,0:T(8,128)S(1)}, f32[32,512]{1,0:T(8,128)S(1)}, u32[]{:S(2)}, u32[]{:S(2)}) collective-permute-start(f32[32,512]{1,0:T(8,128)S(1)} %maximum_select_fusion.1.passed_ref), channel_id=1, source_target_pairs={{0,8},{1,9},{2,10},{3,11},{4,12},{5,13},{6,14},{7,15},{8,0},{9,1},... | collective-permute-start | bytes 196616 | tf_op jit(solution)/shard_map/ppermute | solution.py:25
  19.4 8.7 %collective-permute-start.8 = (f32[64,1024]{1,0:T(8,128)}, f32[64,1024]{1,0:T(8,128)S(1)}, u32[]{:S(2)}, u32[]{:S(2)}) collective-permute-start(f32[64,1024]{1,0:T(8,128)} %refs_0_.1), channel_id=1, source_target_pairs={{0,1},{1,0},{2,3},{3,2},{4,5},{5,4},{6,7},{7,6},{8,9},{9,8},{10,11... | collective-permute-start | bytes 786440 | tf_op jit(solution)/shard_map/ppermute | solution.py:25
  19.4 8.7 %collective-permute-start.9 = (f32[64,1024]{1,0:T(8,128)S(1)}, f32[64,1024]{1,0:T(8,128)S(1)}, u32[]{:S(2)}, u32[]{:S(2)}) collective-permute-start(f32[64,1024]{1,0:T(8,128)S(1)} %collective-permute-done.5.refs_1_), channel_id=1, source_target_pairs={{0,1},{1,0},{2,3},{3,2},{4,5},{5,4},{6,7},{7,6},{8,9},{9,8},{10,11... | collective-permute-start | bytes 786440 | tf_op jit(solution)/shard_map/ppermute | solution.py:25
  19.9 8.2 %collective-permute-start.10 = (f32[64,1024]{1,0:T(8,128)S(1)}, f32[64,1024]{1,0:T(8,128)S(1)}, u32[]{:S(2)}, u32[]{:S(2)}) collective-permute-start(f32[64,1024]{1,0:T(8,128)S(1)} %collective-permute-done.6.refs_2_), channel_id=1, source_target_pairs={{0,1},{1,0},{2,3},{3,2},{4,5},{5,4},{6,7},{7,6},{8,9},{9,8},{10,11... | collective-permute-start | bytes 786440 | tf_op jit(solution)/shard_map/ppermute | solution.py:25
  21.8 6.4 %collective-permute-start.11 = (f32[64,1024]{1,0:T(8,128)S(1)}, f32[64,1024]{1,0:T(8,128)S(1)}, u32[]{:S(2)}, u32[]{:S(2)}) collective-permute-start(f32[64,1024]{1,0:T(8,128)S(1)} %collective-permute-done.7.refs_3_), channel_id=1, source_target_pairs={{0,1},{1,0},{2,3},{3,2},{4,5},{5,4},{6,7},{7,6},{8,9},{9,8},{10,11... | collective-permute-start | bytes 786440 | tf_op jit(solution)/shard_map/ppermute | solution.py:25
  26.5 36.4 %copy-start = (f32[32,1024]{1,0:T(8,128)}, f32[32,1024]{1,0:T(8,128)S(1)}, u32[]{:S(2)}) copy-start(f32[32,1024]{1,0:T(8,128)S(1)} %maximum_select_fusion.state_ref) | copy-start | bytes 393220
  28.1 0.7 copy-start.3
  30.4 11.1 %collective-permute-start.12 = (f32[16,512]{1,0:T(8,128)S(1)}, f32[16,512]{1,0:T(8,128)S(1)}, u32[]{:S(2)}, u32[]{:S(2)}) collective-permute-start(f32[16,512]{1,0:T(8,128)S(1)} %constant_dynamic-update-slice_fusion.passed_ref), channel_id=1, source_target_pairs={{0,8},{1,9},{2,10},{3,11},{4,12},{5,13},{6,14},{7,15},{8,0},{9,1},... | collective-permute-start | bytes 98312 | tf_op jit(solution)/shard_map/ppermute | solution.py:25
  62.9 5.7 %copy-start.1 = (f32[48,64]{1,0:T(8,128)}, f32[48,64]{1,0:T(8,128)S(1)}, u32[]{:S(2)}) copy-start(f32[48,64]{1,0:T(8,128)S(1)} %get-tuple-element.42.own_ref) | copy-start | bytes 36868
  62.9 5.1 %collective-permute-start.13 = (f32[16,512]{1,0:T(8,128)S(1)}, f32[16,512]{1,0:T(8,128)S(1)}, u32[]{:S(2)}, u32[]{:S(2)}) collective-permute-start(f32[16,512]{1,0:T(8,128)S(1)} %get-tuple-element.38), channel_id=1, source_target_pairs={{0,8},{1,9},{2,10},{3,11},{4,12},{5,13},{6,14},{7,15},{8,0},{9,1},... | collective-permute-start | bytes 98312 | tf_op jit(solution)/shard_map/ppermute | solution.py:25
  68.7 1.3 %collective-permute-start.14 = (f32[16,1024]{1,0:T(8,128)S(1)}, f32[16,1024]{1,0:T(8,128)S(1)}, u32[]{:S(2)}, u32[]{:S(2)}) collective-permute-start(f32[16,1024]{1,0:T(8,128)S(1)} %image_rows.1), channel_id=1, source_target_pairs={{0,1},{1,0},{2,3},{3,2},{4,5},{5,4},{6,7},{7,6},{8,9},{9,8},{10,11... | collective-permute-start | bytes 196616 | tf_op jit(solution)/shard_map/ppermute | solution.py:25
  70.0 4.3 %collective-permute-start.15 = (f32[16,1024]{1,0:T(8,128)S(1)}, f32[16,1024]{1,0:T(8,128)S(1)}, u32[]{:S(2)}, u32[]{:S(2)}) collective-permute-start(f32[16,1024]{1,0:T(8,128)S(1)} %add.9), channel_id=1, source_target_pairs={{0,2},{1,3},{2,0},{3,1},{4,6},{5,7},{6,4},{7,5},{8,10},{9,11},{10,... | collective-permute-start | bytes 196616 | tf_op jit(solution)/shard_map/ppermute | solution.py:25
  74.3 4.3 %collective-permute-start.16 = (f32[16,1024]{1,0:T(8,128)S(1)}, f32[16,1024]{1,0:T(8,128)S(1)}, u32[]{:S(2)}, u32[]{:S(2)}) collective-permute-start(f32[16,1024]{1,0:T(8,128)S(1)} %add.10), channel_id=1, source_target_pairs={{0,4},{1,5},{2,6},{3,7},{4,0},{5,1},{6,2},{7,3},{8,12},{9,13},{10,... | collective-permute-start | bytes 196616 | tf_op jit(solution)/shard_map/ppermute | solution.py:25
  78.6 5.6 %copy-start.2 = (f32[16,1024]{1,0:T(8,128)}, f32[16,1024]{1,0:T(8,128)S(1)}, u32[]{:S(2)}) copy-start(f32[16,1024]{1,0:T(8,128)S(1)} %add.11.image_ref) | copy-start | bytes 196612
  78.7 5.6 %collective-permute-start.17 = (f32[16,1024]{1,0:T(8,128)S(1)}, f32[16,1024]{1,0:T(8,128)S(1)}, u32[]{:S(2)}, u32[]{:S(2)}) collective-permute-start(f32[16,1024]{1,0:T(8,128)S(1)} %add.11.image_ref), channel_id=1, source_target_pairs={{0,8},{1,9},{2,10},{3,11},{4,12},{5,13},{6,14},{7,15},{8,0},{9,1},... | collective-permute-start | bytes 196616 | tf_op jit(solution)/shard_map/ppermute | solution.py:25
  84.2 0.6 copy-start.4

commit v8 on v7

--- a/solution.py
+++ b/solution.py
@@ -9,10 +9,14 @@
 from jax.sharding import PartitionSpec as P
 
 LATTICE = 65521
+MIDDLE = LATTICE // 2
 
 ridge_weight = 0.25
 STORE_BYTES = 12 << 20
 HELD_BYTES = 16 << 20
+WIDTH = 256
+STORED_MIXED = 16
+PRODUCTS_MIXED = 4
 VMEM = pl.BlockSpec(memory_space=pltpu.VMEM)
 FREE = pl.BlockSpec(memory_space=pl.ANY)
 HBM = pl.BlockSpec(memory_space=pltpu.HBM)
@@ -51,29 +55,85 @@
     return value[:outs] + (value[outs : 2 * outs] + value[2 * outs :])
 
 
-def kernel_tile(points, centre_ref, shift_ref, floor_ref, first, width):
+def bilinear_terms(sources, count, columns):
+    place = lax.broadcasted_iota(jnp.int32, (count * 16, columns), 1)
+    row = lax.broadcasted_iota(jnp.int32, (count * 16, columns), 0)
+    term = place & 15
+    source = jnp.full_like(place, -16)
+    for k, which in enumerate(sources):
+        source = jnp.where(term == k, which, source)
+    return jnp.where(row == source * 16 + (place >> 4), 1.0, 0.0).astype(BF16)
+
+
+def point_block(coordinates, constants, mixed, pick_ref, lhs_ref):
+    scale, curve, base = constants
+    centred = coordinates - MIDDLE
+    if mixed:
+        real = centred.astype(F32)
+        unit = real * (1.0 / LATTICE)
+        large = jnp.floor(real * (1.0 / 256.0) + 0.5) * 256.0
+        alone = curve * (unit * unit + unit) + base
+        ones = jnp.ones(real.shape, BF16)
+        sources = [*split3(alone), large.astype(BF16), (real - large).astype(BF16), ones]
+        terms = lax.dot_general(
+            jnp.concatenate(sources, axis=0),
+            pick_ref[...],
+            (((0,), (0,)), ((), ())),
+            preferred_element_type=F32,
+        ).astype(BF16)
+        rows = terms.shape[0]
+        for axis_number in range(mixed):
+            lhs_ref[axis_number, :rows] = terms[:, axis_number * 128 : axis_number * 128 + 16]
+    return (centred.astype(F32) * scale).T
+
+
+def kernel_tile(points, mixed, lhs_ref, rhs_ref, centre_ref, shift_ref, floor_ref, first, width):
     rows, dims = points.shape
     product = None
-    for axis_number in range(dims):
-        centre = centre_ref[axis_number : axis_number + 1, pl.ds(first, width)]
+    columns = pl.ds(first, width)
+    for axis_number in kernel_order(dims, mixed):
+        centre = centre_ref[axis_number : axis_number + 1, columns]
         point = jnp.broadcast_to(points[:, axis_number : axis_number + 1], (rows, width))
-        arm = jnp.abs(point - centre) - shift_ref[axis_number]
-        factor = arm * arm + floor_ref[axis_number]
+        if axis_number < mixed:
+            bilinear = jnp.dot(
+                lhs_ref[axis_number, :rows],
+                rhs_ref[pl.ds(axis_number * 16, 16), columns],
+                preferred_element_type=F32,
+            )
+            factor = bilinear - jnp.maximum(point, centre)
+        else:
+            arm = jnp.abs(point - centre) - shift_ref[axis_number]
+            factor = arm * arm + floor_ref[axis_number]
         product = factor if product is None else product * factor
     return product
 
 
-def fill_kernel(rows, points, centre_ref, shift_ref, floor_ref, high_ref, low_ref):
+def kernel_order(dims, mixed):
+    kinds = [list(range(mixed)), list(range(mixed, dims))]
+    order = []
+    while kinds[0] or kinds[1]:
+        first = len(kinds[0]) * (dims - mixed) >= len(kinds[1]) * mixed
+        order.append(kinds[0 if kinds[0] and (first or not kinds[1]) else 1].pop(0))
+    return order
+
+
+def fill_kernel(rows, points, mixed, tables, high_ref, low_ref, between=()):
+    lhs_ref, rhs_ref, centre_ref, shift_ref, floor_ref = tables
     centres_all = centre_ref.shape[1]
-    width = min(512, centres_all)
+    width = min(WIDTH, centres_all)
     span = min(1024, centres_all)
+    between = list(between)
 
     def part(base):
         for piece in range(span // width):
+            if between:
+                between.pop(0)()
             first = base + piece * width
             if not isinstance(first, int):
                 first = pl.multiple_of(first, width)
-            tile = kernel_tile(points, centre_ref, shift_ref, floor_ref, first, width)
+            tile = kernel_tile(
+                points, mixed, lhs_ref, rhs_ref, centre_ref, shift_ref, floor_ref, first, width
+            )
             high = tile.astype(BF16)
             high_ref[rows, pl.ds(first, width)] = high
             low_ref[rows, pl.ds(first, width)] = (tile - high.astype(F32)).astype(BF16)
@@ -81,7 +141,11 @@
     if centres_all == span:
         part(0)
     else:
+        while between:
+            between.pop(0)()
         lax.fori_loop(0, centres_all // span, lambda i, _: part(i * span), None)
+    while between:
+        between.pop(0)()
 
 
 def fetch(pairs, sems):
@@ -106,7 +170,20 @@
     return column
 
 
-def set_up(order_bits, cen_dev, generator_ref, weight_ref, shift_ref, floor_ref, centre_ref):
+def centre_coordinates(order, generator_ref, dims, count):
+    order_bits, cen_dev = order
+    generator = column_of(generator_ref, dims, jnp.int32)
+    place = lax.broadcasted_iota(jnp.int32, (1, count), 1)
+    owner = jnp.zeros_like(place) + lax.axis_index("samp")
+    for k, bit in enumerate(order_bits):
+        owner = jnp.where((place & (cen_dev << k)) != 0, owner ^ bit, owner)
+    column = owner * cen_dev + (place & (cen_dev - 1))
+    upper = modulo(column * (generator >> 8))
+    return modulo(upper * 256 + column * (generator & 255))
+
+
+def set_up(order, mixed, generator_ref, weight_ref, tables, pick_ref):
+    _, rhs_ref, centre_ref, shift_ref, floor_ref = tables
     dims, centres_all = centre_ref.shape
     curves = [math.pi * math.pi * 0.75**weight for weight in range(8)]
     for axis_number in range(dims):
@@ -117,23 +194,39 @@
             floor = jnp.where(weight == k, F32(1.0 - curves[k] / 12.0), floor)
         shift_ref[axis_number] = shift
         floor_ref[axis_number] = floor
-    scale = column_of(shift_ref, dims, F32) * (2.0 / LATTICE)
-    generator = column_of(generator_ref, dims, jnp.int32)
-    place = lax.broadcasted_iota(jnp.int32, (1, centres_all), 1)
-    owner = jnp.zeros_like(place) + lax.axis_index("samp")
-    for k, bit in enumerate(order_bits):
-        owner = jnp.where((place & (cen_dev << k)) != 0, owner ^ bit, owner)
-    column = owner * cen_dev + (place & (cen_dev - 1))
-    upper = modulo(column * (generator >> 8))
-    centre = modulo(upper * 256 + column * (generator & 255))
-    centre_ref[...] = centre.astype(F32) * scale
-    return scale
+    half_root = column_of(shift_ref, dims, F32)
+    curve = 4.0 * half_root * half_root
+    base = column_of(floor_ref, dims, F32) + 0.25 * curve
+    row = lax.broadcasted_iota(jnp.int32, (dims, 1), 0)
+    scale = jnp.where(row < mixed, 2.0 * curve, 2.0 * half_root) * (1.0 / LATTICE)
+    centre = centre_coordinates(order, generator_ref, dims, centres_all)
+    real = (centre - MIDDLE).astype(F32)
+    centre_ref[...] = real * scale
+    if mixed:
+        unit = real * (1.0 / LATTICE)
+        alone = curve * (unit * unit + unit)
+        slope = (-2.0 / LATTICE) * curve * unit
+        ones = jnp.ones(real.shape, BF16)
+        sources = jnp.concatenate([ones, *split3(alone), *split3(slope)], axis=0)
+        pick = bilinear_terms((0, 0, 0, 1, 2, 3, 4, 5, 6, 4, 5, 6), 7, 16 * dims)
+        rhs_ref[...] = lax.dot_general(
+            pick, sources, (((0,), (0,)), ((), ())), preferred_element_type=F32
+        ).astype(BF16)
+        place = lax.broadcasted_iota(jnp.int32, (6 * 16, 128), 1)
+        row = lax.broadcasted_iota(jnp.int32, (6 * 16, 128), 0)
+        source = jnp.full_like(place, -1000)
+        for k, which in enumerate((0, 1, 2, 5, 5, 5, 3, 3, 3, 4, 4, 4)):
+            source = jnp.where(place == k, which * 16, source)
+        for axis_number in range(mixed):
+            columns = slice(axis_number * 128, (axis_number + 1) * 128)
+            pick_ref[:, columns] = jnp.where(row == source + axis_number, 1.0, 0.0).astype(BF16)
+    return scale, curve, base
 
 
 def store_rows(
-    first_row, step_rows, order, generator_hbm, weight_hbm, samples_hbm, passed_ref,
+    first_row, step_rows, order, mixed, generator_hbm, weight_hbm, samples_hbm, passed_ref,
     high_hbm, low_hbm, handed_ref, generator_ref, weight_ref, shift_ref, floor_ref, sample_ref,
-    centre_ref, high_ref, low_ref, in_sems, out_sems,
+    centre_ref, lhs_ref, rhs_ref, pick_ref, high_ref, low_ref, in_sems, out_sems,
 ):
     rows_all = high_hbm.shape[0]
     copies = fetch(
@@ -147,7 +240,8 @@
     handed_ref[...] = passed_ref[...]
     copies[0].wait()
     copies[1].wait()
-    scale = set_up(*order, generator_ref, weight_ref, shift_ref, floor_ref, centre_ref)
+    tables = (lhs_ref, rhs_ref, centre_ref, shift_ref, floor_ref)
+    constants = set_up(order, mixed, generator_ref, weight_ref, tables, pick_ref)
     copies[2].wait()
 
     def sends(step):
@@ -169,10 +263,9 @@
                 copy.wait()
 
         columns = pl.ds(pl.multiple_of(i * step_rows, step_rows), step_rows)
-        points = (sample_ref[:, columns].astype(F32) * scale).T
-        rows = pl.ds(0, step_rows)
+        points = point_block(sample_ref[:, columns], constants, mixed, pick_ref, lhs_ref)
         fill_kernel(
-            rows, points, centre_ref, shift_ref, floor_ref, high_ref.at[slot], low_ref.at[slot]
+            pl.ds(0, step_rows), points, mixed, tables, high_ref.at[slot], low_ref.at[slot]
         )
         for copy in sends(i):
             copy.start()
@@ -183,7 +276,7 @@
             copy.wait()
 
 
-def set_up_scratch(dims, rows, centres_all):
+def set_up_scratch(dims, rows, centres_all, step_rows, mixed):
     return [
         pltpu.SMEM((dims,), jnp.int32),
         pltpu.SMEM((dims,), jnp.int32),
@@ -191,6 +284,9 @@
         pltpu.SMEM((dims,), F32),
         pltpu.VMEM((dims, rows), jnp.int32),
         pltpu.VMEM((dims, centres_all), F32),
+        pltpu.VMEM((max(1, mixed), step_rows, 16), BF16),
+        pltpu.VMEM((16 * dims, centres_all if mixed else 128), BF16),
+        pltpu.VMEM((6 * 16, 128 * max(1, mixed)), BF16),
     ]
 
 
@@ -201,20 +297,20 @@
 def kernel_rows(passed, first_row, rows, order, centres_all, lattice):
     dims = lattice[2].shape[0]
     kept = jax.ShapeDtypeStruct((rows, centres_all), BF16)
-    step_rows = min(128, rows)
+    step_rows = min(256, rows)
     high, low, handed = pl.pallas_call(
-        functools.partial(store_rows, first_row, step_rows, order),
+        functools.partial(store_rows, first_row, step_rows, order, STORED_MIXED),
         in_specs=[HBM, HBM, HBM, VMEM],
         out_specs=[FREE, FREE, VMEM],
         out_shape=[kept, kept, jax.ShapeDtypeStruct(passed.shape, passed.dtype)],
         scratch_shapes=[
-            *set_up_scratch(dims, rows, centres_all),
+            *set_up_scratch(dims, rows, centres_all, step_rows, STORED_MIXED),
             pltpu.VMEM((2, step_rows, centres_all), BF16),
             pltpu.VMEM((2, step_rows, centres_all), BF16),
             pltpu.SemaphoreType.DMA((3,)),
             pltpu.SemaphoreType.DMA((2, 2)),
         ],
-        compiler_params=pltpu.CompilerParams(vmem_limit_bytes=12 << 20),
+        compiler_params=pltpu.CompilerParams(vmem_limit_bytes=16 << 20),
         cost_estimate=pl.CostEstimate(
             flops=6 * dims * rows * centres_all,
             bytes_accessed=4 * rows * centres_all,
@@ -232,11 +328,18 @@
     return add_parts(fitted, outs)
 
 
-def back_products(high, low, coefficients, outs):
-    parts = stack3(apply_kernel(high, low, coefficients, outs))
-    return jnp.dot(parts, high, preferred_element_type=F32) + jnp.dot(
-        parts, low, preferred_element_type=F32
-    )
+def back_products(high_ref, low_ref, coef_ref, outs):
+    result = {}
+
+    def there():
+        result["parts"] = stack3(apply_kernel(high_ref[...], low_ref[...], coef_ref[...], outs))
+
+    def back():
+        parts = result["parts"]
+        total = jnp.dot(parts, high_ref[...], preferred_element_type=F32)
+        result["sum"] = total + jnp.dot(parts, low_ref[...], preferred_element_type=F32)
+
+    return there, back, result
 
 
 def products(
@@ -245,8 +348,11 @@
 ):
     stored_hbm, refs = refs[: 2 * len(stored)], refs[2 * len(stored) :]
     *backward_refs, own_out_ref, own_state_ref = refs[:4]
-    generator_ref, weight_ref, shift_ref, floor_ref, sample_ref, centre_ref = refs[4:10]
-    parts_ref, sum_ref, made_high, made_low, high_ref, low_ref, sems = refs[10:]
+    generator_ref, weight_ref, shift_ref, floor_ref, sample_ref = refs[4:9]
+    centre_ref, lhs_ref, rhs_ref, pick_ref = refs[9:13]
+    parts_ref, sum_ref, *made, high_ref, low_ref, sems = refs[13:]
+    mixed = PRODUCTS_MIXED
+    tables = (lhs_ref, rhs_ref, centre_ref, shift_ref, floor_ref)
     own_rows = own_out_ref.shape[1]
     steps = sample_ref.shape[1] // block_rows
     stored_rows = sum(stored)
@@ -272,40 +378,42 @@
 
     parts_ref[...] = stack3(coef_ref[...])
     sum_ref[...] = jnp.zeros_like(sum_ref)
-    made_high[1] = jnp.zeros(made_high.shape[1:], BF16)
-    made_low[1] = jnp.zeros(made_low.shape[1:], BF16)
+    last_high, last_low = made[2:]
+    last_high[...] = jnp.zeros_like(last_high)
+    last_low[...] = jnp.zeros_like(last_low)
     copies[0].wait()
     copies[1].wait()
-    scale = set_up(*order, generator_ref, weight_ref, shift_ref, floor_ref, centre_ref)
-    own_high, own_low = made_high.at[0], made_low.at[0]
+    constants = set_up(order, mixed, generator_ref, weight_ref, tables, pick_ref)
+    own_high, own_low = made[:2]
     rows = pl.ds(0, own_rows)
-    own_points = centre_ref[:, :own_rows]
-    fill_kernel(rows, own_points.T, centre_ref, shift_ref, floor_ref, own_high, own_low)
+    own_points = centre_coordinates(order, generator_ref, centre_ref.shape[0], own_rows)
+    own_points = point_block(own_points, constants, mixed, pick_ref, lhs_ref)
+    fill_kernel(rows, own_points, mixed, tables, own_high, own_low)
     own_out_ref[...] = apply_kernel(own_high[rows], own_low[rows], parts_ref[...], outs)
     for copy in copies[2:]:
         copy.wait()
 
-    def step(i, _):
-        now = lax.rem(i, 2)
-        before = 1 - now
-        coefficients = parts_ref[...]
-        total = back_products(made_high[before], made_low[before], coefficients, outs)
+    def half_step(i, now, before):
+        work = [back_products(*before, parts_ref, outs)]
         if share:
             rows = pl.ds(pl.multiple_of(i * share, share), share)
-            total = total + back_products(high_ref[rows], low_ref[rows], coefficients, outs)
+            work.append(back_products(high_ref.at[rows], low_ref.at[rows], parts_ref, outs))
+        between = [there for there, _, _ in work] + [back for _, back, _ in work]
         columns = pl.ds(pl.multiple_of(i * block_rows, block_rows), block_rows)
-        points = (sample_ref[:, columns].astype(F32) * scale).T
-        for first in range(0, block_rows, 128):
-            rows = pl.ds(first, 128)
-            fill_kernel(
-                rows, points[first : first + 128], centre_ref, shift_ref, floor_ref,
-                made_high.at[now], made_low.at[now],
-            )
-        sum_ref[...] += total
-
-    lax.fori_loop(0, steps, step, None)
-    now = (steps - 1) % 2
-    last = sum_ref[...] + back_products(made_high[now], made_low[now], parts_ref[...], outs)
+        points = point_block(sample_ref[:, columns], constants, mixed, pick_ref, lhs_ref)
+        fill_kernel(pl.ds(0, block_rows), points, mixed, tables, *now, between)
+        for _, _, result in work:
+            sum_ref[...] += result["sum"]
+
+    def step(i, _):
+        half_step(2 * i, made[:2], made[2:])
+        half_step(2 * i + 1, made[2:], made[:2])
+
+    lax.fori_loop(0, steps // 2, step, None)
+    there, back, result = back_products(*made[2:], parts_ref, outs)
+    there()
+    back()
+    last = sum_ref[...] + result["sum"]
     last = add_parts(last, outs)
     width = last.shape[1] // len(backward_refs)
     for i, backward_ref in enumerate(backward_refs):
@@ -317,7 +425,7 @@
     own_rows = own_state[0].shape[1]
     dims, samples_dev = lattice[2].shape
     stored = tuple(high.shape[0] for high, _ in store)
-    made = pltpu.VMEM((2, block_rows, centres_all), BF16)
+    made = pltpu.VMEM((block_rows, centres_all), BF16)
     kept = pltpu.VMEM((max(16, sum(stored)), centres_all), BF16)
     rows = samples_dev - sum(stored)
     return pl.pallas_call(
@@ -331,17 +439,16 @@
             jax.ShapeDtypeStruct((3 * outs, own_rows), F32),
         ],
         scratch_shapes=[
-            *set_up_scratch(dims, rows, centres_all),
+            *set_up_scratch(dims, rows, centres_all, block_rows, PRODUCTS_MIXED),
             pltpu.VMEM((3 * outs, centres_all), BF16),
             pltpu.VMEM((3 * outs, centres_all), F32),
-            made,
-            made,
+            *[made] * 4,
             kept,
             kept,
             pltpu.SemaphoreType.DMA((6 + 2 * len(stored),)),
         ],
         compiler_params=pltpu.CompilerParams(
-            vmem_limit_bytes=(14 << 20) + (16 * block_rows + 4 * sum(stored)) * centres_all
+            vmem_limit_bytes=(16 << 20) + (16 * block_rows + 4 * sum(stored)) * centres_all
         ),
         cost_estimate=pl.CostEstimate(
             flops=6 * dims * rows * centres_all,
@@ -462,7 +569,7 @@
             state = jnp.where(upper, jnp.concatenate(joined), jnp.concatenate(turned))
         else:
             other = swap(state, bit, devices)
-            mine = fill(256 if 2 * bit == devices else 128, state)
+            mine = fill(256, state)
             state = jnp.where(
                 upper,
                 jnp.concatenate([other, mine], axis=1),
@@ -497,7 +604,7 @@
     parts = [m[1] for m in made]
     for bit in others:
         other = swap(coefficients, bit, devices)
-        mine = fill(512, coefficients)
+        mine = fill(256, coefficients)
         coefficients = jnp.concatenate([mine, other], axis=1)
     coefficients = fill(half, coefficients)
 

time: 87.1 us -> 78.5 us (0.901)
  Pallas kernels: 45.8 us -> 40.5 us
  waiting for transfers between devices: 22.3 us -> 18.7 us
  starting transfers between devices: 15.4 us -> 16.4 us
    pallas_call x1, Pallas kernels: 21.4 us -> 17.3 us  [apply_products(): pl.pallas_call(functools.partial(products, outs, block_rows, stored, orde...]
    ppermute x18, waiting for transfers between devices: 22.3 us -> 18.7 us  [swap(): return lax.ppermute(value, 'samp', [(i, i ^ bit) for i in range(devices)])]
    pallas_call x4, Pallas kernels: 19 us -> 16.7 us  [kernel_rows(): pl.pallas_call(functools.partial(store_rows, first_row, step_rows, order,...]
    ppermute x18, starting transfers between devices: 15.4 us -> 16.4 us  [swap(): return lax.ppermute(value, 'samp', [(i, i ^ bit) for i in range(devices)])]
    pallas_call x2, Pallas kernels: 3.09 us -> 4.04 us  [coefficients_of(): pl.pallas_call(functools.partial(row_products, outs, len(group)), out_sha...]
  transfers between devices with their start and end apart: 18 -> 18, of which waited for: 9 -> 7; matrix products, arithmetic and copies ran while one was open for 1% -> 1% of each run, Pallas kernels for 24% -> 23%
where the time goes in v8:
time: 78.5 us; the launch traced here: 78 us
  Pallas kernels  40.5 us (52%)
  waiting for transfers between devices  18.7 us (24%)
  starting transfers between devices  16.4 us (21%)
  other arithmetic  0.92 us (1%)
  between operations  0.86 us (1%)
    ppermute x18, waiting for transfers between devices, swap(): return lax.ppermute(value, 'samp', [(i, i ^ bit) for i in range(devices)])  18.7 us
    pallas_call x1, Pallas kernels, apply_products(): pl.pallas_call(functools.partial(products, outs, block_rows, stored, orde...  17.3 us
    pallas_call x4, Pallas kernels, kernel_rows(): pl.pallas_call(functools.partial(store_rows, first_row, step_rows, order,...  16.7 us
    ppermute x18, starting transfers between devices, swap(): return lax.ppermute(value, 'samp', [(i, i ^ bit) for i in range(devices)])  16.4 us
    pallas_call x2, Pallas kernels, coefficients_of(): pl.pallas_call(functools.partial(row_products, outs, len(group)), out_sha...  4.04 us
    pallas_call x1, Pallas kernels, body(): pl.pallas_call(finish, out_shape=[own, own, own], scratch_shapes=[pltpu.V...  1.77 us
  transfers between devices with their start and end apart: 18, of which 7 were waited for; matrix products, arithmetic and copies ran while one was open for 1% of the time, Pallas kernels for 23%

profile of v8, /device:TPU:0, one launch (start us, length us, event | category | flops | bytes accessed | tf_op | source)
XLA Modules:
  0.0 78.0 jit_solution(6888645531636668274)
XLA Ops:
  0.6 3.1 %collective-permute-start.5 = (f32[64,1024]{1,0:T(8,128)}, f32[64,1024]{1,0:T(8,128)S(1)}, u32[]{:S(2)}, u32[]{:S(2)}) collective-permute-start(f32[64,1024]{1,0:T(8,128)} %refs_0_.1), channel_id=1, source_target_pairs={{0,4},{1,5},{2,6},{3,7},{4,0},{5,1},{6,2},{7,3},{8,12},{9,13},{10,... | collective-permute-start | bytes 786440 | tf_op jit(solution)/shard_map/ppermute | solution.py:29
  3.7 0.0 collective-permute-start.1
  3.7 0.5 collective-permute-start
  4.2 0.9 %collective-permute-done.1 = f32[16,64]{1,0:T(8,128)S(1)} collective-permute-done((f32[16,64]{1,0:T(8,128)}, f32[16,64]{1,0:T(8,128)S(1)}, u32[]{:S(2)}, u32[]{:S(2)}) %collective-permute-start.1) | collective-permute-done | bytes 4128 | tf_op jit(solution)/shard_map/ppermute | solution.py:29
  5.1 0.2 collective-permute-done
  5.3 0.9 %maximum_select_fusion.3.passed_ref = f32[32,128]{1,0:T(8,128)S(1)} fusion(f32[16,64]{1,0:T(8,128)} %residual_hbm.1, f32[16,64]{1,0:T(8,128)S(1)} %collective-permute-done.1, f32[16,64]{1,0:T(8,128)} %direction_hbm.1, f32[16,64]{1,0:T(8,128)S(1)} %collective-permute-done, pred[]{:T(512)S(6)} %ne.15), kind=kLoop, calls=%fused_computation.4 | loop fusion | flops 28672 | bytes 32769 | tf_op jit(solution)/shard_map/jit(_where)/select_n | solution.py:569
  6.1 1.5 %collective-permute-start.2 = (f32[32,128]{1,0:T(8,128)S(1)}, f32[32,128]{1,0:T(8,128)S(1)}, u32[]{:S(2)}, u32[]{:S(2)}) collective-permute-start(f32[32,128]{1,0:T(8,128)S(1)} %maximum_select_fusion.3.passed_ref), channel_id=1, source_target_pairs={{0,2},{1,3},{2,0},{3,1},{4,6},{5,7},{6,4},{7,5},{8,10},{9,11},{10,... | collective-permute-start | bytes 49160 | tf_op jit(solution)/shard_map/ppermute | solution.py:29
  7.7 0.5 collective-permute-start.6
  8.2 4.3 %kernel_rows.4 = (bf16[256,1024]{1,0:T(8,128)(2,1)S(1)}, bf16[256,1024]{1,0:T(8,128)(2,1)S(1)}, f32[32,128]{1,0:T(8,128)S(1)}) custom-call(s32[16]{0:T(128)} %generator_hbm.9, s32[16]{0:T(128)} %weight_hbm.9, s32[16,2048]{1,0:T(8,128)} %samples_hbm.9, f32[32,128]{1,0:T(8,128)S(1)} %maximum_select_fusion.3.passed_ref), custom_call_target="tpu_custom_call" | custom-call | flops 25165824 | bytes 1048576 | tf_op jit(solution)/shard_map/kernel_rows/pallas_call | solution.py:301
  12.5 0.0 collective-permute-done.5.refs_1_
  12.5 1.6 %collective-permute-start.7 = (f32[64,1024]{1,0:T(8,128)S(1)}, f32[64,1024]{1,0:T(8,128)S(1)}, u32[]{:S(2)}, u32[]{:S(2)}) collective-permute-start(f32[64,1024]{1,0:T(8,128)S(1)} %collective-permute-done.5.refs_1_), channel_id=1, source_target_pairs={{0,2},{1,3},{2,0},{3,1},{4,6},{5,7},{6,4},{7,5},{8,10},{9,11},{10,... | collective-permute-start | bytes 786440 | tf_op jit(solution)/shard_map/ppermute | solution.py:29
  14.1 0.0 collective-permute-done.2
  14.1 0.5 collective-permute-start.3
  14.6 4.1 %kernel_rows.5 = (bf16[256,1024]{1,0:T(8,128)(2,1)S(1)}, bf16[256,1024]{1,0:T(8,128)(2,1)S(1)}, f32[32,256]{1,0:T(8,128)S(1)}) custom-call(s32[16]{0:T(128)} %generator_hbm.9, s32[16]{0:T(128)} %weight_hbm.9, s32[16,2048]{1,0:T(8,128)} %samples_hbm.9, f32[32,256]{1,0:T(8,128)S(1)} %maximum_select_fusion.2.passed_ref), custom_call_target="tpu_custom_call" | custom-call | flops 25165824 | bytes 1048576 | tf_op jit(solution)/shard_map/kernel_rows/pallas_call | solution.py:301
  18.8 0.0 collective-permute-done.3
  18.8 2.7 %collective-permute-start.4 = (f32[32,512]{1,0:T(8,128)S(1)}, f32[32,512]{1,0:T(8,128)S(1)}, u32[]{:S(2)}, u32[]{:S(2)}) collective-permute-start(f32[32,512]{1,0:T(8,128)S(1)} %maximum_select_fusion.1.passed_ref), channel_id=1, source_target_pairs={{0,8},{1,9},{2,10},{3,11},{4,12},{5,13},{6,14},{7,15},{8,0},{9,1},... | collective-permute-start | bytes 196616 | tf_op jit(solution)/shard_map/ppermute | solution.py:29
  21.5 0.0 collective-permute-start.8
  21.5 0.5 collective-permute-start.9
  22.0 0.0 collective-permute-done.6.refs_2_
  22.0 0.0 collective-permute-start.10
  22.0 0.0 collective-permute-done.7.refs_3_
  22.0 0.5 collective-permute-start.11
  22.5 4.1 %kernel_rows.6 = (bf16[256,1024]{1,0:T(8,128)(2,1)S(1)}, bf16[256,1024]{1,0:T(8,128)(2,1)S(1)}, f32[32,512]{1,0:T(8,128)S(1)}) custom-call(s32[16]{0:T(128)} %generator_hbm.9, s32[16]{0:T(128)} %weight_hbm.9, s32[16,2048]{1,0:T(8,128)} %samples_hbm.9, f32[32,512]{1,0:T(8,128)S(1)} %maximum_select_fusion.1.passed_ref), custom_call_target="tpu_custom_call" | custom-call | flops 25165824 | bytes 1048576 | tf_op jit(solution)/shard_map/kernel_rows/pallas_call | solution.py:301
  26.6 0.0 collective-permute-done.4
  26.7 0.0 copy-start
  26.7 1.6 %row_products.2 = (f32[16,256]{1,0:T(8,128)S(1)}, bf16[3,256,1024]{2,1,0:T(8,128)(2,1)S(1)}) custom-call(f32[32,1024]{1,0:T(8,128)S(1)} %maximum_select_fusion.state_ref, f32[64,1024]{1,0:T(8,128)} %refs_0_.1, f32[64,1024]{1,0:T(8,128)S(1)} %collective-permute-done.5.refs_1_, f32[64,1024]{1,0:T(8,128)S(1)} %collective-permute-done.6.refs_2_, ...), custom_call_target="tpu_custom_call" | custom-call | tf_op jit(solution)/shard_map/row_products/pallas_call | solution.py:582
  28.3 0.0 collective-permute-done.8.refs_0_
  28.3 0.0 collective-permute-done.10.refs_2_
  28.3 0.0 collective-permute-done.9.refs_1_
  28.3 0.0 collective-permute-done.11.refs_3_
  28.3 2.5 %row_products.3 = (f32[16,256]{1,0:T(8,128)S(1)}, bf16[3,256,1024]{2,1,0:T(8,128)(2,1)S(1)}) custom-call(f32[32,1024]{1,0:T(8,128)S(1)} %maximum_select_fusion.state_ref, f32[64,1024]{1,0:T(8,128)} %collective-permute-done.8.refs_0_, f32[64,1024]{1,0:T(8,128)S(1)} %collective-permute-done.9.refs_1_, f32[64,1024]{1,0:T(8,128)S(1)} %collective-permute-done.10.refs_2_, ...), custom_call_target="tpu_custom_call" | custom-call | tf_op jit(solution)/shard_map/row_products/pallas_call | solution.py:582
  30.8 1.9 %collective-permute-start.12 = (f32[16,512]{1,0:T(8,128)S(1)}, f32[16,512]{1,0:T(8,128)S(1)}, u32[]{:S(2)}, u32[]{:S(2)}) collective-permute-start(f32[16,512]{1,0:T(8,128)S(1)} %constant_dynamic-update-slice_fusion.passed_ref), channel_id=1, source_target_pairs={{0,8},{1,9},{2,10},{3,11},{4,12},{5,13},{6,14},{7,15},{8,0},{9,1},... | collective-permute-start | bytes 98312 | tf_op jit(solution)/shard_map/ppermute | solution.py:29
  32.7 4.2 %kernel_rows.7 = (bf16[256,1024]{1,0:T(8,128)(2,1)S(1)}, bf16[256,1024]{1,0:T(8,128)(2,1)S(1)}, f32[16,512]{1,0:T(8,128)S(1)}) custom-call(s32[16]{0:T(128)} %generator_hbm.9, s32[16]{0:T(128)} %weight_hbm.9, s32[16,2048]{1,0:T(8,128)} %samples_hbm.9, f32[16,512]{1,0:T(8,128)S(1)} %constant_dynamic-update-slice_fusion.passed_ref), custom_call_target="tpu_custom_call" | custom-call | flops 25165824 | bytes 1048576 | tf_op jit(solution)/shard_map/kernel_rows/pallas_call | solution.py:301
  36.9 0.0 collective-permute-done.12
  36.9 17.3 %products.1 = (f32[16,512]{1,0:T(8,128)S(1)}, f32[16,512]{1,0:T(8,128)S(1)}, f32[16,64]{1,0:T(8,128)S(1)}, f32[48,64]{1,0:T(8,128)S(1)}) custom-call(f32[16,1024]{1,0:T(8,128)S(1)} %pad_maximum_fusion.coef_ref, s32[16]{0:T(128)} %generator_hbm.9, s32[16]{0:T(128)} %weight_hbm.9, s32[16,2048]{1,0:T(8,128)} %samples_hbm.9, f32[16,64]{1,0:T(8,128)} %solution_hbm.1, ...), custom_call_target="tpu_custom_call" | custom-call | flops 100663296 | bytes 4194304 | tf_op jit(solution)/shard_map/products/pallas_call | solution.py:431
  54.3 0.0 copy-done
  54.3 0.0 copy-start.1
  54.3 1.1 %collective-permute-start.13 = (f32[16,512]{1,0:T(8,128)S(1)}, f32[16,512]{1,0:T(8,128)S(1)}, u32[]{:S(2)}, u32[]{:S(2)}) collective-permute-start(f32[16,512]{1,0:T(8,128)S(1)} %get-tuple-element.38), channel_id=1, source_target_pairs={{0,8},{1,9},{2,10},{3,11},{4,12},{5,13},{6,14},{7,15},{8,0},{9,1},... | collective-permute-start | bytes 98312 | tf_op jit(solution)/shard_map/ppermute | solution.py:29
  55.4 4.0 %collective-permute-done.13.came_ref = f32[16,512]{1,0:T(8,128)S(1)} collective-permute-done((f32[16,512]{1,0:T(8,128)S(1)}, f32[16,512]{1,0:T(8,128)S(1)}, u32[]{:S(2)}, u32[]{:S(2)}) %collective-permute-start.13) | collective-permute-done | bytes 32800 | tf_op jit(solution)/shard_map/ppermute | solution.py:29
  59.4 0.6 image_rows.1
  60.0 0.0 copy-done.1
  60.0 0.0 collective-permute-start.14
  60.0 1.3 %collective-permute-done.14 = f32[16,1024]{1,0:T(8,128)S(1)} collective-permute-done((f32[16,1024]{1,0:T(8,128)S(1)}, f32[16,1024]{1,0:T(8,128)S(1)}, u32[]{:S(2)}, u32[]{:S(2)}) %collective-permute-start.14) | collective-permute-done | bytes 65568 | tf_op jit(solution)/shard_map/ppermute | solution.py:29
  61.3 0.8 collective-permute-start.15
  62.0 3.6 %collective-permute-done.15 = f32[16,1024]{1,0:T(8,128)S(1)} collective-permute-done((f32[16,1024]{1,0:T(8,128)S(1)}, f32[16,1024]{1,0:T(8,128)S(1)}, u32[]{:S(2)}, u32[]{:S(2)}) %collective-permute-start.15) | collective-permute-done | bytes 65568 | tf_op jit(solution)/shard_map/ppermute | solution.py:29
  65.6 0.3 collective-permute-start.16
  65.9 4.0 %collective-permute-done.16 = f32[16,1024]{1,0:T(8,128)S(1)} collective-permute-done((f32[16,1024]{1,0:T(8,128)S(1)}, f32[16,1024]{1,0:T(8,128)S(1)}, u32[]{:S(2)}, u32[]{:S(2)}) %collective-permute-start.16) | collective-permute-done | bytes 65568 | tf_op jit(solution)/shard_map/ppermute | solution.py:29
  70.0 0.0 copy-start.2
  70.0 0.9 %collective-permute-start.17 = (f32[16,1024]{1,0:T(8,128)S(1)}, f32[16,1024]{1,0:T(8,128)S(1)}, u32[]{:S(2)}, u32[]{:S(2)}) collective-permute-start(f32[16,1024]{1,0:T(8,128)S(1)} %add.11.image_ref), channel_id=1, source_target_pairs={{0,8},{1,9},{2,10},{3,11},{4,12},{5,13},{6,14},{7,15},{8,0},{9,1},... | collective-permute-start | bytes 196616 | tf_op jit(solution)/shard_map/ppermute | solution.py:29
  70.9 4.7 %collective-permute-done.17.more_ref = f32[16,1024]{1,0:T(8,128)S(1)} collective-permute-done((f32[16,1024]{1,0:T(8,128)S(1)}, f32[16,1024]{1,0:T(8,128)S(1)}, u32[]{:S(2)}, u32[]{:S(2)}) %collective-permute-start.17) | collective-permute-done | bytes 65568 | tf_op jit(solution)/shard_map/ppermute | solution.py:29
  75.6 0.0 copy-start.3
  75.6 0.0 copy-done.2
  75.6 0.6 copy-done.3
  76.2 1.8 %finish.1 = (f32[16,64]{1,0:T(8,128)}, f32[16,64]{1,0:T(8,128)}, f32[16,64]{1,0:T(8,128)}) custom-call(f32[16,1024]{1,0:T(8,128)} %copy-done.2, f32[16,1024]{1,0:T(8,128)} %copy-done.3, f32[32,1024]{1,0:T(8,128)} %copy-done, f32[48,64]{1,0:T(8,128)} %copy-done.1), custom_call_target="tpu_custom_call" | custom-call | tf_op jit(solution)/shard_map/finish/pallas_call | solution.py:635
  (9 shorter events, 0.1 us)
Async XLA Ops:
  0.6 11.9 %collective-permute-start.5 = (f32[64,1024]{1,0:T(8,128)}, f32[64,1024]{1,0:T(8,128)S(1)}, u32[]{:S(2)}, u32[]{:S(2)}) collective-permute-start(f32[64,1024]{1,0:T(8,128)} %refs_0_.1), channel_id=1, source_target_pairs={{0,4},{1,5},{2,6},{3,7},{4,0},{5,1},{6,2},{7,3},{8,12},{9,13},{10,... | collective-permute-start | bytes 786440 | tf_op jit(solution)/shard_map/ppermute | solution.py:29
  3.7 1.4 %collective-permute-start.1 = (f32[16,64]{1,0:T(8,128)}, f32[16,64]{1,0:T(8,128)S(1)}, u32[]{:S(2)}, u32[]{:S(2)}) collective-permute-start(f32[16,64]{1,0:T(8,128)} %residual_hbm.1), channel_id=1, source_target_pairs={{0,1},{1,0},{2,3},{3,2},{4,5},{5,4},{6,7},{7,6},{8,9},{9,8},{10,11... | collective-permute-start | bytes 12296 | tf_op jit(solution)/shard_map/ppermute | solution.py:29
  3.7 1.5 %collective-permute-start = (f32[16,64]{1,0:T(8,128)}, f32[16,64]{1,0:T(8,128)S(1)}, u32[]{:S(2)}, u32[]{:S(2)}) collective-permute-start(f32[16,64]{1,0:T(8,128)} %direction_hbm.1), channel_id=1, source_target_pairs={{0,1},{1,0},{2,3},{3,2},{4,5},{5,4},{6,7},{7,6},{8,9},{9,8},{10,11... | collective-permute-start | bytes 12296 | tf_op jit(solution)/shard_map/ppermute | solution.py:29
  6.1 8.0 %collective-permute-start.2 = (f32[32,128]{1,0:T(8,128)S(1)}, f32[32,128]{1,0:T(8,128)S(1)}, u32[]{:S(2)}, u32[]{:S(2)}) collective-permute-start(f32[32,128]{1,0:T(8,128)S(1)} %maximum_select_fusion.3.passed_ref), channel_id=1, source_target_pairs={{0,2},{1,3},{2,0},{3,1},{4,6},{5,7},{6,4},{7,5},{8,10},{9,11},{10,... | collective-permute-start | bytes 49160 | tf_op jit(solution)/shard_map/ppermute | solution.py:29
  7.7 14.3 %collective-permute-start.6 = (f32[64,1024]{1,0:T(8,128)}, f32[64,1024]{1,0:T(8,128)S(1)}, u32[]{:S(2)}, u32[]{:S(2)}) collective-permute-start(f32[64,1024]{1,0:T(8,128)} %refs_0_.1), channel_id=1, source_target_pairs={{0,2},{1,3},{2,0},{3,1},{4,6},{5,7},{6,4},{7,5},{8,10},{9,11},{10,... | collective-permute-start | bytes 786440 | tf_op jit(solution)/shard_map/ppermute | solution.py:29
  12.5 9.5 %collective-permute-start.7 = (f32[64,1024]{1,0:T(8,128)S(1)}, f32[64,1024]{1,0:T(8,128)S(1)}, u32[]{:S(2)}, u32[]{:S(2)}) collective-permute-start(f32[64,1024]{1,0:T(8,128)S(1)} %collective-permute-done.5.refs_1_), channel_id=1, source_target_pairs={{0,2},{1,3},{2,0},{3,1},{4,6},{5,7},{6,4},{7,5},{8,10},{9,11},{10,... | collective-permute-start | bytes 786440 | tf_op jit(solution)/shard_map/ppermute | solution.py:29
  14.1 4.7 %collective-permute-start.3 = (f32[32,256]{1,0:T(8,128)S(1)}, f32[32,256]{1,0:T(8,128)S(1)}, u32[]{:S(2)}, u32[]{:S(2)}) collective-permute-start(f32[32,256]{1,0:T(8,128)S(1)} %maximum_select_fusion.2.passed_ref), channel_id=1, source_target_pairs={{0,4},{1,5},{2,6},{3,7},{4,0},{5,1},{6,2},{7,3},{8,12},{9,13},{10,... | collective-permute-start | bytes 98312 | tf_op jit(solution)/shard_map/ppermute | solution.py:29
  18.8 7.8 %collective-permute-start.4 = (f32[32,512]{1,0:T(8,128)S(1)}, f32[32,512]{1,0:T(8,128)S(1)}, u32[]{:S(2)}, u32[]{:S(2)}) collective-permute-start(f32[32,512]{1,0:T(8,128)S(1)} %maximum_select_fusion.1.passed_ref), channel_id=1, source_target_pairs={{0,8},{1,9},{2,10},{3,11},{4,12},{5,13},{6,14},{7,15},{8,0},{9,1},... | collective-permute-start | bytes 196616 | tf_op jit(solution)/shard_map/ppermute | solution.py:29
  21.5 6.8 %collective-permute-start.8 = (f32[64,1024]{1,0:T(8,128)}, f32[64,1024]{1,0:T(8,128)}, u32[]{:S(2)}, u32[]{:S(2)}) collective-permute-start(f32[64,1024]{1,0:T(8,128)} %refs_0_.1), channel_id=1, source_target_pairs={{0,1},{1,0},{2,3},{3,2},{4,5},{5,4},{6,7},{7,6},{8,9},{9,8},{10,11... | collective-permute-start | bytes 786440 | tf_op jit(solution)/shard_map/ppermute | solution.py:29
  21.5 6.8 %collective-permute-start.9 = (f32[64,1024]{1,0:T(8,128)S(1)}, f32[64,1024]{1,0:T(8,128)S(1)}, u32[]{:S(2)}, u32[]{:S(2)}) collective-permute-start(f32[64,1024]{1,0:T(8,128)S(1)} %collective-permute-done.5.refs_1_), channel_id=1, source_target_pairs={{0,1},{1,0},{2,3},{3,2},{4,5},{5,4},{6,7},{7,6},{8,9},{9,8},{10,11... | collective-permute-start | bytes 786440 | tf_op jit(solution)/shard_map/ppermute | solution.py:29
  22.0 6.3 %collective-permute-start.10 = (f32[64,1024]{1,0:T(8,128)S(1)}, f32[64,1024]{1,0:T(8,128)S(1)}, u32[]{:S(2)}, u32[]{:S(2)}) collective-permute-start(f32[64,1024]{1,0:T(8,128)S(1)} %collective-permute-done.6.refs_2_), channel_id=1, source_target_pairs={{0,1},{1,0},{2,3},{3,2},{4,5},{5,4},{6,7},{7,6},{8,9},{9,8},{10,11... | collective-permute-start | bytes 786440 | tf_op jit(solution)/shard_map/ppermute | solution.py:29
  22.0 6.3 %collective-permute-start.11 = (f32[64,1024]{1,0:T(8,128)S(1)}, f32[64,1024]{1,0:T(8,128)}, u32[]{:S(2)}, u32[]{:S(2)}) collective-permute-start(f32[64,1024]{1,0:T(8,128)S(1)} %collective-permute-done.7.refs_3_), channel_id=1, source_target_pairs={{0,1},{1,0},{2,3},{3,2},{4,5},{5,4},{6,7},{7,6},{8,9},{9,8},{10,11... | collective-permute-start | bytes 786440 | tf_op jit(solution)/shard_map/ppermute | solution.py:29
  26.7 27.6 %copy-start = (f32[32,1024]{1,0:T(8,128)}, f32[32,1024]{1,0:T(8,128)S(1)}, u32[]{:S(2)}) copy-start(f32[32,1024]{1,0:T(8,128)S(1)} %maximum_select_fusion.state_ref) | copy-start | bytes 393220
  30.8 6.1 %collective-permute-start.12 = (f32[16,512]{1,0:T(8,128)S(1)}, f32[16,512]{1,0:T(8,128)S(1)}, u32[]{:S(2)}, u32[]{:S(2)}) collective-permute-start(f32[16,512]{1,0:T(8,128)S(1)} %constant_dynamic-update-slice_fusion.passed_ref), channel_id=1, source_target_pairs={{0,8},{1,9},{2,10},{3,11},{4,12},{5,13},{6,14},{7,15},{8,0},{9,1},... | collective-permute-start | bytes 98312 | tf_op jit(solution)/shard_map/ppermute | solution.py:29
  54.3 5.7 %copy-start.1 = (f32[48,64]{1,0:T(8,128)}, f32[48,64]{1,0:T(8,128)S(1)}, u32[]{:S(2)}) copy-start(f32[48,64]{1,0:T(8,128)S(1)} %get-tuple-element.42.own_ref) | copy-start | bytes 36868
  54.3 5.1 %collective-permute-start.13 = (f32[16,512]{1,0:T(8,128)S(1)}, f32[16,512]{1,0:T(8,128)S(1)}, u32[]{:S(2)}, u32[]{:S(2)}) collective-permute-start(f32[16,512]{1,0:T(8,128)S(1)} %get-tuple-element.38), channel_id=1, source_target_pairs={{0,8},{1,9},{2,10},{3,11},{4,12},{5,13},{6,14},{7,15},{8,0},{9,1},... | collective-permute-start | bytes 98312 | tf_op jit(solution)/shard_map/ppermute | solution.py:29
  60.0 1.3 %collective-permute-start.14 = (f32[16,1024]{1,0:T(8,128)S(1)}, f32[16,1024]{1,0:T(8,128)S(1)}, u32[]{:S(2)}, u32[]{:S(2)}) collective-permute-start(f32[16,1024]{1,0:T(8,128)S(1)} %image_rows.1), channel_id=1, source_target_pairs={{0,1},{1,0},{2,3},{3,2},{4,5},{5,4},{6,7},{7,6},{8,9},{9,8},{10,11... | collective-permute-start | bytes 196616 | tf_op jit(solution)/shard_map/ppermute | solution.py:29
  61.3 4.3 %collective-permute-start.15 = (f32[16,1024]{1,0:T(8,128)S(1)}, f32[16,1024]{1,0:T(8,128)S(1)}, u32[]{:S(2)}, u32[]{:S(2)}) collective-permute-start(f32[16,1024]{1,0:T(8,128)S(1)} %add.9), channel_id=1, source_target_pairs={{0,2},{1,3},{2,0},{3,1},{4,6},{5,7},{6,4},{7,5},{8,10},{9,11},{10,... | collective-permute-start | bytes 196616 | tf_op jit(solution)/shard_map/ppermute | solution.py:29
  65.6 4.3 %collective-permute-start.16 = (f32[16,1024]{1,0:T(8,128)S(1)}, f32[16,1024]{1,0:T(8,128)S(1)}, u32[]{:S(2)}, u32[]{:S(2)}) collective-permute-start(f32[16,1024]{1,0:T(8,128)S(1)} %add.10), channel_id=1, source_target_pairs={{0,4},{1,5},{2,6},{3,7},{4,0},{5,1},{6,2},{7,3},{8,12},{9,13},{10,... | collective-permute-start | bytes 196616 | tf_op jit(solution)/shard_map/ppermute | solution.py:29
  70.0 5.6 %copy-start.2 = (f32[16,1024]{1,0:T(8,128)}, f32[16,1024]{1,0:T(8,128)S(1)}, u32[]{:S(2)}) copy-start(f32[16,1024]{1,0:T(8,128)S(1)} %add.11.image_ref) | copy-start | bytes 196612
  70.0 5.6 %collective-permute-start.17 = (f32[16,1024]{1,0:T(8,128)S(1)}, f32[16,1024]{1,0:T(8,128)S(1)}, u32[]{:S(2)}, u32[]{:S(2)}) collective-permute-start(f32[16,1024]{1,0:T(8,128)S(1)} %add.11.image_ref), channel_id=1, source_target_pairs={{0,8},{1,9},{2,10},{3,11},{4,12},{5,13},{6,14},{7,15},{8,0},{9,1},... | collective-permute-start | bytes 196616 | tf_op jit(solution)/shard_map/ppermute | solution.py:29
  75.6 0.6 copy-start.3

commit v9 on v8

v9 whole, which is shorter than its diff:
```python
import functools
import math

import jax
import jax.numpy as jnp
from jax import lax
from jax.experimental import pallas as pl
from jax.experimental.pallas import tpu as pltpu
from jax.sharding import PartitionSpec as P

LATTICE = 65521
MIDDLE = LATTICE // 2

ridge_weight = 0.25
STORE_BYTES = 12 << 20
HELD_BYTES = 16 << 20
WIDTH = 256
STORED_MIXED = 16
PRODUCTS_MIXED = 4
VMEM = pl.BlockSpec(memory_space=pltpu.VMEM)
FREE = pl.BlockSpec(memory_space=pl.ANY)
HBM = pl.BlockSpec(memory_space=pltpu.HBM)
SMEM = pl.BlockSpec(memory_space=pltpu.SMEM)
F32 = jnp.float32
BF16 = jnp.bfloat16


def swap(value, bit, devices):
    return lax.ppermute(value, "samp", [(i, i ^ bit) for i in range(devices)])


def plan(devices, piece_bytes):
    bits = [1 << k for k in range(devices.bit_length() - 1)]
    held = []
    for bit in [b for b in (devices // 4, *bits) if 0 < b < devices // 2]:
        if bit not in held and (2 << len(held)) * piece_bytes <= HELD_BYTES:
            held.append(bit)
    held = held[:1] + held[:0:-1] if len(held) > 1 else held
    return held, [b for b in bits if b not in held]


def split3(value):
    high = value.astype(BF16)
    rest = value - high.astype(F32)
    middle = rest.astype(BF16)
    low = (rest - middle.astype(F32)).astype(BF16)
    return high, middle, low


def stack3(value):
    return jnp.concatenate(split3(value), axis=0)


def add_parts(value, outs):
    return value[:outs] + (value[outs : 2 * outs] + value[2 * outs :])


def bilinear_terms(sources, count, columns):
    place = lax.broadcasted_iota(jnp.int32, (count * 16, columns), 1)
    row = lax.broadcasted_iota(jnp.int32, (count * 16, columns), 0)
    term = place & 15
    source = jnp.full_like(place, -16)
    for k, which in enumerate(sources):
        source = jnp.where(term == k, which, source)
    return jnp.where(row == source * 16 + (place >> 4), 1.0, 0.0).astype(BF16)


def point_block(coordinates, tables, mixed, lhs_ref):
    _, _, constant_ref, pick_ref = tables
    curve, base = constant_ref[:, 0:1], constant_ref[:, 1:2]
    scale = scale_of(constant_ref[:, 2:3], curve, mixed)
    centred = coordinates - MIDDLE
    if mixed:
        real = centred.astype(F32)
        unit = real * (1.0 / LATTICE)
        large = jnp.floor(real * (1.0 / 256.0) + 0.5) * 256.0
        alone = curve * (unit * unit + unit) + base
        ones = jnp.ones(real.shape, BF16)
        sources = [*split3(alone), large.astype(BF16), (real - large).astype(BF16), ones]
        terms = lax.dot_general(
            jnp.concatenate(sources, axis=0),
            pick_ref[...],
            (((0,), (0,)), ((), ())),
            preferred_element_type=F32,
        ).astype(BF16)
        rows = terms.shape[0]
        for axis_number in range(mixed):
            lhs_ref[axis_number, :rows] = terms[:, axis_number * 128 : axis_number * 128 + 16]
    return (centred.astype(F32) * scale).T


def scale_of(shift, curve, mixed):
    row = lax.broadcasted_iota(jnp.int32, shift.shape, 0)
    return jnp.where(row < mixed, 2.0 * curve, 2.0 * shift) * (1.0 / LATTICE)


def kernel_tile(points, mixed, lhs_ref, tables, first, width):
    centre_ref, rhs_ref, constant_ref, _ = tables
    rows, dims = points.shape
    product = None
    columns = pl.ds(first, width)
    for axis_number in kernel_order(dims, mixed):
        own = slice(axis_number, axis_number + 1)
        kind = 0 if axis_number < mixed else 1
        centre = centre_ref[kind, own, columns]
        point = jnp.broadcast_to(points[:, axis_number : axis_number + 1], (rows, width))
        if axis_number < mixed:
            bilinear = jnp.dot(
                lhs_ref[axis_number, :rows],
                rhs_ref[pl.ds(axis_number * 16, 16), columns],
                preferred_element_type=F32,
            )
            factor = bilinear - jnp.maximum(point, centre)
        else:
            shift = jnp.broadcast_to(constant_ref[own, 2:3], (rows, width))
            floor = jnp.broadcast_to(constant_ref[own, 3:4], (rows, width))
            arm = jnp.abs(point - centre) - shift
            factor = arm * arm + floor
        product = factor if product is None else product * factor
    return product


def kernel_order(dims, mixed):
    kinds = [list(range(mixed)), list(range(mixed, dims))]
    order = []
    while kinds[0] or kinds[1]:
        first = len(kinds[0]) * (dims - mixed) >= len(kinds[1]) * mixed
        order.append(kinds[0 if kinds[0] and (first or not kinds[1]) else 1].pop(0))
    return order


def fill_kernel(rows, points, mixed, lhs_ref, tables, high_ref, low_ref, between=()):
    centres_all = tables[0].shape[2]
    width = min(WIDTH, centres_all)
    span = min(1024, centres_all)
    between = list(between)

    def part(base):
        for piece in range(span // width):
            if between:
                between.pop(0)()
            first = base + piece * width
            if not isinstance(first, int):
                first = pl.multiple_of(first, width)
            tile = kernel_tile(points, mixed, lhs_ref, tables, first, width)
            high = tile.astype(BF16)
            high_ref[rows, pl.ds(first, width)] = high
            low_ref[rows, pl.ds(first, width)] = (tile - high.astype(F32)).astype(BF16)

    if centres_all == span:
        part(0)
    else:
        while between:
            between.pop(0)()
        lax.fori_loop(0, centres_all // span, lambda i, _: part(i * span), None)
    while between:
        between.pop(0)()


def fetch(pairs, sems):
    copies = [pltpu.make_async_copy(src, dst, sems.at[i]) for i, (src, dst) in enumerate(pairs)]
    for copy in copies:
        copy.start()
    return copies


def modulo(value):
    turns = (value.astype(F32) * (1.0 / LATTICE)).astype(jnp.int32)
    rest = value - turns * LATTICE
    rest = jnp.where(rest < 0, rest + LATTICE, rest)
    return jnp.where(rest >= LATTICE, rest - LATTICE, rest)


def column_of(values_ref, dims, dtype):
    row = lax.broadcasted_iota(jnp.int32, (dims, 1), 0)
    column = jnp.zeros((dims, 1), dtype)
    for axis_number in range(dims):
        column = jnp.where(row == axis_number, values_ref[axis_number], column)
    return column


def centre_coordinates(order, generator_ref, dims, count):
    order_bits, cen_dev = order
    generator = column_of(generator_ref, dims, jnp.int32)
    place = lax.broadcasted_iota(jnp.int32, (1, count), 1)
    owner = jnp.zeros_like(place) + lax.axis_index("samp")
    for k, bit in enumerate(order_bits):
        owner = jnp.where((place & (cen_dev << k)) != 0, owner ^ bit, owner)
    column = owner * cen_dev + (place & (cen_dev - 1))
    upper = modulo(column * (generator >> 8))
    return modulo(upper * 256 + column * (generator & 255))


def begin(
    order, generator_hbm, weight_hbm, samples_hbm, piece_hbm, solution_hbm, residual_hbm, direction_hbm,
    sample_ref, piece_ref, own_state_ref, centre_ref, rhs_ref, constant_ref, pick_ref, own_points_ref,
    generator_ref, weight_ref, sems,
):
    outs = solution_hbm.shape[0]
    copies = fetch(
        [
            (generator_hbm, generator_ref),
            (weight_hbm, weight_ref),
            (samples_hbm, sample_ref),
            (piece_hbm, piece_ref),
            (solution_hbm, own_state_ref.at[pl.ds(0, outs)]),
            (residual_hbm, own_state_ref.at[pl.ds(outs, outs)]),
            (direction_hbm, own_state_ref.at[pl.ds(2 * outs, outs)]),
        ],
        sems,
    )
    _, dims, centres_all = centre_ref.shape
    place = lax.broadcasted_iota(jnp.int32, (6 * dims, 128), 1)
    row = lax.broadcasted_iota(jnp.int32, (6 * dims, 128), 0)
    source = jnp.full_like(place, -1000)
    for k, which in enumerate((0, 1, 2, 5, 5, 5, 3, 3, 3, 4, 4, 4)):
        source = jnp.where(place == k, which * dims, source)
    for axis_number in range(dims):
        columns = slice(axis_number * 128, (axis_number + 1) * 128)
        pick_ref[:, columns] = jnp.where(row == source + axis_number, 1.0, 0.0).astype(BF16)
    pick = bilinear_terms((0, 0, 0, 1, 2, 3, 4, 5, 6, 4, 5, 6), 7, 16 * dims)

    copies[0].wait()
    copies[1].wait()
    curves = [math.pi * math.pi * 0.75**weight for weight in range(8)]
    weight = column_of(weight_ref, dims, jnp.int32)
    shift = jnp.full((dims, 1), 0.5 * math.sqrt(curves[7]), F32)
    for k in range(7):
        shift = jnp.where(weight == k, 0.5 * math.sqrt(curves[k]), shift)
    curve = 4.0 * shift * shift
    floor = 1.0 - curve * (1.0 / 12.0)
    lane = lax.broadcasted_iota(jnp.int32, (dims, 128), 1)
    table = jnp.where(lane == 0, curve, jnp.where(lane == 1, floor + 0.25 * curve, 0.0))
    constant_ref[...] = jnp.where(lane == 2, shift, jnp.where(lane == 3, floor, table))

    centre = centre_coordinates(order, generator_ref, dims, centres_all)
    own_points_ref[...] = centre[:, :128]
    real = (centre - MIDDLE).astype(F32)
    for kind, mixed in ((0, dims), (1, 0)):
        centre_ref[kind] = real * scale_of(shift, curve, mixed)
    unit = real * (1.0 / LATTICE)
    alone = curve * (unit * unit + unit)
    slope = (-2.0 / LATTICE) * curve * unit
    ones = jnp.ones(real.shape, BF16)
    sources = jnp.concatenate([ones, *split3(alone), *split3(slope)], axis=0)
    rhs_ref[...] = lax.dot_general(
        pick, sources, (((0,), (0,)), ((), ())), preferred_element_type=F32
    ).astype(BF16)
    for copy in copies[2:]:
        copy.wait()


def store_rows(
    first_row, mixed, sample_ref, centre_ref, rhs_ref, constant_ref, pick_ref, passed_ref,
    high_ref, low_ref, handed_ref, lhs_ref,
):
    tables = (centre_ref, rhs_ref, constant_ref, pick_ref)
    handed_ref[...] = passed_ref[...]
    step_rows = lhs_ref.shape[1]

    def step(i, _):
        rows = pl.ds(pl.multiple_of(i * step_rows, step_rows), step_rows)
        columns = pl.ds(pl.multiple_of(first_row + i * step_rows, 128), step_rows)
        points = point_block(sample_ref[:, columns], tables, mixed, lhs_ref)
        fill_kernel(rows, points, mixed, lhs_ref, tables, high_ref, low_ref)

    lax.fori_loop(0, high_ref.shape[0] // step_rows, step, None)


def kernel_rows(passed, first_row, rows, tables):
    _, dims, centres_all = tables[1].shape
    kept = jax.ShapeDtypeStruct((rows, centres_all), BF16)
    high, low, handed = pl.pallas_call(
        functools.partial(store_rows, first_row, STORED_MIXED),
        out_shape=[kept, kept, jax.ShapeDtypeStruct(passed.shape, passed.dtype)],
        scratch_shapes=[pltpu.VMEM((max(1, STORED_MIXED), min(256, rows), 16), BF16)],
        compiler_params=pltpu.CompilerParams(vmem_limit_bytes=16 << 20),
        cost_estimate=pl.CostEstimate(
            flops=6 * dims * rows * centres_all,
            bytes_accessed=4 * rows * centres_all,
            transcendentals=0,
        ),
        name="kernel_rows",
    )(*tables, passed)
    return (high, low), handed


def in_hbm(*values):
    return [pltpu.with_memory_space_constraint(value, pltpu.HBM) for value in values]


def apply_kernel(high, low, coefficients, outs):
    contract = (((1,), (1,)), ((), ()))
    fitted = lax.dot_general(coefficients, high, contract, preferred_element_type=F32)
    fitted = fitted + lax.dot_general(coefficients, low, contract, preferred_element_type=F32)
    return add_parts(fitted, outs)


def back_products(high_ref, low_ref, coef_ref, outs):
    result = {}

    def there():
        result["parts"] = stack3(apply_kernel(high_ref[...], low_ref[...], coef_ref[...], outs))

    def back():
        parts = result["parts"]
        total = jnp.dot(parts, high_ref[...], preferred_element_type=F32)
        result["sum"] = total + jnp.dot(parts, low_ref[...], preferred_element_type=F32)

    return there, back, result


def products(
    outs, stored, coef_ref, sample_ref, centre_ref, rhs_ref, constant_ref, pick_ref, own_points_ref, *refs
):
    stored_refs, refs = refs[: 2 * len(stored)], refs[2 * len(stored) :]
    *backward_refs, own_out_ref = refs[:3]
    lhs_ref, parts_ref, sum_ref, *made = refs[3:]
    tables = (centre_ref, rhs_ref, constant_ref, pick_ref)
    mixed = PRODUCTS_MIXED
    own_rows = own_out_ref.shape[1]
    block_rows = made[0].shape[0]
    first_row = sum(stored)
    steps = (sample_ref.shape[1] - first_row) // block_rows

    parts_ref[...] = stack3(coef_ref[...])
    sum_ref[...] = jnp.zeros_like(sum_ref)
    last_high, last_low = made[2:]
    last_high[...] = jnp.zeros_like(last_high)
    last_low[...] = jnp.zeros_like(last_low)
    own_high, own_low = made[:2]
    rows = pl.ds(0, own_rows)
    own_points = point_block(own_points_ref[:, :own_rows], tables, mixed, lhs_ref)
    fill_kernel(rows, own_points, mixed, lhs_ref, tables, own_high, own_low)
    own_out_ref[...] = apply_kernel(own_high[rows], own_low[rows], parts_ref[...], outs)

    def half_step(i, now, before, given):
        work = [back_products(*before, parts_ref, outs)]
        if given:
            work.append(back_products(*given, parts_ref, outs))
        between = [there for there, _, _ in work] + [back for _, back, _ in work]
        columns = pl.ds(pl.multiple_of(first_row + i * block_rows, 128), block_rows)
        points = point_block(sample_ref[:, columns], tables, mixed, lhs_ref)
        fill_kernel(pl.ds(0, block_rows), points, mixed, lhs_ref, tables, *now, between)
        for _, _, result in work:
            sum_ref[...] += result["sum"]

    pairs = [stored_refs[2 * i : 2 * i + 2] for i in range(len(stored))]
    if pairs:
        for i in range(steps):
            now, before = (made[:2], made[2:]) if i % 2 == 0 else (made[2:], made[:2])
            half_step(i, now, before, pairs[i] if i < len(pairs) else None)
    else:

        def step(i, _):
            half_step(2 * i, made[:2], made[2:], None)
            half_step(2 * i + 1, made[2:], made[:2], None)

        lax.fori_loop(0, steps // 2, step, None)
    there, back, result = back_products(*made[2:], parts_ref, outs)
    there()
    back()
    last = sum_ref[...] + result["sum"]
    last = add_parts(last, outs)
    width = last.shape[1] // len(backward_refs)
    for i, backward_ref in enumerate(backward_refs):
        backward_ref[...] = last[:, i * width : (i + 1) * width]


def apply_products(store, coefficients, own_points, block_rows, tables):
    outs, centres_all = coefficients.shape
    dims, samples_dev = tables[0].shape
    own_rows = own_points.shape[1]
    stored = tuple(high.shape[0] for high, _ in store)
    made = pltpu.VMEM((block_rows, centres_all), BF16)
    rows = samples_dev - sum(stored)
    half = jax.ShapeDtypeStruct((outs, centres_all // 2), F32)
    return pl.pallas_call(
        functools.partial(products, outs, stored),
        out_shape=[half, half, jax.ShapeDtypeStruct((outs, own_rows), F32)],
        scratch_shapes=[
            pltpu.VMEM((max(1, PRODUCTS_MIXED), block_rows, 16), BF16),
            pltpu.VMEM((3 * outs, centres_all), BF16),
            pltpu.VMEM((3 * outs, centres_all), F32),
            *[made] * 4,
        ],
        compiler_params=pltpu.CompilerParams(
            vmem_limit_bytes=(16 << 20) + 16 * block_rows * centres_all
        ),
        cost_estimate=pl.CostEstimate(
            flops=6 * dims * rows * centres_all,
            bytes_accessed=4 * sum(stored) * centres_all,
            transcendentals=0,
        ),
        name="products",
    )(coefficients, *tables, own_points, *[part for pair in store for part in pair])


def row_products(outs, count, state_ref, *refs):
    coef_ref, parts_ref = refs[count:]
    state = stack3(state_ref[:outs])
    cen_dev = refs[0].shape[0]
    for i, piece_ref in enumerate(refs[:count]):
        rows = slice(i * cen_dev, (i + 1) * cen_dev)
        for k, part in enumerate(split3(piece_ref[...])):
            parts_ref[k, rows] = part
    total = None
    for k in range(3):
        term = lax.dot_general(
            state, parts_ref[k], (((1,), (1,)), ((), ())), preferred_element_type=F32
        )
        total = term if total is None else total + term
    coef_ref[...] = add_parts(total, outs)


def image_rows(scale_total, ridge, kept_ref, came_ref, own_ref, *refs):
    *part_refs, image_ref = refs
    outs, cen_dev = own_ref.shape
    applied = (kept_ref[...] + came_ref[...]) * (1.0 / scale_total)
    own = ridge * own_ref[...]
    rest = applied.shape[1] - cen_dev
    if rest:
        own = jnp.concatenate([own, jnp.zeros((outs, rest), F32)], axis=1)
    rows = stack3(applied + own)
    total, first = None, 0
    for part_ref in part_refs:
        some = rows[:, first : first + part_ref.shape[1]]
        first += part_ref.shape[1]
        for k in range(3):
            term = jnp.dot(some, part_ref[k], preferred_element_type=F32)
            total = term if total is None else total + term
    image_ref[...] = add_parts(total, outs)


def finish(
    image_ref, more_ref, state_ref, own_ref, new_solution_ref, new_residual_ref, new_direction_ref, total_ref
):
    outs, cen_dev = new_solution_ref.shape
    image = image_ref[...] + more_ref[...]
    total_ref[...] = image
    residual_full = state_ref[outs:]
    norm_old = jnp.sum(residual_full * residual_full, axis=1, keepdims=True)
    curvature = jnp.sum(state_ref[:outs] * image, axis=1, keepdims=True)
    step_length = norm_old / curvature
    next_full = residual_full - step_length * image
    norm_new = jnp.sum(next_full * next_full, axis=1, keepdims=True)
    index = lax.axis_index("samp")
    share = max(1, 128 // cen_dev)
    first = pl.multiple_of((index // share) * 128, 128)
    wide = total_ref[:, pl.ds(first, 128)]
    own_image = wide[:, :cen_dev]
    for k in range(1, share):
        here = lax.rem(index, share) == k
        own_image = jnp.where(here, wide[:, k * cen_dev : (k + 1) * cen_dev], own_image)
    direction = own_ref[2 * outs :]
    new_solution_ref[...] = own_ref[:outs] + step_length * direction
    new_residual = own_ref[outs : 2 * outs] - step_length * own_image
    new_residual_ref[...] = new_residual
    new_direction_ref[...] = new_residual + (norm_new / norm_old) * direction


def body(samples, generator, weight_index, preconditioner, solution, residual, direction):
    devices = lax.axis_size("samp")
    index = lax.axis_index("samp")
    cen_dev, centres_all = preconditioner.shape
    samples_dev = samples.shape[1]
    outs = direction.shape[0]
    held, others = plan(devices, 4 * cen_dev * centres_all)

    order = ((*held, *others), cen_dev)
    dims = samples.shape[0]
    sample_copy, piece_copy, own_state, *tables = pl.pallas_call(
        functools.partial(begin, order),
        in_specs=[HBM] * 7,
        out_shape=[
            jax.ShapeDtypeStruct(samples.shape, jnp.int32),
            jax.ShapeDtypeStruct(preconditioner.shape, F32),
            jax.ShapeDtypeStruct((3 * outs, cen_dev), F32),
            jax.ShapeDtypeStruct((2, dims, centres_all), F32),
            jax.ShapeDtypeStruct((16 * dims, centres_all), BF16),
            jax.ShapeDtypeStruct((dims, 128), F32),
            jax.ShapeDtypeStruct((6 * dims, 128 * dims), BF16),
            jax.ShapeDtypeStruct((dims, 128), jnp.int32),
        ],
        scratch_shapes=[
            pltpu.SMEM((dims,), jnp.int32),
            pltpu.SMEM((dims,), jnp.int32),
            pltpu.SemaphoreType.DMA((7,)),
        ],
        compiler_params=pltpu.CompilerParams(vmem_limit_bytes=32 << 20),
        name="begin",
    )(*in_hbm(generator, weight_index, samples, preconditioner, solution, residual, direction))
    own_points = tables.pop()[:, :cen_dev]
    tables = (sample_copy, *tables)

    half = samples_dev // 2
    use_store = 4 * half * centres_all <= STORE_BYTES
    store, filled = [], 0

    def fill(rows, passed):
        nonlocal filled
        rows = min(rows, half - filled) if use_store else 0
        if rows == 0:
            return passed
        made, handed = kernel_rows(passed, filled, rows, tables)
        store.append(made)
        filled += rows
        return handed

    pieces = [preconditioner]
    early = [swap(preconditioner, bit, devices) for bit in held[:2]]
    pieces += early[:1]
    if len(early) > 1:
        pieces += [early[1], swap(early[0], held[1], devices)]
    bit = 1
    state = None
    while bit < devices:
        upper = (index & bit) != 0
        if state is None:
            mine = [direction, residual]
            other = [swap(direction, bit, devices), swap(residual, bit, devices)]
            joined = [jnp.concatenate(pair, axis=1) for pair in zip(other, mine)]
            turned = [jnp.concatenate(pair, axis=1) for pair in zip(mine, other)]
            state = jnp.where(upper, jnp.concatenate(joined), jnp.concatenate(turned))
        else:
            other = swap(state, bit, devices)
            mine = fill(256, state)
            state = jnp.where(
                upper,
                jnp.concatenate([other, mine], axis=1),
                jnp.concatenate([mine, other], axis=1),
            )
        bit *= 2

    def coefficients_of(group):
        rows = len(group) * cen_dev
        return pl.pallas_call(
            functools.partial(row_products, outs, len(group)),
            out_shape=[
                jax.ShapeDtypeStruct((outs, rows), F32),
                jax.ShapeDtypeStruct((3, rows, centres_all), BF16),
            ],
            compiler_params=pltpu.CompilerParams(
                vmem_limit_bytes=(4 << 20) + 24 * rows * centres_all
            ),
            name="row_products",
        )(state, *group)

    groups = [[piece_copy, *pieces[1:]]]
    for bit in held[2:]:
        groups.append([swap(p, bit, devices) for p in [*pieces, *sum(groups[1:], [])]])
    made = [coefficients_of(group) for group in groups]
    coefficients = jnp.concatenate([m[0] for m in made], axis=1)
    parts = [m[1] for m in made]
    for bit in others:
        other = swap(coefficients, bit, devices)
        mine = fill(256, coefficients)
        coefficients = jnp.concatenate([mine, other], axis=1)
    coefficients = fill(half, coefficients)

    kept, sent, kernel_products = apply_products(store, coefficients, own_points, 256, tables)
    for bit in reversed(others):
        came = swap(sent, bit, devices)
        if bit != others[0]:
            summed = kept + came
            width = summed.shape[1] // 2
            kept, sent = summed[:, :width], summed[:, width:]
    scale_total = float(samples_dev * devices) * float(centres_all)
    image = pl.pallas_call(
        functools.partial(image_rows, scale_total, ridge_weight / centres_all),
        out_shape=jax.ShapeDtypeStruct((outs, centres_all), F32),
        compiler_params=pltpu.CompilerParams(
            vmem_limit_bytes=(4 << 20) + 8 * kept.shape[1] * centres_all
        ),
        name="image_rows",
    )(kept, came, kernel_products, *parts)
    bit = 1
    while 2 * bit < devices:
        image = image + swap(image, bit, devices)
        bit *= 2
    more = swap(image, bit, devices)
    own = jax.ShapeDtypeStruct(solution.shape, F32)
    return pl.pallas_call(
        finish,
        out_shape=[own, own, own],
        scratch_shapes=[pltpu.VMEM((outs, centres_all), F32)],
        name="finish",
    )(image, more, state, own_state)


def solution(mesh):
    placed = (
        P("groups", "samp"),
        P(),
        P(),
        P("samp", None),
        P("groups", "samp"),
        P("groups", "samp"),
        P("groups", "samp"),
    )
    return jax.shard_map(
        body,
        mesh=mesh,
        in_specs=placed,
        out_specs=(P("groups", "samp"), P("groups", "samp"), P("groups", "samp")),
        check_vma=False,
    )
```

time: 78.5 us -> 74.1 us (0.944)
  Pallas kernels: 40.5 us -> 34.4 us
  starting transfers between devices: 16.4 us -> 18 us
    pallas_call x5 -> x6, Pallas kernels: 34.1 us -> 28.5 us  [the longest x1 16.1 us: apply_products(): pl.pallas_call(functools.partial(products, outs, stored), out_shape=[half...]
    ppermute x18, starting transfers between devices: 16.4 us -> 18 us  [swap(): return lax.ppermute(value, 'samp', [(i, i ^ bit) for i in range(devices)])]
  transfers between devices with their start and end apart: 18 -> 18, of which waited for: 7 -> 9; matrix products, arithmetic and copies ran while one was open for 1% -> 1% of each run, Pallas kernels for 23% -> 19%
where the time goes in v9:
time: 74.1 us; the launch traced here: 73.8 us
  Pallas kernels  34.4 us (46%)
  waiting for transfers between devices  18.3 us (25%)
  starting transfers between devices  18 us (24%)
  local copies, waits for them, and re-layouts  1.36 us (2%)
  other arithmetic  0.92 us (1%)
  between operations  0.85 us (1%)
    ppermute x18, waiting for transfers between devices, swap(): return lax.ppermute(value, 'samp', [(i, i ^ bit) for i in range(devices)])  18.3 us
    ppermute x18, starting transfers between devices, swap(): return lax.ppermute(value, 'samp', [(i, i ^ bit) for i in range(devices)])  18 us
    pallas_call x1, Pallas kernels, apply_products(): pl.pallas_call(functools.partial(products, outs, stored), out_shape=[half...  16.1 us
    pallas_call x4, Pallas kernels, kernel_rows(): pl.pallas_call(functools.partial(store_rows, first_row, STORED_MIXED), ou...  11.3 us
    pallas_call x2, Pallas kernels, coefficients_of(): pl.pallas_call(functools.partial(row_products, outs, len(group)), out_sha...  3.46 us
    pallas_call x1, Pallas kernels, body(): pl.pallas_call(finish, out_shape=[own, own, own], scratch_shapes=[pltpu.V...  1.77 us
  transfers between devices with their start and end apart: 18, of which 9 were waited for; matrix products, arithmetic and copies ran while one was open for 1% of the time, Pallas kernels for 19%

profile of v9, /device:TPU:0, one launch (start us, length us, event | category | flops | bytes accessed | tf_op | source)
XLA Modules:
  0.0 73.8 jit_solution(17200693480384135236)
XLA Ops:
  0.6 3.1 %collective-permute-start.5 = (f32[64,1024]{1,0:T(8,128)}, f32[64,1024]{1,0:T(8,128)}, u32[]{:S(2)}, u32[]{:S(2)}) collective-permute-start(f32[64,1024]{1,0:T(8,128)} %piece_hbm.1), channel_id=1, source_target_pairs={{0,4},{1,5},{2,6},{3,7},{4,0},{5,1},{6,2},{7,3},{8,12},{9,13},{10,... | collective-permute-start | bytes 786440 | tf_op jit(solution)/shard_map/ppermute | solution.py:29
  3.7 0.0 collective-permute-start.1
  3.7 0.5 collective-permute-start
  4.2 0.9 %collective-permute-done.1 = f32[16,64]{1,0:T(8,128)S(1)} collective-permute-done((f32[16,64]{1,0:T(8,128)}, f32[16,64]{1,0:T(8,128)S(1)}, u32[]{:S(2)}, u32[]{:S(2)}) %collective-permute-start.1) | collective-permute-done | bytes 4128 | tf_op jit(solution)/shard_map/ppermute | solution.py:29
  5.1 0.2 collective-permute-done
  5.3 0.9 %maximum_select_fusion.3.passed_ref = f32[32,128]{1,0:T(8,128)S(1)} fusion(f32[16,64]{1,0:T(8,128)} %residual_hbm.1, f32[16,64]{1,0:T(8,128)S(1)} %collective-permute-done.1, f32[16,64]{1,0:T(8,128)} %direction_hbm.1, f32[16,64]{1,0:T(8,128)S(1)} %collective-permute-done, pred[]{:T(512)S(6)} %ne.15), kind=kLoop, calls=%fused_computation.4 | loop fusion | flops 28672 | bytes 32769 | tf_op jit(solution)/shard_map/jit(_where)/select_n | solution.py:524
  6.1 1.5 %collective-permute-start.2 = (f32[32,128]{1,0:T(8,128)S(1)}, f32[32,128]{1,0:T(8,128)S(1)}, u32[]{:S(2)}, u32[]{:S(2)}) collective-permute-start(f32[32,128]{1,0:T(8,128)S(1)} %maximum_select_fusion.3.passed_ref), channel_id=1, source_target_pairs={{0,2},{1,3},{2,0},{3,1},{4,6},{5,7},{6,4},{7,5},{8,10},{9,11},{10,... | collective-permute-start | bytes 49160 | tf_op jit(solution)/shard_map/ppermute | solution.py:29
  7.7 0.5 collective-permute-start.6
  8.2 1.1 %begin.1 = (s32[16,2048]{1,0:T(8,128)S(1)}, f32[64,1024]{1,0:T(8,128)S(1)}, f32[48,64]{1,0:T(8,128)S(1)}, f32[2,16,1024]{2,1,0:T(8,128)S(1)}, bf16[256,1024]{1,0...) custom-call(s32[16]{0:T(128)} %generator_hbm.1, s32[16]{0:T(128)} %weight_hbm.1, ...), custom_call_target="tpu_custom_call" | custom-call | tf_op jit(solution)/shard_map/begin/pallas_call | solution.py:472
  9.3 0.0 copy-start.1
  9.3 0.7 copy-done.1
  10.0 0.0 copy-start.3
  10.0 2.8 %kernel_rows.4 = (bf16[256,1024]{1,0:T(8,128)(2,1)S(1)}, bf16[256,1024]{1,0:T(8,128)(2,1)S(1)}, f32[32,128]{1,0:T(8,128)S(1)}) custom-call(s32[16,2048]{1,0:T(8,128)S(1)} %get-tuple-element.30.sample_ref, f32[2,16,1024]{2,1,0:T(8,128)S(1)} %get-tuple-element.31.centre_ref, bf16[256,1024]{1,0:T(8,128)(2,1)S(1)} %get-tuple-element.32.rhs_ref, ...), custom_call_target="tpu_custom_call" | custom-call | flops 25165824 | bytes 1048576 | tf_op jit(solution)/shard_map/kernel_rows/pallas_call | solution.py:273
  12.8 0.0 collective-permute-done.5.refs_1_
  12.8 1.6 %collective-permute-start.7 = (f32[64,1024]{1,0:T(8,128)}, f32[64,1024]{1,0:T(8,128)}, u32[]{:S(2)}, u32[]{:S(2)}) collective-permute-start(f32[64,1024]{1,0:T(8,128)} %collective-permute-done.5.refs_1_), channel_id=1, source_target_pairs={{0,2},{1,3},{2,0},{3,1},{4,6},{5,7},{6,4},{7,5},{8,10},{9,11},{10,... | collective-permute-start | bytes 786440 | tf_op jit(solution)/shard_map/ppermute | solution.py:29
  14.4 0.0 collective-permute-done.2
  14.4 0.0 copy-done.3
  14.4 0.5 collective-permute-start.3
  14.9 2.8 %kernel_rows.5 = (bf16[256,1024]{1,0:T(8,128)(2,1)S(1)}, bf16[256,1024]{1,0:T(8,128)(2,1)S(1)}, f32[32,256]{1,0:T(8,128)S(1)}) custom-call(s32[16,2048]{1,0:T(8,128)S(1)} %get-tuple-element.30.sample_ref, f32[2,16,1024]{2,1,0:T(8,128)S(1)} %get-tuple-element.31.centre_ref, bf16[256,1024]{1,0:T(8,128)(2,1)S(1)} %get-tuple-element.32.rhs_ref, ...), custom_call_target="tpu_custom_call" | custom-call | flops 25165824 | bytes 1048576 | tf_op jit(solution)/shard_map/kernel_rows/pallas_call | solution.py:273
  17.7 0.7 collective-permute-done.3
  18.4 2.7 %collective-permute-start.4 = (f32[32,512]{1,0:T(8,128)S(1)}, f32[32,512]{1,0:T(8,128)S(1)}, u32[]{:S(2)}, u32[]{:S(2)}) collective-permute-start(f32[32,512]{1,0:T(8,128)S(1)} %maximum_select_fusion.1.passed_ref), channel_id=1, source_target_pairs={{0,8},{1,9},{2,10},{3,11},{4,12},{5,13},{6,14},{7,15},{8,0},{9,1},... | collective-permute-start | bytes 196616 | tf_op jit(solution)/shard_map/ppermute | solution.py:29
  21.0 0.0 collective-permute-start.8
  21.0 0.5 collective-permute-start.9
  21.5 0.0 collective-permute-done.6.refs_2_
  21.5 0.0 collective-permute-start.10
  21.5 0.3 collective-permute-done.7.refs_3_
  21.9 0.2 collective-permute-start.11
  22.1 0.0 copy-start.2
  22.1 2.8 %kernel_rows.6 = (bf16[256,1024]{1,0:T(8,128)(2,1)S(1)}, bf16[256,1024]{1,0:T(8,128)(2,1)S(1)}, f32[32,512]{1,0:T(8,128)S(1)}) custom-call(s32[16,2048]{1,0:T(8,128)S(1)} %get-tuple-element.30.sample_ref, f32[2,16,1024]{2,1,0:T(8,128)S(1)} %get-tuple-element.31.centre_ref, bf16[256,1024]{1,0:T(8,128)(2,1)S(1)} %get-tuple-element.32.rhs_ref, ...), custom_call_target="tpu_custom_call" | custom-call | flops 25165824 | bytes 1048576 | tf_op jit(solution)/shard_map/kernel_rows/pallas_call | solution.py:273
  24.8 0.0 collective-permute-done.4
  24.9 0.0 copy-start
  24.9 0.0 copy-done.2
  24.9 1.7 %row_products.2 = (f32[16,256]{1,0:T(8,128)S(1)}, bf16[3,256,1024]{2,1,0:T(8,128)(2,1)S(1)}) custom-call(f32[32,1024]{1,0:T(8,128)S(1)} %maximum_select_fusion.state_ref, f32[64,1024]{1,0:T(8,128)S(1)} %copy-done.2, f32[64,1024]{1,0:T(8,128)} %collective-permute-done.5.refs_1_, f32[64,1024]{1,0:T(8,128)} %collective-permute-done.6.refs_2_, ...), custom_call_target="tpu_custom_call" | custom-call | tf_op jit(solution)/shard_map/row_products/pallas_call | solution.py:537
  26.6 0.0 collective-permute-done.8.refs_0_
  26.7 0.0 collective-permute-done.9.refs_1_
  26.7 0.0 collective-permute-done.10.refs_2_
  26.7 0.0 collective-permute-done.11.refs_3_
  26.7 1.7 %row_products.3 = (f32[16,256]{1,0:T(8,128)S(1)}, bf16[3,256,1024]{2,1,0:T(8,128)(2,1)S(1)}) custom-call(f32[32,1024]{1,0:T(8,128)S(1)} %maximum_select_fusion.state_ref, f32[64,1024]{1,0:T(8,128)} %collective-permute-done.8.refs_0_, f32[64,1024]{1,0:T(8,128)} %collective-permute-done.9.refs_1_, f32[64,1024]{1,0:T(8,128)} %collective-permute-done.10.refs_2_, ...), custom_call_target="tpu_custom_call" | custom-call | tf_op jit(solution)/shard_map/row_products/pallas_call | solution.py:537
  28.5 2.5 %collective-permute-start.12 = (f32[16,512]{1,0:T(8,128)S(1)}, f32[16,512]{1,0:T(8,128)S(1)}, u32[]{:S(2)}, u32[]{:S(2)}) collective-permute-start(f32[16,512]{1,0:T(8,128)S(1)} %constant_dynamic-update-slice_fusion.passed_ref), channel_id=1, source_target_pairs={{0,8},{1,9},{2,10},{3,11},{4,12},{5,13},{6,14},{7,15},{8,0},{9,1},... | collective-permute-start | bytes 98312 | tf_op jit(solution)/shard_map/ppermute | solution.py:29
  31.0 3.0 %kernel_rows.7 = (bf16[256,1024]{1,0:T(8,128)(2,1)S(1)}, bf16[256,1024]{1,0:T(8,128)(2,1)S(1)}, f32[16,512]{1,0:T(8,128)S(1)}) custom-call(s32[16,2048]{1,0:T(8,128)S(1)} %get-tuple-element.30.sample_ref, f32[2,16,1024]{2,1,0:T(8,128)S(1)} %get-tuple-element.31.centre_ref, bf16[256,1024]{1,0:T(8,128)(2,1)S(1)} %get-tuple-element.32.rhs_ref, ...), custom_call_target="tpu_custom_call" | custom-call | flops 25165824 | bytes 1048576 | tf_op jit(solution)/shard_map/kernel_rows/pallas_call | solution.py:273
  33.9 0.0 copy-done
  34.0 0.0 collective-permute-done.12
  34.0 16.1 %products.1 = (f32[16,512]{1,0:T(8,128)S(1)}, f32[16,512]{1,0:T(8,128)S(1)}, f32[16,64]{1,0:T(8,128)S(1)}) custom-call(f32[16,1024]{1,0:T(8,128)S(1)} %pad_maximum_fusion.coef_ref, s32[16,2048]{1,0:T(8,128)S(1)} %get-tuple-element.30.sample_ref, f32[2,16,1024]{2,1,0:T(8,128)S(1)} %get-tuple-element.31.centre_ref, ...), custom_call_target="tpu_custom_call" | custom-call | flops 100663296 | bytes 4194304 | tf_op jit(solution)/shard_map/products/pallas_call | solution.py:378
  50.1 1.8 %collective-permute-start.13 = (f32[16,512]{1,0:T(8,128)S(1)}, f32[16,512]{1,0:T(8,128)S(1)}, u32[]{:S(2)}, u32[]{:S(2)}) collective-permute-start(f32[16,512]{1,0:T(8,128)S(1)} %get-tuple-element.52), channel_id=1, source_target_pairs={{0,8},{1,9},{2,10},{3,11},{4,12},{5,13},{6,14},{7,15},{8,0},{9,1},... | collective-permute-start | bytes 98312 | tf_op jit(solution)/shard_map/ppermute | solution.py:29
  51.9 3.4 %collective-permute-done.13.came_ref = f32[16,512]{1,0:T(8,128)S(1)} collective-permute-done((f32[16,512]{1,0:T(8,128)S(1)}, f32[16,512]{1,0:T(8,128)S(1)}, u32[]{:S(2)}, u32[]{:S(2)}) %collective-permute-start.13) | collective-permute-done | bytes 32800 | tf_op jit(solution)/shard_map/ppermute | solution.py:29
  55.3 0.6 image_rows.1
  55.9 0.0 collective-permute-start.14
  55.9 1.3 %collective-permute-done.14 = f32[16,1024]{1,0:T(8,128)S(1)} collective-permute-done((f32[16,1024]{1,0:T(8,128)S(1)}, f32[16,1024]{1,0:T(8,128)S(1)}, u32[]{:S(2)}, u32[]{:S(2)}) %collective-permute-start.14) | collective-permute-done | bytes 65568 | tf_op jit(solution)/shard_map/ppermute | solution.py:29
  57.2 0.8 %collective-permute-start.15 = (f32[16,1024]{1,0:T(8,128)S(1)}, f32[16,1024]{1,0:T(8,128)S(1)}, u32[]{:S(2)}, u32[]{:S(2)}) collective-permute-start(f32[16,1024]{1,0:T(8,128)S(1)} %add.9), channel_id=1, source_target_pairs={{0,2},{1,3},{2,0},{3,1},{4,6},{5,7},{6,4},{7,5},{8,10},{9,11},{10,... | collective-permute-start | bytes 196616 | tf_op jit(solution)/shard_map/ppermute | solution.py:29
  57.9 3.6 %collective-permute-done.15 = f32[16,1024]{1,0:T(8,128)S(1)} collective-permute-done((f32[16,1024]{1,0:T(8,128)S(1)}, f32[16,1024]{1,0:T(8,128)S(1)}, u32[]{:S(2)}, u32[]{:S(2)}) %collective-permute-start.15) | collective-permute-done | bytes 65568 | tf_op jit(solution)/shard_map/ppermute | solution.py:29
  61.5 0.3 collective-permute-start.16
  61.8 4.0 %collective-permute-done.16 = f32[16,1024]{1,0:T(8,128)S(1)} collective-permute-done((f32[16,1024]{1,0:T(8,128)S(1)}, f32[16,1024]{1,0:T(8,128)S(1)}, u32[]{:S(2)}, u32[]{:S(2)}) %collective-permute-start.16) | collective-permute-done | bytes 65568 | tf_op jit(solution)/shard_map/ppermute | solution.py:29
  65.8 0.0 copy-start.4
  65.8 1.5 %collective-permute-start.17 = (f32[16,1024]{1,0:T(8,128)S(1)}, f32[16,1024]{1,0:T(8,128)S(1)}, u32[]{:S(2)}, u32[]{:S(2)}) collective-permute-start(f32[16,1024]{1,0:T(8,128)S(1)} %add.11.image_ref), channel_id=1, source_target_pairs={{0,8},{1,9},{2,10},{3,11},{4,12},{5,13},{6,14},{7,15},{8,0},{9,1},... | collective-permute-start | bytes 196616 | tf_op jit(solution)/shard_map/ppermute | solution.py:29
  67.4 4.1 %collective-permute-done.17.more_ref = f32[16,1024]{1,0:T(8,128)S(1)} collective-permute-done((f32[16,1024]{1,0:T(8,128)S(1)}, f32[16,1024]{1,0:T(8,128)S(1)}, u32[]{:S(2)}, u32[]{:S(2)}) %collective-permute-start.17) | collective-permute-done | bytes 65568 | tf_op jit(solution)/shard_map/ppermute | solution.py:29
  71.5 0.0 copy-start.5
  71.5 0.0 copy-done.4
  71.5 0.6 copy-done.5
  72.1 1.8 %finish.1 = (f32[16,64]{1,0:T(8,128)}, f32[16,64]{1,0:T(8,128)}, f32[16,64]{1,0:T(8,128)}) custom-call(f32[16,1024]{1,0:T(8,128)} %copy-done.4, f32[16,1024]{1,0:T(8,128)} %copy-done.5, f32[32,1024]{1,0:T(8,128)} %copy-done, f32[48,64]{1,0:T(8,128)} %copy-done.3), custom_call_target="tpu_custom_call" | custom-call | tf_op jit(solution)/shard_map/finish/pallas_call | solution.py:583
  (9 shorter events, 0.1 us)
Async XLA Ops:
  0.6 12.1 %collective-permute-start.5 = (f32[64,1024]{1,0:T(8,128)}, f32[64,1024]{1,0:T(8,128)}, u32[]{:S(2)}, u32[]{:S(2)}) collective-permute-start(f32[64,1024]{1,0:T(8,128)} %piece_hbm.1), channel_id=1, source_target_pairs={{0,4},{1,5},{2,6},{3,7},{4,0},{5,1},{6,2},{7,3},{8,12},{9,13},{10,... | collective-permute-start | bytes 786440 | tf_op jit(solution)/shard_map/ppermute | solution.py:29
  3.7 1.4 %collective-permute-start.1 = (f32[16,64]{1,0:T(8,128)}, f32[16,64]{1,0:T(8,128)S(1)}, u32[]{:S(2)}, u32[]{:S(2)}) collective-permute-start(f32[16,64]{1,0:T(8,128)} %residual_hbm.1), channel_id=1, source_target_pairs={{0,1},{1,0},{2,3},{3,2},{4,5},{5,4},{6,7},{7,6},{8,9},{9,8},{10,11... | collective-permute-start | bytes 12296 | tf_op jit(solution)/shard_map/ppermute | solution.py:29
  3.7 1.5 %collective-permute-start = (f32[16,64]{1,0:T(8,128)}, f32[16,64]{1,0:T(8,128)S(1)}, u32[]{:S(2)}, u32[]{:S(2)}) collective-permute-start(f32[16,64]{1,0:T(8,128)} %direction_hbm.1), channel_id=1, source_target_pairs={{0,1},{1,0},{2,3},{3,2},{4,5},{5,4},{6,7},{7,6},{8,9},{9,8},{10,11... | collective-permute-start | bytes 12296 | tf_op jit(solution)/shard_map/ppermute | solution.py:29
  6.1 8.2 %collective-permute-start.2 = (f32[32,128]{1,0:T(8,128)S(1)}, f32[32,128]{1,0:T(8,128)S(1)}, u32[]{:S(2)}, u32[]{:S(2)}) collective-permute-start(f32[32,128]{1,0:T(8,128)S(1)} %maximum_select_fusion.3.passed_ref), channel_id=1, source_target_pairs={{0,2},{1,3},{2,0},{3,1},{4,6},{5,7},{6,4},{7,5},{8,10},{9,11},{10,... | collective-permute-start | bytes 49160 | tf_op jit(solution)/shard_map/ppermute | solution.py:29
  7.7 13.9 %collective-permute-start.6 = (f32[64,1024]{1,0:T(8,128)}, f32[64,1024]{1,0:T(8,128)}, u32[]{:S(2)}, u32[]{:S(2)}) collective-permute-start(f32[64,1024]{1,0:T(8,128)} %piece_hbm.1), channel_id=1, source_target_pairs={{0,2},{1,3},{2,0},{3,1},{4,6},{5,7},{6,4},{7,5},{8,10},{9,11},{10,... | collective-permute-start | bytes 786440 | tf_op jit(solution)/shard_map/ppermute | solution.py:29
  9.3 0.7 copy-start.1
  10.0 4.4 %copy-start.3 = (f32[48,64]{1,0:T(8,128)}, f32[48,64]{1,0:T(8,128)S(1)}, u32[]{:S(2)}) copy-start(f32[48,64]{1,0:T(8,128)S(1)} %get-tuple-element.56.own_ref) | copy-start | bytes 36868
  12.8 9.1 %collective-permute-start.7 = (f32[64,1024]{1,0:T(8,128)}, f32[64,1024]{1,0:T(8,128)}, u32[]{:S(2)}, u32[]{:S(2)}) collective-permute-start(f32[64,1024]{1,0:T(8,128)} %collective-permute-done.5.refs_1_), channel_id=1, source_target_pairs={{0,2},{1,3},{2,0},{3,1},{4,6},{5,7},{6,4},{7,5},{8,10},{9,11},{10,... | collective-permute-start | bytes 786440 | tf_op jit(solution)/shard_map/ppermute | solution.py:29
  14.4 4.0 %collective-permute-start.3 = (f32[32,256]{1,0:T(8,128)S(1)}, f32[32,256]{1,0:T(8,128)S(1)}, u32[]{:S(2)}, u32[]{:S(2)}) collective-permute-start(f32[32,256]{1,0:T(8,128)S(1)} %maximum_select_fusion.2.passed_ref), channel_id=1, source_target_pairs={{0,4},{1,5},{2,6},{3,7},{4,0},{5,1},{6,2},{7,3},{8,12},{9,13},{10,... | collective-permute-start | bytes 98312 | tf_op jit(solution)/shard_map/ppermute | solution.py:29
  18.4 6.5 %collective-permute-start.4 = (f32[32,512]{1,0:T(8,128)S(1)}, f32[32,512]{1,0:T(8,128)S(1)}, u32[]{:S(2)}, u32[]{:S(2)}) collective-permute-start(f32[32,512]{1,0:T(8,128)S(1)} %maximum_select_fusion.1.passed_ref), channel_id=1, source_target_pairs={{0,8},{1,9},{2,10},{3,11},{4,12},{5,13},{6,14},{7,15},{8,0},{9,1},... | collective-permute-start | bytes 196616 | tf_op jit(solution)/shard_map/ppermute | solution.py:29
  21.0 5.6 %collective-permute-start.8 = (f32[64,1024]{1,0:T(8,128)}, f32[64,1024]{1,0:T(8,128)}, u32[]{:S(2)}, u32[]{:S(2)}) collective-permute-start(f32[64,1024]{1,0:T(8,128)} %piece_hbm.1), channel_id=1, source_target_pairs={{0,1},{1,0},{2,3},{3,2},{4,5},{5,4},{6,7},{7,6},{8,9},{9,8},{10,11... | collective-permute-start | bytes 786440 | tf_op jit(solution)/shard_map/ppermute | solution.py:29
  21.0 5.6 %collective-permute-start.9 = (f32[64,1024]{1,0:T(8,128)}, f32[64,1024]{1,0:T(8,128)}, u32[]{:S(2)}, u32[]{:S(2)}) collective-permute-start(f32[64,1024]{1,0:T(8,128)} %collective-permute-done.5.refs_1_), channel_id=1, source_target_pairs={{0,1},{1,0},{2,3},{3,2},{4,5},{5,4},{6,7},{7,6},{8,9},{9,8},{10,11... | collective-permute-start | bytes 786440 | tf_op jit(solution)/shard_map/ppermute | solution.py:29
  21.5 5.1 %collective-permute-start.10 = (f32[64,1024]{1,0:T(8,128)}, f32[64,1024]{1,0:T(8,128)}, u32[]{:S(2)}, u32[]{:S(2)}) collective-permute-start(f32[64,1024]{1,0:T(8,128)} %collective-permute-done.6.refs_2_), channel_id=1, source_target_pairs={{0,1},{1,0},{2,3},{3,2},{4,5},{5,4},{6,7},{7,6},{8,9},{9,8},{10,11... | collective-permute-start | bytes 786440 | tf_op jit(solution)/shard_map/ppermute | solution.py:29
  21.9 4.8 %collective-permute-start.11 = (f32[64,1024]{1,0:T(8,128)}, f32[64,1024]{1,0:T(8,128)}, u32[]{:S(2)}, u32[]{:S(2)}) collective-permute-start(f32[64,1024]{1,0:T(8,128)} %collective-permute-done.7.refs_3_), channel_id=1, source_target_pairs={{0,1},{1,0},{2,3},{3,2},{4,5},{5,4},{6,7},{7,6},{8,9},{9,8},{10,11... | collective-permute-start | bytes 786440 | tf_op jit(solution)/shard_map/ppermute | solution.py:29
  22.1 2.8 %copy-start.2 = (f32[64,1024]{1,0:T(8,128)S(1)}, f32[64,1024]{1,0:T(8,128)}, u32[]{:S(2)}) copy-start(f32[64,1024]{1,0:T(8,128)} %copy-done.1) | copy-start | bytes 786436
  24.9 9.1 %copy-start = (f32[32,1024]{1,0:T(8,128)}, f32[32,1024]{1,0:T(8,128)S(1)}, u32[]{:S(2)}) copy-start(f32[32,1024]{1,0:T(8,128)S(1)} %maximum_select_fusion.state_ref) | copy-start | bytes 393220
  28.5 5.5 %collective-permute-start.12 = (f32[16,512]{1,0:T(8,128)S(1)}, f32[16,512]{1,0:T(8,128)S(1)}, u32[]{:S(2)}, u32[]{:S(2)}) collective-permute-start(f32[16,512]{1,0:T(8,128)S(1)} %constant_dynamic-update-slice_fusion.passed_ref), channel_id=1, source_target_pairs={{0,8},{1,9},{2,10},{3,11},{4,12},{5,13},{6,14},{7,15},{8,0},{9,1},... | collective-permute-start | bytes 98312 | tf_op jit(solution)/shard_map/ppermute | solution.py:29
  50.1 5.2 %collective-permute-start.13 = (f32[16,512]{1,0:T(8,128)S(1)}, f32[16,512]{1,0:T(8,128)S(1)}, u32[]{:S(2)}, u32[]{:S(2)}) collective-permute-start(f32[16,512]{1,0:T(8,128)S(1)} %get-tuple-element.52), channel_id=1, source_target_pairs={{0,8},{1,9},{2,10},{3,11},{4,12},{5,13},{6,14},{7,15},{8,0},{9,1},... | collective-permute-start | bytes 98312 | tf_op jit(solution)/shard_map/ppermute | solution.py:29
  55.9 1.3 %collective-permute-start.14 = (f32[16,1024]{1,0:T(8,128)S(1)}, f32[16,1024]{1,0:T(8,128)S(1)}, u32[]{:S(2)}, u32[]{:S(2)}) collective-permute-start(f32[16,1024]{1,0:T(8,128)S(1)} %image_rows.1), channel_id=1, source_target_pairs={{0,1},{1,0},{2,3},{3,2},{4,5},{5,4},{6,7},{7,6},{8,9},{9,8},{10,11... | collective-permute-start | bytes 196616 | tf_op jit(solution)/shard_map/ppermute | solution.py:29
  57.2 4.3 %collective-permute-start.15 = (f32[16,1024]{1,0:T(8,128)S(1)}, f32[16,1024]{1,0:T(8,128)S(1)}, u32[]{:S(2)}, u32[]{:S(2)}) collective-permute-start(f32[16,1024]{1,0:T(8,128)S(1)} %add.9), channel_id=1, source_target_pairs={{0,2},{1,3},{2,0},{3,1},{4,6},{5,7},{6,4},{7,5},{8,10},{9,11},{10,... | collective-permute-start | bytes 196616 | tf_op jit(solution)/shard_map/ppermute | solution.py:29
  61.5 4.3 %collective-permute-start.16 = (f32[16,1024]{1,0:T(8,128)S(1)}, f32[16,1024]{1,0:T(8,128)S(1)}, u32[]{:S(2)}, u32[]{:S(2)}) collective-permute-start(f32[16,1024]{1,0:T(8,128)S(1)} %add.10), channel_id=1, source_target_pairs={{0,4},{1,5},{2,6},{3,7},{4,0},{5,1},{6,2},{7,3},{8,12},{9,13},{10,... | collective-permute-start | bytes 196616 | tf_op jit(solution)/shard_map/ppermute | solution.py:29
  65.8 5.6 %copy-start.4 = (f32[16,1024]{1,0:T(8,128)}, f32[16,1024]{1,0:T(8,128)S(1)}, u32[]{:S(2)}) copy-start(f32[16,1024]{1,0:T(8,128)S(1)} %add.11.image_ref) | copy-start | bytes 196612
  65.8 5.6 %collective-permute-start.17 = (f32[16,1024]{1,0:T(8,128)S(1)}, f32[16,1024]{1,0:T(8,128)S(1)}, u32[]{:S(2)}, u32[]{:S(2)}) collective-permute-start(f32[16,1024]{1,0:T(8,128)S(1)} %add.11.image_ref), channel_id=1, source_target_pairs={{0,8},{1,9},{2,10},{3,11},{4,12},{5,13},{6,14},{7,15},{8,0},{9,1},... | collective-permute-start | bytes 196616 | tf_op jit(solution)/shard_map/ppermute | solution.py:29
  71.5 0.6 copy-start.5

commit v10 on v9

--- a/solution.py
+++ b/solution.py
@@ -16,7 +16,7 @@
 HELD_BYTES = 16 << 20
 WIDTH = 256
 STORED_MIXED = 16
-PRODUCTS_MIXED = 4
+PRODUCTS_MIXED = 10
 VMEM = pl.BlockSpec(memory_space=pltpu.VMEM)
 FREE = pl.BlockSpec(memory_space=pl.ANY)
 HBM = pl.BlockSpec(memory_space=pltpu.HBM)
@@ -274,7 +274,7 @@
         functools.partial(store_rows, first_row, STORED_MIXED),
         out_shape=[kept, kept, jax.ShapeDtypeStruct(passed.shape, passed.dtype)],
         scratch_shapes=[pltpu.VMEM((max(1, STORED_MIXED), min(256, rows), 16), BF16)],
-        compiler_params=pltpu.CompilerParams(vmem_limit_bytes=16 << 20),
+        compiler_params=pltpu.CompilerParams(vmem_limit_bytes=10 << 20),
         cost_estimate=pl.CostEstimate(
             flops=6 * dims * rows * centres_all,
             bytes_accessed=4 * rows * centres_all,
@@ -385,7 +385,7 @@
             *[made] * 4,
         ],
         compiler_params=pltpu.CompilerParams(
-            vmem_limit_bytes=(16 << 20) + 16 * block_rows * centres_all
+            vmem_limit_bytes=(14 << 20) + 16 * block_rows * centres_all
         ),
         cost_estimate=pl.CostEstimate(
             flops=6 * dims * rows * centres_all,
@@ -487,7 +487,7 @@
             pltpu.SMEM((dims,), jnp.int32),
             pltpu.SemaphoreType.DMA((7,)),
         ],
-        compiler_params=pltpu.CompilerParams(vmem_limit_bytes=32 << 20),
+        compiler_params=pltpu.CompilerParams(vmem_limit_bytes=(6 << 20) + 1200 * centres_all),
         name="begin",
     )(*in_hbm(generator, weight_index, samples, preconditioner, solution, residual, direction))
     own_points = tables.pop()[:, :cen_dev]
@@ -584,6 +584,7 @@
         finish,
         out_shape=[own, own, own],
         scratch_shapes=[pltpu.VMEM((outs, centres_all), F32)],
+        compiler_params=pltpu.CompilerParams(vmem_limit_bytes=(2 << 20) + 512 * centres_all),
         name="finish",
     )(image, more, state, own_state)
 

time: 74.1 us -> 71.5 us (0.965)
  Pallas kernels: 34.4 us -> 32.4 us
    pallas_call x1, Pallas kernels: 16.1 us -> 15.1 us  [apply_products(): pl.pallas_call(functools.partial(products, outs, stored), out_shape=[half...]
    pallas_call x1, Pallas kernels: 1.77 us -> 0.79 us  [body(): pl.pallas_call(finish, out_shape=[own, own, own], scratch_shapes=[pltpu.V...]
  transfers between devices with their start and end apart: 18 -> 18, of which waited for: 9 -> 9; matrix products, arithmetic and copies ran while one was open for 1% -> 1% of each run, Pallas kernels for 19% -> 20%
where the time goes in v10:
time: 71.5 us; the launch traced here: 71.2 us
  Pallas kernels  32.4 us (45%)
  waiting for transfers between devices  18.4 us (26%)
  starting transfers between devices  17.9 us (25%)
  other arithmetic  0.92 us (1%)
  between operations  0.82 us (1%)
  local copies, waits for them, and re-layouts  0.73 us (1%)
    ppermute x18, waiting for transfers between devices, swap(): return lax.ppermute(value, 'samp', [(i, i ^ bit) for i in range(devices)])  18.4 us
    ppermute x18, starting transfers between devices, swap(): return lax.ppermute(value, 'samp', [(i, i ^ bit) for i in range(devices)])  17.9 us
    pallas_call x1, Pallas kernels, apply_products(): pl.pallas_call(functools.partial(products, outs, stored), out_shape=[half...  15.1 us
    pallas_call x4, Pallas kernels, kernel_rows(): pl.pallas_call(functools.partial(store_rows, first_row, STORED_MIXED), ou...  11.4 us
    pallas_call x2, Pallas kernels, coefficients_of(): pl.pallas_call(functools.partial(row_products, outs, len(group)), out_sha...  3.42 us
  transfers between devices with their start and end apart: 18, of which 9 were waited for; matrix products, arithmetic and copies ran while one was open for 1% of the time, Pallas kernels for 20%

profile of v10, /device:TPU:0, one launch (start us, length us, event | category | flops | bytes accessed | tf_op | source)
XLA Modules:
  0.0 71.2 jit_solution(3303755209074286956)
XLA Ops:
  0.6 3.1 %collective-permute-start.5 = (f32[64,1024]{1,0:T(8,128)}, f32[64,1024]{1,0:T(8,128)}, u32[]{:S(2)}, u32[]{:S(2)}) collective-permute-start(f32[64,1024]{1,0:T(8,128)} %piece_hbm.1), channel_id=1, source_target_pairs={{0,4},{1,5},{2,6},{3,7},{4,0},{5,1},{6,2},{7,3},{8,12},{9,13},{10,... | collective-permute-start | bytes 786440 | tf_op jit(solution)/shard_map/ppermute | solution.py:29
  3.7 0.0 collective-permute-start.1
  3.7 0.5 collective-permute-start
  4.2 0.9 %collective-permute-done.1 = f32[16,64]{1,0:T(8,128)S(1)} collective-permute-done((f32[16,64]{1,0:T(8,128)}, f32[16,64]{1,0:T(8,128)S(1)}, u32[]{:S(2)}, u32[]{:S(2)}) %collective-permute-start.1) | collective-permute-done | bytes 4128 | tf_op jit(solution)/shard_map/ppermute | solution.py:29
  5.1 0.2 collective-permute-done
  5.3 0.9 %maximum_select_fusion.3.passed_ref = f32[32,128]{1,0:T(8,128)S(1)} fusion(f32[16,64]{1,0:T(8,128)} %residual_hbm.1, f32[16,64]{1,0:T(8,128)S(1)} %collective-permute-done.1, f32[16,64]{1,0:T(8,128)} %direction_hbm.1, f32[16,64]{1,0:T(8,128)S(1)} %collective-permute-done, pred[]{:T(512)S(6)} %ne.15), kind=kLoop, calls=%fused_computation.4 | loop fusion | flops 28672 | bytes 32769 | tf_op jit(solution)/shard_map/jit(_where)/select_n | solution.py:524
  6.1 1.5 %collective-permute-start.2 = (f32[32,128]{1,0:T(8,128)S(1)}, f32[32,128]{1,0:T(8,128)S(1)}, u32[]{:S(2)}, u32[]{:S(2)}) collective-permute-start(f32[32,128]{1,0:T(8,128)S(1)} %maximum_select_fusion.3.passed_ref), channel_id=1, source_target_pairs={{0,2},{1,3},{2,0},{3,1},{4,6},{5,7},{6,4},{7,5},{8,10},{9,11},{10,... | collective-permute-start | bytes 49160 | tf_op jit(solution)/shard_map/ppermute | solution.py:29
  7.7 0.5 collective-permute-start.6
  8.2 1.1 %begin.1 = (s32[16,2048]{1,0:T(8,128)S(1)}, f32[64,1024]{1,0:T(8,128)S(1)}, f32[48,64]{1,0:T(8,128)S(1)}, f32[2,16,1024]{2,1,0:T(8,128)S(1)}, bf16[256,1024]{1,0...) custom-call(s32[16]{0:T(128)} %generator_hbm.1, s32[16]{0:T(128)} %weight_hbm.1, ...), custom_call_target="tpu_custom_call" | custom-call | tf_op jit(solution)/shard_map/begin/pallas_call | solution.py:472
  9.3 0.0 copy-start
  9.3 0.7 copy-done
  10.0 2.8 %kernel_rows.4 = (bf16[256,1024]{1,0:T(8,128)(2,1)S(1)}, bf16[256,1024]{1,0:T(8,128)(2,1)S(1)}, f32[32,128]{1,0:T(8,128)S(1)}) custom-call(s32[16,2048]{1,0:T(8,128)S(1)} %get-tuple-element.30.sample_ref, f32[2,16,1024]{2,1,0:T(8,128)S(1)} %get-tuple-element.31.centre_ref, bf16[256,1024]{1,0:T(8,128)(2,1)S(1)} %get-tuple-element.32.rhs_ref, ...), custom_call_target="tpu_custom_call" | custom-call | flops 25165824 | bytes 1048576 | tf_op jit(solution)/shard_map/kernel_rows/pallas_call | solution.py:273
  12.8 0.0 collective-permute-done.5.refs_1_
  12.8 1.6 %collective-permute-start.7 = (f32[64,1024]{1,0:T(8,128)}, f32[64,1024]{1,0:T(8,128)}, u32[]{:S(2)}, u32[]{:S(2)}) collective-permute-start(f32[64,1024]{1,0:T(8,128)} %collective-permute-done.5.refs_1_), channel_id=1, source_target_pairs={{0,2},{1,3},{2,0},{3,1},{4,6},{5,7},{6,4},{7,5},{8,10},{9,11},{10,... | collective-permute-start | bytes 786440 | tf_op jit(solution)/shard_map/ppermute | solution.py:29
  14.4 0.0 collective-permute-done.2
  14.4 0.5 collective-permute-start.3
  14.9 2.8 %kernel_rows.5 = (bf16[256,1024]{1,0:T(8,128)(2,1)S(1)}, bf16[256,1024]{1,0:T(8,128)(2,1)S(1)}, f32[32,256]{1,0:T(8,128)S(1)}) custom-call(s32[16,2048]{1,0:T(8,128)S(1)} %get-tuple-element.30.sample_ref, f32[2,16,1024]{2,1,0:T(8,128)S(1)} %get-tuple-element.31.centre_ref, bf16[256,1024]{1,0:T(8,128)(2,1)S(1)} %get-tuple-element.32.rhs_ref, ...), custom_call_target="tpu_custom_call" | custom-call | flops 25165824 | bytes 1048576 | tf_op jit(solution)/shard_map/kernel_rows/pallas_call | solution.py:273
  17.7 0.7 collective-permute-done.3
  18.4 2.7 %collective-permute-start.4 = (f32[32,512]{1,0:T(8,128)S(1)}, f32[32,512]{1,0:T(8,128)S(1)}, u32[]{:S(2)}, u32[]{:S(2)}) collective-permute-start(f32[32,512]{1,0:T(8,128)S(1)} %maximum_select_fusion.1.passed_ref), channel_id=1, source_target_pairs={{0,8},{1,9},{2,10},{3,11},{4,12},{5,13},{6,14},{7,15},{8,0},{9,1},... | collective-permute-start | bytes 196616 | tf_op jit(solution)/shard_map/ppermute | solution.py:29
  21.0 0.0 collective-permute-start.8
  21.0 0.5 collective-permute-start.9
  21.5 0.0 collective-permute-done.6.refs_2_
  21.6 0.0 collective-permute-start.10
  21.6 0.3 collective-permute-done.7.refs_3_
  21.9 0.2 collective-permute-start.11
  22.1 0.0 copy-start.1
  22.1 2.8 %kernel_rows.6 = (bf16[256,1024]{1,0:T(8,128)(2,1)S(1)}, bf16[256,1024]{1,0:T(8,128)(2,1)S(1)}, f32[32,512]{1,0:T(8,128)S(1)}) custom-call(s32[16,2048]{1,0:T(8,128)S(1)} %get-tuple-element.30.sample_ref, f32[2,16,1024]{2,1,0:T(8,128)S(1)} %get-tuple-element.31.centre_ref, bf16[256,1024]{1,0:T(8,128)(2,1)S(1)} %get-tuple-element.32.rhs_ref, ...), custom_call_target="tpu_custom_call" | custom-call | flops 25165824 | bytes 1048576 | tf_op jit(solution)/shard_map/kernel_rows/pallas_call | solution.py:273
  24.9 0.0 collective-permute-done.4
  24.9 0.0 copy-done.1
  24.9 1.7 %row_products.2 = (f32[16,256]{1,0:T(8,128)S(1)}, bf16[3,256,1024]{2,1,0:T(8,128)(2,1)S(1)}) custom-call(f32[32,1024]{1,0:T(8,128)S(1)} %maximum_select_fusion.state_ref, f32[64,1024]{1,0:T(8,128)S(1)} %copy-done.1, f32[64,1024]{1,0:T(8,128)} %collective-permute-done.5.refs_1_, f32[64,1024]{1,0:T(8,128)} %collective-permute-done.6.refs_2_, ...), custom_call_target="tpu_custom_call" | custom-call | tf_op jit(solution)/shard_map/row_products/pallas_call | solution.py:537
  26.6 0.0 collective-permute-done.8.refs_0_
  26.7 0.0 collective-permute-done.9.refs_1_
  26.7 0.0 collective-permute-done.10.refs_2_
  26.7 0.0 collective-permute-done.11.refs_3_
  26.7 1.7 %row_products.3 = (f32[16,256]{1,0:T(8,128)S(1)}, bf16[3,256,1024]{2,1,0:T(8,128)(2,1)S(1)}) custom-call(f32[32,1024]{1,0:T(8,128)S(1)} %maximum_select_fusion.state_ref, f32[64,1024]{1,0:T(8,128)} %collective-permute-done.8.refs_0_, f32[64,1024]{1,0:T(8,128)} %collective-permute-done.9.refs_1_, f32[64,1024]{1,0:T(8,128)} %collective-permute-done.10.refs_2_, ...), custom_call_target="tpu_custom_call" | custom-call | tf_op jit(solution)/shard_map/row_products/pallas_call | solution.py:537
  28.5 2.5 %collective-permute-start.12 = (f32[16,512]{1,0:T(8,128)S(1)}, f32[16,512]{1,0:T(8,128)S(1)}, u32[]{:S(2)}, u32[]{:S(2)}) collective-permute-start(f32[16,512]{1,0:T(8,128)S(1)} %constant_dynamic-update-slice_fusion.passed_ref), channel_id=1, source_target_pairs={{0,8},{1,9},{2,10},{3,11},{4,12},{5,13},{6,14},{7,15},{8,0},{9,1},... | collective-permute-start | bytes 98312 | tf_op jit(solution)/shard_map/ppermute | solution.py:29
  30.9 3.0 %kernel_rows.7 = (bf16[256,1024]{1,0:T(8,128)(2,1)S(1)}, bf16[256,1024]{1,0:T(8,128)(2,1)S(1)}, f32[16,512]{1,0:T(8,128)S(1)}) custom-call(s32[16,2048]{1,0:T(8,128)S(1)} %get-tuple-element.30.sample_ref, f32[2,16,1024]{2,1,0:T(8,128)S(1)} %get-tuple-element.31.centre_ref, bf16[256,1024]{1,0:T(8,128)(2,1)S(1)} %get-tuple-element.32.rhs_ref, ...), custom_call_target="tpu_custom_call" | custom-call | flops 25165824 | bytes 1048576 | tf_op jit(solution)/shard_map/kernel_rows/pallas_call | solution.py:273
  33.9 0.0 collective-permute-done.12
  34.0 15.1 %products.1 = (f32[16,512]{1,0:T(8,128)S(1)}, f32[16,512]{1,0:T(8,128)S(1)}, f32[16,64]{1,0:T(8,128)S(1)}) custom-call(f32[16,1024]{1,0:T(8,128)S(1)} %pad_maximum_fusion.coef_ref, s32[16,2048]{1,0:T(8,128)S(1)} %get-tuple-element.30.sample_ref, f32[2,16,1024]{2,1,0:T(8,128)S(1)} %get-tuple-element.31.centre_ref, ...), custom_call_target="tpu_custom_call" | custom-call | flops 100663296 | bytes 4194304 | tf_op jit(solution)/shard_map/products/pallas_call | solution.py:378
  49.0 1.8 %collective-permute-start.13 = (f32[16,512]{1,0:T(8,128)S(1)}, f32[16,512]{1,0:T(8,128)S(1)}, u32[]{:S(2)}, u32[]{:S(2)}) collective-permute-start(f32[16,512]{1,0:T(8,128)S(1)} %get-tuple-element.52), channel_id=1, source_target_pairs={{0,8},{1,9},{2,10},{3,11},{4,12},{5,13},{6,14},{7,15},{8,0},{9,1},... | collective-permute-start | bytes 98312 | tf_op jit(solution)/shard_map/ppermute | solution.py:29
  50.8 3.4 %collective-permute-done.13.came_ref = f32[16,512]{1,0:T(8,128)S(1)} collective-permute-done((f32[16,512]{1,0:T(8,128)S(1)}, f32[16,512]{1,0:T(8,128)S(1)}, u32[]{:S(2)}, u32[]{:S(2)}) %collective-permute-start.13) | collective-permute-done | bytes 32800 | tf_op jit(solution)/shard_map/ppermute | solution.py:29
  54.2 0.6 image_rows.1
  54.8 0.0 collective-permute-start.14
  54.8 1.3 %collective-permute-done.14 = f32[16,1024]{1,0:T(8,128)S(1)} collective-permute-done((f32[16,1024]{1,0:T(8,128)S(1)}, f32[16,1024]{1,0:T(8,128)S(1)}, u32[]{:S(2)}, u32[]{:S(2)}) %collective-permute-start.14) | collective-permute-done | bytes 65568 | tf_op jit(solution)/shard_map/ppermute | solution.py:29
  56.1 0.8 %collective-permute-start.15 = (f32[16,1024]{1,0:T(8,128)S(1)}, f32[16,1024]{1,0:T(8,128)S(1)}, u32[]{:S(2)}, u32[]{:S(2)}) collective-permute-start(f32[16,1024]{1,0:T(8,128)S(1)} %add.9), channel_id=1, source_target_pairs={{0,2},{1,3},{2,0},{3,1},{4,6},{5,7},{6,4},{7,5},{8,10},{9,11},{10,... | collective-permute-start | bytes 196616 | tf_op jit(solution)/shard_map/ppermute | solution.py:29
  56.9 3.5 %collective-permute-done.15 = f32[16,1024]{1,0:T(8,128)S(1)} collective-permute-done((f32[16,1024]{1,0:T(8,128)S(1)}, f32[16,1024]{1,0:T(8,128)S(1)}, u32[]{:S(2)}, u32[]{:S(2)}) %collective-permute-start.15) | collective-permute-done | bytes 65568 | tf_op jit(solution)/shard_map/ppermute | solution.py:29
  60.5 0.3 collective-permute-start.16
  60.7 4.1 %collective-permute-done.16 = f32[16,1024]{1,0:T(8,128)S(1)} collective-permute-done((f32[16,1024]{1,0:T(8,128)S(1)}, f32[16,1024]{1,0:T(8,128)S(1)}, u32[]{:S(2)}, u32[]{:S(2)}) %collective-permute-start.16) | collective-permute-done | bytes 65568 | tf_op jit(solution)/shard_map/ppermute | solution.py:29
  64.8 1.5 %collective-permute-start.17 = (f32[16,1024]{1,0:T(8,128)S(1)}, f32[16,1024]{1,0:T(8,128)S(1)}, u32[]{:S(2)}, u32[]{:S(2)}) collective-permute-start(f32[16,1024]{1,0:T(8,128)S(1)} %add.11.image_ref), channel_id=1, source_target_pairs={{0,8},{1,9},{2,10},{3,11},{4,12},{5,13},{6,14},{7,15},{8,0},{9,1},... | collective-permute-start | bytes 196616 | tf_op jit(solution)/shard_map/ppermute | solution.py:29
  66.3 4.1 %collective-permute-done.17.more_ref = f32[16,1024]{1,0:T(8,128)S(1)} collective-permute-done((f32[16,1024]{1,0:T(8,128)S(1)}, f32[16,1024]{1,0:T(8,128)S(1)}, u32[]{:S(2)}, u32[]{:S(2)}) %collective-permute-start.17) | collective-permute-done | bytes 65568 | tf_op jit(solution)/shard_map/ppermute | solution.py:29
  70.4 0.8 %finish.1 = (f32[16,64]{1,0:T(8,128)}, f32[16,64]{1,0:T(8,128)}, f32[16,64]{1,0:T(8,128)}) custom-call(f32[16,1024]{1,0:T(8,128)S(1)} %add.11.image_ref, f32[16,1024]{1,0:T(8,128)S(1)} %collective-permute-done.17.more_ref, f32[32,1024]{1,0:T(8,128)S(1)} %maximum_select_fusion.state_ref, f32[48,64]{1,0:T(8,128)S(1)} %get-tuple-element.56.own_ref), custom_call_target="tpu_custom_call" | custom-call | tf_op jit(solution)/shard_map/finish/pallas_call | solution.py:583
  (9 shorter events, 0.1 us)
Async XLA Ops:
  0.6 12.2 %collective-permute-start.5 = (f32[64,1024]{1,0:T(8,128)}, f32[64,1024]{1,0:T(8,128)}, u32[]{:S(2)}, u32[]{:S(2)}) collective-permute-start(f32[64,1024]{1,0:T(8,128)} %piece_hbm.1), channel_id=1, source_target_pairs={{0,4},{1,5},{2,6},{3,7},{4,0},{5,1},{6,2},{7,3},{8,12},{9,13},{10,... | collective-permute-start | bytes 786440 | tf_op jit(solution)/shard_map/ppermute | solution.py:29
  3.7 1.4 %collective-permute-start.1 = (f32[16,64]{1,0:T(8,128)}, f32[16,64]{1,0:T(8,128)S(1)}, u32[]{:S(2)}, u32[]{:S(2)}) collective-permute-start(f32[16,64]{1,0:T(8,128)} %residual_hbm.1), channel_id=1, source_target_pairs={{0,1},{1,0},{2,3},{3,2},{4,5},{5,4},{6,7},{7,6},{8,9},{9,8},{10,11... | collective-permute-start | bytes 12296 | tf_op jit(solution)/shard_map/ppermute | solution.py:29
  3.7 1.5 %collective-permute-start = (f32[16,64]{1,0:T(8,128)}, f32[16,64]{1,0:T(8,128)S(1)}, u32[]{:S(2)}, u32[]{:S(2)}) collective-permute-start(f32[16,64]{1,0:T(8,128)} %direction_hbm.1), channel_id=1, source_target_pairs={{0,1},{1,0},{2,3},{3,2},{4,5},{5,4},{6,7},{7,6},{8,9},{9,8},{10,11... | collective-permute-start | bytes 12296 | tf_op jit(solution)/shard_map/ppermute | solution.py:29
  6.1 8.3 %collective-permute-start.2 = (f32[32,128]{1,0:T(8,128)S(1)}, f32[32,128]{1,0:T(8,128)S(1)}, u32[]{:S(2)}, u32[]{:S(2)}) collective-permute-start(f32[32,128]{1,0:T(8,128)S(1)} %maximum_select_fusion.3.passed_ref), channel_id=1, source_target_pairs={{0,2},{1,3},{2,0},{3,1},{4,6},{5,7},{6,4},{7,5},{8,10},{9,11},{10,... | collective-permute-start | bytes 49160 | tf_op jit(solution)/shard_map/ppermute | solution.py:29
  7.7 13.9 %collective-permute-start.6 = (f32[64,1024]{1,0:T(8,128)}, f32[64,1024]{1,0:T(8,128)}, u32[]{:S(2)}, u32[]{:S(2)}) collective-permute-start(f32[64,1024]{1,0:T(8,128)} %piece_hbm.1), channel_id=1, source_target_pairs={{0,2},{1,3},{2,0},{3,1},{4,6},{5,7},{6,4},{7,5},{8,10},{9,11},{10,... | collective-permute-start | bytes 786440 | tf_op jit(solution)/shard_map/ppermute | solution.py:29
  9.3 0.7 copy-start
  12.8 9.1 %collective-permute-start.7 = (f32[64,1024]{1,0:T(8,128)}, f32[64,1024]{1,0:T(8,128)}, u32[]{:S(2)}, u32[]{:S(2)}) collective-permute-start(f32[64,1024]{1,0:T(8,128)} %collective-permute-done.5.refs_1_), channel_id=1, source_target_pairs={{0,2},{1,3},{2,0},{3,1},{4,6},{5,7},{6,4},{7,5},{8,10},{9,11},{10,... | collective-permute-start | bytes 786440 | tf_op jit(solution)/shard_map/ppermute | solution.py:29
  14.4 4.0 %collective-permute-start.3 = (f32[32,256]{1,0:T(8,128)S(1)}, f32[32,256]{1,0:T(8,128)S(1)}, u32[]{:S(2)}, u32[]{:S(2)}) collective-permute-start(f32[32,256]{1,0:T(8,128)S(1)} %maximum_select_fusion.2.passed_ref), channel_id=1, source_target_pairs={{0,4},{1,5},{2,6},{3,7},{4,0},{5,1},{6,2},{7,3},{8,12},{9,13},{10,... | collective-permute-start | bytes 98312 | tf_op jit(solution)/shard_map/ppermute | solution.py:29
  18.4 6.5 %collective-permute-start.4 = (f32[32,512]{1,0:T(8,128)S(1)}, f32[32,512]{1,0:T(8,128)S(1)}, u32[]{:S(2)}, u32[]{:S(2)}) collective-permute-start(f32[32,512]{1,0:T(8,128)S(1)} %maximum_select_fusion.1.passed_ref), channel_id=1, source_target_pairs={{0,8},{1,9},{2,10},{3,11},{4,12},{5,13},{6,14},{7,15},{8,0},{9,1},... | collective-permute-start | bytes 196616 | tf_op jit(solution)/shard_map/ppermute | solution.py:29
  21.0 5.6 %collective-permute-start.8 = (f32[64,1024]{1,0:T(8,128)}, f32[64,1024]{1,0:T(8,128)}, u32[]{:S(2)}, u32[]{:S(2)}) collective-permute-start(f32[64,1024]{1,0:T(8,128)} %piece_hbm.1), channel_id=1, source_target_pairs={{0,1},{1,0},{2,3},{3,2},{4,5},{5,4},{6,7},{7,6},{8,9},{9,8},{10,11... | collective-permute-start | bytes 786440 | tf_op jit(solution)/shard_map/ppermute | solution.py:29
  21.0 5.6 %collective-permute-start.9 = (f32[64,1024]{1,0:T(8,128)}, f32[64,1024]{1,0:T(8,128)}, u32[]{:S(2)}, u32[]{:S(2)}) collective-permute-start(f32[64,1024]{1,0:T(8,128)} %collective-permute-done.5.refs_1_), channel_id=1, source_target_pairs={{0,1},{1,0},{2,3},{3,2},{4,5},{5,4},{6,7},{7,6},{8,9},{9,8},{10,11... | collective-permute-start | bytes 786440 | tf_op jit(solution)/shard_map/ppermute | solution.py:29
  21.6 5.1 %collective-permute-start.10 = (f32[64,1024]{1,0:T(8,128)}, f32[64,1024]{1,0:T(8,128)}, u32[]{:S(2)}, u32[]{:S(2)}) collective-permute-start(f32[64,1024]{1,0:T(8,128)} %collective-permute-done.6.refs_2_), channel_id=1, source_target_pairs={{0,1},{1,0},{2,3},{3,2},{4,5},{5,4},{6,7},{7,6},{8,9},{9,8},{10,11... | collective-permute-start | bytes 786440 | tf_op jit(solution)/shard_map/ppermute | solution.py:29
  21.9 4.8 %collective-permute-start.11 = (f32[64,1024]{1,0:T(8,128)}, f32[64,1024]{1,0:T(8,128)}, u32[]{:S(2)}, u32[]{:S(2)}) collective-permute-start(f32[64,1024]{1,0:T(8,128)} %collective-permute-done.7.refs_3_), channel_id=1, source_target_pairs={{0,1},{1,0},{2,3},{3,2},{4,5},{5,4},{6,7},{7,6},{8,9},{9,8},{10,11... | collective-permute-start | bytes 786440 | tf_op jit(solution)/shard_map/ppermute | solution.py:29
  22.1 2.9 %copy-start.1 = (f32[64,1024]{1,0:T(8,128)S(1)}, f32[64,1024]{1,0:T(8,128)}, u32[]{:S(2)}) copy-start(f32[64,1024]{1,0:T(8,128)} %copy-done) | copy-start | bytes 786436
  28.5 5.5 %collective-permute-start.12 = (f32[16,512]{1,0:T(8,128)S(1)}, f32[16,512]{1,0:T(8,128)S(1)}, u32[]{:S(2)}, u32[]{:S(2)}) collective-permute-start(f32[16,512]{1,0:T(8,128)S(1)} %constant_dynamic-update-slice_fusion.passed_ref), channel_id=1, source_target_pairs={{0,8},{1,9},{2,10},{3,11},{4,12},{5,13},{6,14},{7,15},{8,0},{9,1},... | collective-permute-start | bytes 98312 | tf_op jit(solution)/shard_map/ppermute | solution.py:29
  49.0 5.2 %collective-permute-start.13 = (f32[16,512]{1,0:T(8,128)S(1)}, f32[16,512]{1,0:T(8,128)S(1)}, u32[]{:S(2)}, u32[]{:S(2)}) collective-permute-start(f32[16,512]{1,0:T(8,128)S(1)} %get-tuple-element.52), channel_id=1, source_target_pairs={{0,8},{1,9},{2,10},{3,11},{4,12},{5,13},{6,14},{7,15},{8,0},{9,1},... | collective-permute-start | bytes 98312 | tf_op jit(solution)/shard_map/ppermute | solution.py:29
  54.8 1.3 %collective-permute-start.14 = (f32[16,1024]{1,0:T(8,128)S(1)}, f32[16,1024]{1,0:T(8,128)S(1)}, u32[]{:S(2)}, u32[]{:S(2)}) collective-permute-start(f32[16,1024]{1,0:T(8,128)S(1)} %image_rows.1), channel_id=1, source_target_pairs={{0,1},{1,0},{2,3},{3,2},{4,5},{5,4},{6,7},{7,6},{8,9},{9,8},{10,11... | collective-permute-start | bytes 196616 | tf_op jit(solution)/shard_map/ppermute | solution.py:29
  56.1 4.3 %collective-permute-start.15 = (f32[16,1024]{1,0:T(8,128)S(1)}, f32[16,1024]{1,0:T(8,128)S(1)}, u32[]{:S(2)}, u32[]{:S(2)}) collective-permute-start(f32[16,1024]{1,0:T(8,128)S(1)} %add.9), channel_id=1, source_target_pairs={{0,2},{1,3},{2,0},{3,1},{4,6},{5,7},{6,4},{7,5},{8,10},{9,11},{10,... | collective-permute-start | bytes 196616 | tf_op jit(solution)/shard_map/ppermute | solution.py:29
  60.5 4.3 %collective-permute-start.16 = (f32[16,1024]{1,0:T(8,128)S(1)}, f32[16,1024]{1,0:T(8,128)S(1)}, u32[]{:S(2)}, u32[]{:S(2)}) collective-permute-start(f32[16,1024]{1,0:T(8,128)S(1)} %add.10), channel_id=1, source_target_pairs={{0,4},{1,5},{2,6},{3,7},{4,0},{5,1},{6,2},{7,3},{8,12},{9,13},{10,... | collective-permute-start | bytes 196616 | tf_op jit(solution)/shard_map/ppermute | solution.py:29
  64.8 5.6 %collective-permute-start.17 = (f32[16,1024]{1,0:T(8,128)S(1)}, f32[16,1024]{1,0:T(8,128)S(1)}, u32[]{:S(2)}, u32[]{:S(2)}) collective-permute-start(f32[16,1024]{1,0:T(8,128)S(1)} %add.11.image_ref), channel_id=1, source_target_pairs={{0,8},{1,9},{2,10},{3,11},{4,12},{5,13},{6,14},{7,15},{8,0},{9,1},... | collective-permute-start | bytes 196616 | tf_op jit(solution)/shard_map/ppermute | solution.py:29

commit v11 on v10

--- a/solution.py
+++ b/solution.py
@@ -192,20 +192,18 @@
 
 
 def begin(
-    order, generator_hbm, weight_hbm, samples_hbm, piece_hbm, solution_hbm, residual_hbm, direction_hbm,
-    sample_ref, piece_ref, own_state_ref, centre_ref, rhs_ref, constant_ref, pick_ref, own_points_ref,
+    order, generator_hbm, weight_hbm, samples_hbm, solution_hbm, residual_hbm, direction_hbm,
+    sample_ref, solution_ref, residual_ref, direction_ref, centre_ref, rhs_ref, constant_ref, pick_ref, own_points_ref,
     generator_ref, weight_ref, sems,
 ):
-    outs = solution_hbm.shape[0]
     copies = fetch(
         [
             (generator_hbm, generator_ref),
             (weight_hbm, weight_ref),
             (samples_hbm, sample_ref),
-            (piece_hbm, piece_ref),
-            (solution_hbm, own_state_ref.at[pl.ds(0, outs)]),
-            (residual_hbm, own_state_ref.at[pl.ds(outs, outs)]),
-            (direction_hbm, own_state_ref.at[pl.ds(2 * outs, outs)]),
+            (solution_hbm, solution_ref),
+            (residual_hbm, residual_ref),
+            (direction_hbm, direction_ref),
         ],
         sems,
     )
@@ -396,6 +394,35 @@
     )(coefficients, *tables, own_points, *[part for pair in store for part in pair])
 
 
+def join(bit, count, riders, *refs):
+    mine_refs, other_refs, joined_ref = refs[:count], refs[count : 2 * count], refs[2 * count + riders]
+    width = mine_refs[0].shape[1]
+    upper = (lax.axis_index("samp") & bit) != 0
+    first = 0
+    for mine_ref, other_ref in zip(mine_refs, other_refs):
+        rows = slice(first, first + mine_ref.shape[0])
+        first += mine_ref.shape[0]
+        mine, other = mine_ref[...], other_ref[...]
+        joined_ref[rows, :width] = jnp.where(upper, other, mine)
+        joined_ref[rows, width:] = jnp.where(upper, mine, other)
+
+
+def joined(bit, mine, other, riders=()):
+    rows = sum(value.shape[0] for value in mine)
+    count = len(mine)
+    like = [jax.ShapeDtypeStruct(value.shape, value.dtype) for value in riders]
+    value, *riders = pl.pallas_call(
+        functools.partial(join, bit, count, len(riders)),
+        in_specs=[*[VMEM] * (2 * count), *[FREE] * len(riders)],
+        out_specs=[VMEM, *[FREE] * len(riders)],
+        out_shape=[jax.ShapeDtypeStruct((rows, 2 * mine[0].shape[1]), F32), *like],
+        input_output_aliases={2 * count + i: 1 + i for i in range(len(riders))},
+        compiler_params=pltpu.CompilerParams(vmem_limit_bytes=4 << 20),
+        name="join",
+    )(*mine, *other, *riders)
+    return value, riders
+
+
 def row_products(outs, count, state_ref, *refs):
     coef_ref, parts_ref = refs[count:]
     state = stack3(state_ref[:outs])
@@ -433,7 +460,7 @@
 
 
 def finish(
-    image_ref, more_ref, state_ref, own_ref, new_solution_ref, new_residual_ref, new_direction_ref, total_ref
+    image_ref, more_ref, state_ref, solution_ref, residual_ref, direction_ref, new_solution_ref, new_residual_ref, new_direction_ref, total_ref
 ):
     outs, cen_dev = new_solution_ref.shape
     image = image_ref[...] + more_ref[...]
@@ -452,16 +479,15 @@
     for k in range(1, share):
         here = lax.rem(index, share) == k
         own_image = jnp.where(here, wide[:, k * cen_dev : (k + 1) * cen_dev], own_image)
-    direction = own_ref[2 * outs :]
-    new_solution_ref[...] = own_ref[:outs] + step_length * direction
-    new_residual = own_ref[outs : 2 * outs] - step_length * own_image
+    direction = direction_ref[...]
+    new_solution_ref[...] = solution_ref[...] + step_length * direction
+    new_residual = residual_ref[...] - step_length * own_image
     new_residual_ref[...] = new_residual
     new_direction_ref[...] = new_residual + (norm_new / norm_old) * direction
 
 
 def body(samples, generator, weight_index, preconditioner, solution, residual, direction):
     devices = lax.axis_size("samp")
-    index = lax.axis_index("samp")
     cen_dev, centres_all = preconditioner.shape
     samples_dev = samples.shape[1]
     outs = direction.shape[0]
@@ -469,13 +495,12 @@
 
     order = ((*held, *others), cen_dev)
     dims = samples.shape[0]
-    sample_copy, piece_copy, own_state, *tables = pl.pallas_call(
+    sample_copy, *own_state, centre_table, rhs, constant, pick, points = pl.pallas_call(
         functools.partial(begin, order),
-        in_specs=[HBM] * 7,
+        in_specs=[HBM] * 6,
         out_shape=[
             jax.ShapeDtypeStruct(samples.shape, jnp.int32),
-            jax.ShapeDtypeStruct(preconditioner.shape, F32),
-            jax.ShapeDtypeStruct((3 * outs, cen_dev), F32),
+            *[jax.ShapeDtypeStruct(direction.shape, F32)] * 3,
             jax.ShapeDtypeStruct((2, dims, centres_all), F32),
             jax.ShapeDtypeStruct((16 * dims, centres_all), BF16),
             jax.ShapeDtypeStruct((dims, 128), F32),
@@ -485,13 +510,13 @@
         scratch_shapes=[
             pltpu.SMEM((dims,), jnp.int32),
             pltpu.SMEM((dims,), jnp.int32),
-            pltpu.SemaphoreType.DMA((7,)),
+            pltpu.SemaphoreType.DMA((6,)),
         ],
         compiler_params=pltpu.CompilerParams(vmem_limit_bytes=(6 << 20) + 1200 * centres_all),
         name="begin",
-    )(*in_hbm(generator, weight_index, samples, preconditioner, solution, residual, direction))
-    own_points = tables.pop()[:, :cen_dev]
-    tables = (sample_copy, *tables)
+    )(*in_hbm(generator, weight_index, samples, solution, residual, direction))
+    own_points = points[:, :cen_dev]
+    tables = (sample_copy, centre_table, rhs, constant, pick)
 
     half = samples_dev // 2
     use_store = 4 * half * centres_all <= STORE_BYTES
@@ -507,30 +532,25 @@
         filled += rows
         return handed
 
-    pieces = [preconditioner]
     early = [swap(preconditioner, bit, devices) for bit in held[:2]]
-    pieces += early[:1]
-    if len(early) > 1:
-        pieces += [early[1], swap(early[0], held[1], devices)]
+    later = []
     bit = 1
     state = None
     while bit < devices:
-        upper = (index & bit) != 0
         if state is None:
-            mine = [direction, residual]
-            other = [swap(direction, bit, devices), swap(residual, bit, devices)]
-            joined = [jnp.concatenate(pair, axis=1) for pair in zip(other, mine)]
-            turned = [jnp.concatenate(pair, axis=1) for pair in zip(mine, other)]
-            state = jnp.where(upper, jnp.concatenate(joined), jnp.concatenate(turned))
+            other = [swap(value, bit, devices) for value in (direction, residual)]
+            state, _ = joined(bit, [own_state[2], own_state[1]], other)
         else:
             other = swap(state, bit, devices)
-            mine = fill(256, state)
-            state = jnp.where(
-                upper,
-                jnp.concatenate([other, mine], axis=1),
-                jnp.concatenate([mine, other], axis=1),
-            )
+            riders = early if bit == 2 else later if 2 * bit == devices else []
+            state, riders = joined(bit, [fill(256, state)], [other], riders)
+            if bit == 2 and len(early) > 1:
+                early = riders
+                later = [swap(early[0], held[1], devices)]
+            elif riders:
+                later = riders
         bit *= 2
+    pieces = [preconditioner, *early, *later]
 
     def coefficients_of(group):
         rows = len(group) * cen_dev
@@ -546,9 +566,9 @@
             name="row_products",
         )(state, *group)
 
-    groups = [[piece_copy, *pieces[1:]]]
+    groups = [pieces]
     for bit in held[2:]:
-        groups.append([swap(p, bit, devices) for p in [*pieces, *sum(groups[1:], [])]])
+        groups.append([swap(p, bit, devices) for p in sum(groups, [])])
     made = [coefficients_of(group) for group in groups]
     coefficients = jnp.concatenate([m[0] for m in made], axis=1)
     parts = [m[1] for m in made]
@@ -586,7 +606,7 @@
         scratch_shapes=[pltpu.VMEM((outs, centres_all), F32)],
         compiler_params=pltpu.CompilerParams(vmem_limit_bytes=(2 << 20) + 512 * centres_all),
         name="finish",
-    )(image, more, state, own_state)
+    )(image, more, state, *own_state)
 
 
 def solution(mesh):

time: 71.5 us -> 67.5 us (0.944)
  Pallas kernels: 32.4 us -> 29.7 us
  other arithmetic: 0.92 us -> 0.03 us
  local copies, waits for them, and re-layouts: 0.73 us -> 0.01 us
    pallas_call x2, Pallas kernels: 3.42 us -> 1.14 us  [coefficients_of(): pl.pallas_call(functools.partial(row_products, outs, len(group)), out_sha...]
    select_n x4 -> x0, other arithmetic: 0.88 us -> none  [the longest x1 0.85 us: body(): state = jnp.where(upper, jnp.concatenate(joined), jnp.concatenate(turned))]
  transfers between devices with their start and end apart: 18 -> 18, of which waited for: 9 -> 9; matrix products, arithmetic and copies ran while one was open for 1% -> 0% of each run, Pallas kernels for 20% -> 19%
where the time goes in v11:
time: 67.5 us; the launch traced here: 67.4 us
  Pallas kernels  29.7 us (44%)
  starting transfers between devices  18.4 us (27%)
  waiting for transfers between devices  18.4 us (27%)
  between operations  0.77 us (1%)
    ppermute x18, starting transfers between devices, swap(): return lax.ppermute(value, 'samp', [(i, i ^ bit) for i in range(devices)])  18.4 us
    ppermute x18, waiting for transfers between devices, swap(): return lax.ppermute(value, 'samp', [(i, i ^ bit) for i in range(devices)])  18.4 us
    pallas_call x1, Pallas kernels, apply_products(): pl.pallas_call(functools.partial(products, outs, stored), out_shape=[half...  14.6 us
    pallas_call x4, Pallas kernels, kernel_rows(): pl.pallas_call(functools.partial(store_rows, first_row, STORED_MIXED), ou...  11.4 us
  transfers between devices with their start and end apart: 18, of which 9 were waited for; matrix products, arithmetic and copies ran while one was open for 0% of the time, Pallas kernels for 19%

profile of v11, /device:TPU:0, one launch (start us, length us, event | category | flops | bytes accessed | tf_op | source)
XLA Modules:
  0.0 67.4 jit_solution(11144381913289254394)
XLA Ops:
  0.6 3.0 %collective-permute-start.4 = (f32[64,1024]{1,0:T(8,128)}, f32[64,1024]{1,0:T(8,128)S(1)}, u32[]{:S(2)}, u32[]{:S(2)}) collective-permute-start(f32[64,1024]{1,0:T(8,128)} %refs_0_.1), channel_id=1, source_target_pairs={{0,2},{1,3},{2,0},{3,1},{4,6},{5,7},{6,4},{7,5},{8,10},{9,11},{10,... | collective-permute-start | bytes 786440 | tf_op jit(solution)/shard_map/ppermute | solution.py:29
  3.7 1.6 %collective-permute-start.3 = (f32[64,1024]{1,0:T(8,128)}, f32[64,1024]{1,0:T(8,128)S(1)}, u32[]{:S(2)}, u32[]{:S(2)}) collective-permute-start(f32[64,1024]{1,0:T(8,128)} %refs_0_.1), channel_id=1, source_target_pairs={{0,4},{1,5},{2,6},{3,7},{4,0},{5,1},{6,2},{7,3},{8,12},{9,13},{10,... | collective-permute-start | bytes 786440 | tf_op jit(solution)/shard_map/ppermute | solution.py:29
  5.2 0.0 collective-permute-start.1
  5.2 0.5 collective-permute-start
  5.8 1.1 %begin.1 = (s32[16,2048]{1,0:T(8,128)S(1)}, f32[16,64]{1,0:T(8,128)S(1)}, f32[16,64]{1,0:T(8,128)S(1)}, f32[16,64]{1,0:T(8,128)S(1)}, f32[2,16,1024]{2,1,0:T(8,1...) custom-call(s32[16]{0:T(128)} %generator_hbm.1, ...), custom_call_target="tpu_custom_call" | custom-call | tf_op jit(solution)/shard_map/begin/pallas_call | solution.py:498
  6.8 0.0 collective-permute-done.1.refs_3_
  6.9 0.0 collective-permute-done.refs_2_
  6.9 0.1 join.4.passed_ref
  6.9 0.0 copy-start
  6.9 0.5 collective-permute-start.2
  7.5 2.8 %kernel_rows.4 = (bf16[256,1024]{1,0:T(8,128)(2,1)S(1)}, bf16[256,1024]{1,0:T(8,128)(2,1)S(1)}, f32[32,128]{1,0:T(8,128)S(1)}) custom-call(s32[16,2048]{1,0:T(8,128)S(1)} %get-tuple-element.36.sample_ref, f32[2,16,1024]{2,1,0:T(8,128)S(1)} %get-tuple-element.37.centre_ref, bf16[256,1024]{1,0:T(8,128)(2,1)S(1)} %get-tuple-element.38.rhs_ref, ...), custom_call_target="tpu_custom_call" | custom-call | flops 25165824 | bytes 1048576 | tf_op jit(solution)/shard_map/kernel_rows/pallas_call | solution.py:271
  10.3 0.4 collective-permute-done.2.refs_1_
  10.7 0.0 collective-permute-done.4.refs_3_
  10.7 0.9 %collective-permute-done.3.refs_2_ = f32[64,1024]{1,0:T(8,128)S(1)} collective-permute-done((f32[64,1024]{1,0:T(8,128)}, f32[64,1024]{1,0:T(8,128)S(1)}, u32[]{:S(2)}, u32[]{:S(2)}) %collective-permute-start.3) | collective-permute-done | bytes 262176 | tf_op jit(solution)/shard_map/ppermute | solution.py:29
  11.6 0.7 %collective-permute-start.7 = (f32[64,1024]{1,0:T(8,128)S(1)}, f32[64,1024]{1,0:T(8,128)S(1)}, u32[]{:S(2)}, u32[]{:S(2)}) collective-permute-start(f32[64,1024]{1,0:T(8,128)S(1)} %get-tuple-element.47.refs_1_), channel_id=1, source_target_pairs={{0,2},{1,3},{2,0},{3,1},{4,6},{5,7},{6,4},{7,5},{8,10},{9,11},{10,... | collective-permute-start | bytes 786440 | tf_op jit(solution)/shard_map/ppermute | solution.py:29
  12.4 1.6 %collective-permute-start.5 = (f32[32,256]{1,0:T(8,128)S(1)}, f32[32,256]{1,0:T(8,128)S(1)}, u32[]{:S(2)}, u32[]{:S(2)}) collective-permute-start(f32[32,256]{1,0:T(8,128)S(1)} %get-tuple-element.44.passed_ref), channel_id=1, source_target_pairs={{0,4},{1,5},{2,6},{3,7},{4,0},{5,1},{6,2},{7,3},{8,12},{9,13},{10,... | collective-permute-start | bytes 98312 | tf_op jit(solution)/shard_map/ppermute | solution.py:29
  13.9 2.8 %kernel_rows.5 = (bf16[256,1024]{1,0:T(8,128)(2,1)S(1)}, bf16[256,1024]{1,0:T(8,128)(2,1)S(1)}, f32[32,256]{1,0:T(8,128)S(1)}) custom-call(s32[16,2048]{1,0:T(8,128)S(1)} %get-tuple-element.36.sample_ref, f32[2,16,1024]{2,1,0:T(8,128)S(1)} %get-tuple-element.37.centre_ref, bf16[256,1024]{1,0:T(8,128)(2,1)S(1)} %get-tuple-element.38.rhs_ref, ...), custom_call_target="tpu_custom_call" | custom-call | flops 25165824 | bytes 1048576 | tf_op jit(solution)/shard_map/kernel_rows/pallas_call | solution.py:271
  16.7 0.0 collective-permute-done.5.refs_1_
  16.8 2.7 %collective-permute-start.6 = (f32[32,512]{1,0:T(8,128)S(1)}, f32[32,512]{1,0:T(8,128)S(1)}, u32[]{:S(2)}, u32[]{:S(2)}) collective-permute-start(f32[32,512]{1,0:T(8,128)S(1)} %join.6.passed_ref), channel_id=1, source_target_pairs={{0,8},{1,9},{2,10},{3,11},{4,12},{5,13},{6,14},{7,15},{8,0},{9,1},... | collective-permute-start | bytes 196616 | tf_op jit(solution)/shard_map/ppermute | solution.py:29
  19.4 0.0 copy-done
  19.4 0.0 collective-permute-start.8
  19.4 0.5 collective-permute-start.9
  19.9 0.0 collective-permute-start.10
  19.9 2.8 %kernel_rows.6 = (bf16[256,1024]{1,0:T(8,128)(2,1)S(1)}, bf16[256,1024]{1,0:T(8,128)(2,1)S(1)}, f32[32,512]{1,0:T(8,128)S(1)}) custom-call(s32[16,2048]{1,0:T(8,128)S(1)} %get-tuple-element.36.sample_ref, f32[2,16,1024]{2,1,0:T(8,128)S(1)} %get-tuple-element.37.centre_ref, bf16[256,1024]{1,0:T(8,128)(2,1)S(1)} %get-tuple-element.38.rhs_ref, ...), custom_call_target="tpu_custom_call" | custom-call | flops 25165824 | bytes 1048576 | tf_op jit(solution)/shard_map/kernel_rows/pallas_call | solution.py:271
  22.7 0.0 collective-permute-done.6.refs_1_
  22.7 0.0 collective-permute-done.7.refs_2_
  22.8 0.6 collective-permute-start.11
  23.4 0.6 row_products.2
  23.9 0.0 collective-permute-done.8.refs_0_
  24.0 0.0 collective-permute-done.10.refs_2_
  24.0 0.0 collective-permute-done.9.refs_1_
  24.0 0.5 collective-permute-done.11.refs_3_
  24.5 0.6 row_products.3
  25.1 1.8 %collective-permute-start.12 = (f32[16,512]{1,0:T(8,128)S(1)}, f32[16,512]{1,0:T(8,128)S(1)}, u32[]{:S(2)}, u32[]{:S(2)}) collective-permute-start(f32[16,512]{1,0:T(8,128)S(1)} %constant_dynamic-update-slice_fusion.passed_ref), channel_id=1, source_target_pairs={{0,8},{1,9},{2,10},{3,11},{4,12},{5,13},{6,14},{7,15},{8,0},{9,1},... | collective-permute-start | bytes 98312 | tf_op jit(solution)/shard_map/ppermute | solution.py:29
  26.9 3.0 %kernel_rows.7 = (bf16[256,1024]{1,0:T(8,128)(2,1)S(1)}, bf16[256,1024]{1,0:T(8,128)(2,1)S(1)}, f32[16,512]{1,0:T(8,128)S(1)}) custom-call(s32[16,2048]{1,0:T(8,128)S(1)} %get-tuple-element.36.sample_ref, f32[2,16,1024]{2,1,0:T(8,128)S(1)} %get-tuple-element.37.centre_ref, bf16[256,1024]{1,0:T(8,128)(2,1)S(1)} %get-tuple-element.38.rhs_ref, ...), custom_call_target="tpu_custom_call" | custom-call | flops 25165824 | bytes 1048576 | tf_op jit(solution)/shard_map/kernel_rows/pallas_call | solution.py:271
  29.9 0.7 collective-permute-done.12
  30.6 14.6 %products.1 = (f32[16,512]{1,0:T(8,128)S(1)}, f32[16,512]{1,0:T(8,128)S(1)}, f32[16,64]{1,0:T(8,128)S(1)}) custom-call(f32[16,1024]{1,0:T(8,128)S(1)} %pad_maximum_fusion.coef_ref, s32[16,2048]{1,0:T(8,128)S(1)} %get-tuple-element.36.sample_ref, f32[2,16,1024]{2,1,0:T(8,128)S(1)} %get-tuple-element.37.centre_ref, ...), custom_call_target="tpu_custom_call" | custom-call | flops 100663296 | bytes 4194304 | tf_op jit(solution)/shard_map/products/pallas_call | solution.py:376
  45.2 1.2 %collective-permute-start.13 = (f32[16,512]{1,0:T(8,128)S(1)}, f32[16,512]{1,0:T(8,128)S(1)}, u32[]{:S(2)}, u32[]{:S(2)}) collective-permute-start(f32[16,512]{1,0:T(8,128)S(1)} %get-tuple-element.64), channel_id=1, source_target_pairs={{0,8},{1,9},{2,10},{3,11},{4,12},{5,13},{6,14},{7,15},{8,0},{9,1},... | collective-permute-start | bytes 98312 | tf_op jit(solution)/shard_map/ppermute | solution.py:29
  46.4 3.6 %collective-permute-done.13.came_ref = f32[16,512]{1,0:T(8,128)S(1)} collective-permute-done((f32[16,512]{1,0:T(8,128)S(1)}, f32[16,512]{1,0:T(8,128)S(1)}, u32[]{:S(2)}, u32[]{:S(2)}) %collective-permute-start.13) | collective-permute-done | bytes 32800 | tf_op jit(solution)/shard_map/ppermute | solution.py:29
  50.1 0.6 image_rows.1
  50.7 0.0 collective-permute-start.14
  50.7 1.3 %collective-permute-done.14 = f32[16,1024]{1,0:T(8,128)S(1)} collective-permute-done((f32[16,1024]{1,0:T(8,128)S(1)}, f32[16,1024]{1,0:T(8,128)S(1)}, u32[]{:S(2)}, u32[]{:S(2)}) %collective-permute-start.14) | collective-permute-done | bytes 65568 | tf_op jit(solution)/shard_map/ppermute | solution.py:29
  52.0 1.4 %collective-permute-start.15 = (f32[16,1024]{1,0:T(8,128)S(1)}, f32[16,1024]{1,0:T(8,128)S(1)}, u32[]{:S(2)}, u32[]{:S(2)}) collective-permute-start(f32[16,1024]{1,0:T(8,128)S(1)} %add.9), channel_id=1, source_target_pairs={{0,2},{1,3},{2,0},{3,1},{4,6},{5,7},{6,4},{7,5},{8,10},{9,11},{10,... | collective-permute-start | bytes 196616 | tf_op jit(solution)/shard_map/ppermute | solution.py:29
  53.4 2.9 %collective-permute-done.15 = f32[16,1024]{1,0:T(8,128)S(1)} collective-permute-done((f32[16,1024]{1,0:T(8,128)S(1)}, f32[16,1024]{1,0:T(8,128)S(1)}, u32[]{:S(2)}, u32[]{:S(2)}) %collective-permute-start.15) | collective-permute-done | bytes 65568 | tf_op jit(solution)/shard_map/ppermute | solution.py:29
  56.3 1.1 %collective-permute-start.16 = (f32[16,1024]{1,0:T(8,128)S(1)}, f32[16,1024]{1,0:T(8,128)S(1)}, u32[]{:S(2)}, u32[]{:S(2)}) collective-permute-start(f32[16,1024]{1,0:T(8,128)S(1)} %add.10), channel_id=1, source_target_pairs={{0,4},{1,5},{2,6},{3,7},{4,0},{5,1},{6,2},{7,3},{8,12},{9,13},{10,... | collective-permute-start | bytes 196616 | tf_op jit(solution)/shard_map/ppermute | solution.py:29
  57.4 3.2 %collective-permute-done.16 = f32[16,1024]{1,0:T(8,128)S(1)} collective-permute-done((f32[16,1024]{1,0:T(8,128)S(1)}, f32[16,1024]{1,0:T(8,128)S(1)}, u32[]{:S(2)}, u32[]{:S(2)}) %collective-permute-start.16) | collective-permute-done | bytes 65568 | tf_op jit(solution)/shard_map/ppermute | solution.py:29
  60.7 1.2 %collective-permute-start.17 = (f32[16,1024]{1,0:T(8,128)S(1)}, f32[16,1024]{1,0:T(8,128)S(1)}, u32[]{:S(2)}, u32[]{:S(2)}) collective-permute-start(f32[16,1024]{1,0:T(8,128)S(1)} %add.11.image_ref), channel_id=1, source_target_pairs={{0,8},{1,9},{2,10},{3,11},{4,12},{5,13},{6,14},{7,15},{8,0},{9,1},... | collective-permute-start | bytes 196616 | tf_op jit(solution)/shard_map/ppermute | solution.py:29
  61.9 4.7 %collective-permute-done.17.more_ref = f32[16,1024]{1,0:T(8,128)S(1)} collective-permute-done((f32[16,1024]{1,0:T(8,128)S(1)}, f32[16,1024]{1,0:T(8,128)S(1)}, u32[]{:S(2)}, u32[]{:S(2)}) %collective-permute-start.17) | collective-permute-done | bytes 65568 | tf_op jit(solution)/shard_map/ppermute | solution.py:29
  66.6 0.8 %finish.1 = (f32[16,64]{1,0:T(8,128)}, f32[16,64]{1,0:T(8,128)}, f32[16,64]{1,0:T(8,128)}) custom-call(f32[16,1024]{1,0:T(8,128)S(1)} %add.11.image_ref, f32[16,1024]{1,0:T(8,128)S(1)} %collective-permute-done.17.more_ref, f32[32,1024]{1,0:T(8,128)S(1)} %get-tuple-element.48.state_ref, f32[16,64]{1,0:T(8,128)S(1)} %get-tuple-element.68.solution_ref, ...), custom_call_target="tpu_custom_call" | custom-call | tf_op jit(solution)/shard_map/finish/pallas_call | solution.py:603
  (9 shorter events, 0.1 us)
Async XLA Ops:
  0.6 10.1 %collective-permute-start.4 = (f32[64,1024]{1,0:T(8,128)}, f32[64,1024]{1,0:T(8,128)S(1)}, u32[]{:S(2)}, u32[]{:S(2)}) collective-permute-start(f32[64,1024]{1,0:T(8,128)} %refs_0_.1), channel_id=1, source_target_pairs={{0,2},{1,3},{2,0},{3,1},{4,6},{5,7},{6,4},{7,5},{8,10},{9,11},{10,... | collective-permute-start | bytes 786440 | tf_op jit(solution)/shard_map/ppermute | solution.py:29
  3.7 8.0 %collective-permute-start.3 = (f32[64,1024]{1,0:T(8,128)}, f32[64,1024]{1,0:T(8,128)S(1)}, u32[]{:S(2)}, u32[]{:S(2)}) collective-permute-start(f32[64,1024]{1,0:T(8,128)} %refs_0_.1), channel_id=1, source_target_pairs={{0,4},{1,5},{2,6},{3,7},{4,0},{5,1},{6,2},{7,3},{8,12},{9,13},{10,... | collective-permute-start | bytes 786440 | tf_op jit(solution)/shard_map/ppermute | solution.py:29
  5.2 1.6 %collective-permute-start.1 = (f32[16,64]{1,0:T(8,128)}, f32[16,64]{1,0:T(8,128)S(1)}, u32[]{:S(2)}, u32[]{:S(2)}) collective-permute-start(f32[16,64]{1,0:T(8,128)} %residual_hbm.1), channel_id=1, source_target_pairs={{0,1},{1,0},{2,3},{3,2},{4,5},{5,4},{6,7},{7,6},{8,9},{9,8},{10,11... | collective-permute-start | bytes 12296 | tf_op jit(solution)/shard_map/ppermute | solution.py:29
  5.2 1.6 %collective-permute-start = (f32[16,64]{1,0:T(8,128)}, f32[16,64]{1,0:T(8,128)S(1)}, u32[]{:S(2)}, u32[]{:S(2)}) collective-permute-start(f32[16,64]{1,0:T(8,128)} %direction_hbm.1), channel_id=1, source_target_pairs={{0,1},{1,0},{2,3},{3,2},{4,5},{5,4},{6,7},{7,6},{8,9},{9,8},{10,11... | collective-permute-start | bytes 12296 | tf_op jit(solution)/shard_map/ppermute | solution.py:29
  6.9 12.5 %copy-start = (f32[64,1024]{1,0:T(8,128)S(1)}, f32[64,1024]{1,0:T(8,128)}, u32[]{:S(2)}) copy-start(f32[64,1024]{1,0:T(8,128)} %refs_0_.1) | copy-start | bytes 786436
  6.9 3.8 %collective-permute-start.2 = (f32[32,128]{1,0:T(8,128)S(1)}, f32[32,128]{1,0:T(8,128)S(1)}, u32[]{:S(2)}, u32[]{:S(2)}) collective-permute-start(f32[32,128]{1,0:T(8,128)S(1)} %join.4.passed_ref), channel_id=1, source_target_pairs={{0,2},{1,3},{2,0},{3,1},{4,6},{5,7},{6,4},{7,5},{8,10},{9,11},{10,... | collective-permute-start | bytes 49160 | tf_op jit(solution)/shard_map/ppermute | solution.py:29
  11.6 11.1 %collective-permute-start.7 = (f32[64,1024]{1,0:T(8,128)S(1)}, f32[64,1024]{1,0:T(8,128)S(1)}, u32[]{:S(2)}, u32[]{:S(2)}) collective-permute-start(f32[64,1024]{1,0:T(8,128)S(1)} %get-tuple-element.47.refs_1_), channel_id=1, source_target_pairs={{0,2},{1,3},{2,0},{3,1},{4,6},{5,7},{6,4},{7,5},{8,10},{9,11},{10,... | collective-permute-start | bytes 786440 | tf_op jit(solution)/shard_map/ppermute | solution.py:29
  12.4 4.4 %collective-permute-start.5 = (f32[32,256]{1,0:T(8,128)S(1)}, f32[32,256]{1,0:T(8,128)S(1)}, u32[]{:S(2)}, u32[]{:S(2)}) collective-permute-start(f32[32,256]{1,0:T(8,128)S(1)} %get-tuple-element.44.passed_ref), channel_id=1, source_target_pairs={{0,4},{1,5},{2,6},{3,7},{4,0},{5,1},{6,2},{7,3},{8,12},{9,13},{10,... | collective-permute-start | bytes 98312 | tf_op jit(solution)/shard_map/ppermute | solution.py:29
  16.8 6.0 %collective-permute-start.6 = (f32[32,512]{1,0:T(8,128)S(1)}, f32[32,512]{1,0:T(8,128)S(1)}, u32[]{:S(2)}, u32[]{:S(2)}) collective-permute-start(f32[32,512]{1,0:T(8,128)S(1)} %join.6.passed_ref), channel_id=1, source_target_pairs={{0,8},{1,9},{2,10},{3,11},{4,12},{5,13},{6,14},{7,15},{8,0},{9,1},... | collective-permute-start | bytes 196616 | tf_op jit(solution)/shard_map/ppermute | solution.py:29
  19.4 4.5 %collective-permute-start.8 = (f32[64,1024]{1,0:T(8,128)S(1)}, f32[64,1024]{1,0:T(8,128)S(1)}, u32[]{:S(2)}, u32[]{:S(2)}) collective-permute-start(f32[64,1024]{1,0:T(8,128)S(1)} %copy-done), channel_id=1, source_target_pairs={{0,1},{1,0},{2,3},{3,2},{4,5},{5,4},{6,7},{7,6},{8,9},{9,8},{10,11... | collective-permute-start | bytes 786440 | tf_op jit(solution)/shard_map/ppermute | solution.py:29
  19.4 4.6 %collective-permute-start.9 = (f32[64,1024]{1,0:T(8,128)S(1)}, f32[64,1024]{1,0:T(8,128)S(1)}, u32[]{:S(2)}, u32[]{:S(2)}) collective-permute-start(f32[64,1024]{1,0:T(8,128)S(1)} %get-tuple-element.47.refs_1_), channel_id=1, source_target_pairs={{0,1},{1,0},{2,3},{3,2},{4,5},{5,4},{6,7},{7,6},{8,9},{9,8},{10,11... | collective-permute-start | bytes 786440 | tf_op jit(solution)/shard_map/ppermute | solution.py:29
  19.9 4.0 %collective-permute-start.10 = (f32[64,1024]{1,0:T(8,128)S(1)}, f32[64,1024]{1,0:T(8,128)S(1)}, u32[]{:S(2)}, u32[]{:S(2)}) collective-permute-start(f32[64,1024]{1,0:T(8,128)S(1)} %get-tuple-element.49.refs_2_), channel_id=1, source_target_pairs={{0,1},{1,0},{2,3},{3,2},{4,5},{5,4},{6,7},{7,6},{8,9},{9,8},{10,11... | collective-permute-start | bytes 786440 | tf_op jit(solution)/shard_map/ppermute | solution.py:29
  22.8 1.7 %collective-permute-start.11 = (f32[64,1024]{1,0:T(8,128)S(1)}, f32[64,1024]{1,0:T(8,128)S(1)}, u32[]{:S(2)}, u32[]{:S(2)}) collective-permute-start(f32[64,1024]{1,0:T(8,128)S(1)} %get-tuple-element.50.refs_3_), channel_id=1, source_target_pairs={{0,1},{1,0},{2,3},{3,2},{4,5},{5,4},{6,7},{7,6},{8,9},{9,8},{10,11... | collective-permute-start | bytes 786440 | tf_op jit(solution)/shard_map/ppermute | solution.py:29
  25.1 5.5 %collective-permute-start.12 = (f32[16,512]{1,0:T(8,128)S(1)}, f32[16,512]{1,0:T(8,128)S(1)}, u32[]{:S(2)}, u32[]{:S(2)}) collective-permute-start(f32[16,512]{1,0:T(8,128)S(1)} %constant_dynamic-update-slice_fusion.passed_ref), channel_id=1, source_target_pairs={{0,8},{1,9},{2,10},{3,11},{4,12},{5,13},{6,14},{7,15},{8,0},{9,1},... | collective-permute-start | bytes 98312 | tf_op jit(solution)/shard_map/ppermute | solution.py:29
  45.2 4.8 %collective-permute-start.13 = (f32[16,512]{1,0:T(8,128)S(1)}, f32[16,512]{1,0:T(8,128)S(1)}, u32[]{:S(2)}, u32[]{:S(2)}) collective-permute-start(f32[16,512]{1,0:T(8,128)S(1)} %get-tuple-element.64), channel_id=1, source_target_pairs={{0,8},{1,9},{2,10},{3,11},{4,12},{5,13},{6,14},{7,15},{8,0},{9,1},... | collective-permute-start | bytes 98312 | tf_op jit(solution)/shard_map/ppermute | solution.py:29
  50.7 1.3 %collective-permute-start.14 = (f32[16,1024]{1,0:T(8,128)S(1)}, f32[16,1024]{1,0:T(8,128)S(1)}, u32[]{:S(2)}, u32[]{:S(2)}) collective-permute-start(f32[16,1024]{1,0:T(8,128)S(1)} %image_rows.1), channel_id=1, source_target_pairs={{0,1},{1,0},{2,3},{3,2},{4,5},{5,4},{6,7},{7,6},{8,9},{9,8},{10,11... | collective-permute-start | bytes 196616 | tf_op jit(solution)/shard_map/ppermute | solution.py:29
  52.0 4.3 %collective-permute-start.15 = (f32[16,1024]{1,0:T(8,128)S(1)}, f32[16,1024]{1,0:T(8,128)S(1)}, u32[]{:S(2)}, u32[]{:S(2)}) collective-permute-start(f32[16,1024]{1,0:T(8,128)S(1)} %add.9), channel_id=1, source_target_pairs={{0,2},{1,3},{2,0},{3,1},{4,6},{5,7},{6,4},{7,5},{8,10},{9,11},{10,... | collective-permute-start | bytes 196616 | tf_op jit(solution)/shard_map/ppermute | solution.py:29
  56.3 4.3 %collective-permute-start.16 = (f32[16,1024]{1,0:T(8,128)S(1)}, f32[16,1024]{1,0:T(8,128)S(1)}, u32[]{:S(2)}, u32[]{:S(2)}) collective-permute-start(f32[16,1024]{1,0:T(8,128)S(1)} %add.10), channel_id=1, source_target_pairs={{0,4},{1,5},{2,6},{3,7},{4,0},{5,1},{6,2},{7,3},{8,12},{9,13},{10,... | collective-permute-start | bytes 196616 | tf_op jit(solution)/shard_map/ppermute | solution.py:29
  60.7 5.9 %collective-permute-start.17 = (f32[16,1024]{1,0:T(8,128)S(1)}, f32[16,1024]{1,0:T(8,128)S(1)}, u32[]{:S(2)}, u32[]{:S(2)}) collective-permute-start(f32[16,1024]{1,0:T(8,128)S(1)} %add.11.image_ref), channel_id=1, source_target_pairs={{0,8},{1,9},{2,10},{3,11},{4,12},{5,13},{6,14},{7,15},{8,0},{9,1},... | collective-permute-start | bytes 196616 | tf_op jit(solution)/shard_map/ppermute | solution.py:29
